TPU v7x, 32 devices: a whole 2x2x4 slice. The times are simulated.
32 devices in a mesh: req: 8 (over z, x), tp: 4 (over y, core).
Axes of the slice: x: 2, y: 2, z: 4, core: 2. Of those that a mesh axis runs over, the one named last changes fastest.
Arguments:
- hidden_in: bfloat16 [4096, 1024], P('req', 'tp'), may hold values from -6 to 6
- w_qkv: bfloat16 [1024, 3, 1024], P(None, None, 'tp'), may hold values from -0.1875 to 0.1875
- w_out: bfloat16 [1024, 1024], P('tp'), may hold values from -0.75 to 0.75
- first_gain: float32 [1024], replicated, may hold values from 0.1 to 1.9
- w_up: bfloat16 [1024, 4096], P(None, 'tp'), may hold values from -0.1875 to 0.1875
- w_down: bfloat16 [4096, 1024], P('tp'), may hold values from -0.09375 to 0.09375
- second_gain: float32 [1024], replicated, may hold values from 0.1 to 1.9
- cache_pool: bfloat16 [512, 128, 2, 1024], P('req', None, None, 'tp'), may hold values from -600 to 600
- page_table: int32 [64, 8], P('req'), may hold values from 0 to 63, as said below
- cache_len: int32 [64], P('req'), may hold values from 1 to 1024, as said below
- tree_parent: int32 [64, 64], P('req'), may hold values from -1 to 62, as said below
- accept_node: int32 [64], P('req'), may hold values from 0 to 63
Outputs:
- layer_out: bfloat16 [4096, 1024], P('req', 'tp')
- accepted_kv: bfloat16 [64, 64, 2, 1024], P('req', None, None, 'tp')
Inputs may be any that keep to these rules, and one draw needn't show every extreme that they name: `page_table`: on each index e of req, the 8 x 8 entries of its rows are a permutation of the slots 0 to 63; row j, column m holds the slot in e's pool of page j of member m of the index e - j of req (modulo the axis size). `cache_len`: on each index of req exactly 2 requests have lengths over 256, and the others at most 256; the length 1024 occurs in every draw, and so does the length 256. `tree_parent`: node 0 is the root with parent -1; every other node's parent is an earlier node.
All inputs are finite; a program needn't handle non-finite values.
Results may differ from a plain program's by a relative error of at most 0.012.
Values may be sent and summed in bfloat16 or wider, within the bound.
No kernel may reach another device: no remote copies, remote signals or barrier semaphores. Data moves between devices by JAX's collectives and lax.ppermute only.
A program may use at most 128 MiB of HBM per device.

v0:
```python
import functools

import jax
import jax.numpy as jnp
from jax import lax
from jax.experimental import pallas as pl
from jax.experimental.pallas import tpu as pltpu
from jax.sharding import PartitionSpec as P

HD = 64
NEG = -1e30
EPS = 1e-05
META = 16
F32 = jnp.float32
BF16 = jnp.bfloat16

VMEM = pl.BlockSpec(memory_space=pltpu.VMEM)
SMEM = pl.BlockSpec(memory_space=pltpu.SMEM)
ANY = pl.BlockSpec(memory_space=pl.ANY)


def shape_of(dims, dtype):
    return jax.ShapeDtypeStruct(dims, dtype)


def call(kernel, outs, ins, out_specs, scratch, operands, name, flops=0, nbytes=0, vmem=40):
    return pl.pallas_call(
        kernel,
        out_shape=outs,
        in_specs=ins,
        out_specs=out_specs,
        scratch_shapes=scratch,
        compiler_params=pltpu.CompilerParams(vmem_limit_bytes=vmem << 20),
        cost_estimate=pl.CostEstimate(flops=flops, bytes_accessed=nbytes, transcendentals=0),
        name=name,
    )(*operands)


def send_req(value, by):
    size = lax.axis_size("req")
    return lax.ppermute(value, "req", [(i, (i + by) % size) for i in range(size)])


def send_tp(value, flip):
    size = lax.axis_size("tp")
    return lax.ppermute(value, "tp", [(i, i ^ flip) for i in range(size)])


def write_order(len_ref, order_ref, requests, page_len):
    flags = [(len_ref[r] > 2 * page_len).astype(jnp.int32) for r in range(requests)]
    total = sum(flags)
    before = jnp.int32(0)
    for r in range(requests):
        place = jnp.where(flags[r] > 0, before, total + r - before)
        order_ref[place] = jnp.int32(r)
        before = before + flags[r]


def split3(value):
    high = value.astype(BF16)
    rest = value - high.astype(F32)
    middle = rest.astype(BF16)
    low = (rest - middle.astype(F32)).astype(BF16)
    return high, middle, low


def dot_t(a, b):
    return lax.dot_general(a, b, (((1,), (1,)), ((), ())), preferred_element_type=F32)


def head_rows(value, heads):
    lane = lax.broadcasted_iota(jnp.int32, value.shape, 1) // HD
    zero = jnp.zeros_like(value)
    return jnp.concatenate([jnp.where(lane == h, value, zero) for h in range(heads)], axis=0)


def head_lanes(stacked, heads, rows, width):
    lane = lax.broadcasted_iota(jnp.int32, (rows, width), 1) // HD
    out = jnp.zeros((rows, width), stacked.dtype)
    for h in range(heads):
        piece = stacked[h * rows : (h + 1) * rows]
        if piece.shape[1] != width:
            piece = jnp.broadcast_to(piece[:, :1], (rows, width))
        out = jnp.where(lane == h, piece, out)
    return out


def unpick(page_len):
    row = lax.broadcasted_iota(jnp.int32, (2 * page_len, 2 * page_len), 0)
    col = lax.broadcasted_iota(jnp.int32, (2 * page_len, 2 * page_len), 1)
    source = jnp.where(row < page_len, 2 * row, 2 * (row - page_len) + 1)
    return jnp.where(source == col, 1.0, 0.0).astype(BF16)


def split_page(page, picker, page_len):
    flat = page.reshape(2 * page_len, page.shape[2])
    both = jnp.dot(picker, flat, preferred_element_type=F32).astype(BF16)
    return both[:page_len], both[page_len:]


def to_row(column):
    return jnp.transpose(jnp.broadcast_to(column, (column.shape[0], 128)))[:1]


def attend(scores, masks, values):
    kept = [jnp.where(mask, score, NEG) for score, mask in zip(scores, masks)]
    top = functools.reduce(jnp.maximum, [jnp.max(s, axis=-1, keepdims=True) for s in kept])
    weights = [jnp.where(mask, jnp.exp(s - top), 0.0).astype(BF16) for s, mask in zip(kept, masks)]
    total = sum(jnp.sum(w.astype(F32), axis=-1, keepdims=True) for w in weights)
    mixed = sum(jnp.dot(w, v, preferred_element_type=F32) for w, v in zip(weights, values))
    return mixed, top, total


def pick_long_kernel(dims, len_ref, hidden_ref, out_ref, order_ref, sems):
    requests, draft, page_len, long_count = dims
    write_order(len_ref, order_ref, requests, page_len)
    copies = []
    for i in range(long_count):
        row = pl.multiple_of(order_ref[i] * draft, draft)
        copies.append(
            pltpu.make_async_copy(
                hidden_ref.at[pl.ds(row, draft)], out_ref.at[pl.ds(i * draft, draft)], sems.at[i]
            )
        )
    for copy in copies:
        copy.start()
    for copy in copies:
        copy.wait()


def pick_pages_kernel(dims, table_ref, pool_ref, out_ref, sems):
    requests, row = dims
    copies = [
        pltpu.make_async_copy(pool_ref.at[table_ref[row, m]], out_ref.at[m], sems.at[m])
        for m in range(requests)
    ]
    for copy in copies:
        copy.start()
    for copy in copies:
        copy.wait()


def long_query_kernel(dims, len_ref, own_ref, core_ref, y_ref, diag_ref, w_ref, out_ref, order_ref, wq_ref, sem):
    requests, page_len, long_count = dims
    copy = pltpu.make_async_copy(w_ref.at[0], wq_ref, sem)
    copy.start()
    me = lax.axis_index("tp")
    share = own_ref.shape[1]
    rows = own_ref.shape[0]
    width = wq_ref.shape[1]
    write_order(len_ref, order_ref, requests, page_len)
    row = lax.broadcasted_iota(jnp.int32, (META, width), 0)
    facts = jnp.zeros((META, width), jnp.int32)
    for i in range(long_count):
        member = order_ref[i]
        length = len_ref[member]
        facts = jnp.where(row == 3 * i, member, facts)
        facts = jnp.where(row == 3 * i + 1, length // page_len, facts)
        facts = jnp.where(row == 3 * i + 2, length % page_len, facts)
    out_ref[pl.ds(rows, META)] = facts.astype(F32).astype(BF16)
    copy.wait()
    total = jnp.zeros((rows, width), F32)
    for flip, ref in enumerate((own_ref, core_ref, y_ref, diag_ref)):
        at = pl.multiple_of((me ^ flip) * share, share)
        total += jnp.dot(ref[...], wq_ref[pl.ds(at, share), :], preferred_element_type=F32)
    out_ref[pl.ds(0, rows)] = (total * 0.125).astype(BF16)


def remote_kernel(dims, msg_ref, table_ref, pool_ref, out_ref, page_ref, sems):
    page_index, page_len, draft, heads, long_count = dims
    width = heads * HD
    tokens = long_count * draft
    facts = msg_ref[pl.ds(tokens, META), :].astype(F32)
    facts_row = lax.broadcasted_iota(jnp.int32, facts.shape, 0)

    def fact(k):
        return jnp.max(jnp.where(facts_row == k, facts, 0.0)).astype(jnp.int32)

    copies, limits = [], []
    for i in range(long_count):
        slot = table_ref[page_index, fact(3 * i)]
        copy = pltpu.make_async_copy(pool_ref.at[slot], page_ref.at[i], sems.at[i])
        copy.start()
        copies.append(copy)
        length = fact(3 * i + 1) * page_len + fact(3 * i + 2)
        limits.append(length - page_index * page_len)
    picker = unpick(page_len)
    lane = lax.broadcasted_iota(jnp.int32, (heads * draft, page_len), 1)
    stats = []
    for i in range(long_count):
        stacked = head_rows(msg_ref[pl.ds(i * draft, draft), :], heads)
        copies[i].wait()
        keys, values = split_page(page_ref[i], picker, page_len)
        mixed, top, total = attend([dot_t(stacked, keys)], [lane < limits[i]], [values])
        out_ref[pl.ds(i * draft, draft)] = head_lanes(mixed, heads, draft, width).astype(BF16)
        stats += list(split3(to_row(top))) + list(split3(to_row(total)))
    stats.append(jnp.zeros((META - len(stats), width), BF16))
    out_ref[pl.ds(tokens, META)] = jnp.concatenate([s.astype(F32) for s in stats], axis=0).astype(BF16)


def project_kernel(dims, accept_ref, own_ref, core_ref, y_ref, diag_ref, w_ref, parent_ref,
                   q_ref, k_ref, v_ref, reach_ref, acc_k_ref, acc_v_ref, wide_ref):
    requests, draft = dims
    me = lax.axis_index("tp")
    share = own_ref.shape[1]
    group = parent_ref.shape[1] // draft
    side = group * draft
    row = lax.broadcasted_iota(jnp.int32, (side, side), 0)
    col = lax.broadcasted_iota(jnp.int32, (side, side), 1)
    eye = jnp.where(row == col, 1.0, 0.0)
    up = []
    for g in range(requests // group):
        parent = parent_ref[pl.ds(g, 1), :]
        lane = lax.broadcasted_iota(jnp.int32, parent.shape, 1)
        target = jnp.where(parent < 0, -1, parent + (lane // draft) * draft)
        up.append((eye + jnp.where(row == target, 1.0, 0.0)).astype(BF16))
    for sweep in range(max(1, (draft - 1).bit_length())):
        up = [jnp.minimum(jnp.dot(u, u, preferred_element_type=F32), 1.0).astype(BF16) for u in up]
    for part, out in ((0, q_ref), (1, k_ref), (2, v_ref)):
        total = jnp.zeros(q_ref.shape, F32)
        for flip, ref in enumerate((own_ref, core_ref, y_ref, diag_ref)):
            at = pl.multiple_of((me ^ flip) * share, share)
            total += jnp.dot(ref[...], w_ref[part, pl.ds(at, share), :], preferred_element_type=F32)
        if part == 0:
            total = total * 0.125
        out[...] = total.astype(BF16)
    for g in range(requests // group):
        reach = jnp.transpose(up[g].astype(F32))
        wide_ref[...] = reach
        depth = jnp.sum(up[g].astype(F32), axis=0, keepdims=True) - 1.0
        chosen = jnp.zeros((1, side), F32)
        for i in range(group):
            r = g * group + i
            reach_ref[pl.ds(r * draft, draft), :] = reach[i * draft : (i + 1) * draft, i * draft : (i + 1) * draft]
            chosen += wide_ref[pl.ds(i * draft + accept_ref[r], 1), :]
        level = (row % draft).astype(F32)
        select = jnp.where((row // draft == col // draft) & (depth == level), chosen, 0.0).astype(BF16)
        rows = pl.ds(g * side, side)
        acc_k_ref[rows] = jnp.dot(select, k_ref[rows], preferred_element_type=F32).astype(BF16)
        acc_v_ref[rows] = jnp.dot(select, v_ref[rows], preferred_element_type=F32).astype(BF16)


def local_kernel(dims, len_ref, table_ref, q_ref, k_ref, v_ref, reach_ref, near_ref, pool_ref,
                 rest_ref, long_ref, stats_ref, order_ref, first_ref, second_ref, sems):
    requests, draft, heads, page_len, long_count = dims
    width = heads * HD
    write_order(len_ref, order_ref, requests, page_len)
    copies = []
    for p in range(requests):
        r = order_ref[p]
        one = pltpu.make_async_copy(pool_ref.at[table_ref[0, r]], first_ref.at[p], sems.at[p, 0])
        two = pltpu.make_async_copy(near_ref.at[r], second_ref.at[p], sems.at[p, 1])
        one.start()
        two.start()
        copies.append((one, two))
    picker = unpick(page_len)
    lane = lax.broadcasted_iota(jnp.int32, (heads * draft, page_len), 1)
    stats = []
    for p in range(requests):
        r = order_ref[p]
        rows = pl.ds(pl.multiple_of(r * draft, draft), draft)
        length = len_ref[r]
        stacked = head_rows(q_ref[rows, :], heads)
        tree_ok = jnp.concatenate([reach_ref[rows, :]] * heads, axis=0) > 0.5
        for copy in copies[p]:
            copy.wait()
        key_0, value_0 = split_page(first_ref[p], picker, page_len)
        key_1, value_1 = split_page(second_ref[p], picker, page_len)
        mixed, top, total = attend(
            [dot_t(stacked, k_ref[rows, :]), dot_t(stacked, key_0), dot_t(stacked, key_1)],
            [tree_ok, lane < length, lane < length - page_len],
            [v_ref[rows, :], value_0, value_1],
        )
        if p < long_count:
            long_ref[pl.ds(p * draft, draft)] = head_lanes(mixed, heads, draft, width)
            stats += [to_row(top), to_row(total)]
        else:
            whole = head_lanes(mixed, heads, draft, width) / head_lanes(total, heads, draft, width)
            rest_ref[pl.ds((p - long_count) * draft, draft)] = whole.astype(BF16)
    stats.append(jnp.zeros((META - len(stats), width), F32))
    stats_ref[...] = jnp.concatenate(stats, axis=0)


def merge_kernel(dims, count, own_ref, stats_ref, *refs):
    draft, heads, long_count = dims
    width = heads * HD
    msgs, out_ref = refs[:count], refs[count]
    tokens = long_count * draft
    own = stats_ref[...]
    facts = [ref[pl.ds(tokens, META), :].astype(F32) for ref in msgs]
    for i in range(long_count):
        tops = [own[2 * i : 2 * i + 1]]
        totals = [own[2 * i + 1 : 2 * i + 2]]
        for f in facts:
            b = 6 * i
            tops.append(f[b : b + 1] + f[b + 1 : b + 2] + f[b + 2 : b + 3])
            totals.append(f[b + 3 : b + 4] + f[b + 4 : b + 5] + f[b + 5 : b + 6])
        best = functools.reduce(jnp.maximum, tops)
        scales = [jnp.exp(t - best) for t in tops]
        denom = sum(s * t for s, t in zip(scales, totals))
        factors = jnp.concatenate([s / denom for s in scales] + [jnp.zeros((128 - len(scales), width), F32)], axis=0)
        factors = jnp.transpose(factors)
        rows = pl.ds(i * draft, draft)
        out = own_ref[rows, :] * head_lanes(factors[:, :1], heads, draft, width)
        for j, ref in enumerate(msgs):
            out += ref[rows, :].astype(F32) * head_lanes(factors[:, j + 1 : j + 2], heads, draft, width)
        out_ref[rows] = out.astype(BF16)


def norm(values, sums, squares, gain, width_all):
    center = sums / width_all
    spread = squares / width_all - center * center
    return (values - center) * lax.rsqrt(spread + EPS) * gain


def forward_kernel(dims, len_ref, *refs):
    requests, draft, page_len, first, count = dims
    att, hid, wout = refs[0:4], refs[4:8], refs[8:12]
    gain_ref, up_ref, down_ref = refs[12:15]
    parts, normed_ref = refs[15:19], refs[19]
    order_ref, z_ref, up_v, down_v, sems = refs[20:]
    copies = [
        pltpu.make_async_copy(up_ref, up_v, sems.at[0]),
        pltpu.make_async_copy(down_ref, down_v, sems.at[1]),
    ]
    for copy in copies:
        copy.start()
    me = lax.axis_index("tp")
    share = hid[0].shape[1]
    width_all = z_ref.shape[1]
    write_order(len_ref, order_ref, requests, page_len)
    for p in range(count):
        rows = pl.ds(pl.multiple_of(order_ref[first + p] * draft, draft), draft)
        for flip in range(4):
            at = pl.ds(pl.multiple_of((me ^ flip) * share, share), share)
            z_ref[pl.ds(p * draft, draft), at] = hid[flip][rows, :].astype(F32)
    branch = sum(jnp.dot(a[...], w[...], preferred_element_type=F32) for a, w in zip(att, wout))
    z = z_ref[...] + branch
    sums = jnp.sum(z, axis=-1, keepdims=True)
    squares = jnp.sum(z * z, axis=-1, keepdims=True)
    normed_wide = norm(z, sums, squares, gain_ref[...], width_all)
    normed = normed_wide.astype(BF16)
    z_ref[...] = normed_wide
    normed_ref[...] = z_ref[:, pl.ds(pl.multiple_of(me * share, share), share)].astype(BF16)
    copies[0].wait()
    inner = jnp.dot(normed, up_v[...], preferred_element_type=F32)
    inner = (0.5 * inner * (1.0 + lax.erf(inner * (0.5 ** 0.5)))).astype(BF16)
    copies[1].wait()
    for flip in range(4):
        at = pl.ds(pl.multiple_of((me ^ flip) * share, share), share)
        parts[flip][...] = jnp.dot(inner, down_v[:, at], preferred_element_type=F32).astype(BF16)


def gather_sum_kernel(a_ref, b_ref, c_ref, d_ref, normed_ref, x_ref, stats_ref):
    x = normed_ref[...].astype(F32) + (
        (a_ref[...].astype(F32) + b_ref[...].astype(F32)) + (c_ref[...].astype(F32) + d_ref[...].astype(F32))
    )
    x_ref[...] = x
    row = lax.broadcasted_iota(jnp.int32, stats_ref.shape, 0)
    sums = to_row(jnp.sum(x, axis=-1, keepdims=True))
    squares = to_row(jnp.sum(x * x, axis=-1, keepdims=True))
    stats_ref[...] = jnp.where(row == 0, sums, jnp.where(row == 1, squares, 0.0))


def finish_kernel(dims, len_ref, gain_ref, *refs):
    requests, draft, page_len, counts = dims
    order_ref = refs[-1]
    out_ref = refs[-2]
    me = lax.axis_index("tp")
    write_order(len_ref, order_ref, requests, page_len)
    share = out_ref.shape[1]
    gain = gain_ref[:, pl.ds(pl.multiple_of(me * share, share), share)]
    width_all = gain_ref.shape[1]
    place = 0
    for g, count in enumerate(counts):
        x_ref = refs[5 * g]
        stats = sum(ref[...] for ref in refs[5 * g + 1 : 5 * g + 5])
        stats = jnp.transpose(jnp.concatenate([stats] * (128 // stats.shape[0]), axis=0))
        y = norm(x_ref[...], stats[:, 0:1], stats[:, 1:2], gain, width_all).astype(BF16)
        for p in range(count):
            rows = pl.ds(pl.multiple_of(order_ref[place] * draft, draft), draft)
            out_ref[rows, :] = y[p * draft : (p + 1) * draft]
            place += 1


def shards(hidden_in, w_qkv, w_out, first_gain, w_up, w_down, second_gain, cache_pool,
           page_table, cache_len, tree_parent, accept_node):
    tokens, share = hidden_in.shape
    requests, draft = tree_parent.shape
    width = w_qkv.shape[2]
    heads = width // HD
    pages = page_table.shape[0]
    page_len = cache_pool.shape[1]
    width_all = w_qkv.shape[0]
    long_count = (requests + 3) // 4
    long_rows = long_count * draft
    msg_rows = long_rows + META
    side = 4 * draft
    dma = pltpu.SemaphoreType.DMA
    order = pltpu.SMEM((requests,), jnp.int32)

    w_planes = jnp.transpose(w_qkv, (1, 0, 2))
    gain_1 = first_gain.reshape(1, -1)
    gain_2 = second_gain.reshape(1, -1)
    parents = tree_parent.reshape(requests * draft // side, side)

    hidden_long = call(
        functools.partial(pick_long_kernel, (requests, draft, page_len, long_count)),
        shape_of((long_rows, share), BF16), [SMEM, ANY], VMEM, [order, dma((long_count,))],
        (cache_len, hidden_in), "pick_long",
    )
    long_core = send_tp(hidden_long, 1)
    long_y = send_tp(hidden_long, 2)
    long_diag = send_tp(long_y, 1)

    near = call(
        functools.partial(pick_pages_kernel, (requests, 1)),
        shape_of((requests,) + cache_pool.shape[1:], BF16), [SMEM, ANY], ANY, [dma((requests,))],
        (page_table, cache_pool), "pick_pages",
    )
    near = send_req(near, -1)

    message = call(
        functools.partial(long_query_kernel, (requests, page_len, long_count)),
        shape_of((msg_rows, width), BF16), [SMEM, VMEM, VMEM, VMEM, VMEM, ANY], VMEM,
        [order, pltpu.VMEM((width_all, width), BF16), dma(())],
        (cache_len, hidden_long, long_core, long_y, long_diag, w_planes), "long_queries",
        flops=2 * long_rows * width_all * width, nbytes=2 * width_all * width,
    )
    queue = sorted(range(2, pages), key=lambda j: (abs(2 * j - pages), j))
    asked = {j: send_req(message, j) for j in queue}

    hid_core = send_tp(hidden_in, 1)
    hid_y = send_tp(hidden_in, 2)
    hid_diag = send_tp(hid_y, 1)
    hid = (hidden_in, hid_core, hid_y, hid_diag)
    wout_core = send_tp(w_out, 1)
    wout_y = send_tp(w_out, 2)
    wout_diag = send_tp(wout_y, 1)
    wout = (w_out, wout_core, wout_y, wout_diag)

    block = shape_of((tokens, width), BF16)
    queries, key_new, value_new, reach, acc_k, acc_v = call(
        functools.partial(project_kernel, (requests, draft)),
        [block, block, block, shape_of((tokens, draft), F32), block, block],
        [SMEM] + [VMEM] * 6, [VMEM] * 6, [pltpu.VMEM((side, side), F32)],
        (accept_node, *hid, w_planes, parents), "project",
        flops=2 * tokens * width_all * width * 3, nbytes=2 * width_all * width * 3,
    )

    answers = []
    for j in queue:
        answer = call(
            functools.partial(remote_kernel, (j, page_len, draft, heads, long_count)),
            shape_of((msg_rows, width), BF16), [VMEM, SMEM, ANY], VMEM,
            [pltpu.VMEM((long_count,) + cache_pool.shape[1:], BF16), dma((long_count,))],
            (asked[j], page_table, cache_pool), "remote_%d" % j,
            flops=long_count * 6 * 256 ** 3, nbytes=long_count * 131072,
        )
        answers.append(send_req(answer, -j))

    rest, long_own, long_stats = call(
        functools.partial(local_kernel, (requests, draft, heads, page_len, long_count)),
        [shape_of((tokens - long_rows, width), BF16), shape_of((long_rows, width), F32), shape_of((META, width), F32)],
        [SMEM, SMEM, VMEM, VMEM, VMEM, VMEM, ANY, ANY], [VMEM] * 3,
        [order, pltpu.VMEM((requests,) + cache_pool.shape[1:], BF16),
         pltpu.VMEM((requests,) + cache_pool.shape[1:], BF16), dma((requests, 2))],
        (cache_len, page_table, queries, key_new, value_new, reach, near, cache_pool), "local_attention",
        flops=requests * 14 * 256 ** 3, nbytes=requests * 2 * 131072,
    )

    def forward(attended, first, count, name):
        rows = count * draft
        att_core = send_tp(attended, 1)
        att_y = send_tp(attended, 2)
        att_diag = send_tp(att_y, 1)
        part = shape_of((rows, share), BF16)
        outs = call(
            functools.partial(forward_kernel, (requests, draft, page_len, first, count)),
            [part] * 5, [SMEM] + [VMEM] * 13 + [ANY, ANY], [VMEM] * 5,
            [order, pltpu.VMEM((rows, width_all), F32), pltpu.VMEM(w_up.shape, BF16),
             pltpu.VMEM(w_down.shape, BF16), dma((2,))],
            (cache_len, attended, att_core, att_y, att_diag, *hid, *wout, gain_1, w_up, w_down), name,
            flops=2 * rows * width_all * (width_all + 2 * w_up.shape[1]), nbytes=3 * 2 * 1024 * 1024,
        )
        got = [send_tp(outs[flip], flip) for flip in (2, 3, 1)]
        x, stats = call(
            gather_sum_kernel,
            [shape_of((rows, share), F32), shape_of((8, rows), F32)], [VMEM] * 5, [VMEM] * 2, [],
            (outs[0], *got, outs[4]), name + "_sum",
        )
        return (x, stats) + tuple(send_tp(stats, flip) for flip in (2, 3, 1))

    tail_rest = forward(rest, long_count, requests - long_count, "forward_short")

    merged = call(
        functools.partial(merge_kernel, (draft, heads, long_count), len(answers)),
        shape_of((long_rows, width), BF16), [VMEM] * (2 + len(answers)), VMEM, [],
        (long_own, long_stats, *answers), "merge",
    )
    tail_long = forward(merged, 0, long_count, "forward_long")

    layer_out = call(
        functools.partial(finish_kernel, (requests, draft, page_len, (long_count, requests - long_count))),
        shape_of((tokens, share), BF16), [SMEM] + [VMEM] * 11, VMEM, [order],
        (cache_len, gain_2, *tail_long, *tail_rest), "finish",
    )
    accepted_kv = jnp.stack(
        [acc_k.reshape(requests, draft, width), acc_v.reshape(requests, draft, width)], axis=2
    )
    return (layer_out, accepted_kv)


def solution(mesh):
    placed = (
        P("req", "tp"),
        P(None, None, "tp"),
        P("tp", None),
        P(),
        P(None, "tp"),
        P("tp", None),
        P(),
        P("req", None, None, "tp"),
        P("req", None),
        P("req"),
        P("req", None),
        P("req"),
    )
    return jax.shard_map(
        shards,
        mesh=mesh,
        in_specs=placed,
        out_specs=(P("req", "tp"), P("req", None, None, "tp")),
        check_vma=False,
    )
```

profile of v0, /device:TPU:0, one launch (start us, length us, event | category | flops | bytes accessed | tf_op | source)
XLA Modules:
  0.0 134.8 jit_solution(16693379026023435826)
XLA Ops:
  0.6 3.4 %copy-done = bf16[64,128,2,256]{3,2,1,0:T(2,128)(2,1)S(1)} copy-done((bf16[64,128,2,256]{3,2,1,0:T(2,128)(2,1)S(1)}, bf16[64,128,2,256]{3,2,1,0:T(2,128)(2,1)}, u32[]{:S(2)}) %copy-start) | copy-done | bytes 8388632
  4.7 1.7 %pick_pages.1 = bf16[8,128,2,256]{3,2,1,0:T(2,128)(2,1)} custom-call(s32[8,8]{1,0:T(8,128)S(1)} %copy-done.8, bf16[64,128,2,256]{3,2,1,0:T(2,128)(2,1)S(1)} %copy-done), custom_call_target="tpu_custom_call" | custom-call | tf_op jit(solution)/shard_map/pick_pages/pallas_call | solution.py:27
  6.4 6.0 %collective-permute-start.3 = (bf16[8,128,2,256]{3,2,1,0:T(2,128)(2,1)}, bf16[8,128,2,256]{3,2,1,0:T(2,128)(2,1)S(1)}, u32[]{:S(2)}, u32[]{:S(2)}) collective-permute-start(bf16[8,128,2,256]{3,2,1,0:T(2,128)(2,1)} %pick_pages.1), channel_id=1, source_target_pairs={{0,28},{4,0},{8,4},{12,8},{16,12},{20,16},{24,20},{28,24},{1,29},{... | collective-permute-start | bytes 3145736 | tf_op jit(solution)/shard_map/ppermute | solution.py:41
  12.5 1.5 %collective-permute-start.1 = (bf16[512,256]{1,0:T(8,128)(2,1)S(1)}, bf16[512,256]{1,0:T(8,128)(2,1)}, u32[]{:S(2)}, u32[]{:S(2)}) collective-permute-start(bf16[512,256]{1,0:T(8,128)(2,1)S(1)} %copy-done.6), channel_id=1, source_target_pairs={{0,2},{1,3},{2,0},{3,1},{4,6},{5,7},{6,4},{7,5},{8,10},{9,11},{10,... | collective-permute-start | bytes 786440 | tf_op jit(solution)/shard_map/ppermute | solution.py:46
  14.5 7.3 %collective-permute-done.1.y_ref.refs_6_ = bf16[512,256]{1,0:T(8,128)(2,1)} collective-permute-done((bf16[512,256]{1,0:T(8,128)(2,1)S(1)}, bf16[512,256]{1,0:T(8,128)(2,1)}, u32[]{:S(2)}, u32[]{:S(2)}) %collective-permute-start.1) | collective-permute-done | bytes 262176 | tf_op jit(solution)/shard_map/ppermute | solution.py:46
  24.0 1.5 %collective-permute-start.5 = (bf16[128,256]{1,0:T(8,128)(2,1)S(1)}, bf16[128,256]{1,0:T(8,128)(2,1)}, u32[]{:S(2)}, u32[]{:S(2)}) collective-permute-start(bf16[128,256]{1,0:T(8,128)(2,1)S(1)} %pick_long.1.own_ref), channel_id=1, source_target_pairs={{0,2},{1,3},{2,0},{3,1},{4,6},{5,7},{6,4},{7,5},{8,10},{9,11},{10,... | collective-permute-start | bytes 196616 | tf_op jit(solution)/shard_map/ppermute | solution.py:46
  25.5 7.5 %collective-permute-done.5.y_ref = bf16[128,256]{1,0:T(8,128)(2,1)} collective-permute-done((bf16[128,256]{1,0:T(8,128)(2,1)S(1)}, bf16[128,256]{1,0:T(8,128)(2,1)}, u32[]{:S(2)}, u32[]{:S(2)}) %collective-permute-start.5) | collective-permute-done | bytes 65568 | tf_op jit(solution)/shard_map/ppermute | solution.py:46
  33.1 1.5 %collective-permute-done.6.diag_ref = bf16[128,256]{1,0:T(8,128)(2,1)} collective-permute-done((bf16[128,256]{1,0:T(8,128)(2,1)}, bf16[128,256]{1,0:T(8,128)(2,1)}, u32[]{:S(2)}, u32[]{:S(2)}) %collective-permute-start.6) | collective-permute-done | bytes 65568 | tf_op jit(solution)/shard_map/ppermute | solution.py:46
  34.6 1.2 long_queries.1
  37.0 2.8 %collective-permute-start.11 = (bf16[144,256]{1,0:T(8,128)(2,1)S(1)}, bf16[144,256]{1,0:T(8,128)(2,1)S(1)}, u32[]{:S(2)}, u32[]{:S(2)}) collective-permute-start(bf16[144,256]{1,0:T(8,128)(2,1)S(1)} %long_queries.1), channel_id=1, source_target_pairs={{0,20},{4,24},{8,28},{12,0},{16,4},{20,8},{24,12},{28,16},{1,21},{... | collective-permute-start | bytes 221192 | tf_op jit(solution)/shard_map/ppermute | solution.py:41
  39.8 3.6 %project.1 = (bf16[512,256]{1,0:T(8,128)(2,1)S(1)}, bf16[512,256]{1,0:T(8,128)(2,1)S(1)}, bf16[512,256]{1,0:T(8,128)(2,1)S(1)}, f32[512,64]{1,0:T(8,128)S(1)}, b...) custom-call(s32[8]{0:T(128)S(1)} %copy-done.17, bf16[512,256]{1,0:T(8,128)(2,1)S(1)} %copy-done.6, ...), custom_call_target="tpu_custom_call" | custom-call | flops 805306368 | bytes 1572864 | tf_op jit(solution)/shard_map/project/pallas_call | solution.py:27
  45.8 2.9 %collective-permute-start.15 = (bf16[144,256]{1,0:T(8,128)(2,1)S(1)}, bf16[144,256]{1,0:T(8,128)(2,1)S(1)}, u32[]{:S(2)}, u32[]{:S(2)}) collective-permute-start(bf16[144,256]{1,0:T(8,128)(2,1)S(1)} %long_queries.1), channel_id=1, source_target_pairs={{0,24},{4,28},{8,0},{12,4},{16,8},{20,12},{24,16},{28,20},{1,25},{... | collective-permute-start | bytes 221192 | tf_op jit(solution)/shard_map/ppermute | solution.py:41
  49.2 3.4 %copy-done.1 = bf16[64,128,2,256]{3,2,1,0:T(2,128)(2,1)S(1)} copy-done((bf16[64,128,2,256]{3,2,1,0:T(2,128)(2,1)S(1)}, bf16[64,128,2,256]{3,2,1,0:T(2,128)(2,1)}, u32[]{:S(2)}) %copy-start.1) | copy-done | bytes 8388632
  52.5 10.0 %local_attention.1 = (bf16[384,256]{1,0:T(8,128)(2,1)S(1)}, f32[128,256]{1,0:T(8,128)S(1)}, f32[16,256]{1,0:T(8,128)S(1)}) custom-call(s32[8]{0:T(128)S(1)} %copy-done.14, s32[8,8]{1,0:T(8,128)S(1)} %copy-done.9, bf16[512,256]{1,0:T(8,128)(2,1)S(1)} %get-tuple-element.25.q_ref, bf16[512,256]{1,0:T(8,128)(2,1)S(1)} %get-tuple-element.26.k_ref, ...), custom_call_target="tpu_custom_call" | custom-call | flops 1879048192 | bytes 2097152 | tf_op jit(solution)/shard_map/local_attention/pallas_call | solution.py:27
  62.6 1.6 %collective-permute-start.32 = (bf16[384,256]{1,0:T(8,128)(2,1)S(1)}, bf16[384,256]{1,0:T(8,128)(2,1)S(1)}, u32[]{:S(2)}, u32[]{:S(2)}) collective-permute-start(bf16[384,256]{1,0:T(8,128)(2,1)S(1)} %get-tuple-element.38.refs_0_), channel_id=1, source_target_pairs={{0,2},{1,3},{2,0},{3,1},{4,6},{5,7},{6,4},{7,5},{8,10},{9,11},{10,... | collective-permute-start | bytes 589832 | tf_op jit(solution)/shard_map/ppermute | solution.py:46
  64.2 2.7 %remote_4.1 = bf16[144,256]{1,0:T(8,128)(2,1)S(1)} custom-call(bf16[144,256]{1,0:T(8,128)(2,1)S(1)} %collective-permute-done.7.msg_ref, s32[8,8]{1,0:T(8,128)S(1)} %copy-done.9, bf16[64,128,2,256]{3,2,1,0:T(2,128)(2,1)S(1)} %copy-done.2), custom_call_target="tpu_custom_call" | custom-call | flops 201326592 | bytes 262144 | tf_op jit(solution)/shard_map/remote_4/pallas_call | solution.py:27
  68.0 2.7 %remote_3.1 = bf16[144,256]{1,0:T(8,128)(2,1)S(1)} custom-call(bf16[144,256]{1,0:T(8,128)(2,1)S(1)} %collective-permute-done.9.msg_ref, s32[8,8]{1,0:T(8,128)S(1)} %copy-done.9, bf16[64,128,2,256]{3,2,1,0:T(2,128)(2,1)S(1)} %copy-done.2), custom_call_target="tpu_custom_call" | custom-call | flops 201326592 | bytes 262144 | tf_op jit(solution)/shard_map/remote_3/pallas_call | solution.py:27
  70.7 2.9 %collective-permute-start.10 = (bf16[144,256]{1,0:T(8,128)(2,1)S(1)}, bf16[144,256]{1,0:T(8,128)(2,1)S(1)}, u32[]{:S(2)}, u32[]{:S(2)}) collective-permute-start(bf16[144,256]{1,0:T(8,128)(2,1)S(1)} %remote_3.1), channel_id=1, source_target_pairs={{0,20},{4,24},{8,28},{12,0},{16,4},{20,8},{24,12},{28,16},{1,21},{... | collective-permute-start | bytes 221192 | tf_op jit(solution)/shard_map/ppermute | solution.py:41
  73.6 2.7 %remote_5.1 = bf16[144,256]{1,0:T(8,128)(2,1)S(1)} custom-call(bf16[144,256]{1,0:T(8,128)(2,1)S(1)} %collective-permute-done.11.msg_ref, s32[8,8]{1,0:T(8,128)S(1)} %copy-done.9, bf16[64,128,2,256]{3,2,1,0:T(2,128)(2,1)S(1)} %copy-done.2), custom_call_target="tpu_custom_call" | custom-call | flops 201326592 | bytes 262144 | tf_op jit(solution)/shard_map/remote_5/pallas_call | solution.py:27
  76.6 2.7 %remote_2.1 = bf16[144,256]{1,0:T(8,128)(2,1)S(1)} custom-call(bf16[144,256]{1,0:T(8,128)(2,1)S(1)} %collective-permute-done.13.msg_ref, s32[8,8]{1,0:T(8,128)S(1)} %copy-done.9, bf16[64,128,2,256]{3,2,1,0:T(2,128)(2,1)S(1)} %copy-done.2), custom_call_target="tpu_custom_call" | custom-call | flops 201326592 | bytes 262144 | tf_op jit(solution)/shard_map/remote_2/pallas_call | solution.py:27
  79.3 5.1 %collective-permute-start.14 = (bf16[144,256]{1,0:T(8,128)(2,1)S(1)}, bf16[144,256]{1,0:T(8,128)(2,1)S(1)}, u32[]{:S(2)}, u32[]{:S(2)}) collective-permute-start(bf16[144,256]{1,0:T(8,128)(2,1)S(1)} %remote_2.1), channel_id=1, source_target_pairs={{0,24},{4,28},{8,0},{12,4},{16,8},{20,12},{24,16},{28,20},{1,25},{... | collective-permute-start | bytes 221192 | tf_op jit(solution)/shard_map/ppermute | solution.py:41
  84.3 2.7 %remote_6.1 = bf16[144,256]{1,0:T(8,128)(2,1)S(1)} custom-call(bf16[144,256]{1,0:T(8,128)(2,1)S(1)} %collective-permute-done.15.msg_ref, s32[8,8]{1,0:T(8,128)S(1)} %copy-done.9, bf16[64,128,2,256]{3,2,1,0:T(2,128)(2,1)S(1)} %copy-done.2), custom_call_target="tpu_custom_call" | custom-call | flops 201326592 | bytes 262144 | tf_op jit(solution)/shard_map/remote_6/pallas_call | solution.py:27
  87.7 2.7 %remote_7.1 = bf16[144,256]{1,0:T(8,128)(2,1)S(1)} custom-call(bf16[144,256]{1,0:T(8,128)(2,1)S(1)} %collective-permute-done.17.msg_ref, s32[8,8]{1,0:T(8,128)S(1)} %copy-done.9, bf16[64,128,2,256]{3,2,1,0:T(2,128)(2,1)S(1)} %copy-done.2), custom_call_target="tpu_custom_call" | custom-call | flops 201326592 | bytes 262144 | tf_op jit(solution)/shard_map/remote_7/pallas_call | solution.py:27
  90.4 2.9 %collective-permute-done.16.refs_4_ = bf16[144,256]{1,0:T(8,128)(2,1)S(1)} collective-permute-done((bf16[144,256]{1,0:T(8,128)(2,1)S(1)}, bf16[144,256]{1,0:T(8,128)(2,1)S(1)}, u32[]{:S(2)}, u32[]{:S(2)}) %collective-permute-start.16) | collective-permute-done | bytes 73760 | tf_op jit(solution)/shard_map/ppermute | solution.py:41
  93.2 7.0 %collective-permute-done.18.refs_5_ = bf16[144,256]{1,0:T(8,128)(2,1)S(1)} collective-permute-done((bf16[144,256]{1,0:T(8,128)(2,1)S(1)}, bf16[144,256]{1,0:T(8,128)(2,1)S(1)}, u32[]{:S(2)}, u32[]{:S(2)}) %collective-permute-start.18) | collective-permute-done | bytes 73760 | tf_op jit(solution)/shard_map/ppermute | solution.py:41
  101.7 3.8 %collective-permute-done.20.refs_2_ = bf16[128,256]{1,0:T(8,128)(2,1)S(1)} collective-permute-done((bf16[128,256]{1,0:T(8,128)(2,1)S(1)}, bf16[128,256]{1,0:T(8,128)(2,1)S(1)}, u32[]{:S(2)}, u32[]{:S(2)}) %collective-permute-start.20) | collective-permute-done | bytes 65568 | tf_op jit(solution)/shard_map/ppermute | solution.py:46
  105.5 5.1 %forward_short.1 = (bf16[384,256]{1,0:T(8,128)(2,1)S(1)}, bf16[384,256]{1,0:T(8,128)(2,1)S(1)}, bf16[384,256]{1,0:T(8,128)(2,1)S(1)}, bf16[384,256]{1,0:T(8,128)(2,1)S(1)}, bf16[384,256]{1,0:T(8,128)(2,1)S(1)}) custom-call(s32[8]{0:T(128)S(1)} %copy-done.14, bf16[384,256]{1,0:T(8,128)(2,1)S(1)} %get-tuple-element.38.refs_0_, ...), custom_call_target="tpu_custom_call" | custom-call | flops 2415919104 | bytes 6291456 | tf_op jit(solution)/shard_map/forward_short/pallas_call | solution.py:27
  111.2 1.3 collective-permute-start.35
  112.8 3.2 %forward_long.1 = (bf16[128,256]{1,0:T(8,128)(2,1)S(1)}, bf16[128,256]{1,0:T(8,128)(2,1)S(1)}, bf16[128,256]{1,0:T(8,128)(2,1)S(1)}, bf16[128,256]{1,0:T(8,128)(2,1)S(1)}, bf16[128,256]{1,0:T(8,128)(2,1)S(1)}) custom-call(s32[8]{0:T(128)S(1)} %copy-done.14, bf16[128,256]{1,0:T(8,128)(2,1)S(1)} %merge.1.refs_0_, ...), custom_call_target="tpu_custom_call" | custom-call | flops 805306368 | bytes 6291456 | tf_op jit(solution)/shard_map/forward_long/pallas_call | solution.py:27
  117.6 6.3 %collective-permute-done.25.b_ref = bf16[128,256]{1,0:T(8,128)(2,1)S(1)} collective-permute-done((bf16[128,256]{1,0:T(8,128)(2,1)S(1)}, bf16[128,256]{1,0:T(8,128)(2,1)S(1)}, u32[]{:S(2)}, u32[]{:S(2)}) %collective-permute-start.25) | collective-permute-done | bytes 65568 | tf_op jit(solution)/shard_map/ppermute | solution.py:46
  131.1 2.0 %pad_maximum_fusion = bf16[8,64,2,256]{3,2,1,0:T(2,128)(2,1)} fusion(bf16[8,64,1,256]{3,2,1,0:T(2,128)(2,1)S(1)} %copy.15, bf16[8,64,1,256]{3,2,1,0:T(2,128)(2,1)S(1)} %copy.14), kind=kLoop, calls=%fused_computation | loop fusion | flops 1048576 | bytes 1048576 | tf_op jit(solution)/shard_map/stack | solution.py:508
  133.1 1.7 %finish.1 = bf16[512,256]{1,0:T(8,128)(2,1)} custom-call(s32[8]{0:T(128)S(1)} %copy-done.14, f32[1,1024]{1,0:T(1,128)S(1)} %bitcast.11, f32[128,256]{1,0:T(8,128)S(1)} %get-tuple-element.36.refs_0_, f32[8,128]{1,0:T(8,128)S(1)} %get-tuple-element.37.refs_1_, f32[8,128]{1,0:T(8,128)S(1)} %collective-permute-done.28.refs_2_, ...), custom_call_target="tpu_custom_call" | custom-call | tf_op jit(solution)/shard_map/finish/pallas_call | solution.py:27
  (107 shorter events, 20.6 us)
Async XLA Ops:
  6.4 42.7 %collective-permute-start.3 = (bf16[8,128,2,256]{3,2,1,0:T(2,128)(2,1)}, bf16[8,128,2,256]{3,2,1,0:T(2,128)(2,1)S(1)}, u32[]{:S(2)}, u32[]{:S(2)}) collective-permute-start(bf16[8,128,2,256]{3,2,1,0:T(2,128)(2,1)} %pick_pages.1), channel_id=1, source_target_pairs={{0,28},{4,0},{8,4},{12,8},{16,12},{20,16},{24,20},{28,24},{1,29},{... | collective-permute-start | bytes 3145736 | tf_op jit(solution)/shard_map/ppermute | solution.py:41
  12.5 9.3 %collective-permute-start.1 = (bf16[512,256]{1,0:T(8,128)(2,1)S(1)}, bf16[512,256]{1,0:T(8,128)(2,1)}, u32[]{:S(2)}, u32[]{:S(2)}) collective-permute-start(bf16[512,256]{1,0:T(8,128)(2,1)S(1)} %copy-done.6), channel_id=1, source_target_pairs={{0,2},{1,3},{2,0},{3,1},{4,6},{5,7},{6,4},{7,5},{8,10},{9,11},{10,... | collective-permute-start | bytes 786440 | tf_op jit(solution)/shard_map/ppermute | solution.py:46
  14.0 34.7 %collective-permute-start.23 = (bf16[256,1024]{1,0:T(8,128)(2,1)S(1)}, bf16[256,1024]{1,0:T(8,128)(2,1)}, u32[]{:S(2)}, u32[]{:S(2)}) collective-permute-start(bf16[256,1024]{1,0:T(8,128)(2,1)S(1)} %copy-done.7), channel_id=1, source_target_pairs={{0,2},{1,3},{2,0},{3,1},{4,6},{5,7},{6,4},{7,5},{8,10},{9,11},{10,... | collective-permute-start | bytes 1572872 | tf_op jit(solution)/shard_map/ppermute | solution.py:46
  14.5 21.4 %collective-permute-start = (bf16[512,256]{1,0:T(8,128)(2,1)S(1)}, bf16[512,256]{1,0:T(8,128)(2,1)}, u32[]{:S(2)}, u32[]{:S(2)}) collective-permute-start(bf16[512,256]{1,0:T(8,128)(2,1)S(1)} %copy-done.6), channel_id=1, source_target_pairs={{0,1},{1,0},{2,3},{3,2},{4,5},{5,4},{6,7},{7,6},{8,9},{9,8},{10,11... | collective-permute-start | bytes 786440 | tf_op jit(solution)/shard_map/ppermute | solution.py:46
  21.8 15.2 %collective-permute-start.2 = (bf16[512,256]{1,0:T(8,128)(2,1)}, bf16[512,256]{1,0:T(8,128)(2,1)}, u32[]{:S(2)}, u32[]{:S(2)}) collective-permute-start(bf16[512,256]{1,0:T(8,128)(2,1)} %collective-permute-done.1.y_ref.refs_6_), channel_id=1, source_target_pairs={{0,1},{1,0},{2,3},{3,2},{4,5},{5,4},{6,7},{7,6},{8,9},{9,8},{10,11... | collective-permute-start | bytes 786440 | tf_op jit(solution)/shard_map/ppermute | solution.py:46
  24.0 9.0 %collective-permute-start.5 = (bf16[128,256]{1,0:T(8,128)(2,1)S(1)}, bf16[128,256]{1,0:T(8,128)(2,1)}, u32[]{:S(2)}, u32[]{:S(2)}) collective-permute-start(bf16[128,256]{1,0:T(8,128)(2,1)S(1)} %pick_long.1.own_ref), channel_id=1, source_target_pairs={{0,2},{1,3},{2,0},{3,1},{4,6},{5,7},{6,4},{7,5},{8,10},{9,11},{10,... | collective-permute-start | bytes 196616 | tf_op jit(solution)/shard_map/ppermute | solution.py:46
  35.8 9.0 %collective-permute-start.7 = (bf16[144,256]{1,0:T(8,128)(2,1)S(1)}, bf16[144,256]{1,0:T(8,128)(2,1)S(1)}, u32[]{:S(2)}, u32[]{:S(2)}) collective-permute-start(bf16[144,256]{1,0:T(8,128)(2,1)S(1)} %long_queries.1), channel_id=1, source_target_pairs={{0,16},{4,20},{8,24},{12,28},{16,0},{20,4},{24,8},{28,12},{1,17},{... | collective-permute-start | bytes 221192 | tf_op jit(solution)/shard_map/ppermute | solution.py:41
  35.9 8.9 %collective-permute-start.9 = (bf16[144,256]{1,0:T(8,128)(2,1)S(1)}, bf16[144,256]{1,0:T(8,128)(2,1)S(1)}, u32[]{:S(2)}, u32[]{:S(2)}) collective-permute-start(bf16[144,256]{1,0:T(8,128)(2,1)S(1)} %long_queries.1), channel_id=1, source_target_pairs={{0,12},{4,16},{8,20},{12,24},{16,28},{20,0},{24,4},{28,8},{1,13},{... | collective-permute-start | bytes 221192 | tf_op jit(solution)/shard_map/ppermute | solution.py:41
  37.0 8.8 %collective-permute-start.11 = (bf16[144,256]{1,0:T(8,128)(2,1)S(1)}, bf16[144,256]{1,0:T(8,128)(2,1)S(1)}, u32[]{:S(2)}, u32[]{:S(2)}) collective-permute-start(bf16[144,256]{1,0:T(8,128)(2,1)S(1)} %long_queries.1), channel_id=1, source_target_pairs={{0,20},{4,24},{8,28},{12,0},{16,4},{20,8},{24,12},{28,16},{1,21},{... | collective-permute-start | bytes 221192 | tf_op jit(solution)/shard_map/ppermute | solution.py:41
  44.8 56.9 %collective-permute-start.22 = (bf16[256,1024]{1,0:T(8,128)(2,1)S(1)}, bf16[256,1024]{1,0:T(8,128)(2,1)S(1)}, u32[]{:S(2)}, u32[]{:S(2)}) collective-permute-start(bf16[256,1024]{1,0:T(8,128)(2,1)S(1)} %copy-done.7), channel_id=1, source_target_pairs={{0,1},{1,0},{2,3},{3,2},{4,5},{5,4},{6,7},{7,6},{8,9},{9,8},{10,11... | collective-permute-start | bytes 1572872 | tf_op jit(solution)/shard_map/ppermute | solution.py:46
  44.9 17.7 %collective-permute-start.13 = (bf16[144,256]{1,0:T(8,128)(2,1)S(1)}, bf16[144,256]{1,0:T(8,128)(2,1)S(1)}, u32[]{:S(2)}, u32[]{:S(2)}) collective-permute-start(bf16[144,256]{1,0:T(8,128)(2,1)S(1)} %long_queries.1), channel_id=1, source_target_pairs={{0,8},{4,12},{8,16},{12,20},{16,24},{20,28},{24,0},{28,4},{1,9},{5... | collective-permute-start | bytes 221192 | tf_op jit(solution)/shard_map/ppermute | solution.py:41
  45.8 21.0 %collective-permute-start.15 = (bf16[144,256]{1,0:T(8,128)(2,1)S(1)}, bf16[144,256]{1,0:T(8,128)(2,1)S(1)}, u32[]{:S(2)}, u32[]{:S(2)}) collective-permute-start(bf16[144,256]{1,0:T(8,128)(2,1)S(1)} %long_queries.1), channel_id=1, source_target_pairs={{0,24},{4,28},{8,0},{12,4},{16,8},{20,12},{24,16},{28,20},{1,25},{... | collective-permute-start | bytes 221192 | tf_op jit(solution)/shard_map/ppermute | solution.py:41
  48.7 22.0 %collective-permute-start.17 = (bf16[144,256]{1,0:T(8,128)(2,1)S(1)}, bf16[144,256]{1,0:T(8,128)(2,1)S(1)}, u32[]{:S(2)}, u32[]{:S(2)}) collective-permute-start(bf16[144,256]{1,0:T(8,128)(2,1)S(1)} %long_queries.1), channel_id=1, source_target_pairs={{0,28},{4,0},{8,4},{12,8},{16,12},{20,16},{24,20},{28,24},{1,29},{... | collective-permute-start | bytes 221192 | tf_op jit(solution)/shard_map/ppermute | solution.py:41
  49.1 56.3 %collective-permute-start.24 = (bf16[256,1024]{1,0:T(8,128)(2,1)}, bf16[256,1024]{1,0:T(8,128)(2,1)S(1)}, u32[]{:S(2)}, u32[]{:S(2)}) collective-permute-start(bf16[256,1024]{1,0:T(8,128)(2,1)} %collective-permute-done.23.refs_10_), channel_id=1, source_target_pairs={{0,1},{1,0},{2,3},{3,2},{4,5},{5,4},{6,7},{7,6},{8,9},{9,8},{10,11... | collective-permute-start | bytes 1572872 | tf_op jit(solution)/shard_map/ppermute | solution.py:46
  62.6 24.6 %collective-permute-start.32 = (bf16[384,256]{1,0:T(8,128)(2,1)S(1)}, bf16[384,256]{1,0:T(8,128)(2,1)S(1)}, u32[]{:S(2)}, u32[]{:S(2)}) collective-permute-start(bf16[384,256]{1,0:T(8,128)(2,1)S(1)} %get-tuple-element.38.refs_0_), channel_id=1, source_target_pairs={{0,2},{1,3},{2,0},{3,1},{4,6},{5,7},{6,4},{7,5},{8,10},{9,11},{10,... | collective-permute-start | bytes 589832 | tf_op jit(solution)/shard_map/ppermute | solution.py:46
  66.8 9.4 %collective-permute-start.8 = (bf16[144,256]{1,0:T(8,128)(2,1)S(1)}, bf16[144,256]{1,0:T(8,128)(2,1)S(1)}, u32[]{:S(2)}, u32[]{:S(2)}) collective-permute-start(bf16[144,256]{1,0:T(8,128)(2,1)S(1)} %remote_4.1), channel_id=1, source_target_pairs={{0,16},{4,20},{8,24},{12,28},{16,0},{20,4},{24,8},{28,12},{1,17},{... | collective-permute-start | bytes 221192 | tf_op jit(solution)/shard_map/ppermute | solution.py:41
  70.7 8.6 %collective-permute-start.10 = (bf16[144,256]{1,0:T(8,128)(2,1)S(1)}, bf16[144,256]{1,0:T(8,128)(2,1)S(1)}, u32[]{:S(2)}, u32[]{:S(2)}) collective-permute-start(bf16[144,256]{1,0:T(8,128)(2,1)S(1)} %remote_3.1), channel_id=1, source_target_pairs={{0,20},{4,24},{8,28},{12,0},{16,4},{20,8},{24,12},{28,16},{1,21},{... | collective-permute-start | bytes 221192 | tf_op jit(solution)/shard_map/ppermute | solution.py:41
  76.3 10.7 %collective-permute-start.12 = (bf16[144,256]{1,0:T(8,128)(2,1)S(1)}, bf16[144,256]{1,0:T(8,128)(2,1)S(1)}, u32[]{:S(2)}, u32[]{:S(2)}) collective-permute-start(bf16[144,256]{1,0:T(8,128)(2,1)S(1)} %remote_5.1), channel_id=1, source_target_pairs={{0,12},{4,16},{8,20},{12,24},{16,28},{20,0},{24,4},{28,8},{1,13},{... | collective-permute-start | bytes 221192 | tf_op jit(solution)/shard_map/ppermute | solution.py:41
  79.3 7.8 %collective-permute-start.14 = (bf16[144,256]{1,0:T(8,128)(2,1)S(1)}, bf16[144,256]{1,0:T(8,128)(2,1)S(1)}, u32[]{:S(2)}, u32[]{:S(2)}) collective-permute-start(bf16[144,256]{1,0:T(8,128)(2,1)S(1)} %remote_2.1), channel_id=1, source_target_pairs={{0,24},{4,28},{8,0},{12,4},{16,8},{20,12},{24,16},{28,20},{1,25},{... | collective-permute-start | bytes 221192 | tf_op jit(solution)/shard_map/ppermute | solution.py:41
  87.0 6.2 %collective-permute-start.16 = (bf16[144,256]{1,0:T(8,128)(2,1)S(1)}, bf16[144,256]{1,0:T(8,128)(2,1)S(1)}, u32[]{:S(2)}, u32[]{:S(2)}) collective-permute-start(bf16[144,256]{1,0:T(8,128)(2,1)S(1)} %remote_6.1), channel_id=1, source_target_pairs={{0,8},{4,12},{8,16},{12,20},{16,24},{20,28},{24,0},{28,4},{1,9},{5... | collective-permute-start | bytes 221192 | tf_op jit(solution)/shard_map/ppermute | solution.py:41
  87.1 18.3 %collective-permute-start.31 = (bf16[384,256]{1,0:T(8,128)(2,1)S(1)}, bf16[384,256]{1,0:T(8,128)(2,1)S(1)}, u32[]{:S(2)}, u32[]{:S(2)}) collective-permute-start(bf16[384,256]{1,0:T(8,128)(2,1)S(1)} %get-tuple-element.38.refs_0_), channel_id=1, source_target_pairs={{0,1},{1,0},{2,3},{3,2},{4,5},{5,4},{6,7},{7,6},{8,9},{9,8},{10,11... | collective-permute-start | bytes 589832 | tf_op jit(solution)/shard_map/ppermute | solution.py:46
  87.2 18.3 %collective-permute-start.33 = (bf16[384,256]{1,0:T(8,128)(2,1)S(1)}, bf16[384,256]{1,0:T(8,128)(2,1)S(1)}, u32[]{:S(2)}, u32[]{:S(2)}) collective-permute-start(bf16[384,256]{1,0:T(8,128)(2,1)S(1)} %collective-permute-done.32.refs_2_), channel_id=1, source_target_pairs={{0,1},{1,0},{2,3},{3,2},{4,5},{5,4},{6,7},{7,6},{8,9},{9,8},{10,11... | collective-permute-start | bytes 589832 | tf_op jit(solution)/shard_map/ppermute | solution.py:46
  93.2 7.0 %collective-permute-start.18 = (bf16[144,256]{1,0:T(8,128)(2,1)S(1)}, bf16[144,256]{1,0:T(8,128)(2,1)S(1)}, u32[]{:S(2)}, u32[]{:S(2)}) collective-permute-start(bf16[144,256]{1,0:T(8,128)(2,1)S(1)} %remote_7.1), channel_id=1, source_target_pairs={{0,4},{4,8},{8,12},{12,16},{16,20},{20,24},{24,28},{28,0},{1,5},{5... | collective-permute-start | bytes 221192 | tf_op jit(solution)/shard_map/ppermute | solution.py:41
  101.7 11.1 %collective-permute-start.19 = (bf16[128,256]{1,0:T(8,128)(2,1)S(1)}, bf16[128,256]{1,0:T(8,128)(2,1)S(1)}, u32[]{:S(2)}, u32[]{:S(2)}) collective-permute-start(bf16[128,256]{1,0:T(8,128)(2,1)S(1)} %merge.1.refs_0_), channel_id=1, source_target_pairs={{0,1},{1,0},{2,3},{3,2},{4,5},{5,4},{6,7},{7,6},{8,9},{9,8},{10,11... | collective-permute-start | bytes 196616 | tf_op jit(solution)/shard_map/ppermute | solution.py:46
  105.5 7.3 %collective-permute-start.21 = (bf16[128,256]{1,0:T(8,128)(2,1)S(1)}, bf16[128,256]{1,0:T(8,128)(2,1)S(1)}, u32[]{:S(2)}, u32[]{:S(2)}) collective-permute-start(bf16[128,256]{1,0:T(8,128)(2,1)S(1)} %collective-permute-done.20.refs_2_), channel_id=1, source_target_pairs={{0,1},{1,0},{2,3},{3,2},{4,5},{5,4},{6,7},{7,6},{8,9},{9,8},{10,11... | collective-permute-start | bytes 196616 | tf_op jit(solution)/shard_map/ppermute | solution.py:46
  110.6 17.3 %collective-permute-start.34 = (bf16[384,256]{1,0:T(8,128)(2,1)S(1)}, bf16[384,256]{1,0:T(8,128)(2,1)S(1)}, u32[]{:S(2)}, u32[]{:S(2)}) collective-permute-start(bf16[384,256]{1,0:T(8,128)(2,1)S(1)} %get-tuple-element.40), channel_id=1, source_target_pairs={{0,2},{1,3},{2,0},{3,1},{4,6},{5,7},{6,4},{7,5},{8,10},{9,11},{10,... | collective-permute-start | bytes 589832 | tf_op jit(solution)/shard_map/ppermute | solution.py:46
  111.2 17.4 %collective-permute-start.35 = (bf16[384,256]{1,0:T(8,128)(2,1)S(1)}, bf16[384,256]{1,0:T(8,128)(2,1)S(1)}, u32[]{:S(2)}, u32[]{:S(2)}) collective-permute-start(bf16[384,256]{1,0:T(8,128)(2,1)S(1)} %get-tuple-element.41), channel_id=1, source_target_pairs={{0,3},{1,2},{2,1},{3,0},{4,7},{5,6},{6,5},{7,4},{8,11},{9,10},{10,... | collective-permute-start | bytes 589832 | tf_op jit(solution)/shard_map/ppermute | solution.py:46
  112.5 16.0 %collective-permute-start.36 = (bf16[384,256]{1,0:T(8,128)(2,1)S(1)}, bf16[384,256]{1,0:T(8,128)(2,1)S(1)}, u32[]{:S(2)}, u32[]{:S(2)}) collective-permute-start(bf16[384,256]{1,0:T(8,128)(2,1)S(1)} %get-tuple-element.42), channel_id=1, source_target_pairs={{0,1},{1,0},{2,3},{3,2},{4,5},{5,4},{6,7},{7,6},{8,9},{9,8},{10,11... | collective-permute-start | bytes 589832 | tf_op jit(solution)/shard_map/ppermute | solution.py:46
  116.0 8.0 %collective-permute-start.25 = (bf16[128,256]{1,0:T(8,128)(2,1)S(1)}, bf16[128,256]{1,0:T(8,128)(2,1)S(1)}, u32[]{:S(2)}, u32[]{:S(2)}) collective-permute-start(bf16[128,256]{1,0:T(8,128)(2,1)S(1)} %get-tuple-element.32), channel_id=1, source_target_pairs={{0,2},{1,3},{2,0},{3,1},{4,6},{5,7},{6,4},{7,5},{8,10},{9,11},{10,... | collective-permute-start | bytes 196616 | tf_op jit(solution)/shard_map/ppermute | solution.py:46
  116.6 8.0 %collective-permute-start.26 = (bf16[128,256]{1,0:T(8,128)(2,1)S(1)}, bf16[128,256]{1,0:T(8,128)(2,1)S(1)}, u32[]{:S(2)}, u32[]{:S(2)}) collective-permute-start(bf16[128,256]{1,0:T(8,128)(2,1)S(1)} %get-tuple-element.33), channel_id=1, source_target_pairs={{0,3},{1,2},{2,1},{3,0},{4,7},{5,6},{6,5},{7,4},{8,11},{9,10},{10,... | collective-permute-start | bytes 196616 | tf_op jit(solution)/shard_map/ppermute | solution.py:46
  126.9 6.2 %collective-permute-start.29 = (f32[8,128]{1,0:T(8,128)S(1)}, f32[8,128]{1,0:T(8,128)S(1)}, u32[]{:S(2)}, u32[]{:S(2)}) collective-permute-start(f32[8,128]{1,0:T(8,128)S(1)} %get-tuple-element.37.refs_1_), channel_id=1, source_target_pairs={{0,3},{1,2},{2,1},{3,0},{4,7},{5,6},{6,5},{7,4},{8,11},{9,10},{10,... | collective-permute-start | bytes 12296 | tf_op jit(solution)/shard_map/ppermute | solution.py:46
  127.9 5.2 %collective-permute-start.30 = (f32[8,128]{1,0:T(8,128)S(1)}, f32[8,128]{1,0:T(8,128)S(1)}, u32[]{:S(2)}, u32[]{:S(2)}) collective-permute-start(f32[8,128]{1,0:T(8,128)S(1)} %get-tuple-element.37.refs_1_), channel_id=1, source_target_pairs={{0,1},{1,0},{2,3},{3,2},{4,5},{5,4},{6,7},{7,6},{8,9},{9,8},{10,11... | collective-permute-start | bytes 12296 | tf_op jit(solution)/shard_map/ppermute | solution.py:46
  (27 other events, 275.5 us)
where the time goes:
time: 135 us
  Pallas kernels  44.5 us (33%)
  starting transfers between devices  38.9 us (29%)
  waiting for transfers between devices  38.6 us (29%)
  local copies, waits for them, and re-layouts  9.84 us (7%)
  other arithmetic  1.98 us (1%)
    pallas_call x17, Pallas kernels, call(): pl.pallas_call(kernel, out_shape=outs, in_specs=ins, out_specs=out_specs,...  44.5 us
    ppermute x27, waiting for transfers between devices, send_tp(): return lax.ppermute(value, 'tp', [(i, i ^ flip) for i in range(size)])  28.6 us
    ppermute x13, starting transfers between devices, send_req(): lax.ppermute(value, 'req', [(i, (i + by) % size) for i in range(size)])  23.8 us
    ppermute x27, starting transfers between devices, send_tp(): return lax.ppermute(value, 'tp', [(i, i ^ flip) for i in range(size)])  15.1 us
    ppermute x13, waiting for transfers between devices, send_req(): lax.ppermute(value, 'req', [(i, (i + by) % size) for i in range(size)])  9.96 us
    unnamed x38, local copies, waits for them, and re-layouts  8.9 us
  transfers between devices with their start and end apart: 40, of which 10 were waited for; matrix products, arithmetic and copies ran while one was open for 2% of the time, Pallas kernels for 30%

commit v1 on v0

v1 whole, which is shorter than its diff:
```python
import functools

import jax
import jax.numpy as jnp
from jax import lax
from jax.experimental import pallas as pl
from jax.experimental.pallas import tpu as pltpu
from jax.sharding import PartitionSpec as P

HD = 64
NEG = -1e30
EPS = 1e-05
META = 16
F32 = jnp.float32
BF16 = jnp.bfloat16

VMEM = pl.BlockSpec(memory_space=pltpu.VMEM)
SMEM = pl.BlockSpec(memory_space=pltpu.SMEM)
ANY = pl.BlockSpec(memory_space=pl.ANY)
HBM = pl.BlockSpec(memory_space=pltpu.HBM)


def shape_of(dims, dtype):
    return jax.ShapeDtypeStruct(dims, dtype)


def call(kernel, outs, ins, out_specs, scratch, operands, name, flops=0, nbytes=0, after=()):
    split = len(operands)

    def body(*refs):
        kernel(*refs[:split], *refs[split + len(after) :])

    return pl.pallas_call(
        body,
        out_shape=outs,
        in_specs=list(ins) + [ANY] * len(after),
        out_specs=out_specs,
        scratch_shapes=scratch,
        compiler_params=pltpu.CompilerParams(vmem_limit_bytes=24 << 20),
        cost_estimate=pl.CostEstimate(flops=flops, bytes_accessed=nbytes, transcendentals=0),
        name=name,
    )(*operands, *after)


def send_req(value, by):
    size = lax.axis_size("req")
    return lax.ppermute(value, "req", [(i, (i + by) % size) for i in range(size)])


def send_tp(value, flip):
    size = lax.axis_size("tp")
    return lax.ppermute(value, "tp", [(i, i ^ flip) for i in range(size)])


def write_order(len_ref, order_ref, requests, page_len):
    flags = [(len_ref[r] > 2 * page_len).astype(jnp.int32) for r in range(requests)]
    total = sum(flags)
    before = jnp.int32(0)
    for r in range(requests):
        place = jnp.where(flags[r] > 0, before, total + r - before)
        order_ref[place] = jnp.int32(r)
        before = before + flags[r]


def split3(value):
    high = value.astype(BF16)
    rest = value - high.astype(F32)
    middle = rest.astype(BF16)
    low = (rest - middle.astype(F32)).astype(BF16)
    return high, middle, low


def dot_t(a, b):
    return lax.dot_general(a, b, (((1,), (1,)), ((), ())), preferred_element_type=F32)


def head_rows(value, heads):
    lane = lax.broadcasted_iota(jnp.int32, value.shape, 1) // HD
    zero = jnp.zeros_like(value)
    return jnp.concatenate([jnp.where(lane == h, value, zero) for h in range(heads)], axis=0)


def head_lanes(stacked, heads, rows, width):
    lane = lax.broadcasted_iota(jnp.int32, (rows, width), 1) // HD
    out = jnp.zeros((rows, width), stacked.dtype)
    for h in range(heads):
        piece = stacked[h * rows : (h + 1) * rows]
        if piece.shape[1] != width:
            piece = jnp.broadcast_to(piece[:, :1], (rows, width))
        out = jnp.where(lane == h, piece, out)
    return out


def unpick(page_len):
    row = lax.broadcasted_iota(jnp.int32, (2 * page_len, 2 * page_len), 0)
    col = lax.broadcasted_iota(jnp.int32, (2 * page_len, 2 * page_len), 1)
    source = jnp.where(row < page_len, 2 * row, 2 * (row - page_len) + 1)
    return jnp.where(source == col, 1.0, 0.0).astype(BF16)


def split_page(page, picker, page_len):
    flat = page.reshape(2 * page_len, page.shape[2])
    both = jnp.dot(picker, flat, preferred_element_type=F32).astype(BF16)
    return both[:page_len], both[page_len:]


def to_row(column):
    return jnp.transpose(jnp.broadcast_to(column, (column.shape[0], 128)))[:1]


def attend(scores, values):
    top = functools.reduce(jnp.maximum, [jnp.max(s, axis=-1, keepdims=True) for s in scores])
    weights = [jnp.exp(s - top).astype(BF16) for s in scores]
    total = sum(jnp.sum(w.astype(F32), axis=-1, keepdims=True) for w in weights)
    mixed = sum(jnp.dot(w, v, preferred_element_type=F32) for w, v in zip(weights, values))
    return mixed, top, total


def pick_pages_kernel(dims, table_ref, pool_ref, out_ref, sems):
    requests, row = dims
    copies = [
        pltpu.make_async_copy(pool_ref.at[table_ref[row, m]], out_ref.at[m], sems.at[m])
        for m in range(requests)
    ]
    for copy in copies:
        copy.start()
    for copy in copies:
        copy.wait()


def full_product(hid, w_ref, part):
    me = lax.axis_index("tp")
    share = hid[0].shape[1]
    total = None
    for flip, ref in enumerate(hid):
        at = pl.multiple_of((me ^ flip) * share, share)
        term = jnp.dot(ref[...], w_ref[part, pl.ds(at, share), :], preferred_element_type=F32)
        total = term if total is None else total + term
    return total


def tree_kernel(dims, accept_ref, parent_ref, bias_ref, select_ref, wide_ref):
    requests, draft = dims
    group = parent_ref.shape[1] // draft
    side = group * draft
    row = lax.broadcasted_iota(jnp.int32, (side, side), 0)
    col = lax.broadcasted_iota(jnp.int32, (side, side), 1)
    eye = jnp.where(row == col, 1.0, 0.0)
    up = []
    for g in range(requests // group):
        parent = parent_ref[pl.ds(g, 1), :]
        lane = lax.broadcasted_iota(jnp.int32, parent.shape, 1)
        target = jnp.where(parent < 0, -1, parent + (lane // draft) * draft)
        up.append((eye + jnp.where(row == target, 1.0, 0.0)).astype(BF16))
    for sweep in range(max(1, (draft - 1).bit_length())):
        up = [jnp.minimum(jnp.dot(u, u, preferred_element_type=F32), 1.0).astype(BF16) for u in up]
    row = lax.broadcasted_iota(jnp.int32, (2 * side, 2 * side), 0)
    col = lax.broadcasted_iota(jnp.int32, (2 * side, 2 * side), 1)
    fits = (row % 2 == col // side) & (row // (2 * draft) == (col % side) // draft)
    level = ((row // 2) % draft).astype(F32)
    for g in range(requests // group):
        wide = up[g].astype(F32)
        reach = jnp.transpose(wide)
        wide_ref[...] = reach
        depth = jnp.sum(wide, axis=0, keepdims=True) - 1.0
        chosen = jnp.zeros((1, side), F32)
        for i in range(group):
            r = g * group + i
            own = reach[i * draft : (i + 1) * draft, i * draft : (i + 1) * draft]
            bias_ref[pl.ds(r * draft, draft), :] = jnp.where(own > 0.5, 0.0, NEG)
            chosen += wide_ref[pl.ds(i * draft + accept_ref[r], 1), :]
        depth = jnp.concatenate([depth, depth], axis=1)
        chosen = jnp.concatenate([chosen, chosen], axis=1)
        select_ref[g] = jnp.where(fits & (depth == level), chosen, 0.0).astype(BF16)


def query_kernel(dims, len_ref, own_ref, core_ref, y_ref, diag_ref, w_ref, q_ref, out_ref, order_ref):
    requests, draft, page_len, long_count = dims
    rows = long_count * draft
    width = q_ref.shape[1]
    write_order(len_ref, order_ref, requests, page_len)
    row = lax.broadcasted_iota(jnp.int32, (META, width), 0)
    facts = jnp.zeros((META, width), jnp.int32)
    for i in range(long_count):
        member = order_ref[i]
        length = len_ref[member]
        facts = jnp.where(row == 3 * i, member, facts)
        facts = jnp.where(row == 3 * i + 1, length // page_len, facts)
        facts = jnp.where(row == 3 * i + 2, length % page_len, facts)
    out_ref[pl.ds(rows, META)] = facts.astype(F32).astype(BF16)
    q_ref[...] = (full_product((own_ref, core_ref, y_ref, diag_ref), w_ref, 0) * 0.125).astype(BF16)
    for i in range(long_count):
        at = pl.multiple_of(order_ref[i] * draft, draft)
        out_ref[pl.ds(i * draft, draft)] = q_ref[pl.ds(at, draft), :]


def key_value_kernel(own_ref, core_ref, y_ref, diag_ref, w_ref, select_ref, k_ref, v_ref, acc_ref):
    hid = (own_ref, core_ref, y_ref, diag_ref)
    k_ref[...] = full_product(hid, w_ref, 1).astype(BF16)
    v_ref[...] = full_product(hid, w_ref, 2).astype(BF16)
    groups, side = select_ref.shape[0], select_ref.shape[1] // 2
    for g in range(groups):
        rows = pl.ds(g * side, side)
        pairs = jnp.concatenate([k_ref[rows], v_ref[rows]], axis=0)
        path = jnp.dot(select_ref[g], pairs, preferred_element_type=F32).astype(BF16)
        acc_ref[rows] = path.reshape(side, 2, path.shape[1])


def remote_kernel(dims, page_indices, *refs):
    page_len, draft, heads, long_count = dims
    count = len(page_indices)
    msgs, table_ref, pool_ref = refs[:count], refs[count], refs[count + 1]
    outs = refs[count + 2 : 2 * count + 2]
    page_ref, sems = refs[2 * count + 2 :]
    width = heads * HD
    tokens = long_count * draft
    copies, limits = [], []
    for n, page_index in enumerate(page_indices):
        facts = msgs[n][pl.ds(tokens, META), :].astype(F32)[:, :page_len]
        for i in range(long_count):
            member = jnp.max(facts[3 * i : 3 * i + 1]).astype(jnp.int32)
            copy = pltpu.make_async_copy(
                pool_ref.at[table_ref[page_index, member]], page_ref.at[n, i], sems.at[n, i]
            )
            copy.start()
            copies.append(copy)
            length = facts[3 * i + 1 : 3 * i + 2] * page_len + facts[3 * i + 2 : 3 * i + 3]
            limits.append(length - page_index * page_len)
    picker = unpick(page_len)
    lane = lax.broadcasted_iota(jnp.int32, (heads * draft, page_len), 1).astype(F32)
    for copy in copies:
        copy.wait()
    for n in range(count):
        stats = []
        for i in range(long_count):
            stacked = head_rows(msgs[n][pl.ds(i * draft, draft), :], heads)
            keys, values = split_page(page_ref[n, i], picker, page_len)
            scores = jnp.where(lane < limits[n * long_count + i], dot_t(stacked, keys), NEG)
            mixed, top, total = attend([scores], [values])
            outs[n][pl.ds(i * draft, draft)] = head_lanes(mixed, heads, draft, width).astype(BF16)
            stats += list(split3(to_row(top))) + list(split3(to_row(total)))
        stats.append(jnp.zeros((META - len(stats), width), BF16))
        outs[n][pl.ds(tokens, META)] = jnp.concatenate([s.astype(F32) for s in stats], axis=0).astype(BF16)


def local_kernel(dims, len_ref, table_ref, q_ref, k_ref, v_ref, bias_ref, near_ref, pool_ref,
                 rest_ref, long_ref, stats_ref, order_ref, first_ref, second_ref, sems):
    requests, draft, heads, page_len, long_count = dims
    width = heads * HD
    write_order(len_ref, order_ref, requests, page_len)
    copies = []
    for p in range(requests):
        r = order_ref[p]
        copies.append(pltpu.make_async_copy(pool_ref.at[table_ref[0, r]], first_ref.at[p], sems.at[p, 0]))
        copies.append(pltpu.make_async_copy(near_ref.at[r], second_ref.at[p], sems.at[p, 1]))
    for copy in copies:
        copy.start()
    picker = unpick(page_len)
    lane = lax.broadcasted_iota(jnp.int32, (heads * draft, 2 * page_len), 1)
    for copy in copies:
        copy.wait()
    stats = []
    for p in range(requests):
        r = order_ref[p]
        rows = pl.ds(pl.multiple_of(r * draft, draft), draft)
        stacked = head_rows(q_ref[rows, :], heads)
        bias = jnp.concatenate([bias_ref[rows, :]] * heads, axis=0)
        key_0, value_0 = split_page(first_ref[p], picker, page_len)
        key_1, value_1 = split_page(second_ref[p], picker, page_len)
        paged = dot_t(stacked, jnp.concatenate([key_0, key_1], axis=0))
        mixed, top, total = attend(
            [jnp.where(lane < len_ref[r], paged, NEG), dot_t(stacked, k_ref[rows, :]) + bias],
            [jnp.concatenate([value_0, value_1], axis=0), v_ref[rows, :]],
        )
        if p < long_count:
            long_ref[pl.ds(p * draft, draft)] = head_lanes(mixed, heads, draft, width)
            stats += [to_row(top), to_row(total)]
        else:
            whole = head_lanes(mixed, heads, draft, width) / head_lanes(total, heads, draft, width)
            rest_ref[pl.ds((p - long_count) * draft, draft)] = whole.astype(BF16)
    stats.append(jnp.zeros((META - len(stats), width), F32))
    stats_ref[...] = jnp.concatenate(stats, axis=0)


def merge_kernel(dims, count, own_ref, stats_ref, *refs):
    draft, heads, long_count = dims
    width = heads * HD
    msgs, out_ref = refs[:count], refs[count]
    tokens = long_count * draft
    own = stats_ref[...]
    facts = [ref[pl.ds(tokens, META), :].astype(F32) for ref in msgs]
    for i in range(long_count):
        tops = [own[2 * i : 2 * i + 1]]
        totals = [own[2 * i + 1 : 2 * i + 2]]
        for f in facts:
            b = 6 * i
            tops.append(f[b : b + 1] + f[b + 1 : b + 2] + f[b + 2 : b + 3])
            totals.append(f[b + 3 : b + 4] + f[b + 4 : b + 5] + f[b + 5 : b + 6])
        best = functools.reduce(jnp.maximum, tops)
        scales = [jnp.exp(t - best) for t in tops]
        denom = sum(s * t for s, t in zip(scales, totals))
        factors = jnp.concatenate([s / denom for s in scales] + [jnp.zeros((128 - len(scales), width), F32)], axis=0)
        factors = jnp.transpose(factors)
        rows = pl.ds(i * draft, draft)
        out = own_ref[rows, :] * head_lanes(factors[:, :1], heads, draft, width)
        for j, ref in enumerate(msgs):
            out += ref[rows, :].astype(F32) * head_lanes(factors[:, j + 1 : j + 2], heads, draft, width)
        out_ref[rows] = out.astype(BF16)


def norm(values, sums, squares, gain, width_all):
    center = sums / width_all
    spread = squares / width_all - center * center
    return (values - center) * lax.rsqrt(spread + EPS) * gain


def forward_kernel(dims, len_ref, *refs):
    requests, draft, page_len, first, count = dims
    att, hid, wout = refs[0:4], refs[4:8], refs[8:12]
    gain_ref, up_ref, down_ref = refs[12:15]
    parts, normed_ref = refs[15:19], refs[19]
    order_ref, z_ref = refs[20:]
    me = lax.axis_index("tp")
    share = hid[0].shape[1]
    width_all = z_ref.shape[1]
    write_order(len_ref, order_ref, requests, page_len)
    for p in range(count):
        rows = pl.ds(pl.multiple_of(order_ref[first + p] * draft, draft), draft)
        for flip in range(4):
            at = pl.ds(pl.multiple_of((me ^ flip) * share, share), share)
            z_ref[pl.ds(p * draft, draft), at] = hid[flip][rows, :].astype(F32)
    branch = sum(jnp.dot(a[...], w[...], preferred_element_type=F32) for a, w in zip(att, wout))
    z = z_ref[...] + branch
    sums = jnp.sum(z, axis=-1, keepdims=True)
    squares = jnp.sum(z * z, axis=-1, keepdims=True)
    normed_wide = norm(z, sums, squares, gain_ref[...], width_all)
    normed = normed_wide.astype(BF16)
    z_ref[...] = normed_wide
    normed_ref[...] = z_ref[:, pl.ds(pl.multiple_of(me * share, share), share)].astype(BF16)
    inner = jnp.dot(normed, up_ref[...], preferred_element_type=F32)
    inner = (0.5 * inner * (1.0 + lax.erf(inner * (0.5 ** 0.5)))).astype(BF16)
    for flip in range(4):
        at = pl.ds(pl.multiple_of((me ^ flip) * share, share), share)
        parts[flip][...] = jnp.dot(inner, down_ref[:, at], preferred_element_type=F32).astype(BF16)


def gather_sum_kernel(a_ref, b_ref, c_ref, d_ref, normed_ref, x_ref, stats_ref):
    x = normed_ref[...].astype(F32) + (
        (a_ref[...].astype(F32) + b_ref[...].astype(F32)) + (c_ref[...].astype(F32) + d_ref[...].astype(F32))
    )
    x_ref[...] = x
    row = lax.broadcasted_iota(jnp.int32, stats_ref.shape, 0)
    sums = to_row(jnp.sum(x, axis=-1, keepdims=True))
    squares = to_row(jnp.sum(x * x, axis=-1, keepdims=True))
    stats_ref[...] = jnp.where(row == 0, sums, jnp.where(row == 1, squares, 0.0))


def finish_kernel(dims, len_ref, gain_ref, *refs):
    requests, draft, page_len, counts = dims
    order_ref = refs[-1]
    out_ref = refs[-2]
    me = lax.axis_index("tp")
    write_order(len_ref, order_ref, requests, page_len)
    share = out_ref.shape[1]
    gain = gain_ref[:, pl.ds(pl.multiple_of(me * share, share), share)]
    width_all = gain_ref.shape[1]
    place = 0
    for g, count in enumerate(counts):
        x_ref = refs[5 * g]
        stats = sum(ref[...] for ref in refs[5 * g + 1 : 5 * g + 5])
        stats = jnp.transpose(jnp.concatenate([stats] * (128 // stats.shape[0]), axis=0))
        y = norm(x_ref[...], stats[:, 0:1], stats[:, 1:2], gain, width_all).astype(BF16)
        for p in range(count):
            rows = pl.ds(pl.multiple_of(order_ref[place] * draft, draft), draft)
            out_ref[rows, :] = y[p * draft : (p + 1) * draft]
            place += 1


def shards(hidden_in, w_qkv, w_out, first_gain, w_up, w_down, second_gain, cache_pool,
           page_table, cache_len, tree_parent, accept_node):
    tokens, share = hidden_in.shape
    requests, draft = tree_parent.shape
    width = w_qkv.shape[2]
    heads = width // HD
    pages = page_table.shape[0]
    page_len = cache_pool.shape[1]
    width_all = w_qkv.shape[0]
    long_count = (requests + 3) // 4
    long_rows = long_count * draft
    msg_rows = long_rows + META
    side = 4 * draft
    dma = pltpu.SemaphoreType.DMA
    order = pltpu.SMEM((requests,), jnp.int32)

    w_planes = jnp.transpose(w_qkv, (1, 0, 2))
    gain_1 = first_gain.reshape(1, -1)
    gain_2 = second_gain.reshape(1, -1)
    parents = tree_parent.reshape(requests * draft // side, side)

    hid_y = send_tp(hidden_in, 2)
    hid_core = send_tp(hidden_in, 1)
    hid_diag = send_tp(hid_y, 1)
    hid = (hidden_in, hid_core, hid_y, hid_diag)
    near = call(
        functools.partial(pick_pages_kernel, (requests, 1)),
        shape_of((requests,) + cache_pool.shape[1:], BF16), [SMEM, HBM], HBM, [dma((requests,))],
        (page_table, cache_pool), "pick_pages", after=(hid_core,),
    )
    near = send_req(near, -1)

    bias, select = call(
        functools.partial(tree_kernel, (requests, draft)),
        [shape_of((tokens, draft), F32), shape_of((requests * draft // side, 2 * side, 2 * side), BF16)],
        [SMEM, VMEM], [VMEM] * 2, [pltpu.VMEM((side, side), F32)],
        (accept_node, parents), "tree", flops=14 * 256 ** 3 * 2,
    )

    block = shape_of((tokens, width), BF16)
    queries, message = call(
        functools.partial(query_kernel, (requests, draft, page_len, long_count)),
        [block, shape_of((msg_rows, width), BF16)],
        [SMEM] + [VMEM] * 5, [VMEM] * 2, [order],
        (cache_len, *hid, w_planes), "queries",
        flops=2 * tokens * width_all * width, nbytes=2 * width_all * width, after=(bias,),
    )
    queue = sorted(range(2, pages), key=lambda j: (abs(2 * j - pages), j))
    asked = {j: send_req(message, j) for j in queue}

    w_later, _ = lax.optimization_barrier((w_out, queries))
    wout_core = send_tp(w_later, 1)
    wout_y = send_tp(w_later, 2)
    wout_diag = send_tp(wout_y, 1)
    wout = (w_out, wout_core, wout_y, wout_diag)

    key_new, value_new, accepted = call(
        key_value_kernel,
        [block, block, shape_of((tokens, 2, width), BF16)],
        [VMEM] * 6, [VMEM] * 3, [],
        (*hid, w_planes, select), "keys_values",
        flops=2 * tokens * width_all * width * 2, nbytes=2 * width_all * width * 2, after=(message,),
    )

    answers, last = [], (key_new,)
    half = (len(queue) + 1) // 2
    for group in (queue[:half], queue[half:]):
        outs = call(
            functools.partial(remote_kernel, (page_len, draft, heads, long_count), tuple(group)),
            [shape_of((msg_rows, width), BF16)] * len(group),
            [VMEM] * len(group) + [SMEM, HBM], [VMEM] * len(group),
            [pltpu.VMEM((len(group), long_count) + cache_pool.shape[1:], BF16), dma((len(group), long_count))],
            (*[asked[j] for j in group], page_table, cache_pool), "remote_%d" % group[0],
            flops=len(group) * long_count * 6 * 256 ** 3, nbytes=len(group) * long_count * 131072, after=last,
        )
        answers += [send_req(answer, -j) for j, answer in zip(group, outs)]
        last = (outs[0],)

    rest, long_own, long_stats = call(
        functools.partial(local_kernel, (requests, draft, heads, page_len, long_count)),
        [shape_of((tokens - long_rows, width), BF16), shape_of((long_rows, width), F32), shape_of((META, width), F32)],
        [SMEM, SMEM, VMEM, VMEM, VMEM, VMEM, HBM, HBM], [VMEM] * 3,
        [order, pltpu.VMEM((requests,) + cache_pool.shape[1:], BF16),
         pltpu.VMEM((requests,) + cache_pool.shape[1:], BF16), dma((requests, 2))],
        (cache_len, page_table, queries, key_new, value_new, bias, near, cache_pool), "local_attention",
        flops=requests * 14 * 256 ** 3, nbytes=requests * 2 * 131072, after=last,
    )

    def forward(attended, first, count, name):
        rows = count * draft
        att_core = send_tp(attended, 1)
        att_y = send_tp(attended, 2)
        att_diag = send_tp(att_y, 1)
        part = shape_of((rows, share), BF16)
        outs = call(
            functools.partial(forward_kernel, (requests, draft, page_len, first, count)),
            [part] * 5, [SMEM] + [VMEM] * 15, [VMEM] * 5,
            [order, pltpu.VMEM((rows, width_all), F32)],
            (cache_len, attended, att_core, att_y, att_diag, *hid, *wout, gain_1, w_up, w_down), name,
            flops=2 * rows * width_all * (width_all + 2 * w_up.shape[1]), nbytes=3 * 2 * 1024 * 1024,
        )
        got = [send_tp(outs[flip], flip) for flip in (2, 3, 1)]
        x, stats = call(
            gather_sum_kernel,
            [shape_of((rows, share), F32), shape_of((8, rows), F32)], [VMEM] * 5, [VMEM] * 2, [],
            (outs[0], *got, outs[4]), name + "_sum",
        )
        return (x, stats) + tuple(send_tp(stats, flip) for flip in (2, 3, 1))

    tail_rest = forward(rest, long_count, requests - long_count, "forward_short")

    merged = call(
        functools.partial(merge_kernel, (draft, heads, long_count), len(answers)),
        shape_of((long_rows, width), BF16), [VMEM] * (2 + len(answers)), VMEM, [],
        (long_own, long_stats, *answers), "merge",
    )
    tail_long = forward(merged, 0, long_count, "forward_long")

    layer_out = call(
        functools.partial(finish_kernel, (requests, draft, page_len, (long_count, requests - long_count))),
        shape_of((tokens, share), BF16), [SMEM] + [VMEM] * 11, VMEM, [order],
        (cache_len, gain_2, *tail_long, *tail_rest), "finish",
    )
    accepted_kv = accepted.reshape(requests, draft, 2, width)
    return (layer_out, accepted_kv)


def solution(mesh):
    placed = (
        P("req", "tp"),
        P(None, None, "tp"),
        P("tp", None),
        P(),
        P(None, "tp"),
        P("tp", None),
        P(),
        P("req", None, None, "tp"),
        P("req", None),
        P("req"),
        P("req", None),
        P("req"),
    )
    return jax.shard_map(
        shards,
        mesh=mesh,
        in_specs=placed,
        out_specs=(P("req", "tp"), P("req", None, None, "tp")),
        check_vma=False,
    )
```

time: 135 us -> 126 us (0.933)
  Pallas kernels: 44.5 us -> 31.3 us
  waiting for transfers between devices: 38.6 us -> 49.2 us
  starting transfers between devices: 38.9 us -> 36.3 us
  local copies, waits for them, and re-layouts: 9.84 us -> 7.58 us
  other arithmetic: 1.98 us -> 0.01 us
    ppermute x13, waiting for transfers between devices: 9.96 us -> 42.6 us  [send_req(): lax.ppermute(value, 'req', [(i, (i + by) % size) for i in range(size)])]
    ppermute x27 -> x24, waiting for transfers between devices: 28.6 us -> 6.63 us  [send_tp(): return lax.ppermute(value, 'tp', [(i, i ^ flip) for i in range(size)])]
    pallas_call x17 -> x13, Pallas kernels: 44.5 us -> 31.3 us  [call(): pl.pallas_call(body, out_shape=outs, in_specs=list(ins) + [ANY] * len(aft...]
    ppermute x13, starting transfers between devices: 23.8 us -> 19.4 us  [send_req(): lax.ppermute(value, 'req', [(i, (i + by) % size) for i in range(size)])]
    another operation x1 -> x0, other arithmetic: 1.98 us -> none  [shards(): jnp.stack([acc_k.reshape(requests, draft, width), acc_v.reshape(requests,...]
    ppermute x27 -> x24, starting transfers between devices: 15.1 us -> 16.8 us  [send_tp(): return lax.ppermute(value, 'tp', [(i, i ^ flip) for i in range(size)])]
    unnamed x38 -> x32, local copies, waits for them, and re-layouts: 8.9 us -> 7.51 us
  transfers between devices with their start and end apart: 40 -> 37, of which waited for: 10 -> 11; matrix products, arithmetic and copies ran while one was open for 2% -> 0% of each run, Pallas kernels for 30% -> 24%
where the time goes in v1:
time: 126 us; the launch traced here: 125 us
  waiting for transfers between devices  49.2 us (39%)
  starting transfers between devices  36.3 us (29%)
  Pallas kernels  31.3 us (25%)
  local copies, waits for them, and re-layouts  7.58 us (6%)
    ppermute x13, waiting for transfers between devices, send_req(): lax.ppermute(value, 'req', [(i, (i + by) % size) for i in range(size)])  42.6 us
    pallas_call x13, Pallas kernels, call(): pl.pallas_call(body, out_shape=outs, in_specs=list(ins) + [ANY] * len(aft...  31.3 us
    ppermute x13, starting transfers between devices, send_req(): lax.ppermute(value, 'req', [(i, (i + by) % size) for i in range(size)])  19.4 us
    ppermute x24, starting transfers between devices, send_tp(): return lax.ppermute(value, 'tp', [(i, i ^ flip) for i in range(size)])  16.8 us
    unnamed x32, local copies, waits for them, and re-layouts  7.51 us
    ppermute x24, waiting for transfers between devices, send_tp(): return lax.ppermute(value, 'tp', [(i, i ^ flip) for i in range(size)])  6.63 us
  transfers between devices with their start and end apart: 37, of which 11 were waited for; matrix products, arithmetic and copies ran while one was open for 0% of the time, Pallas kernels for 24%

profile of v1, /device:TPU:0, one launch (start us, length us, event | category | flops | bytes accessed | tf_op | source)
XLA Modules:
  0.0 125.3 jit_solution(13910122045128122167)
XLA Ops:
  1.1 2.6 %collective-permute-start.1 = (bf16[512,256]{1,0:T(8,128)(2,1)}, bf16[512,256]{1,0:T(8,128)(2,1)S(1)}, u32[]{:S(2)}, u32[]{:S(2)}) collective-permute-start(bf16[512,256]{1,0:T(8,128)(2,1)} %refs_5_.3), channel_id=1, source_target_pairs={{0,2},{1,3},{2,0},{3,1},{4,6},{5,7},{6,4},{7,5},{8,10},{9,11},{10,... | collective-permute-start | bytes 786440 | tf_op jit(solution)/shard_map/ppermute | solution.py:52
  3.7 3.4 %copy-done = bf16[64,128,2,256]{3,2,1,0:T(2,128)(2,1)S(1)} copy-done((bf16[64,128,2,256]{3,2,1,0:T(2,128)(2,1)S(1)}, bf16[64,128,2,256]{3,2,1,0:T(2,128)(2,1)}, u32[]{:S(2)}) %copy-start) | copy-done | bytes 8388632
  7.8 1.7 %pick_pages.1 = bf16[8,128,2,256]{3,2,1,0:T(2,128)(2,1)} custom-call(s32[8,8]{1,0:T(8,128)S(1)} %copy-done.7, bf16[64,128,2,256]{3,2,1,0:T(2,128)(2,1)S(1)} %copy-done, bf16[512,256]{1,0:T(8,128)(2,1)S(1)} %collective-permute-done.refs_2_.refs_1_.refs_6_), custom_call_target="tpu_custom_call" | custom-call | tf_op jit(solution)/shard_map/pick_pages/pallas_call | solution.py:33
  9.6 4.7 %collective-permute-start.3 = (bf16[8,128,2,256]{3,2,1,0:T(2,128)(2,1)}, bf16[8,128,2,256]{3,2,1,0:T(2,128)(2,1)}, u32[]{:S(2)}, u32[]{:S(2)}) collective-permute-start(bf16[8,128,2,256]{3,2,1,0:T(2,128)(2,1)} %pick_pages.1), channel_id=1, source_target_pairs={{0,28},{4,0},{8,4},{12,8},{16,12},{20,16},{24,20},{28,24},{1,29},{... | collective-permute-start | bytes 3145736 | tf_op jit(solution)/shard_map/ppermute | solution.py:47
  14.4 2.3 %tree.1 = (f32[512,64]{1,0:T(8,128)S(1)}, bf16[2,512,512]{2,1,0:T(8,128)(2,1)S(1)}) custom-call(s32[8]{0:T(128)S(1)} %copy-done.12, s32[2,256]{1,0:T(2,128)S(1)} %reshape.17.refs_1_), custom_call_target="tpu_custom_call" | custom-call | flops 469762048 | tf_op jit(solution)/shard_map/tree/pallas_call | solution.py:33
  17.8 1.6 %collective-permute-start.20 = (bf16[256,1024]{1,0:T(8,128)(2,1)S(1)}, bf16[256,1024]{1,0:T(8,128)(2,1)S(1)}, u32[]{:S(2)}, u32[]{:S(2)}) collective-permute-start(bf16[256,1024]{1,0:T(8,128)(2,1)S(1)} %copy-done.6), channel_id=1, source_target_pairs={{0,2},{1,3},{2,0},{3,1},{4,6},{5,7},{6,4},{7,5},{8,10},{9,11},{10,... | collective-permute-start | bytes 1572872 | tf_op jit(solution)/shard_map/ppermute | solution.py:52
  19.4 1.9 %collective-permute-start.8 = (bf16[144,256]{1,0:T(8,128)(2,1)S(1)}, bf16[144,256]{1,0:T(8,128)(2,1)S(1)}, u32[]{:S(2)}, u32[]{:S(2)}) collective-permute-start(bf16[144,256]{1,0:T(8,128)(2,1)S(1)} %get-tuple-element.36.refs_6_), channel_id=1, source_target_pairs={{0,12},{4,16},{8,20},{12,24},{16,28},{20,0},{24,4},{28,8},{1,13},{... | collective-permute-start | bytes 221192 | tf_op jit(solution)/shard_map/ppermute | solution.py:47
  21.3 1.9 %collective-permute-start.9 = (bf16[144,256]{1,0:T(8,128)(2,1)S(1)}, bf16[144,256]{1,0:T(8,128)(2,1)S(1)}, u32[]{:S(2)}, u32[]{:S(2)}) collective-permute-start(bf16[144,256]{1,0:T(8,128)(2,1)S(1)} %get-tuple-element.36.refs_6_), channel_id=1, source_target_pairs={{0,20},{4,24},{8,28},{12,0},{16,4},{20,8},{24,12},{28,16},{1,21},{... | collective-permute-start | bytes 221192 | tf_op jit(solution)/shard_map/ppermute | solution.py:47
  23.2 21.0 %collective-permute-done.7.refs_0_ = bf16[144,256]{1,0:T(8,128)(2,1)S(1)} collective-permute-done((bf16[144,256]{1,0:T(8,128)(2,1)S(1)}, bf16[144,256]{1,0:T(8,128)(2,1)S(1)}, u32[]{:S(2)}, u32[]{:S(2)}) %collective-permute-start.7) | collective-permute-done | bytes 73760 | tf_op jit(solution)/shard_map/ppermute | solution.py:47
  44.2 3.8 %collective-permute-start.5 = (bf16[144,256]{1,0:T(8,128)(2,1)S(1)}, bf16[144,256]{1,0:T(8,128)(2,1)S(1)}, u32[]{:S(2)}, u32[]{:S(2)}) collective-permute-start(bf16[144,256]{1,0:T(8,128)(2,1)S(1)} %get-tuple-element.36.refs_6_), channel_id=1, source_target_pairs={{0,24},{4,28},{8,0},{12,4},{16,8},{20,12},{24,16},{28,20},{1,25},{... | collective-permute-start | bytes 221192 | tf_op jit(solution)/shard_map/ppermute | solution.py:47
  48.0 2.4 %collective-permute-start.6 = (bf16[144,256]{1,0:T(8,128)(2,1)S(1)}, bf16[144,256]{1,0:T(8,128)(2,1)S(1)}, u32[]{:S(2)}, u32[]{:S(2)}) collective-permute-start(bf16[144,256]{1,0:T(8,128)(2,1)S(1)} %get-tuple-element.36.refs_6_), channel_id=1, source_target_pairs={{0,28},{4,0},{8,4},{12,8},{16,12},{20,16},{24,20},{28,24},{1,29},{... | collective-permute-start | bytes 221192 | tf_op jit(solution)/shard_map/ppermute | solution.py:47
  50.4 1.9 %keys_values.1 = (bf16[512,256]{1,0:T(8,128)(2,1)S(1)}, bf16[512,256]{1,0:T(8,128)(2,1)S(1)}, bf16[512,2,256]{2,1,0:T(2,128)(2,1)}) custom-call(bf16[512,256]{1,0:T(8,128)(2,1)S(1)} %copy-done.3, bf16[512,256]{1,0:T(8,128)(2,1)S(1)} %collective-permute-done.refs_2_.refs_1_.refs_6_, bf16[512,256]{1,0:T(8,128)(2,1)S(1)} %collective-permute-done.1.refs_3_.refs_2_.refs_7_, ...), custom_call_target="tpu_custom_call" | custom-call | flops 536870912 | bytes 1048576 | tf_op jit(solution)/shard_map/keys_values/pallas_call | solution.py:33
  52.3 3.4 %copy-done.1 = bf16[64,128,2,256]{3,2,1,0:T(2,128)(2,1)S(1)} copy-done((bf16[64,128,2,256]{3,2,1,0:T(2,128)(2,1)S(1)}, bf16[64,128,2,256]{3,2,1,0:T(2,128)(2,1)}, u32[]{:S(2)}) %copy-start.1) | copy-done | bytes 8388632
  55.7 4.7 %remote_4.1 = (bf16[144,256]{1,0:T(8,128)(2,1)S(1)}, bf16[144,256]{1,0:T(8,128)(2,1)S(1)}, bf16[144,256]{1,0:T(8,128)(2,1)S(1)}) custom-call(bf16[144,256]{1,0:T(8,128)(2,1)S(1)} %collective-permute-done.7.refs_0_, bf16[144,256]{1,0:T(8,128)(2,1)S(1)} %collective-permute-done.8.refs_1_, bf16[144,256]{1,0:T(8,128)(2,1)S(1)} %collective-permute-done.9.refs_2_, ...), custom_call_target="tpu_custom_call" | custom-call | flops 603979776 | bytes 786432 | tf_op jit(solution)/shard_map/remote_4/pallas_call | solution.py:33
  60.5 4.7 %remote_2.1 = (bf16[144,256]{1,0:T(8,128)(2,1)S(1)}, bf16[144,256]{1,0:T(8,128)(2,1)S(1)}, bf16[144,256]{1,0:T(8,128)(2,1)S(1)}) custom-call(bf16[144,256]{1,0:T(8,128)(2,1)S(1)} %collective-permute-done.4.refs_0_, bf16[144,256]{1,0:T(8,128)(2,1)S(1)} %collective-permute-done.5.refs_1_, bf16[144,256]{1,0:T(8,128)(2,1)S(1)} %collective-permute-done.6.refs_2_, ...), custom_call_target="tpu_custom_call" | custom-call | flops 603979776 | bytes 786432 | tf_op jit(solution)/shard_map/remote_2/pallas_call | solution.py:33
  65.8 6.4 %local_attention.1 = (bf16[384,256]{1,0:T(8,128)(2,1)S(1)}, f32[128,256]{1,0:T(8,128)S(1)}, f32[16,256]{1,0:T(8,128)S(1)}) custom-call(s32[8]{0:T(128)S(1)} %copy-done.9, s32[8,8]{1,0:T(8,128)S(1)} %copy-done.8, bf16[512,256]{1,0:T(8,128)(2,1)S(1)} %get-tuple-element.34.refs_2_, bf16[512,256]{1,0:T(8,128)(2,1)S(1)} %get-tuple-element.37.refs_5_.refs_3_, ...), custom_call_target="tpu_custom_call" | custom-call | flops 1879048192 | bytes 2097152 | tf_op jit(solution)/shard_map/local_attention/pallas_call | solution.py:33
  72.3 1.6 %collective-permute-start.29 = (bf16[384,256]{1,0:T(8,128)(2,1)S(1)}, bf16[384,256]{1,0:T(8,128)(2,1)S(1)}, u32[]{:S(2)}, u32[]{:S(2)}) collective-permute-start(bf16[384,256]{1,0:T(8,128)(2,1)S(1)} %get-tuple-element.55.refs_1_), channel_id=1, source_target_pairs={{0,2},{1,3},{2,0},{3,1},{4,6},{5,7},{6,4},{7,5},{8,10},{9,11},{10,... | collective-permute-start | bytes 589832 | tf_op jit(solution)/shard_map/ppermute | solution.py:52
  73.9 2.0 %collective-permute-start.11 = (bf16[144,256]{1,0:T(8,128)(2,1)S(1)}, bf16[144,256]{1,0:T(8,128)(2,1)S(1)}, u32[]{:S(2)}, u32[]{:S(2)}) collective-permute-start(bf16[144,256]{1,0:T(8,128)(2,1)S(1)} %get-tuple-element.43), channel_id=1, source_target_pairs={{0,20},{4,24},{8,28},{12,0},{16,4},{20,8},{24,12},{28,16},{1,21},{... | collective-permute-start | bytes 221192 | tf_op jit(solution)/shard_map/ppermute | solution.py:47
  75.9 4.9 %collective-permute-done.10.refs_2_ = bf16[144,256]{1,0:T(8,128)(2,1)S(1)} collective-permute-done((bf16[144,256]{1,0:T(8,128)(2,1)S(1)}, bf16[144,256]{1,0:T(8,128)(2,1)S(1)}, u32[]{:S(2)}, u32[]{:S(2)}) %collective-permute-start.10) | collective-permute-done | bytes 73760 | tf_op jit(solution)/shard_map/ppermute | solution.py:47
  80.7 1.8 %collective-permute-start.13 = (bf16[144,256]{1,0:T(8,128)(2,1)S(1)}, bf16[144,256]{1,0:T(8,128)(2,1)S(1)}, u32[]{:S(2)}, u32[]{:S(2)}) collective-permute-start(bf16[144,256]{1,0:T(8,128)(2,1)S(1)} %get-tuple-element.40.refs_8_), channel_id=1, source_target_pairs={{0,24},{4,28},{8,0},{12,4},{16,8},{20,12},{24,16},{28,20},{1,25},{... | collective-permute-start | bytes 221192 | tf_op jit(solution)/shard_map/ppermute | solution.py:47
  82.6 4.3 %collective-permute-done.12.refs_4_ = bf16[144,256]{1,0:T(8,128)(2,1)S(1)} collective-permute-done((bf16[144,256]{1,0:T(8,128)(2,1)S(1)}, bf16[144,256]{1,0:T(8,128)(2,1)S(1)}, u32[]{:S(2)}, u32[]{:S(2)}) %collective-permute-start.12) | collective-permute-done | bytes 73760 | tf_op jit(solution)/shard_map/ppermute | solution.py:47
  87.4 6.1 %collective-permute-done.14.refs_6_ = bf16[144,256]{1,0:T(8,128)(2,1)S(1)} collective-permute-done((bf16[144,256]{1,0:T(8,128)(2,1)S(1)}, bf16[144,256]{1,0:T(8,128)(2,1)S(1)}, u32[]{:S(2)}, u32[]{:S(2)}) %collective-permute-start.14) | collective-permute-done | bytes 73760 | tf_op jit(solution)/shard_map/ppermute | solution.py:47
  94.4 6.2 %collective-permute-done.15.refs_7_ = bf16[144,256]{1,0:T(8,128)(2,1)S(1)} collective-permute-done((bf16[144,256]{1,0:T(8,128)(2,1)S(1)}, bf16[144,256]{1,0:T(8,128)(2,1)S(1)}, u32[]{:S(2)}, u32[]{:S(2)}) %collective-permute-start.15) | collective-permute-done | bytes 73760 | tf_op jit(solution)/shard_map/ppermute | solution.py:47
  102.0 3.7 %forward_short.1 = (bf16[384,256]{1,0:T(8,128)(2,1)S(1)}, bf16[384,256]{1,0:T(8,128)(2,1)S(1)}, bf16[384,256]{1,0:T(8,128)(2,1)S(1)}, bf16[384,256]{1,0:T(8,128)(2,1)S(1)}, bf16[384,256]{1,0:T(8,128)(2,1)S(1)}) custom-call(s32[8]{0:T(128)S(1)} %copy-done.9, bf16[384,256]{1,0:T(8,128)(2,1)S(1)} %get-tuple-element.55.refs_1_, ...), custom_call_target="tpu_custom_call" | custom-call | flops 2415919104 | bytes 6291456 | tf_op jit(solution)/shard_map/forward_short/pallas_call | solution.py:33
  105.7 1.6 %collective-permute-start.31 = (bf16[384,256]{1,0:T(8,128)(2,1)S(1)}, bf16[384,256]{1,0:T(8,128)(2,1)S(1)}, u32[]{:S(2)}, u32[]{:S(2)}) collective-permute-start(bf16[384,256]{1,0:T(8,128)(2,1)S(1)} %get-tuple-element.57), channel_id=1, source_target_pairs={{0,2},{1,3},{2,0},{3,1},{4,6},{5,7},{6,4},{7,5},{8,10},{9,11},{10,... | collective-permute-start | bytes 589832 | tf_op jit(solution)/shard_map/ppermute | solution.py:52
  108.7 1.9 %forward_long.1 = (bf16[128,256]{1,0:T(8,128)(2,1)S(1)}, bf16[128,256]{1,0:T(8,128)(2,1)S(1)}, bf16[128,256]{1,0:T(8,128)(2,1)S(1)}, bf16[128,256]{1,0:T(8,128)(2,1)S(1)}, bf16[128,256]{1,0:T(8,128)(2,1)S(1)}) custom-call(s32[8]{0:T(128)S(1)} %copy-done.9, bf16[128,256]{1,0:T(8,128)(2,1)S(1)} %merge.1.refs_1_, ...), custom_call_target="tpu_custom_call" | custom-call | flops 805306368 | bytes 6291456 | tf_op jit(solution)/shard_map/forward_long/pallas_call | solution.py:33
  110.7 1.3 %collective-permute-start.22 = (bf16[128,256]{1,0:T(8,128)(2,1)S(1)}, bf16[128,256]{1,0:T(8,128)(2,1)S(1)}, u32[]{:S(2)}, u32[]{:S(2)}) collective-permute-start(bf16[128,256]{1,0:T(8,128)(2,1)S(1)} %get-tuple-element.49), channel_id=1, source_target_pairs={{0,2},{1,3},{2,0},{3,1},{4,6},{5,7},{6,4},{7,5},{8,10},{9,11},{10,... | collective-permute-start | bytes 196616 | tf_op jit(solution)/shard_map/ppermute | solution.py:52
  112.9 3.2 %collective-permute-done.32.refs_2_ = bf16[384,256]{1,0:T(8,128)(2,1)S(1)} collective-permute-done((bf16[384,256]{1,0:T(8,128)(2,1)S(1)}, bf16[384,256]{1,0:T(8,128)(2,1)S(1)}, u32[]{:S(2)}, u32[]{:S(2)}) %collective-permute-start.32) | collective-permute-done | bytes 196640 | tf_op jit(solution)/shard_map/ppermute | solution.py:52
  116.5 2.0 %collective-permute-start.35 = (f32[8,384]{1,0:T(8,128)S(1)}, f32[8,384]{1,0:T(8,128)S(1)}, u32[]{:S(2)}, u32[]{:S(2)}) collective-permute-start(f32[8,384]{1,0:T(8,128)S(1)} %get-tuple-element.62.refs_8_), channel_id=1, source_target_pairs={{0,3},{1,2},{2,1},{3,0},{4,7},{5,6},{6,5},{7,4},{8,11},{9,10},{10,... | collective-permute-start | bytes 36872 | tf_op jit(solution)/shard_map/ppermute | solution.py:52
  118.8 1.6 %collective-permute-start.25 = (f32[8,128]{1,0:T(8,128)S(1)}, f32[8,128]{1,0:T(8,128)S(1)}, u32[]{:S(2)}, u32[]{:S(2)}) collective-permute-start(f32[8,128]{1,0:T(8,128)S(1)} %get-tuple-element.54.refs_3_), channel_id=1, source_target_pairs={{0,2},{1,3},{2,0},{3,1},{4,6},{5,7},{6,4},{7,5},{8,10},{9,11},{10,... | collective-permute-start | bytes 12296 | tf_op jit(solution)/shard_map/ppermute | solution.py:52
  120.6 1.9 %collective-permute-done.25.refs_4_ = f32[8,128]{1,0:T(8,128)S(1)} collective-permute-done((f32[8,128]{1,0:T(8,128)S(1)}, f32[8,128]{1,0:T(8,128)S(1)}, u32[]{:S(2)}, u32[]{:S(2)}) %collective-permute-start.25) | collective-permute-done | bytes 4128 | tf_op jit(solution)/shard_map/ppermute | solution.py:52
  123.7 1.7 %finish.1 = bf16[512,256]{1,0:T(8,128)(2,1)} custom-call(s32[8]{0:T(128)S(1)} %copy-done.9, f32[1,1024]{1,0:T(1,128)S(1)} %bitcast.10, f32[128,256]{1,0:T(8,128)S(1)} %get-tuple-element.53.refs_2_, f32[8,128]{1,0:T(8,128)S(1)} %get-tuple-element.54.refs_3_, f32[8,128]{1,0:T(8,128)S(1)} %collective-permute-done.25.refs_4_, ...), custom_call_target="tpu_custom_call" | custom-call | tf_op jit(solution)/shard_map/finish/pallas_call | solution.py:33
  (89 shorter events, 10.2 us)
Async XLA Ops:
  0.6 3.1 %collective-permute-start = (bf16[512,256]{1,0:T(8,128)(2,1)}, bf16[512,256]{1,0:T(8,128)(2,1)S(1)}, u32[]{:S(2)}, u32[]{:S(2)}) collective-permute-start(bf16[512,256]{1,0:T(8,128)(2,1)} %refs_5_.3), channel_id=1, source_target_pairs={{0,1},{1,0},{2,3},{3,2},{4,5},{5,4},{6,7},{7,6},{8,9},{9,8},{10,11... | collective-permute-start | bytes 786440 | tf_op jit(solution)/shard_map/ppermute | solution.py:52
  1.1 13.1 %collective-permute-start.1 = (bf16[512,256]{1,0:T(8,128)(2,1)}, bf16[512,256]{1,0:T(8,128)(2,1)S(1)}, u32[]{:S(2)}, u32[]{:S(2)}) collective-permute-start(bf16[512,256]{1,0:T(8,128)(2,1)} %refs_5_.3), channel_id=1, source_target_pairs={{0,2},{1,3},{2,0},{3,1},{4,6},{5,7},{6,4},{7,5},{8,10},{9,11},{10,... | collective-permute-start | bytes 786440 | tf_op jit(solution)/shard_map/ppermute | solution.py:52
  9.6 56.3 %collective-permute-start.3 = (bf16[8,128,2,256]{3,2,1,0:T(2,128)(2,1)}, bf16[8,128,2,256]{3,2,1,0:T(2,128)(2,1)}, u32[]{:S(2)}, u32[]{:S(2)}) collective-permute-start(bf16[8,128,2,256]{3,2,1,0:T(2,128)(2,1)} %pick_pages.1), channel_id=1, source_target_pairs={{0,28},{4,0},{8,4},{12,8},{16,12},{20,16},{24,20},{28,24},{1,29},{... | collective-permute-start | bytes 3145736 | tf_op jit(solution)/shard_map/ppermute | solution.py:47
  17.8 47.5 %collective-permute-start.20 = (bf16[256,1024]{1,0:T(8,128)(2,1)S(1)}, bf16[256,1024]{1,0:T(8,128)(2,1)S(1)}, u32[]{:S(2)}, u32[]{:S(2)}) collective-permute-start(bf16[256,1024]{1,0:T(8,128)(2,1)S(1)} %copy-done.6), channel_id=1, source_target_pairs={{0,2},{1,3},{2,0},{3,1},{4,6},{5,7},{6,4},{7,5},{8,10},{9,11},{10,... | collective-permute-start | bytes 1572872 | tf_op jit(solution)/shard_map/ppermute | solution.py:52
  19.4 24.8 %collective-permute-start.7 = (bf16[144,256]{1,0:T(8,128)(2,1)S(1)}, bf16[144,256]{1,0:T(8,128)(2,1)S(1)}, u32[]{:S(2)}, u32[]{:S(2)}) collective-permute-start(bf16[144,256]{1,0:T(8,128)(2,1)S(1)} %get-tuple-element.36.refs_6_), channel_id=1, source_target_pairs={{0,16},{4,20},{8,24},{12,28},{16,0},{20,4},{24,8},{28,12},{1,17},{... | collective-permute-start | bytes 221192 | tf_op jit(solution)/shard_map/ppermute | solution.py:47
  19.4 24.9 %collective-permute-start.8 = (bf16[144,256]{1,0:T(8,128)(2,1)S(1)}, bf16[144,256]{1,0:T(8,128)(2,1)S(1)}, u32[]{:S(2)}, u32[]{:S(2)}) collective-permute-start(bf16[144,256]{1,0:T(8,128)(2,1)S(1)} %get-tuple-element.36.refs_6_), channel_id=1, source_target_pairs={{0,12},{4,16},{8,20},{12,24},{16,28},{20,0},{24,4},{28,8},{1,13},{... | collective-permute-start | bytes 221192 | tf_op jit(solution)/shard_map/ppermute | solution.py:47
  21.3 26.8 %collective-permute-start.9 = (bf16[144,256]{1,0:T(8,128)(2,1)S(1)}, bf16[144,256]{1,0:T(8,128)(2,1)S(1)}, u32[]{:S(2)}, u32[]{:S(2)}) collective-permute-start(bf16[144,256]{1,0:T(8,128)(2,1)S(1)} %get-tuple-element.36.refs_6_), channel_id=1, source_target_pairs={{0,20},{4,24},{8,28},{12,0},{16,4},{20,8},{24,12},{28,16},{1,21},{... | collective-permute-start | bytes 221192 | tf_op jit(solution)/shard_map/ppermute | solution.py:47
  44.2 16.2 %collective-permute-start.4 = (bf16[144,256]{1,0:T(8,128)(2,1)S(1)}, bf16[144,256]{1,0:T(8,128)(2,1)S(1)}, u32[]{:S(2)}, u32[]{:S(2)}) collective-permute-start(bf16[144,256]{1,0:T(8,128)(2,1)S(1)} %get-tuple-element.36.refs_6_), channel_id=1, source_target_pairs={{0,8},{4,12},{8,16},{12,20},{16,24},{20,28},{24,0},{28,4},{1,9},{5... | collective-permute-start | bytes 221192 | tf_op jit(solution)/shard_map/ppermute | solution.py:47
  44.2 16.3 %collective-permute-start.5 = (bf16[144,256]{1,0:T(8,128)(2,1)S(1)}, bf16[144,256]{1,0:T(8,128)(2,1)S(1)}, u32[]{:S(2)}, u32[]{:S(2)}) collective-permute-start(bf16[144,256]{1,0:T(8,128)(2,1)S(1)} %get-tuple-element.36.refs_6_), channel_id=1, source_target_pairs={{0,24},{4,28},{8,0},{12,4},{16,8},{20,12},{24,16},{28,20},{1,25},{... | collective-permute-start | bytes 221192 | tf_op jit(solution)/shard_map/ppermute | solution.py:47
  48.0 12.5 %collective-permute-start.6 = (bf16[144,256]{1,0:T(8,128)(2,1)S(1)}, bf16[144,256]{1,0:T(8,128)(2,1)S(1)}, u32[]{:S(2)}, u32[]{:S(2)}) collective-permute-start(bf16[144,256]{1,0:T(8,128)(2,1)S(1)} %get-tuple-element.36.refs_6_), channel_id=1, source_target_pairs={{0,28},{4,0},{8,4},{12,8},{16,12},{20,16},{24,20},{28,24},{1,29},{... | collective-permute-start | bytes 221192 | tf_op jit(solution)/shard_map/ppermute | solution.py:47
  60.4 41.6 %collective-permute-start.19 = (bf16[256,1024]{1,0:T(8,128)(2,1)S(1)}, bf16[256,1024]{1,0:T(8,128)(2,1)S(1)}, u32[]{:S(2)}, u32[]{:S(2)}) collective-permute-start(bf16[256,1024]{1,0:T(8,128)(2,1)S(1)} %copy-done.6), channel_id=1, source_target_pairs={{0,1},{1,0},{2,3},{3,2},{4,5},{5,4},{6,7},{7,6},{8,9},{9,8},{10,11... | collective-permute-start | bytes 1572872 | tf_op jit(solution)/shard_map/ppermute | solution.py:52
  65.3 36.7 %collective-permute-start.21 = (bf16[256,1024]{1,0:T(8,128)(2,1)S(1)}, bf16[256,1024]{1,0:T(8,128)(2,1)S(1)}, u32[]{:S(2)}, u32[]{:S(2)}) collective-permute-start(bf16[256,1024]{1,0:T(8,128)(2,1)S(1)} %collective-permute-done.20.refs_11_), channel_id=1, source_target_pairs={{0,1},{1,0},{2,3},{3,2},{4,5},{5,4},{6,7},{7,6},{8,9},{9,8},{10,11... | collective-permute-start | bytes 1572872 | tf_op jit(solution)/shard_map/ppermute | solution.py:52
  72.3 14.6 %collective-permute-start.29 = (bf16[384,256]{1,0:T(8,128)(2,1)S(1)}, bf16[384,256]{1,0:T(8,128)(2,1)S(1)}, u32[]{:S(2)}, u32[]{:S(2)}) collective-permute-start(bf16[384,256]{1,0:T(8,128)(2,1)S(1)} %get-tuple-element.55.refs_1_), channel_id=1, source_target_pairs={{0,2},{1,3},{2,0},{3,1},{4,6},{5,7},{6,4},{7,5},{8,10},{9,11},{10,... | collective-permute-start | bytes 589832 | tf_op jit(solution)/shard_map/ppermute | solution.py:52
  73.9 6.9 %collective-permute-start.10 = (bf16[144,256]{1,0:T(8,128)(2,1)S(1)}, bf16[144,256]{1,0:T(8,128)(2,1)S(1)}, u32[]{:S(2)}, u32[]{:S(2)}) collective-permute-start(bf16[144,256]{1,0:T(8,128)(2,1)S(1)} %get-tuple-element.39.refs_5_), channel_id=1, source_target_pairs={{0,16},{4,20},{8,24},{12,28},{16,0},{20,4},{24,8},{28,12},{1,17},{... | collective-permute-start | bytes 221192 | tf_op jit(solution)/shard_map/ppermute | solution.py:47
  73.9 6.9 %collective-permute-start.11 = (bf16[144,256]{1,0:T(8,128)(2,1)S(1)}, bf16[144,256]{1,0:T(8,128)(2,1)S(1)}, u32[]{:S(2)}, u32[]{:S(2)}) collective-permute-start(bf16[144,256]{1,0:T(8,128)(2,1)S(1)} %get-tuple-element.43), channel_id=1, source_target_pairs={{0,20},{4,24},{8,28},{12,0},{16,4},{20,8},{24,12},{28,16},{1,21},{... | collective-permute-start | bytes 221192 | tf_op jit(solution)/shard_map/ppermute | solution.py:47
  80.7 6.2 %collective-permute-start.12 = (bf16[144,256]{1,0:T(8,128)(2,1)S(1)}, bf16[144,256]{1,0:T(8,128)(2,1)S(1)}, u32[]{:S(2)}, u32[]{:S(2)}) collective-permute-start(bf16[144,256]{1,0:T(8,128)(2,1)S(1)} %get-tuple-element.44), channel_id=1, source_target_pairs={{0,12},{4,16},{8,20},{12,24},{16,28},{20,0},{24,4},{28,8},{1,13},{... | collective-permute-start | bytes 221192 | tf_op jit(solution)/shard_map/ppermute | solution.py:47
  80.7 6.7 %collective-permute-start.13 = (bf16[144,256]{1,0:T(8,128)(2,1)S(1)}, bf16[144,256]{1,0:T(8,128)(2,1)S(1)}, u32[]{:S(2)}, u32[]{:S(2)}) collective-permute-start(bf16[144,256]{1,0:T(8,128)(2,1)S(1)} %get-tuple-element.40.refs_8_), channel_id=1, source_target_pairs={{0,24},{4,28},{8,0},{12,4},{16,8},{20,12},{24,16},{28,20},{1,25},{... | collective-permute-start | bytes 221192 | tf_op jit(solution)/shard_map/ppermute | solution.py:47
  86.9 15.1 %collective-permute-start.28 = (bf16[384,256]{1,0:T(8,128)(2,1)S(1)}, bf16[384,256]{1,0:T(8,128)(2,1)S(1)}, u32[]{:S(2)}, u32[]{:S(2)}) collective-permute-start(bf16[384,256]{1,0:T(8,128)(2,1)S(1)} %get-tuple-element.55.refs_1_), channel_id=1, source_target_pairs={{0,1},{1,0},{2,3},{3,2},{4,5},{5,4},{6,7},{7,6},{8,9},{9,8},{10,11... | collective-permute-start | bytes 589832 | tf_op jit(solution)/shard_map/ppermute | solution.py:52
  86.9 15.1 %collective-permute-start.30 = (bf16[384,256]{1,0:T(8,128)(2,1)S(1)}, bf16[384,256]{1,0:T(8,128)(2,1)S(1)}, u32[]{:S(2)}, u32[]{:S(2)}) collective-permute-start(bf16[384,256]{1,0:T(8,128)(2,1)S(1)} %collective-permute-done.29.refs_3_), channel_id=1, source_target_pairs={{0,1},{1,0},{2,3},{3,2},{4,5},{5,4},{6,7},{7,6},{8,9},{9,8},{10,11... | collective-permute-start | bytes 589832 | tf_op jit(solution)/shard_map/ppermute | solution.py:52
  87.4 6.2 %collective-permute-start.14 = (bf16[144,256]{1,0:T(8,128)(2,1)S(1)}, bf16[144,256]{1,0:T(8,128)(2,1)S(1)}, u32[]{:S(2)}, u32[]{:S(2)}) collective-permute-start(bf16[144,256]{1,0:T(8,128)(2,1)S(1)} %get-tuple-element.45), channel_id=1, source_target_pairs={{0,8},{4,12},{8,16},{12,20},{16,24},{20,28},{24,0},{28,4},{1,9},{5... | collective-permute-start | bytes 221192 | tf_op jit(solution)/shard_map/ppermute | solution.py:47
  93.5 7.1 %collective-permute-start.15 = (bf16[144,256]{1,0:T(8,128)(2,1)S(1)}, bf16[144,256]{1,0:T(8,128)(2,1)S(1)}, u32[]{:S(2)}, u32[]{:S(2)}) collective-permute-start(bf16[144,256]{1,0:T(8,128)(2,1)S(1)} %get-tuple-element.46), channel_id=1, source_target_pairs={{0,4},{4,8},{8,12},{12,16},{16,20},{20,24},{24,28},{28,0},{1,5},{5... | collective-permute-start | bytes 221192 | tf_op jit(solution)/shard_map/ppermute | solution.py:47
  101.4 5.9 %collective-permute-start.17 = (bf16[128,256]{1,0:T(8,128)(2,1)S(1)}, bf16[128,256]{1,0:T(8,128)(2,1)S(1)}, u32[]{:S(2)}, u32[]{:S(2)}) collective-permute-start(bf16[128,256]{1,0:T(8,128)(2,1)S(1)} %merge.1.refs_1_), channel_id=1, source_target_pairs={{0,2},{1,3},{2,0},{3,1},{4,6},{5,7},{6,4},{7,5},{8,10},{9,11},{10,... | collective-permute-start | bytes 196616 | tf_op jit(solution)/shard_map/ppermute | solution.py:52
  105.7 6.7 %collective-permute-start.31 = (bf16[384,256]{1,0:T(8,128)(2,1)S(1)}, bf16[384,256]{1,0:T(8,128)(2,1)S(1)}, u32[]{:S(2)}, u32[]{:S(2)}) collective-permute-start(bf16[384,256]{1,0:T(8,128)(2,1)S(1)} %get-tuple-element.57), channel_id=1, source_target_pairs={{0,2},{1,3},{2,0},{3,1},{4,6},{5,7},{6,4},{7,5},{8,10},{9,11},{10,... | collective-permute-start | bytes 589832 | tf_op jit(solution)/shard_map/ppermute | solution.py:52
  107.8 8.3 %collective-permute-start.32 = (bf16[384,256]{1,0:T(8,128)(2,1)S(1)}, bf16[384,256]{1,0:T(8,128)(2,1)S(1)}, u32[]{:S(2)}, u32[]{:S(2)}) collective-permute-start(bf16[384,256]{1,0:T(8,128)(2,1)S(1)} %get-tuple-element.58), channel_id=1, source_target_pairs={{0,3},{1,2},{2,1},{3,0},{4,7},{5,6},{6,5},{7,4},{8,11},{9,10},{10,... | collective-permute-start | bytes 589832 | tf_op jit(solution)/shard_map/ppermute | solution.py:52
  107.9 8.2 %collective-permute-start.33 = (bf16[384,256]{1,0:T(8,128)(2,1)S(1)}, bf16[384,256]{1,0:T(8,128)(2,1)S(1)}, u32[]{:S(2)}, u32[]{:S(2)}) collective-permute-start(bf16[384,256]{1,0:T(8,128)(2,1)S(1)} %get-tuple-element.59), channel_id=1, source_target_pairs={{0,1},{1,0},{2,3},{3,2},{4,5},{5,4},{6,7},{7,6},{8,9},{9,8},{10,11... | collective-permute-start | bytes 589832 | tf_op jit(solution)/shard_map/ppermute | solution.py:52
  110.7 7.8 %collective-permute-start.22 = (bf16[128,256]{1,0:T(8,128)(2,1)S(1)}, bf16[128,256]{1,0:T(8,128)(2,1)S(1)}, u32[]{:S(2)}, u32[]{:S(2)}) collective-permute-start(bf16[128,256]{1,0:T(8,128)(2,1)S(1)} %get-tuple-element.49), channel_id=1, source_target_pairs={{0,2},{1,3},{2,0},{3,1},{4,6},{5,7},{6,4},{7,5},{8,10},{9,11},{10,... | collective-permute-start | bytes 196616 | tf_op jit(solution)/shard_map/ppermute | solution.py:52
  112.0 6.7 %collective-permute-start.23 = (bf16[128,256]{1,0:T(8,128)(2,1)S(1)}, bf16[128,256]{1,0:T(8,128)(2,1)S(1)}, u32[]{:S(2)}, u32[]{:S(2)}) collective-permute-start(bf16[128,256]{1,0:T(8,128)(2,1)S(1)} %get-tuple-element.50), channel_id=1, source_target_pairs={{0,3},{1,2},{2,1},{3,0},{4,7},{5,6},{6,5},{7,4},{8,11},{9,10},{10,... | collective-permute-start | bytes 196616 | tf_op jit(solution)/shard_map/ppermute | solution.py:52
  112.4 6.2 %collective-permute-start.24 = (bf16[128,256]{1,0:T(8,128)(2,1)S(1)}, bf16[128,256]{1,0:T(8,128)(2,1)S(1)}, u32[]{:S(2)}, u32[]{:S(2)}) collective-permute-start(bf16[128,256]{1,0:T(8,128)(2,1)S(1)} %get-tuple-element.51), channel_id=1, source_target_pairs={{0,1},{1,0},{2,3},{3,2},{4,5},{5,4},{6,7},{7,6},{8,9},{9,8},{10,11... | collective-permute-start | bytes 196616 | tf_op jit(solution)/shard_map/ppermute | solution.py:52
  116.5 7.2 %collective-permute-start.34 = (f32[8,384]{1,0:T(8,128)S(1)}, f32[8,384]{1,0:T(8,128)S(1)}, u32[]{:S(2)}, u32[]{:S(2)}) collective-permute-start(f32[8,384]{1,0:T(8,128)S(1)} %get-tuple-element.62.refs_8_), channel_id=1, source_target_pairs={{0,2},{1,3},{2,0},{3,1},{4,6},{5,7},{6,4},{7,5},{8,10},{9,11},{10,... | collective-permute-start | bytes 36872 | tf_op jit(solution)/shard_map/ppermute | solution.py:52
  116.5 7.1 %collective-permute-start.35 = (f32[8,384]{1,0:T(8,128)S(1)}, f32[8,384]{1,0:T(8,128)S(1)}, u32[]{:S(2)}, u32[]{:S(2)}) collective-permute-start(f32[8,384]{1,0:T(8,128)S(1)} %get-tuple-element.62.refs_8_), channel_id=1, source_target_pairs={{0,3},{1,2},{2,1},{3,0},{4,7},{5,6},{6,5},{7,4},{8,11},{9,10},{10,... | collective-permute-start | bytes 36872 | tf_op jit(solution)/shard_map/ppermute | solution.py:52
  118.5 5.2 %collective-permute-start.36 = (f32[8,384]{1,0:T(8,128)S(1)}, f32[8,384]{1,0:T(8,128)S(1)}, u32[]{:S(2)}, u32[]{:S(2)}) collective-permute-start(f32[8,384]{1,0:T(8,128)S(1)} %get-tuple-element.62.refs_8_), channel_id=1, source_target_pairs={{0,1},{1,0},{2,3},{3,2},{4,5},{5,4},{6,7},{7,6},{8,9},{9,8},{10,11... | collective-permute-start | bytes 36872 | tf_op jit(solution)/shard_map/ppermute | solution.py:52
  118.8 3.6 %collective-permute-start.25 = (f32[8,128]{1,0:T(8,128)S(1)}, f32[8,128]{1,0:T(8,128)S(1)}, u32[]{:S(2)}, u32[]{:S(2)}) collective-permute-start(f32[8,128]{1,0:T(8,128)S(1)} %get-tuple-element.54.refs_3_), channel_id=1, source_target_pairs={{0,2},{1,3},{2,0},{3,1},{4,6},{5,7},{6,4},{7,5},{8,10},{9,11},{10,... | collective-permute-start | bytes 12296 | tf_op jit(solution)/shard_map/ppermute | solution.py:52
  (21 other events, 268.1 us)

commit v2 on v1

v2 whole, which is shorter than its diff:
```python
import functools

import jax
import jax.numpy as jnp
from jax import lax
from jax.experimental import pallas as pl
from jax.experimental.pallas import tpu as pltpu
from jax.sharding import PartitionSpec as P

HD = 64
NEG = -1e30
EPS = 1e-05
META = 16
F32 = jnp.float32
BF16 = jnp.bfloat16

VMEM = pl.BlockSpec(memory_space=pltpu.VMEM)
SMEM = pl.BlockSpec(memory_space=pltpu.SMEM)
ANY = pl.BlockSpec(memory_space=pl.ANY)


def shape_of(dims, dtype):
    return jax.ShapeDtypeStruct(dims, dtype)


def call(kernel, outs, ins, out_specs, scratch, operands, name, flops=0, nbytes=0, after=(), vmem=24):
    split = len(operands)

    def body(*refs):
        kernel(*refs[:split], *refs[split + len(after) :])

    return pl.pallas_call(
        body,
        out_shape=outs,
        in_specs=list(ins) + [ANY] * len(after),
        out_specs=out_specs,
        scratch_shapes=scratch,
        compiler_params=pltpu.CompilerParams(vmem_limit_bytes=vmem << 20),
        cost_estimate=pl.CostEstimate(flops=flops, bytes_accessed=nbytes, transcendentals=0),
        name=name,
    )(*operands, *after)


def send_req(value, by):
    size = lax.axis_size("req")
    return lax.ppermute(value, "req", [(i, (i + by) % size) for i in range(size)])


def send_tp(value, flip):
    size = lax.axis_size("tp")
    return lax.ppermute(value, "tp", [(i, i ^ flip) for i in range(size)])


def write_order(len_ref, order_ref, requests, page_len):
    flags = [(len_ref[r] > 2 * page_len).astype(jnp.int32) for r in range(requests)]
    total = sum(flags)
    before = jnp.int32(0)
    for r in range(requests):
        place = jnp.where(flags[r] > 0, before, total + r - before)
        order_ref[place] = jnp.int32(r)
        before = before + flags[r]


def split3(value):
    high = value.astype(BF16)
    rest = value - high.astype(F32)
    middle = rest.astype(BF16)
    low = (rest - middle.astype(F32)).astype(BF16)
    return high, middle, low


def dot_t(a, b):
    return lax.dot_general(a, b, (((1,), (1,)), ((), ())), preferred_element_type=F32)


def head_rows(value, heads):
    lane = lax.broadcasted_iota(jnp.int32, value.shape, 1) // HD
    zero = jnp.zeros_like(value)
    return jnp.concatenate([jnp.where(lane == h, value, zero) for h in range(heads)], axis=0)


def head_lanes(stacked, heads, rows, width):
    lane = lax.broadcasted_iota(jnp.int32, (rows, width), 1) // HD
    out = jnp.zeros((rows, width), stacked.dtype)
    for h in range(heads):
        piece = stacked[h * rows : (h + 1) * rows]
        if piece.shape[1] != width:
            piece = jnp.broadcast_to(piece[:, :1], (rows, width))
        out = jnp.where(lane == h, piece, out)
    return out


def unpick(page_len):
    row = lax.broadcasted_iota(jnp.int32, (2 * page_len, 2 * page_len), 0)
    col = lax.broadcasted_iota(jnp.int32, (2 * page_len, 2 * page_len), 1)
    source = jnp.where(row < page_len, 2 * row, 2 * (row - page_len) + 1)
    return jnp.where(source == col, 1.0, 0.0).astype(BF16)


def split_page(page, picker, page_len):
    flat = page.reshape(2 * page_len, page.shape[2])
    both = jnp.dot(picker, flat, preferred_element_type=F32).astype(BF16)
    return both[:page_len], both[page_len:]


def to_row(column):
    return jnp.transpose(jnp.broadcast_to(column, (column.shape[0], 128)))[:1]


def attend(scores, values):
    top = functools.reduce(jnp.maximum, [jnp.max(s, axis=-1, keepdims=True) for s in scores])
    weights = [jnp.exp(s - top).astype(BF16) for s in scores]
    total = sum(jnp.sum(w.astype(F32), axis=-1, keepdims=True) for w in weights)
    mixed = sum(jnp.dot(w, v, preferred_element_type=F32) for w, v in zip(weights, values))
    return mixed, top, total


def pages_kernel(table_ref, pool_ref, key_ref, value_ref, page_ref, sems):
    rows, requests, page_len = key_ref.shape[:3]
    copies = [
        pltpu.make_async_copy(pool_ref.at[table_ref[j, m]], page_ref.at[j, m], sems.at[j, m])
        for j in range(rows)
        for m in range(requests)
    ]
    for copy in copies:
        copy.start()
    picker = unpick(page_len)
    for copy in copies:
        copy.wait()
    for j in range(rows):
        for m in range(requests):
            key_ref[j, m], value_ref[j, m] = split_page(page_ref[j, m], picker, page_len)


def full_product(hid, w_ref, part):
    me = lax.axis_index("tp")
    share = hid[0].shape[1]
    total = None
    for flip, ref in enumerate(hid):
        at = pl.multiple_of((me ^ flip) * share, share)
        term = jnp.dot(ref[...], w_ref[part, pl.ds(at, share), :], preferred_element_type=F32)
        total = term if total is None else total + term
    return total


def tree_kernel(dims, accept_ref, parent_ref, bias_ref, select_ref, wide_ref):
    requests, draft = dims
    group = parent_ref.shape[1] // draft
    side = group * draft
    row = lax.broadcasted_iota(jnp.int32, (side, side), 0)
    col = lax.broadcasted_iota(jnp.int32, (side, side), 1)
    eye = jnp.where(row == col, 1.0, 0.0)
    up = []
    for g in range(requests // group):
        parent = parent_ref[pl.ds(g, 1), :]
        lane = lax.broadcasted_iota(jnp.int32, parent.shape, 1)
        target = jnp.where(parent < 0, -1, parent + (lane // draft) * draft)
        up.append((eye + jnp.where(row == target, 1.0, 0.0)).astype(BF16))
    for sweep in range(max(1, (draft - 1).bit_length())):
        up = [jnp.minimum(jnp.dot(u, u, preferred_element_type=F32), 1.0).astype(BF16) for u in up]
    row = lax.broadcasted_iota(jnp.int32, (2 * side, 2 * side), 0)
    col = lax.broadcasted_iota(jnp.int32, (2 * side, 2 * side), 1)
    fits = (row % 2 == col // side) & (row // (2 * draft) == (col % side) // draft)
    level = ((row // 2) % draft).astype(F32)
    for g in range(requests // group):
        wide = up[g].astype(F32)
        reach = jnp.transpose(wide)
        wide_ref[...] = reach
        depth = jnp.sum(wide, axis=0, keepdims=True) - 1.0
        chosen = jnp.zeros((1, side), F32)
        for i in range(group):
            r = g * group + i
            own = reach[i * draft : (i + 1) * draft, i * draft : (i + 1) * draft]
            bias_ref[pl.ds(r * draft, draft), :] = jnp.where(own > 0.5, 0.0, NEG)
            chosen += wide_ref[pl.ds(i * draft + accept_ref[r], 1), :]
        depth = jnp.concatenate([depth, depth], axis=1)
        chosen = jnp.concatenate([chosen, chosen], axis=1)
        select_ref[g] = jnp.where(fits & (depth == level), chosen, 0.0).astype(BF16)


def query_kernel(dims, len_ref, own_ref, core_ref, y_ref, diag_ref, w_ref, q_ref, out_ref, near_ref, order_ref):
    requests, draft, page_len, long_count = dims
    rows = long_count * draft
    width = q_ref.shape[1]
    write_order(len_ref, order_ref, requests, page_len)
    row = lax.broadcasted_iota(jnp.int32, (META, width), 0)
    facts = jnp.zeros((META, width), jnp.int32)
    for i in range(long_count):
        member = order_ref[i]
        length = len_ref[member]
        facts = jnp.where(row == 3 * i, member, facts)
        facts = jnp.where(row == 3 * i + 1, length // page_len, facts)
        facts = jnp.where(row == 3 * i + 2, length % page_len, facts)
    out_ref[pl.ds(rows, META)] = facts.astype(F32).astype(BF16)
    limits = jnp.zeros((META, width), jnp.int32)
    for r in range(requests):
        limits = jnp.where(row == r, jnp.clip(len_ref[r] - page_len, 0, page_len), limits)
    near_ref[pl.ds(requests * draft, META)] = limits.astype(F32).astype(BF16)
    queries = (full_product((own_ref, core_ref, y_ref, diag_ref), w_ref, 0) * 0.125).astype(BF16)
    q_ref[...] = queries
    near_ref[pl.ds(0, requests * draft)] = queries
    for i in range(long_count):
        at = pl.multiple_of(order_ref[i] * draft, draft)
        out_ref[pl.ds(i * draft, draft)] = q_ref[pl.ds(at, draft), :]


def key_value_kernel(own_ref, core_ref, y_ref, diag_ref, w_ref, select_ref, k_ref, v_ref, acc_ref):
    hid = (own_ref, core_ref, y_ref, diag_ref)
    k_ref[...] = full_product(hid, w_ref, 1).astype(BF16)
    v_ref[...] = full_product(hid, w_ref, 2).astype(BF16)
    groups, side = select_ref.shape[0], select_ref.shape[1] // 2
    for g in range(groups):
        rows = pl.ds(g * side, side)
        pairs = jnp.concatenate([k_ref[rows], v_ref[rows]], axis=0)
        path = jnp.dot(select_ref[g], pairs, preferred_element_type=F32).astype(BF16)
        acc_ref[rows] = path.reshape(side, 2, path.shape[1])


def remote_kernel(dims, page_indices, *refs, between=None):
    page_len, draft, heads, long_count = dims
    count = len(page_indices)
    msgs, table_ref, pool_ref = refs[:count], refs[count], refs[count + 1]
    outs = refs[count + 2 : 2 * count + 2]
    page_ref, sems = refs[2 * count + 2 :]
    width = heads * HD
    tokens = long_count * draft
    copies, limits = [], []
    for n, page_index in enumerate(page_indices):
        facts = msgs[n][pl.ds(tokens, META), :].astype(F32)[:, :page_len]
        for i in range(long_count):
            member = jnp.max(facts[3 * i : 3 * i + 1]).astype(jnp.int32)
            copy = pltpu.make_async_copy(
                pool_ref.at[table_ref[page_index, member]], page_ref.at[n, i], sems.at[n, i]
            )
            copy.start()
            copies.append(copy)
            length = facts[3 * i + 1 : 3 * i + 2] * page_len + facts[3 * i + 2 : 3 * i + 3]
            limits.append(length - page_index * page_len)
    picker = unpick(page_len)
    lane = lax.broadcasted_iota(jnp.int32, (heads * draft, page_len), 1).astype(F32)
    if between is not None:
        between()
    for copy in copies:
        copy.wait()
    for n in range(count):
        stats = []
        for i in range(long_count):
            stacked = head_rows(msgs[n][pl.ds(i * draft, draft), :], heads)
            keys, values = split_page(page_ref[n, i], picker, page_len)
            scores = jnp.where(lane < limits[n * long_count + i], dot_t(stacked, keys), NEG)
            mixed, top, total = attend([scores], [values])
            outs[n][pl.ds(i * draft, draft)] = head_lanes(mixed, heads, draft, width).astype(BF16)
            stats += list(split3(to_row(top))) + list(split3(to_row(total)))
        stats.append(jnp.zeros((META - len(stats), width), BF16))
        outs[n][pl.ds(tokens, META)] = jnp.concatenate([s.astype(F32) for s in stats], axis=0).astype(BF16)


def near_pages(dims, msg_ref, key_ref, value_ref, out_ref):
    draft, heads = dims
    requests, page_len, width = key_ref.shape[1:]
    tokens = requests * draft
    limits = msg_ref[pl.ds(tokens, META), :].astype(F32)[:, :page_len]
    lane = lax.broadcasted_iota(jnp.int32, (heads * draft, page_len), 1).astype(F32)
    stats = []
    for r in range(requests):
        stacked = head_rows(msg_ref[pl.ds(r * draft, draft), :], heads)
        scores = jnp.where(lane < limits[r : r + 1], dot_t(stacked, key_ref[1, r]), NEG)
        mixed, top, total = attend([scores], [value_ref[1, r]])
        out_ref[pl.ds(r * draft, draft)] = head_lanes(mixed, heads, draft, width).astype(BF16)
        stats += list(split3(to_row(top))) + list(split3(to_row(total)))
    out_ref[pl.ds(tokens, len(stats))] = jnp.concatenate([s.astype(F32) for s in stats], axis=0).astype(BF16)


def visiting_kernel(dims, page_indices, msg_ref, key_ref, value_ref, *refs):
    page_len, draft, heads, long_count = dims
    count = len(page_indices)
    near = functools.partial(near_pages, (draft, heads), msg_ref, key_ref, value_ref, refs[count + 2])
    remote_kernel(dims, page_indices, *refs[: count + 2], *refs[count + 3 :], between=near)


def local_kernel(dims, len_ref, q_ref, k_ref, v_ref, bias_ref, key_ref, value_ref, keep_ref, out_ref, stats_ref, kept_ref):
    kept_ref[...] = keep_ref[...]
    requests, draft, heads = dims
    page_len, width = key_ref.shape[2:]
    lane = lax.broadcasted_iota(jnp.int32, (heads * draft, page_len), 1)
    stats = []
    for r in range(requests):
        rows = pl.ds(r * draft, draft)
        stacked = head_rows(q_ref[rows, :], heads)
        bias = jnp.concatenate([bias_ref[rows, :]] * heads, axis=0)
        mixed, top, total = attend(
            [jnp.where(lane < len_ref[r], dot_t(stacked, key_ref[0, r]), NEG), dot_t(stacked, k_ref[rows, :]) + bias],
            [value_ref[0, r], v_ref[rows, :]],
        )
        out_ref[rows] = head_lanes(mixed, heads, draft, width)
        stats += [to_row(top), to_row(total)]
    stats_ref[...] = jnp.concatenate(stats, axis=0)


def merge_kernel(dims, span, len_ref, own_ref, stats_ref, near_ref, *refs):
    requests, draft, heads, page_len = dims
    width = heads * HD
    msgs, out_ref, order_ref, facts_ref = refs[:-3], refs[-3], refs[-2], refs[-1]
    write_order(len_ref, order_ref, requests, page_len)
    tokens = requests * draft
    facts_ref[...] = near_ref[pl.ds(tokens, 6 * requests), :].astype(F32)
    far = [ref[pl.ds(ref.shape[0] - META, META), :].astype(F32) for ref in msgs]
    factors = []
    for i, p in enumerate(range(*span)):
        r = order_ref[p]
        near = [facts_ref[pl.ds(6 * r + k, 1), :] for k in range(6)]
        tops = [stats_ref[pl.ds(2 * r, 1), :], near[0] + near[1] + near[2]]
        totals = [stats_ref[pl.ds(2 * r + 1, 1), :], near[3] + near[4] + near[5]]
        for f in far:
            part = [f[6 * i + k : 6 * i + k + 1] for k in range(6)]
            tops.append(part[0] + part[1] + part[2])
            totals.append(part[3] + part[4] + part[5])
        best = functools.reduce(jnp.maximum, tops)
        scales = [jnp.exp(t - best) for t in tops]
        denom = sum(s * t for s, t in zip(scales, totals))
        factors += [s / denom for s in scales]
    each = 2 + len(far)
    factors.append(jnp.zeros((128 - len(factors), width), F32))
    columns = jnp.transpose(jnp.concatenate(factors, axis=0))
    for i, p in enumerate(range(*span)):
        rows = pl.ds(pl.multiple_of(order_ref[p] * draft, draft), draft)
        parts = [own_ref[rows, :], near_ref[rows, :].astype(F32)]
        parts += [ref[pl.ds(i * draft, draft), :].astype(F32) for ref in msgs]
        out = None
        for j, part in enumerate(parts):
            c = each * i + j
            term = part * head_lanes(columns[:, c : c + 1], heads, draft, width)
            out = term if out is None else out + term
        out_ref[pl.ds(i * draft, draft)] = out.astype(BF16)


def norm(values, sums, squares, gain, width_all):
    center = sums / width_all
    spread = squares / width_all - center * center
    return (values - center) * lax.rsqrt(spread + EPS) * gain


def forward_kernel(dims, len_ref, *refs):
    requests, draft, page_len, first, count = dims
    att, hid = refs[0:4], refs[4:8]
    wout_ref, gain_ref, up_ref, down_ref = refs[8:12]
    parts, normed_ref = refs[12:16], refs[16]
    order_ref, z_ref, hid_v, wout_v, up_v, down_v, sems = refs[17:]
    pairs = [(hid[k], hid_v.at[k]) for k in range(4)] + [(wout_ref, wout_v), (up_ref, up_v), (down_ref, down_v)]
    copies = [pltpu.make_async_copy(src, dst, sems.at[n]) for n, (src, dst) in enumerate(pairs)]
    for copy in copies:
        copy.start()
    me = lax.axis_index("tp")
    share = hid[0].shape[1]
    width_all = z_ref.shape[1]
    write_order(len_ref, order_ref, requests, page_len)
    for copy in copies[:4]:
        copy.wait()
    for p in range(count):
        rows = pl.ds(pl.multiple_of(order_ref[first + p] * draft, draft), draft)
        for flip in range(4):
            at = pl.ds(pl.multiple_of((me ^ flip) * share, share), share)
            z_ref[pl.ds(p * draft, draft), at] = hid_v[flip, rows, :].astype(F32)
    copies[4].wait()
    branch = None
    for flip in range(4):
        at = pl.ds(pl.multiple_of((me ^ flip) * share, share), share)
        term = jnp.dot(att[flip][...], wout_v[at, :], preferred_element_type=F32)
        branch = term if branch is None else branch + term
    z = z_ref[...] + branch
    sums = jnp.sum(z, axis=-1, keepdims=True)
    squares = jnp.sum(z * z, axis=-1, keepdims=True)
    normed_wide = norm(z, sums, squares, gain_ref[...], width_all)
    normed = normed_wide.astype(BF16)
    z_ref[...] = normed_wide
    normed_ref[...] = z_ref[:, pl.ds(pl.multiple_of(me * share, share), share)].astype(BF16)
    copies[5].wait()
    inner = jnp.dot(normed, up_v[...], preferred_element_type=F32)
    inner = (0.5 * inner * (1.0 + lax.erf(inner * (0.5 ** 0.5)))).astype(BF16)
    copies[6].wait()
    for flip in range(4):
        at = pl.ds(pl.multiple_of((me ^ flip) * share, share), share)
        parts[flip][...] = jnp.dot(inner, down_v[:, at], preferred_element_type=F32).astype(BF16)


def gather_sum_kernel(*refs):
    groups = (len(refs) - 1) // 6
    stats_ref = refs[-1]
    place = 0
    for g in range(groups):
        a_ref, b_ref, c_ref, d_ref, normed_ref = refs[5 * g : 5 * g + 5]
        x = normed_ref[...].astype(F32) + (
            (a_ref[...].astype(F32) + b_ref[...].astype(F32)) + (c_ref[...].astype(F32) + d_ref[...].astype(F32))
        )
        refs[5 * groups + g][...] = x
        rows = x.shape[0]
        row = lax.broadcasted_iota(jnp.int32, (stats_ref.shape[0], rows), 0)
        sums = to_row(jnp.sum(x, axis=-1, keepdims=True))
        squares = to_row(jnp.sum(x * x, axis=-1, keepdims=True))
        stats_ref[:, pl.ds(place, rows)] = jnp.where(row == 0, sums, jnp.where(row == 1, squares, 0.0))
        place += rows


def finish_kernel(dims, len_ref, gain_ref, *refs):
    requests, draft, page_len = dims
    order_ref = refs[-1]
    out_ref = refs[-2]
    stats_refs = refs[-6:-2]
    me = lax.axis_index("tp")
    write_order(len_ref, order_ref, requests, page_len)
    share = out_ref.shape[1]
    gain = gain_ref[:, pl.ds(pl.multiple_of(me * share, share), share)]
    width_all = gain_ref.shape[1]
    stats = sum(ref[...] for ref in stats_refs)
    stats = jnp.transpose(jnp.concatenate([stats] * (128 // stats.shape[0]), axis=0))
    place = 0
    for x_ref in refs[:-6]:
        count = x_ref.shape[0] // draft
        own = stats[place * draft : (place + count) * draft]
        y = norm(x_ref[...], own[:, 0:1], own[:, 1:2], gain, width_all).astype(BF16)
        for p in range(count):
            rows = pl.ds(pl.multiple_of(order_ref[place] * draft, draft), draft)
            out_ref[rows, :] = y[p * draft : (p + 1) * draft]
            place += 1


def shards(hidden_in, w_qkv, w_out, first_gain, w_up, w_down, second_gain, cache_pool,
           page_table, cache_len, tree_parent, accept_node):
    tokens, share = hidden_in.shape
    cache_pool, w_up, w_down = [pltpu.with_memory_space_constraint(a, pltpu.HBM) for a in (cache_pool, w_up, w_down)]
    requests, draft = tree_parent.shape
    width = w_qkv.shape[2]
    heads = width // HD
    pages = page_table.shape[0]
    page_len = cache_pool.shape[1]
    width_all = w_qkv.shape[0]
    long_count = (requests + 3) // 4
    long_rows = long_count * draft
    msg_rows = long_rows + META
    side = 4 * draft
    dma = pltpu.SemaphoreType.DMA
    order = pltpu.SMEM((requests,), jnp.int32)

    w_planes = jnp.transpose(w_qkv, (1, 0, 2))
    gain_1 = first_gain.reshape(1, -1)
    gain_2 = second_gain.reshape(1, -1)
    parents = tree_parent.reshape(requests * draft // side, side)

    hid_y = send_tp(hidden_in, 2)
    hid_core = send_tp(hidden_in, 1)
    wout = lax.all_gather(w_out, "tp", axis=0, tiled=True)

    bias, select = call(
        functools.partial(tree_kernel, (requests, draft)),
        [shape_of((tokens, draft), F32), shape_of((requests * draft // side, 2 * side, 2 * side), BF16)],
        [SMEM, VMEM], [VMEM] * 2, [pltpu.VMEM((side, side), F32)],
        (accept_node, parents), "tree", flops=14 * 256 ** 3 * 2,
    )
    split = shape_of((2, requests, page_len, width), BF16)
    page_keys, page_values = call(
        pages_kernel, [split, split], [SMEM, ANY], [VMEM] * 2,
        [pltpu.VMEM((2, requests) + cache_pool.shape[1:], BF16), dma((2, requests))],
        (page_table, cache_pool), "pages", flops=2 * requests * 2 * 256 ** 3,
    )

    hid_y, _, _ = lax.optimization_barrier((hid_y, bias, page_keys))
    hid_diag = send_tp(hid_y, 1)
    hid = (hidden_in, hid_core, hid_y, hid_diag)
    block = shape_of((tokens, width), BF16)
    queries, message, near_message = call(
        functools.partial(query_kernel, (requests, draft, page_len, long_count)),
        [block, shape_of((msg_rows, width), BF16), shape_of((tokens + META, width), BF16)],
        [SMEM] + [VMEM] * 5, [VMEM] * 3, [order],
        (cache_len, *hid, w_planes), "queries",
        flops=2 * tokens * width_all * width, nbytes=2 * width_all * width, after=(bias, page_keys),
    )
    near_asked = send_req(near_message, 1)
    queue = sorted(range(2, pages), key=lambda j: (abs(2 * j - pages), j))
    early, late = queue[:4], queue[4:]
    asked = {j: send_req(message, j) for j in early}

    key_new, value_new, accepted = call(
        key_value_kernel,
        [block, block, shape_of((tokens, 2, width), BF16)],
        [VMEM] * 6, [VMEM] * 3, [],
        (*hid, w_planes, select), "keys_values",
        flops=2 * tokens * width_all * width * 2, nbytes=2 * width_all * width * 2, after=(message,),
    )
    own, own_stats, message = call(
        functools.partial(local_kernel, (requests, draft, heads)),
        [shape_of((tokens, width), F32), shape_of((2 * requests, width), F32), shape_of((msg_rows, width), BF16)],
        [SMEM] + [VMEM] * 7, [VMEM] * 3, [],
        (cache_len, queries, key_new, value_new, bias, page_keys, page_values, message), "local_attention",
    )
    asked |= {j: send_req(message, j) for j in late}

    answer = shape_of((msg_rows, width), BF16)
    buffers = lambda n: [pltpu.VMEM((n, long_count) + cache_pool.shape[1:], BF16), dma((n, long_count))]
    near_answer, *outs = call(
        functools.partial(visiting_kernel, (page_len, draft, heads, long_count), tuple(early)),
        [shape_of((tokens + 6 * requests, width), BF16)] + [answer] * len(early),
        [VMEM] * (3 + len(early)) + [SMEM, ANY], [VMEM] * (1 + len(early)), buffers(len(early)),
        (near_asked, page_keys, page_values, *[asked[j] for j in early], page_table, cache_pool), "visitors_early",
        after=(own,),
    )
    near_got = send_req(near_answer, -1)
    answers = [send_req(out, -j) for j, out in zip(early, outs)]
    outs = call(
        functools.partial(remote_kernel, (page_len, draft, heads, long_count), tuple(late)),
        [answer] * len(late), [VMEM] * len(late) + [SMEM, ANY], [VMEM] * len(late), buffers(len(late)),
        (*[asked[j] for j in late], page_table, cache_pool), "visitors_late", after=(near_answer,),
    )
    answers += [send_req(out, -j) for j, out in zip(late, outs)]
    last = (outs[0],)

    def merge(span, msgs, name, after):
        return call(
            functools.partial(merge_kernel, (requests, draft, heads, page_len), span),
            shape_of(((span[1] - span[0]) * draft, width), BF16), [SMEM] + [VMEM] * (3 + len(msgs)), VMEM,
            [order, pltpu.VMEM((6 * requests, width), F32)],
            (cache_len, own, own_stats, near_got, *msgs), name, after=after,
        )

    def forward(attended, first, count, name, after):
        rows = count * draft
        att_y = send_tp(attended, 2)
        att_core = send_tp(attended, 1)
        att_diag = send_tp(att_y, 1)
        part = shape_of((rows, share), BF16)
        outs = call(
            functools.partial(forward_kernel, (requests, draft, page_len, first, count)),
            [part] * 5, [SMEM] + [VMEM] * 4 + [ANY] * 5 + [VMEM] + [ANY] * 2, [VMEM] * 5,
            [order, pltpu.VMEM((rows, width_all), F32), pltpu.VMEM((4, tokens, share), BF16)]
            + [pltpu.VMEM(w.shape, BF16) for w in (wout, w_up, w_down)] + [dma((7,))],
            (cache_len, attended, att_core, att_y, att_diag, *stay, gain_1, w_up, w_down), name,
            flops=2 * rows * width_all * (width_all + 2 * w_up.shape[1]), nbytes=3 * 2 * 1024 * 1024, after=after,
        )
        got = [send_tp(outs[flip], flip) for flip in (2, 3, 1)]
        return outs, [outs[0], *got, outs[4]]

    stay = tuple(pltpu.with_memory_space_constraint(a, pltpu.HBM) for a in (*hid, wout))
    merged_short = merge((long_count, requests), (), "merge_short", last)
    outs_short, parts_short = forward(merged_short, long_count, requests - long_count, "forward_short", ())
    merged_long = merge((0, long_count), answers, "merge_long", (merged_short,))
    outs_long, parts_long = forward(merged_long, 0, long_count, "forward_long", (outs_short[4],))

    x_long, x_short, stats = call(
        gather_sum_kernel,
        [shape_of((long_rows, share), F32), shape_of((tokens - long_rows, share), F32), shape_of((8, tokens), F32)],
        [VMEM] * 10, [VMEM] * 3, [], (*parts_long, *parts_short), "gather_sum",
    )
    all_stats = (stats,) + tuple(send_tp(stats, flip) for flip in (2, 3, 1))
    layer_out = call(
        functools.partial(finish_kernel, (requests, draft, page_len)),
        shape_of((tokens, share), BF16), [SMEM] + [VMEM] * 7, VMEM, [order],
        (cache_len, gain_2, x_long, x_short, *all_stats), "finish",
    )
    accepted_kv = accepted.reshape(requests, draft, 2, width)
    return (layer_out, accepted_kv)


def solution(mesh):
    placed = (
        P("req", "tp"),
        P(None, None, "tp"),
        P("tp", None),
        P(),
        P(None, "tp"),
        P("tp", None),
        P(),
        P("req", None, None, "tp"),
        P("req", None),
        P("req"),
        P("req", None),
        P("req"),
    )
    return jax.shard_map(
        shards,
        mesh=mesh,
        in_specs=placed,
        out_specs=(P("req", "tp"), P("req", None, None, "tp")),
        check_vma=False,
    )
```

time: 126 us -> 123 us (0.976)
  between operations: 0.93 us -> 14.2 us
  waiting for transfers between devices: 49.2 us -> 37.3 us
  local copies, waits for them, and re-layouts: 7.58 us -> 1.46 us
  Pallas kernels: 31.3 us -> 35.7 us
  starting transfers between devices: 36.3 us -> 34.5 us
    ppermute x13 -> x14, waiting for transfers between devices: 42.6 us -> 23.3 us  [send_req(): lax.ppermute(value, 'req', [(i, (i + by) % size) for i in range(size)])]
    unnamed x32 -> x20, local copies, waits for them, and re-layouts: 7.51 us -> 0.7 us
    ppermute x24 -> x18, waiting for transfers between devices: 6.63 us -> 13.3 us  [send_tp(): return lax.ppermute(value, 'tp', [(i, i ^ flip) for i in range(size)])]
    ppermute x24 -> x18, starting transfers between devices: 16.8 us -> 12.1 us  [send_tp(): return lax.ppermute(value, 'tp', [(i, i ^ flip) for i in range(size)])]
    pallas_call x13, Pallas kernels: 31.3 us -> 35.7 us  [call(): pl.pallas_call(body, out_shape=outs, in_specs=list(ins) + [ANY] * len(aft...]
    ppermute x13 -> x14, starting transfers between devices: 19.4 us -> 22.3 us  [send_req(): lax.ppermute(value, 'req', [(i, (i + by) % size) for i in range(size)])]
  transfers between devices with their start and end apart: 37 -> 33, of which waited for: 11 -> 14; matrix products, arithmetic and copies ran while one was open for 0% -> 1% of each run, Pallas kernels for 24% -> 27%
where the time goes in v2:
time: 123 us
  waiting for transfers between devices  37.3 us (30%)
  Pallas kernels  35.7 us (29%)
  starting transfers between devices  34.5 us (28%)
  between operations  14.2 us (12%)
  local copies, waits for them, and re-layouts  1.46 us (1%)
    pallas_call x13, Pallas kernels, call(): pl.pallas_call(body, out_shape=outs, in_specs=list(ins) + [ANY] * len(aft...  35.7 us
    ppermute x14, waiting for transfers between devices, send_req(): lax.ppermute(value, 'req', [(i, (i + by) % size) for i in range(size)])  23.3 us
    ppermute x14, starting transfers between devices, send_req(): lax.ppermute(value, 'req', [(i, (i + by) % size) for i in range(size)])  22.3 us
    ppermute x18, waiting for transfers between devices, send_tp(): return lax.ppermute(value, 'tp', [(i, i ^ flip) for i in range(size)])  13.3 us
    ppermute x18, starting transfers between devices, send_tp(): return lax.ppermute(value, 'tp', [(i, i ^ flip) for i in range(size)])  12.1 us
  transfers between devices with their start and end apart: 33, of which 14 were waited for; matrix products, arithmetic and copies ran while one was open for 1% of the time, Pallas kernels for 27%

profile of v2, /device:TPU:0, one launch (start us, length us, event | category | flops | bytes accessed | tf_op | source)
XLA Modules:
  0.0 123.2 jit_solution(13947725783938473455)
XLA Ops:
  7.9 3.0 %collective-permute-start.1 = (bf16[512,256]{1,0:T(8,128)(2,1)}, bf16[512,256]{1,0:T(8,128)(2,1)S(1)}, u32[]{:S(2)}, u32[]{:S(2)}) collective-permute-start(bf16[512,256]{1,0:T(8,128)(2,1)} %refs_5_.3), channel_id=1, source_target_pairs={{0,2},{1,3},{2,0},{3,1},{4,6},{5,7},{6,4},{7,5},{8,10},{9,11},{10,... | collective-permute-start | bytes 786440 | tf_op jit(solution)/shard_map/ppermute | solution.py:51
  12.4 2.3 %tree.1 = (f32[512,64]{1,0:T(8,128)S(1)}, bf16[2,512,512]{2,1,0:T(8,128)(2,1)S(1)}) custom-call(s32[8]{0:T(128)S(1)} %copy-done.9, s32[2,256]{1,0:T(2,128)S(1)} %reshape.17.refs_1_), custom_call_target="tpu_custom_call" | custom-call | flops 469762048 | tf_op jit(solution)/shard_map/tree/pallas_call | solution.py:32
  14.7 3.3 %pages.1 = (bf16[2,8,128,256]{3,2,1,0:T(8,128)(2,1)S(1)}, bf16[2,8,128,256]{3,2,1,0:T(8,128)(2,1)S(1)}) custom-call(s32[8,8]{1,0:T(8,128)S(1)} %copy-done.5, bf16[64,128,2,256]{3,2,1,0:T(2,128)(2,1)} %refs_3_.1), custom_call_target="tpu_custom_call" | custom-call | flops 536870912 | tf_op jit(solution)/shard_map/pages/pallas_call | solution.py:32
  20.9 1.6 %collective-permute-start.3 = (bf16[528,256]{1,0:T(8,128)(2,1)S(1)}, bf16[528,256]{1,0:T(8,128)(2,1)S(1)}, u32[]{:S(2)}, u32[]{:S(2)}) collective-permute-start(bf16[528,256]{1,0:T(8,128)(2,1)S(1)} %get-tuple-element.47), channel_id=1, source_target_pairs={{0,4},{4,8},{8,12},{12,16},{16,20},{20,24},{24,28},{28,0},{1,5},{5... | collective-permute-start | bytes 811016 | tf_op jit(solution)/shard_map/ppermute | solution.py:46
  22.4 2.6 %collective-permute-start.4 = (bf16[144,256]{1,0:T(8,128)(2,1)S(1)}, bf16[144,256]{1,0:T(8,128)(2,1)S(1)}, u32[]{:S(2)}, u32[]{:S(2)}) collective-permute-start(bf16[144,256]{1,0:T(8,128)(2,1)S(1)} %get-tuple-element.41.refs_6_.refs_7_), channel_id=1, source_target_pairs={{0,16},{4,20},{8,24},{12,28},{16,0},{20,4},{24,8},{28,12},{1,17},{... | collective-permute-start | bytes 221192 | tf_op jit(solution)/shard_map/ppermute | solution.py:46
  25.0 1.2 collective-permute-start.5
  26.2 2.6 %collective-permute-start.6 = (bf16[144,256]{1,0:T(8,128)(2,1)S(1)}, bf16[144,256]{1,0:T(8,128)(2,1)S(1)}, u32[]{:S(2)}, u32[]{:S(2)}) collective-permute-start(bf16[144,256]{1,0:T(8,128)(2,1)S(1)} %get-tuple-element.41.refs_6_.refs_7_), channel_id=1, source_target_pairs={{0,20},{4,24},{8,28},{12,0},{16,4},{20,8},{24,12},{28,16},{1,21},{... | collective-permute-start | bytes 221192 | tf_op jit(solution)/shard_map/ppermute | solution.py:46
  28.8 1.6 %collective-permute-start.7 = (bf16[144,256]{1,0:T(8,128)(2,1)S(1)}, bf16[144,256]{1,0:T(8,128)(2,1)S(1)}, u32[]{:S(2)}, u32[]{:S(2)}) collective-permute-start(bf16[144,256]{1,0:T(8,128)(2,1)S(1)} %get-tuple-element.41.refs_6_.refs_7_), channel_id=1, source_target_pairs={{0,8},{4,12},{8,16},{12,20},{16,24},{20,28},{24,0},{28,4},{1,9},{5... | collective-permute-start | bytes 221192 | tf_op jit(solution)/shard_map/ppermute | solution.py:46
  30.4 1.9 %keys_values.1 = (bf16[512,256]{1,0:T(8,128)(2,1)S(1)}, bf16[512,256]{1,0:T(8,128)(2,1)S(1)}, bf16[512,2,256]{2,1,0:T(2,128)(2,1)}) custom-call(bf16[512,256]{1,0:T(8,128)(2,1)S(1)} %copy-done.1, bf16[512,256]{1,0:T(8,128)(2,1)S(1)} %collective-permute-done.refs_2_.refs_1_.refs_6_, bf16[512,256]{1,0:T(8,128)(2,1)S(1)} %collective-permute-done.1.refs_3_.refs_2_.refs_7_, ...), custom_call_target="tpu_custom_call" | custom-call | flops 536870912 | bytes 1048576 | tf_op jit(solution)/shard_map/keys_values/pallas_call | solution.py:32
  32.3 2.8 %local_attention.1 = (f32[512,256]{1,0:T(8,128)S(1)}, f32[16,256]{1,0:T(8,128)S(1)}, bf16[144,256]{1,0:T(8,128)(2,1)S(1)}) custom-call(s32[8]{0:T(128)S(1)} %copy-done.6, bf16[512,256]{1,0:T(8,128)(2,1)S(1)} %get-tuple-element.39.refs_1_, bf16[512,256]{1,0:T(8,128)(2,1)S(1)} %get-tuple-element.42.refs_2_, bf16[512,256]{1,0:T(8,128)(2,1)S(1)} %get-tuple-element.43.refs_3_, ...), custom_call_target="tpu_custom_call" | custom-call | tf_op jit(solution)/shard_map/local_attention/pallas_call | solution.py:32
  35.1 5.3 %collective-permute-done.5.refs_4_ = bf16[144,256]{1,0:T(8,128)(2,1)S(1)} collective-permute-done((bf16[144,256]{1,0:T(8,128)(2,1)S(1)}, bf16[144,256]{1,0:T(8,128)(2,1)S(1)}, u32[]{:S(2)}, u32[]{:S(2)}) %collective-permute-start.5) | collective-permute-done | bytes 73760 | tf_op jit(solution)/shard_map/ppermute | solution.py:46
  40.5 5.6 %visitors_early.1 = (bf16[560,256]{1,0:T(8,128)(2,1)S(1)}, bf16[144,256]{1,0:T(8,128)(2,1)S(1)}, bf16[144,256]{1,0:T(8,128)(2,1)S(1)}, bf16[144,256]{1,0:T(8,128)(2,1)S(1)}, bf16[144,256]{1,0:T(8,128)(2,1)S(1)}) custom-call(bf16[528,256]{1,0:T(8,128)(2,1)S(1)} %collective-permute-done.3.refs_0_, ...), custom_call_target="tpu_custom_call" | custom-call | tf_op jit(solution)/shard_map/visitors_early/pallas_call | solution.py:32
  46.6 3.1 %collective-permute-start.13 = (bf16[144,256]{1,0:T(8,128)(2,1)S(1)}, bf16[144,256]{1,0:T(8,128)(2,1)S(1)}, u32[]{:S(2)}, u32[]{:S(2)}) collective-permute-start(bf16[144,256]{1,0:T(8,128)(2,1)S(1)} %get-tuple-element.53), channel_id=1, source_target_pairs={{0,24},{4,28},{8,0},{12,4},{16,8},{20,12},{24,16},{28,20},{1,25},{... | collective-permute-start | bytes 221192 | tf_op jit(solution)/shard_map/ppermute | solution.py:46
  49.8 7.6 %collective-permute-done.13.refs_0_ = bf16[144,256]{1,0:T(8,128)(2,1)S(1)} collective-permute-done((bf16[144,256]{1,0:T(8,128)(2,1)S(1)}, bf16[144,256]{1,0:T(8,128)(2,1)S(1)}, u32[]{:S(2)}, u32[]{:S(2)}) %collective-permute-start.13) | collective-permute-done | bytes 73760 | tf_op jit(solution)/shard_map/ppermute | solution.py:46
  57.5 3.8 %visitors_late.1 = (bf16[144,256]{1,0:T(8,128)(2,1)S(1)}, bf16[144,256]{1,0:T(8,128)(2,1)S(1)}) custom-call(bf16[144,256]{1,0:T(8,128)(2,1)S(1)} %collective-permute-done.13.refs_0_, bf16[144,256]{1,0:T(8,128)(2,1)S(1)} %collective-permute-done.14.refs_1_, s32[8,8]{1,0:T(8,128)S(1)} %copy-done.5, bf16[64,128,2,256]{3,2,1,0:T(2,128)(2,1)} %refs_3_.1, ...), custom_call_target="tpu_custom_call" | custom-call | tf_op jit(solution)/shard_map/visitors_late/pallas_call | solution.py:32
  61.3 1.2 %merge_short.1.refs_10_.refs_1_ = bf16[384,256]{1,0:T(8,128)(2,1)S(1)} custom-call(s32[8]{0:T(128)S(1)} %copy-done.6, f32[512,256]{1,0:T(8,128)S(1)} %get-tuple-element.45.refs_9_.refs_1_, f32[16,256]{1,0:T(8,128)S(1)} %get-tuple-element.46.refs_2_, bf16[560,256]{1,0:T(8,128)(2,1)S(1)} %collective-permute-done.8.refs_3_, ...), custom_call_target="tpu_custom_call" | custom-call | tf_op jit(solution)/shard_map/merge_short/pallas_call | solution.py:32
  64.3 3.8 %collective-permute-start.10 = (bf16[144,256]{1,0:T(8,128)(2,1)S(1)}, bf16[144,256]{1,0:T(8,128)(2,1)S(1)}, u32[]{:S(2)}, u32[]{:S(2)}) collective-permute-start(bf16[144,256]{1,0:T(8,128)(2,1)S(1)} %get-tuple-element.50), channel_id=1, source_target_pairs={{0,20},{4,24},{8,28},{12,0},{16,4},{20,8},{24,12},{28,16},{1,21},{... | collective-permute-start | bytes 221192 | tf_op jit(solution)/shard_map/ppermute | solution.py:46
  68.6 3.8 %collective-permute-done.9.refs_4_ = bf16[144,256]{1,0:T(8,128)(2,1)S(1)} collective-permute-done((bf16[144,256]{1,0:T(8,128)(2,1)S(1)}, bf16[144,256]{1,0:T(8,128)(2,1)S(1)}, u32[]{:S(2)}, u32[]{:S(2)}) %collective-permute-start.9) | collective-permute-done | bytes 73760 | tf_op jit(solution)/shard_map/ppermute | solution.py:46
  72.4 3.8 %collective-permute-start.12 = (bf16[144,256]{1,0:T(8,128)(2,1)S(1)}, bf16[144,256]{1,0:T(8,128)(2,1)S(1)}, u32[]{:S(2)}, u32[]{:S(2)}) collective-permute-start(bf16[144,256]{1,0:T(8,128)(2,1)S(1)} %get-tuple-element.52), channel_id=1, source_target_pairs={{0,24},{4,28},{8,0},{12,4},{16,8},{20,12},{24,16},{28,20},{1,25},{... | collective-permute-start | bytes 221192 | tf_op jit(solution)/shard_map/ppermute | solution.py:46
  76.7 1.5 %collective-permute-done.12.refs_7_ = bf16[144,256]{1,0:T(8,128)(2,1)S(1)} collective-permute-done((bf16[144,256]{1,0:T(8,128)(2,1)S(1)}, bf16[144,256]{1,0:T(8,128)(2,1)S(1)}, u32[]{:S(2)}, u32[]{:S(2)}) %collective-permute-start.12) | collective-permute-done | bytes 73760 | tf_op jit(solution)/shard_map/ppermute | solution.py:46
  78.7 4.6 %collective-permute-done.16.refs_9_ = bf16[144,256]{1,0:T(8,128)(2,1)S(1)} collective-permute-done((bf16[144,256]{1,0:T(8,128)(2,1)S(1)}, bf16[144,256]{1,0:T(8,128)(2,1)S(1)}, u32[]{:S(2)}, u32[]{:S(2)}) %collective-permute-start.16) | collective-permute-done | bytes 73760 | tf_op jit(solution)/shard_map/ppermute | solution.py:46
  83.3 1.4 %merge_long.1.refs_1_ = bf16[128,256]{1,0:T(8,128)(2,1)S(1)} custom-call(s32[8]{0:T(128)S(1)} %copy-done.6, f32[512,256]{1,0:T(8,128)S(1)} %get-tuple-element.45.refs_9_.refs_1_, f32[16,256]{1,0:T(8,128)S(1)} %get-tuple-element.46.refs_2_, bf16[560,256]{1,0:T(8,128)(2,1)S(1)} %collective-permute-done.8.refs_3_, ...), custom_call_target="tpu_custom_call" | custom-call | tf_op jit(solution)/shard_map/merge_long/pallas_call | solution.py:32
  84.7 1.3 %collective-permute-start.18 = (bf16[128,256]{1,0:T(8,128)(2,1)S(1)}, bf16[128,256]{1,0:T(8,128)(2,1)S(1)}, u32[]{:S(2)}, u32[]{:S(2)}) collective-permute-start(bf16[128,256]{1,0:T(8,128)(2,1)S(1)} %merge_long.1.refs_1_), channel_id=1, source_target_pairs={{0,2},{1,3},{2,0},{3,1},{4,6},{5,7},{6,4},{7,5},{8,10},{9,11},{10,... | collective-permute-start | bytes 196616 | tf_op jit(solution)/shard_map/ppermute | solution.py:51
  86.0 3.0 %collective-permute-done.18.refs_3_ = bf16[128,256]{1,0:T(8,128)(2,1)S(1)} collective-permute-done((bf16[128,256]{1,0:T(8,128)(2,1)S(1)}, bf16[128,256]{1,0:T(8,128)(2,1)S(1)}, u32[]{:S(2)}, u32[]{:S(2)}) %collective-permute-start.18) | collective-permute-done | bytes 65568 | tf_op jit(solution)/shard_map/ppermute | solution.py:51
  89.1 6.0 %forward_short.1 = (bf16[384,256]{1,0:T(8,128)(2,1)S(1)}, bf16[384,256]{1,0:T(8,128)(2,1)S(1)}, bf16[384,256]{1,0:T(8,128)(2,1)S(1)}, bf16[384,256]{1,0:T(8,128)(2,1)S(1)}, bf16[384,256]{1,0:T(8,128)(2,1)S(1)}) custom-call(s32[8]{0:T(128)S(1)} %copy-done.6, bf16[384,256]{1,0:T(8,128)(2,1)S(1)} %merge_short.1.refs_10_.refs_1_, ...), custom_call_target="tpu_custom_call" | custom-call | flops 2415919104 | bytes 6291456 | tf_op jit(solution)/shard_map/forward_short/pallas_call | solution.py:32
  95.0 1.4 %collective-permute-start.26 = (bf16[384,256]{1,0:T(8,128)(2,1)S(1)}, bf16[384,256]{1,0:T(8,128)(2,1)S(1)}, u32[]{:S(2)}, u32[]{:S(2)}) collective-permute-start(bf16[384,256]{1,0:T(8,128)(2,1)S(1)} %get-tuple-element.63), channel_id=1, source_target_pairs={{0,2},{1,3},{2,0},{3,1},{4,6},{5,7},{6,4},{7,5},{8,10},{9,11},{10,... | collective-permute-start | bytes 589832 | tf_op jit(solution)/shard_map/ppermute | solution.py:51
  97.3 4.3 %forward_long.1 = (bf16[128,256]{1,0:T(8,128)(2,1)S(1)}, bf16[128,256]{1,0:T(8,128)(2,1)S(1)}, bf16[128,256]{1,0:T(8,128)(2,1)S(1)}, bf16[128,256]{1,0:T(8,128)(2,1)S(1)}, bf16[128,256]{1,0:T(8,128)(2,1)S(1)}) custom-call(s32[8]{0:T(128)S(1)} %copy-done.6, bf16[128,256]{1,0:T(8,128)(2,1)S(1)} %merge_long.1.refs_1_, ...), custom_call_target="tpu_custom_call" | custom-call | flops 805306368 | bytes 6291456 | tf_op jit(solution)/shard_map/forward_long/pallas_call | solution.py:32
  101.5 1.4 %collective-permute-start.23 = (bf16[128,256]{1,0:T(8,128)(2,1)S(1)}, bf16[128,256]{1,0:T(8,128)(2,1)S(1)}, u32[]{:S(2)}, u32[]{:S(2)}) collective-permute-start(bf16[128,256]{1,0:T(8,128)(2,1)S(1)} %get-tuple-element.58), channel_id=1, source_target_pairs={{0,2},{1,3},{2,0},{3,1},{4,6},{5,7},{6,4},{7,5},{8,10},{9,11},{10,... | collective-permute-start | bytes 196616 | tf_op jit(solution)/shard_map/ppermute | solution.py:51
  103.1 5.3 %collective-permute-done.23.refs_1_ = bf16[128,256]{1,0:T(8,128)(2,1)S(1)} collective-permute-done((bf16[128,256]{1,0:T(8,128)(2,1)S(1)}, bf16[128,256]{1,0:T(8,128)(2,1)S(1)}, u32[]{:S(2)}, u32[]{:S(2)}) %collective-permute-start.23) | collective-permute-done | bytes 65568 | tf_op jit(solution)/shard_map/ppermute | solution.py:51
  110.1 1.3 %collective-permute-start.29 = (f32[8,512]{1,0:T(8,128)S(1)}, f32[8,512]{1,0:T(8,128)S(1)}, u32[]{:S(2)}, u32[]{:S(2)}) collective-permute-start(f32[8,512]{1,0:T(8,128)S(1)} %get-tuple-element.68.refs_4_), channel_id=1, source_target_pairs={{0,2},{1,3},{2,0},{3,1},{4,6},{5,7},{6,4},{7,5},{8,10},{9,11},{10,... | collective-permute-start | bytes 49160 | tf_op jit(solution)/shard_map/ppermute | solution.py:51
  112.3 1.6 %collective-permute-done.29.refs_5_ = f32[8,512]{1,0:T(8,128)S(1)} collective-permute-done((f32[8,512]{1,0:T(8,128)S(1)}, f32[8,512]{1,0:T(8,128)S(1)}, u32[]{:S(2)}, u32[]{:S(2)}) %collective-permute-start.29) | collective-permute-done | bytes 16416 | tf_op jit(solution)/shard_map/ppermute | solution.py:51
  114.7 1.6 %finish.1 = bf16[512,256]{1,0:T(8,128)(2,1)} custom-call(s32[8]{0:T(128)S(1)} %copy-done.6, f32[1,1024]{1,0:T(1,128)S(1)} %bitcast.8, f32[128,256]{1,0:T(8,128)S(1)} %get-tuple-element.66.refs_2_, f32[384,256]{1,0:T(8,128)S(1)} %get-tuple-element.67.refs_3_, f32[8,512]{1,0:T(8,128)S(1)} %get-tuple-element.68.refs_4_, ...), custom_call_target="tpu_custom_call" | custom-call | tf_op jit(solution)/shard_map/finish/pallas_call | solution.py:32
  (69 shorter events, 13.3 us)
Async XLA Ops:
  7.2 81.9 %all-gather.2.cloned.1.call-start = ((), (), s32[]{:S(2)}) async-start(), calls=%async_computation | async-start | bytes 2621440 | tf_op jit(solution)/shard_map/all_gather | solution.py:451
  7.9 10.1 %collective-permute-start.1 = (bf16[512,256]{1,0:T(8,128)(2,1)}, bf16[512,256]{1,0:T(8,128)(2,1)S(1)}, u32[]{:S(2)}, u32[]{:S(2)}) collective-permute-start(bf16[512,256]{1,0:T(8,128)(2,1)} %refs_5_.3), channel_id=1, source_target_pairs={{0,2},{1,3},{2,0},{3,1},{4,6},{5,7},{6,4},{7,5},{8,10},{9,11},{10,... | collective-permute-start | bytes 786440 | tf_op jit(solution)/shard_map/ppermute | solution.py:51
  10.9 7.7 %collective-permute-start = (bf16[512,256]{1,0:T(8,128)(2,1)}, bf16[512,256]{1,0:T(8,128)(2,1)S(1)}, u32[]{:S(2)}, u32[]{:S(2)}) collective-permute-start(bf16[512,256]{1,0:T(8,128)(2,1)} %refs_5_.3), channel_id=1, source_target_pairs={{0,1},{1,0},{2,3},{3,2},{4,5},{5,4},{6,7},{7,6},{8,9},{9,8},{10,11... | collective-permute-start | bytes 786440 | tf_op jit(solution)/shard_map/ppermute | solution.py:51
  18.0 1.8 %collective-permute-start.2 = (bf16[512,256]{1,0:T(8,128)(2,1)S(1)}, bf16[512,256]{1,0:T(8,128)(2,1)S(1)}, u32[]{:S(2)}, u32[]{:S(2)}) collective-permute-start(bf16[512,256]{1,0:T(8,128)(2,1)S(1)} %collective-permute-done.1.refs_3_.refs_2_.refs_7_), channel_id=1, source_target_pairs={{0,1},{1,0},{2,3},{3,2},{4,5},{5,4},{6,7},{7,6},{8,9},{9,8},{10,11... | collective-permute-start | bytes 786440 | tf_op jit(solution)/shard_map/ppermute | solution.py:51
  20.9 19.6 %collective-permute-start.3 = (bf16[528,256]{1,0:T(8,128)(2,1)S(1)}, bf16[528,256]{1,0:T(8,128)(2,1)S(1)}, u32[]{:S(2)}, u32[]{:S(2)}) collective-permute-start(bf16[528,256]{1,0:T(8,128)(2,1)S(1)} %get-tuple-element.47), channel_id=1, source_target_pairs={{0,4},{4,8},{8,12},{12,16},{16,20},{20,24},{24,28},{28,0},{1,5},{5... | collective-permute-start | bytes 811016 | tf_op jit(solution)/shard_map/ppermute | solution.py:46
  22.4 12.7 %collective-permute-start.4 = (bf16[144,256]{1,0:T(8,128)(2,1)S(1)}, bf16[144,256]{1,0:T(8,128)(2,1)S(1)}, u32[]{:S(2)}, u32[]{:S(2)}) collective-permute-start(bf16[144,256]{1,0:T(8,128)(2,1)S(1)} %get-tuple-element.41.refs_6_.refs_7_), channel_id=1, source_target_pairs={{0,16},{4,20},{8,24},{12,28},{16,0},{20,4},{24,8},{28,12},{1,17},{... | collective-permute-start | bytes 221192 | tf_op jit(solution)/shard_map/ppermute | solution.py:46
  25.0 15.5 %collective-permute-start.5 = (bf16[144,256]{1,0:T(8,128)(2,1)S(1)}, bf16[144,256]{1,0:T(8,128)(2,1)S(1)}, u32[]{:S(2)}, u32[]{:S(2)}) collective-permute-start(bf16[144,256]{1,0:T(8,128)(2,1)S(1)} %get-tuple-element.41.refs_6_.refs_7_), channel_id=1, source_target_pairs={{0,12},{4,16},{8,20},{12,24},{16,28},{20,0},{24,4},{28,8},{1,13},{... | collective-permute-start | bytes 221192 | tf_op jit(solution)/shard_map/ppermute | solution.py:46
  26.2 14.3 %collective-permute-start.6 = (bf16[144,256]{1,0:T(8,128)(2,1)S(1)}, bf16[144,256]{1,0:T(8,128)(2,1)S(1)}, u32[]{:S(2)}, u32[]{:S(2)}) collective-permute-start(bf16[144,256]{1,0:T(8,128)(2,1)S(1)} %get-tuple-element.41.refs_6_.refs_7_), channel_id=1, source_target_pairs={{0,20},{4,24},{8,28},{12,0},{16,4},{20,8},{24,12},{28,16},{1,21},{... | collective-permute-start | bytes 221192 | tf_op jit(solution)/shard_map/ppermute | solution.py:46
  28.8 11.6 %collective-permute-start.7 = (bf16[144,256]{1,0:T(8,128)(2,1)S(1)}, bf16[144,256]{1,0:T(8,128)(2,1)S(1)}, u32[]{:S(2)}, u32[]{:S(2)}) collective-permute-start(bf16[144,256]{1,0:T(8,128)(2,1)S(1)} %get-tuple-element.41.refs_6_.refs_7_), channel_id=1, source_target_pairs={{0,8},{4,12},{8,16},{12,20},{16,24},{20,28},{24,0},{28,4},{1,9},{5... | collective-permute-start | bytes 221192 | tf_op jit(solution)/shard_map/ppermute | solution.py:46
  46.1 15.1 %collective-permute-start.8 = (bf16[560,256]{1,0:T(8,128)(2,1)S(1)}, bf16[560,256]{1,0:T(8,128)(2,1)S(1)}, u32[]{:S(2)}, u32[]{:S(2)}) collective-permute-start(bf16[560,256]{1,0:T(8,128)(2,1)S(1)} %get-tuple-element.48.refs_4_), channel_id=1, source_target_pairs={{0,28},{4,0},{8,4},{12,8},{16,12},{20,16},{24,20},{28,24},{1,29},{... | collective-permute-start | bytes 860168 | tf_op jit(solution)/shard_map/ppermute | solution.py:46
  46.6 10.8 %collective-permute-start.13 = (bf16[144,256]{1,0:T(8,128)(2,1)S(1)}, bf16[144,256]{1,0:T(8,128)(2,1)S(1)}, u32[]{:S(2)}, u32[]{:S(2)}) collective-permute-start(bf16[144,256]{1,0:T(8,128)(2,1)S(1)} %get-tuple-element.53), channel_id=1, source_target_pairs={{0,24},{4,28},{8,0},{12,4},{16,8},{20,12},{24,16},{28,20},{1,25},{... | collective-permute-start | bytes 221192 | tf_op jit(solution)/shard_map/ppermute | solution.py:46
  49.8 7.7 %collective-permute-start.14 = (bf16[144,256]{1,0:T(8,128)(2,1)S(1)}, bf16[144,256]{1,0:T(8,128)(2,1)S(1)}, u32[]{:S(2)}, u32[]{:S(2)}) collective-permute-start(bf16[144,256]{1,0:T(8,128)(2,1)S(1)} %get-tuple-element.53), channel_id=1, source_target_pairs={{0,28},{4,0},{8,4},{12,8},{16,12},{20,16},{24,20},{28,24},{1,29},{... | collective-permute-start | bytes 221192 | tf_op jit(solution)/shard_map/ppermute | solution.py:46
  62.5 5.8 %collective-permute-start.21 = (bf16[384,256]{1,0:T(8,128)(2,1)S(1)}, bf16[384,256]{1,0:T(8,128)(2,1)S(1)}, u32[]{:S(2)}, u32[]{:S(2)}) collective-permute-start(bf16[384,256]{1,0:T(8,128)(2,1)S(1)} %merge_short.1.refs_10_.refs_1_), channel_id=1, source_target_pairs={{0,2},{1,3},{2,0},{3,1},{4,6},{5,7},{6,4},{7,5},{8,10},{9,11},{10,... | collective-permute-start | bytes 589832 | tf_op jit(solution)/shard_map/ppermute | solution.py:51
  63.3 9.1 %collective-permute-start.9 = (bf16[144,256]{1,0:T(8,128)(2,1)S(1)}, bf16[144,256]{1,0:T(8,128)(2,1)S(1)}, u32[]{:S(2)}, u32[]{:S(2)}) collective-permute-start(bf16[144,256]{1,0:T(8,128)(2,1)S(1)} %get-tuple-element.49), channel_id=1, source_target_pairs={{0,16},{4,20},{8,24},{12,28},{16,0},{20,4},{24,8},{28,12},{1,17},{... | collective-permute-start | bytes 221192 | tf_op jit(solution)/shard_map/ppermute | solution.py:46
  64.3 8.1 %collective-permute-start.10 = (bf16[144,256]{1,0:T(8,128)(2,1)S(1)}, bf16[144,256]{1,0:T(8,128)(2,1)S(1)}, u32[]{:S(2)}, u32[]{:S(2)}) collective-permute-start(bf16[144,256]{1,0:T(8,128)(2,1)S(1)} %get-tuple-element.50), channel_id=1, source_target_pairs={{0,20},{4,24},{8,28},{12,0},{16,4},{20,8},{24,12},{28,16},{1,21},{... | collective-permute-start | bytes 221192 | tf_op jit(solution)/shard_map/ppermute | solution.py:46
  68.1 8.2 %collective-permute-start.11 = (bf16[144,256]{1,0:T(8,128)(2,1)S(1)}, bf16[144,256]{1,0:T(8,128)(2,1)S(1)}, u32[]{:S(2)}, u32[]{:S(2)}) collective-permute-start(bf16[144,256]{1,0:T(8,128)(2,1)S(1)} %get-tuple-element.51), channel_id=1, source_target_pairs={{0,12},{4,16},{8,20},{12,24},{16,28},{20,0},{24,4},{28,8},{1,13},{... | collective-permute-start | bytes 221192 | tf_op jit(solution)/shard_map/ppermute | solution.py:46
  68.1 20.9 %collective-permute-start.20 = (bf16[384,256]{1,0:T(8,128)(2,1)S(1)}, bf16[384,256]{1,0:T(8,128)(2,1)S(1)}, u32[]{:S(2)}, u32[]{:S(2)}) collective-permute-start(bf16[384,256]{1,0:T(8,128)(2,1)S(1)} %merge_short.1.refs_10_.refs_1_), channel_id=1, source_target_pairs={{0,1},{1,0},{2,3},{3,2},{4,5},{5,4},{6,7},{7,6},{8,9},{9,8},{10,11... | collective-permute-start | bytes 589832 | tf_op jit(solution)/shard_map/ppermute | solution.py:51
  68.2 20.8 %collective-permute-start.22 = (bf16[384,256]{1,0:T(8,128)(2,1)S(1)}, bf16[384,256]{1,0:T(8,128)(2,1)S(1)}, u32[]{:S(2)}, u32[]{:S(2)}) collective-permute-start(bf16[384,256]{1,0:T(8,128)(2,1)S(1)} %collective-permute-done.21.refs_3_), channel_id=1, source_target_pairs={{0,1},{1,0},{2,3},{3,2},{4,5},{5,4},{6,7},{7,6},{8,9},{9,8},{10,11... | collective-permute-start | bytes 589832 | tf_op jit(solution)/shard_map/ppermute | solution.py:51
  72.4 6.3 %collective-permute-start.15 = (bf16[144,256]{1,0:T(8,128)(2,1)S(1)}, bf16[144,256]{1,0:T(8,128)(2,1)S(1)}, u32[]{:S(2)}, u32[]{:S(2)}) collective-permute-start(bf16[144,256]{1,0:T(8,128)(2,1)S(1)} %get-tuple-element.54.refs_4_), channel_id=1, source_target_pairs={{0,8},{4,12},{8,16},{12,20},{16,24},{20,28},{24,0},{28,4},{1,9},{5... | collective-permute-start | bytes 221192 | tf_op jit(solution)/shard_map/ppermute | solution.py:46
  72.4 5.8 %collective-permute-start.12 = (bf16[144,256]{1,0:T(8,128)(2,1)S(1)}, bf16[144,256]{1,0:T(8,128)(2,1)S(1)}, u32[]{:S(2)}, u32[]{:S(2)}) collective-permute-start(bf16[144,256]{1,0:T(8,128)(2,1)S(1)} %get-tuple-element.52), channel_id=1, source_target_pairs={{0,24},{4,28},{8,0},{12,4},{16,8},{20,12},{24,16},{28,20},{1,25},{... | collective-permute-start | bytes 221192 | tf_op jit(solution)/shard_map/ppermute | solution.py:46
  76.2 7.1 %collective-permute-start.16 = (bf16[144,256]{1,0:T(8,128)(2,1)S(1)}, bf16[144,256]{1,0:T(8,128)(2,1)S(1)}, u32[]{:S(2)}, u32[]{:S(2)}) collective-permute-start(bf16[144,256]{1,0:T(8,128)(2,1)S(1)} %get-tuple-element.55), channel_id=1, source_target_pairs={{0,4},{4,8},{8,12},{12,16},{16,20},{20,24},{24,28},{28,0},{1,5},{5... | collective-permute-start | bytes 221192 | tf_op jit(solution)/shard_map/ppermute | solution.py:46
  84.7 4.3 %collective-permute-start.18 = (bf16[128,256]{1,0:T(8,128)(2,1)S(1)}, bf16[128,256]{1,0:T(8,128)(2,1)S(1)}, u32[]{:S(2)}, u32[]{:S(2)}) collective-permute-start(bf16[128,256]{1,0:T(8,128)(2,1)S(1)} %merge_long.1.refs_1_), channel_id=1, source_target_pairs={{0,2},{1,3},{2,0},{3,1},{4,6},{5,7},{6,4},{7,5},{8,10},{9,11},{10,... | collective-permute-start | bytes 196616 | tf_op jit(solution)/shard_map/ppermute | solution.py:51
  86.0 11.2 %collective-permute-start.17 = (bf16[128,256]{1,0:T(8,128)(2,1)S(1)}, bf16[128,256]{1,0:T(8,128)(2,1)S(1)}, u32[]{:S(2)}, u32[]{:S(2)}) collective-permute-start(bf16[128,256]{1,0:T(8,128)(2,1)S(1)} %merge_long.1.refs_1_), channel_id=1, source_target_pairs={{0,1},{1,0},{2,3},{3,2},{4,5},{5,4},{6,7},{7,6},{8,9},{9,8},{10,11... | collective-permute-start | bytes 196616 | tf_op jit(solution)/shard_map/ppermute | solution.py:51
  89.0 8.3 %collective-permute-start.19 = (bf16[128,256]{1,0:T(8,128)(2,1)S(1)}, bf16[128,256]{1,0:T(8,128)(2,1)S(1)}, u32[]{:S(2)}, u32[]{:S(2)}) collective-permute-start(bf16[128,256]{1,0:T(8,128)(2,1)S(1)} %collective-permute-done.18.refs_3_), channel_id=1, source_target_pairs={{0,1},{1,0},{2,3},{3,2},{4,5},{5,4},{6,7},{7,6},{8,9},{9,8},{10,11... | collective-permute-start | bytes 196616 | tf_op jit(solution)/shard_map/ppermute | solution.py:51
  95.0 14.6 %collective-permute-start.26 = (bf16[384,256]{1,0:T(8,128)(2,1)S(1)}, bf16[384,256]{1,0:T(8,128)(2,1)S(1)}, u32[]{:S(2)}, u32[]{:S(2)}) collective-permute-start(bf16[384,256]{1,0:T(8,128)(2,1)S(1)} %get-tuple-element.63), channel_id=1, source_target_pairs={{0,2},{1,3},{2,0},{3,1},{4,6},{5,7},{6,4},{7,5},{8,10},{9,11},{10,... | collective-permute-start | bytes 589832 | tf_op jit(solution)/shard_map/ppermute | solution.py:51
  96.4 13.3 %collective-permute-start.27 = (bf16[384,256]{1,0:T(8,128)(2,1)S(1)}, bf16[384,256]{1,0:T(8,128)(2,1)S(1)}, u32[]{:S(2)}, u32[]{:S(2)}) collective-permute-start(bf16[384,256]{1,0:T(8,128)(2,1)S(1)} %get-tuple-element.64), channel_id=1, source_target_pairs={{0,3},{1,2},{2,1},{3,0},{4,7},{5,6},{6,5},{7,4},{8,11},{9,10},{10,... | collective-permute-start | bytes 589832 | tf_op jit(solution)/shard_map/ppermute | solution.py:51
  96.9 12.7 %collective-permute-start.28 = (bf16[384,256]{1,0:T(8,128)(2,1)S(1)}, bf16[384,256]{1,0:T(8,128)(2,1)S(1)}, u32[]{:S(2)}, u32[]{:S(2)}) collective-permute-start(bf16[384,256]{1,0:T(8,128)(2,1)S(1)} %get-tuple-element.65), channel_id=1, source_target_pairs={{0,1},{1,0},{2,3},{3,2},{4,5},{5,4},{6,7},{7,6},{8,9},{9,8},{10,11... | collective-permute-start | bytes 589832 | tf_op jit(solution)/shard_map/ppermute | solution.py:51
  101.5 6.9 %collective-permute-start.23 = (bf16[128,256]{1,0:T(8,128)(2,1)S(1)}, bf16[128,256]{1,0:T(8,128)(2,1)S(1)}, u32[]{:S(2)}, u32[]{:S(2)}) collective-permute-start(bf16[128,256]{1,0:T(8,128)(2,1)S(1)} %get-tuple-element.58), channel_id=1, source_target_pairs={{0,2},{1,3},{2,0},{3,1},{4,6},{5,7},{6,4},{7,5},{8,10},{9,11},{10,... | collective-permute-start | bytes 196616 | tf_op jit(solution)/shard_map/ppermute | solution.py:51
  102.9 6.1 %collective-permute-start.24 = (bf16[128,256]{1,0:T(8,128)(2,1)S(1)}, bf16[128,256]{1,0:T(8,128)(2,1)S(1)}, u32[]{:S(2)}, u32[]{:S(2)}) collective-permute-start(bf16[128,256]{1,0:T(8,128)(2,1)S(1)} %get-tuple-element.59), channel_id=1, source_target_pairs={{0,3},{1,2},{2,1},{3,0},{4,7},{5,6},{6,5},{7,4},{8,11},{9,10},{10,... | collective-permute-start | bytes 196616 | tf_op jit(solution)/shard_map/ppermute | solution.py:51
  110.1 3.8 %collective-permute-start.29 = (f32[8,512]{1,0:T(8,128)S(1)}, f32[8,512]{1,0:T(8,128)S(1)}, u32[]{:S(2)}, u32[]{:S(2)}) collective-permute-start(f32[8,512]{1,0:T(8,128)S(1)} %get-tuple-element.68.refs_4_), channel_id=1, source_target_pairs={{0,2},{1,3},{2,0},{3,1},{4,6},{5,7},{6,4},{7,5},{8,10},{9,11},{10,... | collective-permute-start | bytes 49160 | tf_op jit(solution)/shard_map/ppermute | solution.py:51
  111.4 3.3 %collective-permute-start.30 = (f32[8,512]{1,0:T(8,128)S(1)}, f32[8,512]{1,0:T(8,128)S(1)}, u32[]{:S(2)}, u32[]{:S(2)}) collective-permute-start(f32[8,512]{1,0:T(8,128)S(1)} %get-tuple-element.68.refs_4_), channel_id=1, source_target_pairs={{0,3},{1,2},{2,1},{3,0},{4,7},{5,6},{6,5},{7,4},{8,11},{9,10},{10,... | collective-permute-start | bytes 49160 | tf_op jit(solution)/shard_map/ppermute | solution.py:51
  111.7 3.1 %collective-permute-start.31 = (f32[8,512]{1,0:T(8,128)S(1)}, f32[8,512]{1,0:T(8,128)S(1)}, u32[]{:S(2)}, u32[]{:S(2)}) collective-permute-start(f32[8,512]{1,0:T(8,128)S(1)} %get-tuple-element.68.refs_4_), channel_id=1, source_target_pairs={{0,1},{1,0},{2,3},{3,2},{4,5},{5,4},{6,7},{7,6},{8,9},{9,8},{10,11... | collective-permute-start | bytes 49160 | tf_op jit(solution)/shard_map/ppermute | solution.py:51
  (11 other events, 110.5 us)
Sparse Core Ops, SparseCore 0:
  9.6 25.2 all-gather.1

commit v3 on v2

--- a/solution.py
+++ b/solution.py
@@ -343,10 +343,11 @@
 def forward_kernel(dims, len_ref, *refs):
     requests, draft, page_len, first, count = dims
     att, hid = refs[0:4], refs[4:8]
-    wout_ref, gain_ref, up_ref, down_ref = refs[8:12]
-    parts, normed_ref = refs[12:16], refs[16]
-    order_ref, z_ref, hid_v, wout_v, up_v, down_v, sems = refs[17:]
-    pairs = [(hid[k], hid_v.at[k]) for k in range(4)] + [(wout_ref, wout_v), (up_ref, up_v), (down_ref, down_v)]
+    wout, (gain_ref, up_ref, down_ref) = refs[8:12], refs[12:15]
+    parts, normed_ref = refs[15:19], refs[19]
+    order_ref, z_ref, hid_v, wout_v, up_v, down_v, sems = refs[20:]
+    pairs = [(hid[k], hid_v.at[k]) for k in range(4)] + [(wout[k], wout_v.at[k]) for k in range(4)]
+    pairs += [(up_ref, up_v), (down_ref, down_v)]
     copies = [pltpu.make_async_copy(src, dst, sems.at[n]) for n, (src, dst) in enumerate(pairs)]
     for copy in copies:
         copy.start()
@@ -361,11 +362,11 @@
         for flip in range(4):
             at = pl.ds(pl.multiple_of((me ^ flip) * share, share), share)
             z_ref[pl.ds(p * draft, draft), at] = hid_v[flip, rows, :].astype(F32)
-    copies[4].wait()
+    for copy in copies[4:8]:
+        copy.wait()
     branch = None
     for flip in range(4):
-        at = pl.ds(pl.multiple_of((me ^ flip) * share, share), share)
-        term = jnp.dot(att[flip][...], wout_v[at, :], preferred_element_type=F32)
+        term = jnp.dot(att[flip][...], wout_v[flip], preferred_element_type=F32)
         branch = term if branch is None else branch + term
     z = z_ref[...] + branch
     sums = jnp.sum(z, axis=-1, keepdims=True)
@@ -374,10 +375,10 @@
     normed = normed_wide.astype(BF16)
     z_ref[...] = normed_wide
     normed_ref[...] = z_ref[:, pl.ds(pl.multiple_of(me * share, share), share)].astype(BF16)
-    copies[5].wait()
+    copies[8].wait()
     inner = jnp.dot(normed, up_v[...], preferred_element_type=F32)
     inner = (0.5 * inner * (1.0 + lax.erf(inner * (0.5 ** 0.5)))).astype(BF16)
-    copies[6].wait()
+    copies[9].wait()
     for flip in range(4):
         at = pl.ds(pl.multiple_of((me ^ flip) * share, share), share)
         parts[flip][...] = jnp.dot(inner, down_v[:, at], preferred_element_type=F32).astype(BF16)
@@ -448,8 +449,6 @@
 
     hid_y = send_tp(hidden_in, 2)
     hid_core = send_tp(hidden_in, 1)
-    wout = lax.all_gather(w_out, "tp", axis=0, tiled=True)
-
     bias, select = call(
         functools.partial(tree_kernel, (requests, draft)),
         [shape_of((tokens, draft), F32), shape_of((requests * draft // side, 2 * side, 2 * side), BF16)],
@@ -476,7 +475,7 @@
     )
     near_asked = send_req(near_message, 1)
     queue = sorted(range(2, pages), key=lambda j: (abs(2 * j - pages), j))
-    early, late = queue[:4], queue[4:]
+    early, late = queue, []
     asked = {j: send_req(message, j) for j in early}
 
     key_new, value_new, accepted = call(
@@ -505,13 +504,11 @@
     )
     near_got = send_req(near_answer, -1)
     answers = [send_req(out, -j) for j, out in zip(early, outs)]
-    outs = call(
-        functools.partial(remote_kernel, (page_len, draft, heads, long_count), tuple(late)),
-        [answer] * len(late), [VMEM] * len(late) + [SMEM, ANY], [VMEM] * len(late), buffers(len(late)),
-        (*[asked[j] for j in late], page_table, cache_pool), "visitors_late", after=(near_answer,),
-    )
-    answers += [send_req(out, -j) for j, out in zip(late, outs)]
-    last = (outs[0],)
+    last = (near_answer,)
+
+    w_later, _ = lax.optimization_barrier((w_out, near_answer))
+    wout_core = send_tp(w_later, 1)
+    wout_y = send_tp(w_later, 2)
 
     def merge(span, msgs, name, after):
         return call(
@@ -529,17 +526,19 @@
         part = shape_of((rows, share), BF16)
         outs = call(
             functools.partial(forward_kernel, (requests, draft, page_len, first, count)),
-            [part] * 5, [SMEM] + [VMEM] * 4 + [ANY] * 5 + [VMEM] + [ANY] * 2, [VMEM] * 5,
+            [part] * 5, [SMEM] + [VMEM] * 4 + [ANY] * 8 + [VMEM] + [ANY] * 2, [VMEM] * 5,
             [order, pltpu.VMEM((rows, width_all), F32), pltpu.VMEM((4, tokens, share), BF16)]
-            + [pltpu.VMEM(w.shape, BF16) for w in (wout, w_up, w_down)] + [dma((7,))],
+            + [pltpu.VMEM((4,) + w_out.shape, BF16), pltpu.VMEM(w_up.shape, BF16), pltpu.VMEM(w_down.shape, BF16), dma((10,))],
             (cache_len, attended, att_core, att_y, att_diag, *stay, gain_1, w_up, w_down), name,
             flops=2 * rows * width_all * (width_all + 2 * w_up.shape[1]), nbytes=3 * 2 * 1024 * 1024, after=after,
         )
         got = [send_tp(outs[flip], flip) for flip in (2, 3, 1)]
         return outs, [outs[0], *got, outs[4]]
 
-    stay = tuple(pltpu.with_memory_space_constraint(a, pltpu.HBM) for a in (*hid, wout))
-    merged_short = merge((long_count, requests), (), "merge_short", last)
+    wout_y_later, _ = lax.optimization_barrier((wout_y, near_got))
+    wout = (w_out, wout_core, wout_y, send_tp(wout_y_later, 1))
+    stay = tuple(pltpu.with_memory_space_constraint(a, pltpu.HBM) for a in (*hid, *wout))
+    merged_short = merge((long_count, requests), (), "merge_short", last + tuple(answers) + (wout_y,))
     outs_short, parts_short = forward(merged_short, long_count, requests - long_count, "forward_short", ())
     merged_long = merge((0, long_count), answers, "merge_long", (merged_short,))
     outs_long, parts_long = forward(merged_long, 0, long_count, "forward_long", (outs_short[4],))

time: 123 us -> 110 us (0.89)
  between operations: 14.2 us -> 0.82 us
  starting transfers between devices: 34.5 us -> 37.7 us
  Pallas kernels: 35.7 us -> 33.6 us
  waiting for transfers between devices: 37.3 us -> 35.2 us
  local copies, waits for them, and re-layouts: 1.46 us -> 2.91 us
    ppermute x14, waiting for transfers between devices: 23.3 us -> 16 us  [send_req(): lax.ppermute(value, 'req', [(i, (i + by) % size) for i in range(size)])]
    ppermute x18 -> x21, waiting for transfers between devices: 13.3 us -> 19.1 us  [send_tp(): return lax.ppermute(value, 'tp', [(i, i ^ flip) for i in range(size)])]
    pallas_call x13 -> x12, Pallas kernels: 35.7 us -> 33.6 us  [call(): pl.pallas_call(body, out_shape=outs, in_specs=list(ins) + [ANY] * len(aft...]
    ppermute x14, starting transfers between devices: 22.3 us -> 24.1 us  [send_req(): lax.ppermute(value, 'req', [(i, (i + by) % size) for i in range(size)])]
    ppermute x18 -> x21, starting transfers between devices: 12.1 us -> 13.7 us  [send_tp(): return lax.ppermute(value, 'tp', [(i, i ^ flip) for i in range(size)])]
    unnamed x20 -> x28, local copies, waits for them, and re-layouts: 0.7 us -> 2.15 us
  transfers between devices with their start and end apart: 33 -> 35, of which waited for: 14 -> 15; matrix products, arithmetic and copies ran while one was open for 1% -> 1% of each run, Pallas kernels for 27% -> 22%
where the time goes in v3:
time: 110 us
  starting transfers between devices  37.7 us (34%)
  waiting for transfers between devices  35.2 us (32%)
  Pallas kernels  33.6 us (31%)
  local copies, waits for them, and re-layouts  2.91 us (3%)
    pallas_call x12, Pallas kernels, call(): pl.pallas_call(body, out_shape=outs, in_specs=list(ins) + [ANY] * len(aft...  33.6 us
    ppermute x14, starting transfers between devices, send_req(): lax.ppermute(value, 'req', [(i, (i + by) % size) for i in range(size)])  24.1 us
    ppermute x21, waiting for transfers between devices, send_tp(): return lax.ppermute(value, 'tp', [(i, i ^ flip) for i in range(size)])  19.1 us
    ppermute x14, waiting for transfers between devices, send_req(): lax.ppermute(value, 'req', [(i, (i + by) % size) for i in range(size)])  16 us
    ppermute x21, starting transfers between devices, send_tp(): return lax.ppermute(value, 'tp', [(i, i ^ flip) for i in range(size)])  13.7 us
  transfers between devices with their start and end apart: 35, of which 15 were waited for; matrix products, arithmetic and copies ran while one was open for 1% of the time, Pallas kernels for 22%

profile of v3, /device:TPU:0, one launch (start us, length us, event | category | flops | bytes accessed | tf_op | source)
XLA Modules:
  0.0 110.2 jit_solution(17217286588399012862)
XLA Ops:
  0.6 3.0 %collective-permute-start.1 = (bf16[512,256]{1,0:T(8,128)(2,1)}, bf16[512,256]{1,0:T(8,128)(2,1)S(1)}, u32[]{:S(2)}, u32[]{:S(2)}) collective-permute-start(bf16[512,256]{1,0:T(8,128)(2,1)} %refs_5_.3), channel_id=1, source_target_pairs={{0,2},{1,3},{2,0},{3,1},{4,6},{5,7},{6,4},{7,5},{8,10},{9,11},{10,... | collective-permute-start | bytes 786440 | tf_op jit(solution)/shard_map/ppermute | solution.py:51
  5.1 2.3 %tree.1 = (f32[512,64]{1,0:T(8,128)S(1)}, bf16[2,512,512]{2,1,0:T(8,128)(2,1)S(1)}) custom-call(s32[8]{0:T(128)S(1)} %copy-done.10, s32[2,256]{1,0:T(2,128)S(1)} %reshape.17.refs_1_), custom_call_target="tpu_custom_call" | custom-call | flops 469762048 | tf_op jit(solution)/shard_map/tree/pallas_call | solution.py:32
  8.1 3.3 %pages.1 = (bf16[2,8,128,256]{3,2,1,0:T(8,128)(2,1)S(1)}, bf16[2,8,128,256]{3,2,1,0:T(8,128)(2,1)S(1)}) custom-call(s32[8,8]{1,0:T(8,128)S(1)} %copy-done.7, bf16[64,128,2,256]{3,2,1,0:T(2,128)(2,1)} %refs_10_.1), custom_call_target="tpu_custom_call" | custom-call | flops 536870912 | tf_op jit(solution)/shard_map/pages/pallas_call | solution.py:32
  14.2 1.6 %collective-permute-start.3 = (bf16[528,256]{1,0:T(8,128)(2,1)S(1)}, bf16[528,256]{1,0:T(8,128)(2,1)S(1)}, u32[]{:S(2)}, u32[]{:S(2)}) collective-permute-start(bf16[528,256]{1,0:T(8,128)(2,1)S(1)} %get-tuple-element.48), channel_id=1, source_target_pairs={{0,4},{4,8},{8,12},{12,16},{16,20},{20,24},{24,28},{28,0},{1,5},{5... | collective-permute-start | bytes 811016 | tf_op jit(solution)/shard_map/ppermute | solution.py:46
  15.8 3.2 %collective-permute-start.9 = (bf16[144,256]{1,0:T(8,128)(2,1)S(1)}, bf16[144,256]{1,0:T(8,128)(2,1)S(1)}, u32[]{:S(2)}, u32[]{:S(2)}) collective-permute-start(bf16[144,256]{1,0:T(8,128)(2,1)S(1)} %get-tuple-element.42.refs_6_.refs_7_), channel_id=1, source_target_pairs={{0,28},{4,0},{8,4},{12,8},{16,12},{20,16},{24,20},{28,24},{1,29},{... | collective-permute-start | bytes 221192 | tf_op jit(solution)/shard_map/ppermute | solution.py:46
  19.0 1.8 %collective-permute-start.8 = (bf16[144,256]{1,0:T(8,128)(2,1)S(1)}, bf16[144,256]{1,0:T(8,128)(2,1)S(1)}, u32[]{:S(2)}, u32[]{:S(2)}) collective-permute-start(bf16[144,256]{1,0:T(8,128)(2,1)S(1)} %get-tuple-element.42.refs_6_.refs_7_), channel_id=1, source_target_pairs={{0,24},{4,28},{8,0},{12,4},{16,8},{20,12},{24,16},{28,20},{1,25},{... | collective-permute-start | bytes 221192 | tf_op jit(solution)/shard_map/ppermute | solution.py:46
  21.9 4.2 %collective-permute-start.5 = (bf16[144,256]{1,0:T(8,128)(2,1)S(1)}, bf16[144,256]{1,0:T(8,128)(2,1)S(1)}, u32[]{:S(2)}, u32[]{:S(2)}) collective-permute-start(bf16[144,256]{1,0:T(8,128)(2,1)S(1)} %get-tuple-element.42.refs_6_.refs_7_), channel_id=1, source_target_pairs={{0,12},{4,16},{8,20},{12,24},{16,28},{20,0},{24,4},{28,8},{1,13},{... | collective-permute-start | bytes 221192 | tf_op jit(solution)/shard_map/ppermute | solution.py:46
  26.1 2.3 %collective-permute-start.4 = (bf16[144,256]{1,0:T(8,128)(2,1)S(1)}, bf16[144,256]{1,0:T(8,128)(2,1)S(1)}, u32[]{:S(2)}, u32[]{:S(2)}) collective-permute-start(bf16[144,256]{1,0:T(8,128)(2,1)S(1)} %get-tuple-element.42.refs_6_.refs_7_), channel_id=1, source_target_pairs={{0,16},{4,20},{8,24},{12,28},{16,0},{20,4},{24,8},{28,12},{1,17},{... | collective-permute-start | bytes 221192 | tf_op jit(solution)/shard_map/ppermute | solution.py:46
  28.4 1.9 %keys_values.1 = (bf16[512,256]{1,0:T(8,128)(2,1)S(1)}, bf16[512,256]{1,0:T(8,128)(2,1)S(1)}, bf16[512,2,256]{2,1,0:T(2,128)(2,1)}) custom-call(bf16[512,256]{1,0:T(8,128)(2,1)S(1)} %copy-done.1, bf16[512,256]{1,0:T(8,128)(2,1)S(1)} %collective-permute-done.refs_2_.refs_1_.refs_6_, bf16[512,256]{1,0:T(8,128)(2,1)S(1)} %collective-permute-done.1.refs_3_.refs_2_.refs_7_, ...), custom_call_target="tpu_custom_call" | custom-call | flops 536870912 | bytes 1048576 | tf_op jit(solution)/shard_map/keys_values/pallas_call | solution.py:32
  30.3 3.4 %local_attention.1 = (f32[512,256]{1,0:T(8,128)S(1)}, f32[16,256]{1,0:T(8,128)S(1)}, bf16[144,256]{1,0:T(8,128)(2,1)}) custom-call(s32[8]{0:T(128)S(1)} %copy-done.6, bf16[512,256]{1,0:T(8,128)(2,1)S(1)} %get-tuple-element.40.refs_1_, bf16[512,256]{1,0:T(8,128)(2,1)S(1)} %get-tuple-element.43.refs_2_, bf16[512,256]{1,0:T(8,128)(2,1)S(1)} %get-tuple-element.44.refs_3_, ...), custom_call_target="tpu_custom_call" | custom-call | tf_op jit(solution)/shard_map/local_attention/pallas_call | solution.py:32
  33.7 1.7 %collective-permute-done.5.refs_4_ = bf16[144,256]{1,0:T(8,128)(2,1)S(1)} collective-permute-done((bf16[144,256]{1,0:T(8,128)(2,1)S(1)}, bf16[144,256]{1,0:T(8,128)(2,1)S(1)}, u32[]{:S(2)}, u32[]{:S(2)}) %collective-permute-start.5) | collective-permute-done | bytes 73760 | tf_op jit(solution)/shard_map/ppermute | solution.py:46
  35.4 6.8 %visitors_early.1 = (bf16[560,256]{1,0:T(8,128)(2,1)S(1)}, bf16[144,256]{1,0:T(8,128)(2,1)S(1)}, bf16[144,256]{1,0:T(8,128)(2,1)S(1)}, bf16[144,256]{1,0:T(8,128...) custom-call(bf16[528,256]{1,0:T(8,128)(2,1)S(1)} %collective-permute-done.3.ref, ...), custom_call_target="tpu_custom_call" | custom-call | tf_op jit(solution)/shard_map/visitors_early/pallas_call | solution.py:32
  42.8 4.1 %collective-permute-start.10 = (bf16[560,256]{1,0:T(8,128)(2,1)S(1)}, bf16[560,256]{1,0:T(8,128)(2,1)S(1)}, u32[]{:S(2)}, u32[]{:S(2)}) collective-permute-start(bf16[560,256]{1,0:T(8,128)(2,1)S(1)} %get-tuple-element.49.refs_4_), channel_id=1, source_target_pairs={{0,28},{4,0},{8,4},{12,8},{16,12},{20,16},{24,20},{28,24},{1,29},{... | collective-permute-start | bytes 860168 | tf_op jit(solution)/shard_map/ppermute | solution.py:46
  47.2 2.6 %collective-permute-start.13 = (bf16[144,256]{1,0:T(8,128)(2,1)S(1)}, bf16[144,256]{1,0:T(8,128)(2,1)S(1)}, u32[]{:S(2)}, u32[]{:S(2)}) collective-permute-start(bf16[144,256]{1,0:T(8,128)(2,1)S(1)} %get-tuple-element.52), channel_id=1, source_target_pairs={{0,12},{4,16},{8,20},{12,24},{16,28},{20,0},{24,4},{28,8},{1,13},{... | collective-permute-start | bytes 221192 | tf_op jit(solution)/shard_map/ppermute | solution.py:46
  49.8 4.9 %collective-permute-done.10.refs_3_ = bf16[560,256]{1,0:T(8,128)(2,1)S(1)} collective-permute-done((bf16[560,256]{1,0:T(8,128)(2,1)S(1)}, bf16[560,256]{1,0:T(8,128)(2,1)S(1)}, u32[]{:S(2)}, u32[]{:S(2)}) %collective-permute-start.10) | collective-permute-done | bytes 286752 | tf_op jit(solution)/shard_map/ppermute | solution.py:46
  56.1 3.0 %collective-permute-done.11.refs_5_.refs_4_ = bf16[144,256]{1,0:T(8,128)(2,1)S(1)} collective-permute-done((bf16[144,256]{1,0:T(8,128)(2,1)S(1)}, bf16[144,256]{1,0:T(8,128)(2,1)S(1)}, u32[]{:S(2)}, u32[]{:S(2)}) %collective-permute-start.11) | collective-permute-done | bytes 73760 | tf_op jit(solution)/shard_map/ppermute | solution.py:46
  59.1 2.2 %collective-permute-start.14 = (bf16[144,256]{1,0:T(8,128)(2,1)S(1)}, bf16[144,256]{1,0:T(8,128)(2,1)S(1)}, u32[]{:S(2)}, u32[]{:S(2)}) collective-permute-start(bf16[144,256]{1,0:T(8,128)(2,1)S(1)} %get-tuple-element.53), channel_id=1, source_target_pairs={{0,24},{4,28},{8,0},{12,4},{16,8},{20,12},{24,16},{28,20},{1,25},{... | collective-permute-start | bytes 221192 | tf_op jit(solution)/shard_map/ppermute | solution.py:46
  62.0 1.6 %collective-permute-done.14.refs_8_.refs_7_ = bf16[144,256]{1,0:T(8,128)(2,1)S(1)} collective-permute-done((bf16[144,256]{1,0:T(8,128)(2,1)S(1)}, bf16[144,256]{1,0:T(8,128)(2,1)S(1)}, u32[]{:S(2)}, u32[]{:S(2)}) %collective-permute-start.14) | collective-permute-done | bytes 73760 | tf_op jit(solution)/shard_map/ppermute | solution.py:46
  63.7 3.8 %collective-permute-done.15.refs_9_.refs_8_ = bf16[144,256]{1,0:T(8,128)(2,1)S(1)} collective-permute-done((bf16[144,256]{1,0:T(8,128)(2,1)S(1)}, bf16[144,256]{1,0:T(8,128)(2,1)S(1)}, u32[]{:S(2)}, u32[]{:S(2)}) %collective-permute-start.15) | collective-permute-done | bytes 73760 | tf_op jit(solution)/shard_map/ppermute | solution.py:46
  69.7 1.6 %collective-permute-start.24 = (bf16[384,256]{1,0:T(8,128)(2,1)S(1)}, bf16[384,256]{1,0:T(8,128)(2,1)S(1)}, u32[]{:S(2)}, u32[]{:S(2)}) collective-permute-start(bf16[384,256]{1,0:T(8,128)(2,1)S(1)} %merge_short.1.refs_10_.refs_1_), channel_id=1, source_target_pairs={{0,2},{1,3},{2,0},{3,1},{4,6},{5,7},{6,4},{7,5},{8,10},{9,11},{10,... | collective-permute-start | bytes 589832 | tf_op jit(solution)/shard_map/ppermute | solution.py:51
  71.3 4.1 %collective-permute-done.24.refs_3_ = bf16[384,256]{1,0:T(8,128)(2,1)S(1)} collective-permute-done((bf16[384,256]{1,0:T(8,128)(2,1)S(1)}, bf16[384,256]{1,0:T(8,128)(2,1)S(1)}, u32[]{:S(2)}, u32[]{:S(2)}) %collective-permute-start.24) | collective-permute-done | bytes 196640 | tf_op jit(solution)/shard_map/ppermute | solution.py:51
  75.4 1.4 %merge_long.1.refs_1_ = bf16[128,256]{1,0:T(8,128)(2,1)S(1)} custom-call(s32[8]{0:T(128)S(1)} %copy-done.6, f32[512,256]{1,0:T(8,128)S(1)} %get-tuple-element.46.refs_11_.refs_1_, f32[16,256]{1,0:T(8,128)S(1)} %get-tuple-element.47.refs_2_, bf16[560,256]{1,0:T(8,128)(2,1)S(1)} %collective-permute-done.10.refs_3_, ...), custom_call_target="tpu_custom_call" | custom-call | tf_op jit(solution)/shard_map/merge_long/pallas_call | solution.py:32
  76.8 1.6 %collective-permute-start.19 = (bf16[128,256]{1,0:T(8,128)(2,1)S(1)}, bf16[128,256]{1,0:T(8,128)(2,1)S(1)}, u32[]{:S(2)}, u32[]{:S(2)}) collective-permute-start(bf16[128,256]{1,0:T(8,128)(2,1)S(1)} %merge_long.1.refs_1_), channel_id=1, source_target_pairs={{0,2},{1,3},{2,0},{3,1},{4,6},{5,7},{6,4},{7,5},{8,10},{9,11},{10,... | collective-permute-start | bytes 196616 | tf_op jit(solution)/shard_map/ppermute | solution.py:51
  78.6 2.7 %collective-permute-done.19.refs_3_ = bf16[128,256]{1,0:T(8,128)(2,1)S(1)} collective-permute-done((bf16[128,256]{1,0:T(8,128)(2,1)S(1)}, bf16[128,256]{1,0:T(8,128)(2,1)S(1)}, u32[]{:S(2)}, u32[]{:S(2)}) %collective-permute-start.19) | collective-permute-done | bytes 65568 | tf_op jit(solution)/shard_map/ppermute | solution.py:51
  82.2 5.9 %forward_short.1 = (bf16[384,256]{1,0:T(8,128)(2,1)S(1)}, bf16[384,256]{1,0:T(8,128)(2,1)S(1)}, bf16[384,256]{1,0:T(8,128)(2,1)S(1)}, bf16[384,256]{1,0:T(8,128)(2,1)S(1)}, bf16[384,256]{1,0:T(8,128)(2,1)S(1)}) custom-call(s32[8]{0:T(128)S(1)} %copy-done.6, bf16[384,256]{1,0:T(8,128)(2,1)S(1)} %merge_short.1.refs_10_.refs_1_, ...), custom_call_target="tpu_custom_call" | custom-call | flops 2415919104 | bytes 6291456 | tf_op jit(solution)/shard_map/forward_short/pallas_call | solution.py:32
  88.1 1.6 %collective-permute-start.29 = (bf16[384,256]{1,0:T(8,128)(2,1)S(1)}, bf16[384,256]{1,0:T(8,128)(2,1)S(1)}, u32[]{:S(2)}, u32[]{:S(2)}) collective-permute-start(bf16[384,256]{1,0:T(8,128)(2,1)S(1)} %get-tuple-element.65), channel_id=1, source_target_pairs={{0,2},{1,3},{2,0},{3,1},{4,6},{5,7},{6,4},{7,5},{8,10},{9,11},{10,... | collective-permute-start | bytes 589832 | tf_op jit(solution)/shard_map/ppermute | solution.py:51
  90.3 4.3 %forward_long.1 = (bf16[128,256]{1,0:T(8,128)(2,1)S(1)}, bf16[128,256]{1,0:T(8,128)(2,1)S(1)}, bf16[128,256]{1,0:T(8,128)(2,1)S(1)}, bf16[128,256]{1,0:T(8,128)(2,1)S(1)}, bf16[128,256]{1,0:T(8,128)(2,1)S(1)}) custom-call(s32[8]{0:T(128)S(1)} %copy-done.6, bf16[128,256]{1,0:T(8,128)(2,1)S(1)} %merge_long.1.refs_1_, ...), custom_call_target="tpu_custom_call" | custom-call | flops 805306368 | bytes 6291456 | tf_op jit(solution)/shard_map/forward_long/pallas_call | solution.py:32
  94.6 1.6 %collective-permute-start.26 = (bf16[128,256]{1,0:T(8,128)(2,1)S(1)}, bf16[128,256]{1,0:T(8,128)(2,1)S(1)}, u32[]{:S(2)}, u32[]{:S(2)}) collective-permute-start(bf16[128,256]{1,0:T(8,128)(2,1)S(1)} %get-tuple-element.60), channel_id=1, source_target_pairs={{0,2},{1,3},{2,0},{3,1},{4,6},{5,7},{6,4},{7,5},{8,10},{9,11},{10,... | collective-permute-start | bytes 196616 | tf_op jit(solution)/shard_map/ppermute | solution.py:51
  96.3 5.2 %collective-permute-done.26.refs_1_ = bf16[128,256]{1,0:T(8,128)(2,1)S(1)} collective-permute-done((bf16[128,256]{1,0:T(8,128)(2,1)S(1)}, bf16[128,256]{1,0:T(8,128)(2,1)S(1)}, u32[]{:S(2)}, u32[]{:S(2)}) %collective-permute-start.26) | collective-permute-done | bytes 65568 | tf_op jit(solution)/shard_map/ppermute | solution.py:51
  103.4 1.5 %collective-permute-start.33 = (f32[8,512]{1,0:T(8,128)S(1)}, f32[8,512]{1,0:T(8,128)S(1)}, u32[]{:S(2)}, u32[]{:S(2)}) collective-permute-start(f32[8,512]{1,0:T(8,128)S(1)} %get-tuple-element.70.refs_4_), channel_id=1, source_target_pairs={{0,3},{1,2},{2,1},{3,0},{4,7},{5,6},{6,5},{7,4},{8,11},{9,10},{10,... | collective-permute-start | bytes 49160 | tf_op jit(solution)/shard_map/ppermute | solution.py:51
  106.5 2.1 %collective-permute-done.32.refs_5_ = f32[8,512]{1,0:T(8,128)S(1)} collective-permute-done((f32[8,512]{1,0:T(8,128)S(1)}, f32[8,512]{1,0:T(8,128)S(1)}, u32[]{:S(2)}, u32[]{:S(2)}) %collective-permute-start.32) | collective-permute-done | bytes 16416 | tf_op jit(solution)/shard_map/ppermute | solution.py:51
  108.6 1.6 %finish.1 = bf16[512,256]{1,0:T(8,128)(2,1)} custom-call(s32[8]{0:T(128)S(1)} %copy-done.6, f32[1,1024]{1,0:T(1,128)S(1)} %bitcast.8, f32[128,256]{1,0:T(8,128)S(1)} %get-tuple-element.68.refs_2_, f32[384,256]{1,0:T(8,128)S(1)} %get-tuple-element.69.refs_3_, f32[8,512]{1,0:T(8,128)S(1)} %get-tuple-element.70.refs_4_, ...), custom_call_target="tpu_custom_call" | custom-call | tf_op jit(solution)/shard_map/finish/pallas_call | solution.py:32
  (79 shorter events, 16.3 us)
Async XLA Ops:
  0.6 10.8 %collective-permute-start.1 = (bf16[512,256]{1,0:T(8,128)(2,1)}, bf16[512,256]{1,0:T(8,128)(2,1)S(1)}, u32[]{:S(2)}, u32[]{:S(2)}) collective-permute-start(bf16[512,256]{1,0:T(8,128)(2,1)} %refs_5_.3), channel_id=1, source_target_pairs={{0,2},{1,3},{2,0},{3,1},{4,6},{5,7},{6,4},{7,5},{8,10},{9,11},{10,... | collective-permute-start | bytes 786440 | tf_op jit(solution)/shard_map/ppermute | solution.py:51
  3.7 8.3 %collective-permute-start = (bf16[512,256]{1,0:T(8,128)(2,1)}, bf16[512,256]{1,0:T(8,128)(2,1)S(1)}, u32[]{:S(2)}, u32[]{:S(2)}) collective-permute-start(bf16[512,256]{1,0:T(8,128)(2,1)} %refs_5_.3), channel_id=1, source_target_pairs={{0,1},{1,0},{2,3},{3,2},{4,5},{5,4},{6,7},{7,6},{8,9},{9,8},{10,11... | collective-permute-start | bytes 786440 | tf_op jit(solution)/shard_map/ppermute | solution.py:51
  14.2 21.2 %collective-permute-start.3 = (bf16[528,256]{1,0:T(8,128)(2,1)S(1)}, bf16[528,256]{1,0:T(8,128)(2,1)S(1)}, u32[]{:S(2)}, u32[]{:S(2)}) collective-permute-start(bf16[528,256]{1,0:T(8,128)(2,1)S(1)} %get-tuple-element.48), channel_id=1, source_target_pairs={{0,4},{4,8},{8,12},{12,16},{16,20},{20,24},{24,28},{28,0},{1,5},{5... | collective-permute-start | bytes 811016 | tf_op jit(solution)/shard_map/ppermute | solution.py:46
  15.8 6.1 %collective-permute-start.9 = (bf16[144,256]{1,0:T(8,128)(2,1)S(1)}, bf16[144,256]{1,0:T(8,128)(2,1)S(1)}, u32[]{:S(2)}, u32[]{:S(2)}) collective-permute-start(bf16[144,256]{1,0:T(8,128)(2,1)S(1)} %get-tuple-element.42.refs_6_.refs_7_), channel_id=1, source_target_pairs={{0,28},{4,0},{8,4},{12,8},{16,12},{20,16},{24,20},{28,24},{1,29},{... | collective-permute-start | bytes 221192 | tf_op jit(solution)/shard_map/ppermute | solution.py:46
  19.0 7.1 %collective-permute-start.8 = (bf16[144,256]{1,0:T(8,128)(2,1)S(1)}, bf16[144,256]{1,0:T(8,128)(2,1)S(1)}, u32[]{:S(2)}, u32[]{:S(2)}) collective-permute-start(bf16[144,256]{1,0:T(8,128)(2,1)S(1)} %get-tuple-element.42.refs_6_.refs_7_), channel_id=1, source_target_pairs={{0,24},{4,28},{8,0},{12,4},{16,8},{20,12},{24,16},{28,20},{1,25},{... | collective-permute-start | bytes 221192 | tf_op jit(solution)/shard_map/ppermute | solution.py:46
  20.8 12.9 %collective-permute-start.7 = (bf16[144,256]{1,0:T(8,128)(2,1)S(1)}, bf16[144,256]{1,0:T(8,128)(2,1)S(1)}, u32[]{:S(2)}, u32[]{:S(2)}) collective-permute-start(bf16[144,256]{1,0:T(8,128)(2,1)S(1)} %get-tuple-element.42.refs_6_.refs_7_), channel_id=1, source_target_pairs={{0,8},{4,12},{8,16},{12,20},{16,24},{20,28},{24,0},{28,4},{1,9},{5... | collective-permute-start | bytes 221192 | tf_op jit(solution)/shard_map/ppermute | solution.py:46
  21.0 12.7 %collective-permute-start.6 = (bf16[144,256]{1,0:T(8,128)(2,1)S(1)}, bf16[144,256]{1,0:T(8,128)(2,1)S(1)}, u32[]{:S(2)}, u32[]{:S(2)}) collective-permute-start(bf16[144,256]{1,0:T(8,128)(2,1)S(1)} %get-tuple-element.42.refs_6_.refs_7_), channel_id=1, source_target_pairs={{0,20},{4,24},{8,28},{12,0},{16,4},{20,8},{24,12},{28,16},{1,21},{... | collective-permute-start | bytes 221192 | tf_op jit(solution)/shard_map/ppermute | solution.py:46
  21.9 13.5 %collective-permute-start.5 = (bf16[144,256]{1,0:T(8,128)(2,1)S(1)}, bf16[144,256]{1,0:T(8,128)(2,1)S(1)}, u32[]{:S(2)}, u32[]{:S(2)}) collective-permute-start(bf16[144,256]{1,0:T(8,128)(2,1)S(1)} %get-tuple-element.42.refs_6_.refs_7_), channel_id=1, source_target_pairs={{0,12},{4,16},{8,20},{12,24},{16,28},{20,0},{24,4},{28,8},{1,13},{... | collective-permute-start | bytes 221192 | tf_op jit(solution)/shard_map/ppermute | solution.py:46
  26.1 9.3 %collective-permute-start.4 = (bf16[144,256]{1,0:T(8,128)(2,1)S(1)}, bf16[144,256]{1,0:T(8,128)(2,1)S(1)}, u32[]{:S(2)}, u32[]{:S(2)}) collective-permute-start(bf16[144,256]{1,0:T(8,128)(2,1)S(1)} %get-tuple-element.42.refs_6_.refs_7_), channel_id=1, source_target_pairs={{0,16},{4,20},{8,24},{12,28},{16,0},{20,4},{24,8},{28,12},{1,17},{... | collective-permute-start | bytes 221192 | tf_op jit(solution)/shard_map/ppermute | solution.py:46
  42.3 13.8 %collective-permute-start.17 = (bf16[256,1024]{1,0:T(8,128)(2,1)S(1)}, bf16[256,1024]{1,0:T(8,128)(2,1)S(1)}, u32[]{:S(2)}, u32[]{:S(2)}) collective-permute-start(bf16[256,1024]{1,0:T(8,128)(2,1)S(1)} %copy-done.11), channel_id=1, source_target_pairs={{0,2},{1,3},{2,0},{3,1},{4,6},{5,7},{6,4},{7,5},{8,10},{9,11},{10,... | collective-permute-start | bytes 1572872 | tf_op jit(solution)/shard_map/ppermute | solution.py:51
  42.8 11.9 %collective-permute-start.10 = (bf16[560,256]{1,0:T(8,128)(2,1)S(1)}, bf16[560,256]{1,0:T(8,128)(2,1)S(1)}, u32[]{:S(2)}, u32[]{:S(2)}) collective-permute-start(bf16[560,256]{1,0:T(8,128)(2,1)S(1)} %get-tuple-element.49.refs_4_), channel_id=1, source_target_pairs={{0,28},{4,0},{8,4},{12,8},{16,12},{20,16},{24,20},{28,24},{1,29},{... | collective-permute-start | bytes 860168 | tf_op jit(solution)/shard_map/ppermute | solution.py:46
  46.9 12.2 %collective-permute-start.11 = (bf16[144,256]{1,0:T(8,128)(2,1)S(1)}, bf16[144,256]{1,0:T(8,128)(2,1)S(1)}, u32[]{:S(2)}, u32[]{:S(2)}) collective-permute-start(bf16[144,256]{1,0:T(8,128)(2,1)S(1)} %get-tuple-element.50), channel_id=1, source_target_pairs={{0,16},{4,20},{8,24},{12,28},{16,0},{20,4},{24,8},{28,12},{1,17},{... | collective-permute-start | bytes 221192 | tf_op jit(solution)/shard_map/ppermute | solution.py:46
  46.9 14.4 %collective-permute-start.12 = (bf16[144,256]{1,0:T(8,128)(2,1)S(1)}, bf16[144,256]{1,0:T(8,128)(2,1)S(1)}, u32[]{:S(2)}, u32[]{:S(2)}) collective-permute-start(bf16[144,256]{1,0:T(8,128)(2,1)S(1)} %get-tuple-element.51), channel_id=1, source_target_pairs={{0,20},{4,24},{8,28},{12,0},{16,4},{20,8},{24,12},{28,16},{1,21},{... | collective-permute-start | bytes 221192 | tf_op jit(solution)/shard_map/ppermute | solution.py:46
  47.2 14.1 %collective-permute-start.13 = (bf16[144,256]{1,0:T(8,128)(2,1)S(1)}, bf16[144,256]{1,0:T(8,128)(2,1)S(1)}, u32[]{:S(2)}, u32[]{:S(2)}) collective-permute-start(bf16[144,256]{1,0:T(8,128)(2,1)S(1)} %get-tuple-element.52), channel_id=1, source_target_pairs={{0,12},{4,16},{8,20},{12,24},{16,28},{20,0},{24,4},{28,8},{1,13},{... | collective-permute-start | bytes 221192 | tf_op jit(solution)/shard_map/ppermute | solution.py:46
  54.7 23.7 %collective-permute-start.21 = (bf16[256,1024]{1,0:T(8,128)(2,1)S(1)}, bf16[256,1024]{1,0:T(8,128)(2,1)S(1)}, u32[]{:S(2)}, u32[]{:S(2)}) collective-permute-start(bf16[256,1024]{1,0:T(8,128)(2,1)S(1)} %copy-done.11), channel_id=1, source_target_pairs={{0,1},{1,0},{2,3},{3,2},{4,5},{5,4},{6,7},{7,6},{8,9},{9,8},{10,11... | collective-permute-start | bytes 1572872 | tf_op jit(solution)/shard_map/ppermute | solution.py:51
  56.1 25.3 %collective-permute-start.22 = (bf16[256,1024]{1,0:T(8,128)(2,1)S(1)}, bf16[256,1024]{1,0:T(8,128)(2,1)S(1)}, u32[]{:S(2)}, u32[]{:S(2)}) collective-permute-start(bf16[256,1024]{1,0:T(8,128)(2,1)S(1)} %collective-permute-done.17.refs_11_), channel_id=1, source_target_pairs={{0,1},{1,0},{2,3},{3,2},{4,5},{5,4},{6,7},{7,6},{8,9},{9,8},{10,11... | collective-permute-start | bytes 1572872 | tf_op jit(solution)/shard_map/ppermute | solution.py:51
  59.1 4.6 %collective-permute-start.14 = (bf16[144,256]{1,0:T(8,128)(2,1)S(1)}, bf16[144,256]{1,0:T(8,128)(2,1)S(1)}, u32[]{:S(2)}, u32[]{:S(2)}) collective-permute-start(bf16[144,256]{1,0:T(8,128)(2,1)S(1)} %get-tuple-element.53), channel_id=1, source_target_pairs={{0,24},{4,28},{8,0},{12,4},{16,8},{20,12},{24,16},{28,20},{1,25},{... | collective-permute-start | bytes 221192 | tf_op jit(solution)/shard_map/ppermute | solution.py:46
  61.3 6.2 %collective-permute-start.15 = (bf16[144,256]{1,0:T(8,128)(2,1)S(1)}, bf16[144,256]{1,0:T(8,128)(2,1)S(1)}, u32[]{:S(2)}, u32[]{:S(2)}) collective-permute-start(bf16[144,256]{1,0:T(8,128)(2,1)S(1)} %get-tuple-element.54), channel_id=1, source_target_pairs={{0,8},{4,12},{8,16},{12,20},{16,24},{20,28},{24,0},{28,4},{1,9},{5... | collective-permute-start | bytes 221192 | tf_op jit(solution)/shard_map/ppermute | solution.py:46
  61.3 7.1 %collective-permute-start.16 = (bf16[144,256]{1,0:T(8,128)(2,1)S(1)}, bf16[144,256]{1,0:T(8,128)(2,1)S(1)}, u32[]{:S(2)}, u32[]{:S(2)}) collective-permute-start(bf16[144,256]{1,0:T(8,128)(2,1)S(1)} %get-tuple-element.55), channel_id=1, source_target_pairs={{0,4},{4,8},{8,12},{12,16},{16,20},{20,24},{24,28},{28,0},{1,5},{5... | collective-permute-start | bytes 221192 | tf_op jit(solution)/shard_map/ppermute | solution.py:46
  69.7 5.7 %collective-permute-start.24 = (bf16[384,256]{1,0:T(8,128)(2,1)S(1)}, bf16[384,256]{1,0:T(8,128)(2,1)S(1)}, u32[]{:S(2)}, u32[]{:S(2)}) collective-permute-start(bf16[384,256]{1,0:T(8,128)(2,1)S(1)} %merge_short.1.refs_10_.refs_1_), channel_id=1, source_target_pairs={{0,2},{1,3},{2,0},{3,1},{4,6},{5,7},{6,4},{7,5},{8,10},{9,11},{10,... | collective-permute-start | bytes 589832 | tf_op jit(solution)/shard_map/ppermute | solution.py:51
  71.3 10.1 %collective-permute-start.23 = (bf16[384,256]{1,0:T(8,128)(2,1)S(1)}, bf16[384,256]{1,0:T(8,128)(2,1)S(1)}, u32[]{:S(2)}, u32[]{:S(2)}) collective-permute-start(bf16[384,256]{1,0:T(8,128)(2,1)S(1)} %merge_short.1.refs_10_.refs_1_), channel_id=1, source_target_pairs={{0,1},{1,0},{2,3},{3,2},{4,5},{5,4},{6,7},{7,6},{8,9},{9,8},{10,11... | collective-permute-start | bytes 589832 | tf_op jit(solution)/shard_map/ppermute | solution.py:51
  75.4 6.0 %collective-permute-start.25 = (bf16[384,256]{1,0:T(8,128)(2,1)S(1)}, bf16[384,256]{1,0:T(8,128)(2,1)S(1)}, u32[]{:S(2)}, u32[]{:S(2)}) collective-permute-start(bf16[384,256]{1,0:T(8,128)(2,1)S(1)} %collective-permute-done.24.refs_3_), channel_id=1, source_target_pairs={{0,1},{1,0},{2,3},{3,2},{4,5},{5,4},{6,7},{7,6},{8,9},{9,8},{10,11... | collective-permute-start | bytes 589832 | tf_op jit(solution)/shard_map/ppermute | solution.py:51
  76.8 4.6 %collective-permute-start.19 = (bf16[128,256]{1,0:T(8,128)(2,1)S(1)}, bf16[128,256]{1,0:T(8,128)(2,1)S(1)}, u32[]{:S(2)}, u32[]{:S(2)}) collective-permute-start(bf16[128,256]{1,0:T(8,128)(2,1)S(1)} %merge_long.1.refs_1_), channel_id=1, source_target_pairs={{0,2},{1,3},{2,0},{3,1},{4,6},{5,7},{6,4},{7,5},{8,10},{9,11},{10,... | collective-permute-start | bytes 196616 | tf_op jit(solution)/shard_map/ppermute | solution.py:51
  78.4 11.9 %collective-permute-start.18 = (bf16[128,256]{1,0:T(8,128)(2,1)S(1)}, bf16[128,256]{1,0:T(8,128)(2,1)S(1)}, u32[]{:S(2)}, u32[]{:S(2)}) collective-permute-start(bf16[128,256]{1,0:T(8,128)(2,1)S(1)} %merge_long.1.refs_1_), channel_id=1, source_target_pairs={{0,1},{1,0},{2,3},{3,2},{4,5},{5,4},{6,7},{7,6},{8,9},{9,8},{10,11... | collective-permute-start | bytes 196616 | tf_op jit(solution)/shard_map/ppermute | solution.py:51
  81.4 8.9 %collective-permute-start.20 = (bf16[128,256]{1,0:T(8,128)(2,1)S(1)}, bf16[128,256]{1,0:T(8,128)(2,1)S(1)}, u32[]{:S(2)}, u32[]{:S(2)}) collective-permute-start(bf16[128,256]{1,0:T(8,128)(2,1)S(1)} %collective-permute-done.19.refs_3_), channel_id=1, source_target_pairs={{0,1},{1,0},{2,3},{3,2},{4,5},{5,4},{6,7},{7,6},{8,9},{9,8},{10,11... | collective-permute-start | bytes 196616 | tf_op jit(solution)/shard_map/ppermute | solution.py:51
  88.1 14.6 %collective-permute-start.29 = (bf16[384,256]{1,0:T(8,128)(2,1)S(1)}, bf16[384,256]{1,0:T(8,128)(2,1)S(1)}, u32[]{:S(2)}, u32[]{:S(2)}) collective-permute-start(bf16[384,256]{1,0:T(8,128)(2,1)S(1)} %get-tuple-element.65), channel_id=1, source_target_pairs={{0,2},{1,3},{2,0},{3,1},{4,6},{5,7},{6,4},{7,5},{8,10},{9,11},{10,... | collective-permute-start | bytes 589832 | tf_op jit(solution)/shard_map/ppermute | solution.py:51
  89.7 13.0 %collective-permute-start.30 = (bf16[384,256]{1,0:T(8,128)(2,1)S(1)}, bf16[384,256]{1,0:T(8,128)(2,1)S(1)}, u32[]{:S(2)}, u32[]{:S(2)}) collective-permute-start(bf16[384,256]{1,0:T(8,128)(2,1)S(1)} %get-tuple-element.66), channel_id=1, source_target_pairs={{0,3},{1,2},{2,1},{3,0},{4,7},{5,6},{6,5},{7,4},{8,11},{9,10},{10,... | collective-permute-start | bytes 589832 | tf_op jit(solution)/shard_map/ppermute | solution.py:51
  90.0 12.7 %collective-permute-start.31 = (bf16[384,256]{1,0:T(8,128)(2,1)S(1)}, bf16[384,256]{1,0:T(8,128)(2,1)S(1)}, u32[]{:S(2)}, u32[]{:S(2)}) collective-permute-start(bf16[384,256]{1,0:T(8,128)(2,1)S(1)} %get-tuple-element.67), channel_id=1, source_target_pairs={{0,1},{1,0},{2,3},{3,2},{4,5},{5,4},{6,7},{7,6},{8,9},{9,8},{10,11... | collective-permute-start | bytes 589832 | tf_op jit(solution)/shard_map/ppermute | solution.py:51
  94.6 6.9 %collective-permute-start.26 = (bf16[128,256]{1,0:T(8,128)(2,1)S(1)}, bf16[128,256]{1,0:T(8,128)(2,1)S(1)}, u32[]{:S(2)}, u32[]{:S(2)}) collective-permute-start(bf16[128,256]{1,0:T(8,128)(2,1)S(1)} %get-tuple-element.60), channel_id=1, source_target_pairs={{0,2},{1,3},{2,0},{3,1},{4,6},{5,7},{6,4},{7,5},{8,10},{9,11},{10,... | collective-permute-start | bytes 196616 | tf_op jit(solution)/shard_map/ppermute | solution.py:51
  96.2 5.9 %collective-permute-start.27 = (bf16[128,256]{1,0:T(8,128)(2,1)S(1)}, bf16[128,256]{1,0:T(8,128)(2,1)S(1)}, u32[]{:S(2)}, u32[]{:S(2)}) collective-permute-start(bf16[128,256]{1,0:T(8,128)(2,1)S(1)} %get-tuple-element.61), channel_id=1, source_target_pairs={{0,3},{1,2},{2,1},{3,0},{4,7},{5,6},{6,5},{7,4},{8,11},{9,10},{10,... | collective-permute-start | bytes 196616 | tf_op jit(solution)/shard_map/ppermute | solution.py:51
  103.4 3.2 %collective-permute-start.33 = (f32[8,512]{1,0:T(8,128)S(1)}, f32[8,512]{1,0:T(8,128)S(1)}, u32[]{:S(2)}, u32[]{:S(2)}) collective-permute-start(f32[8,512]{1,0:T(8,128)S(1)} %get-tuple-element.70.refs_4_), channel_id=1, source_target_pairs={{0,3},{1,2},{2,1},{3,0},{4,7},{5,6},{6,5},{7,4},{8,11},{9,10},{10,... | collective-permute-start | bytes 49160 | tf_op jit(solution)/shard_map/ppermute | solution.py:51
  104.9 3.7 %collective-permute-start.32 = (f32[8,512]{1,0:T(8,128)S(1)}, f32[8,512]{1,0:T(8,128)S(1)}, u32[]{:S(2)}, u32[]{:S(2)}) collective-permute-start(f32[8,512]{1,0:T(8,128)S(1)} %get-tuple-element.70.refs_4_), channel_id=1, source_target_pairs={{0,2},{1,3},{2,0},{3,1},{4,6},{5,7},{6,4},{7,5},{8,10},{9,11},{10,... | collective-permute-start | bytes 49160 | tf_op jit(solution)/shard_map/ppermute | solution.py:51
  (17 other events, 170.2 us)

commit v4 on v3

--- a/solution.py
+++ b/solution.py
@@ -297,41 +297,41 @@
     stats_ref[...] = jnp.concatenate(stats, axis=0)
 
 
-def merge_kernel(dims, span, len_ref, own_ref, stats_ref, near_ref, *refs):
-    requests, draft, heads, page_len = dims
+def merge_kernel(dims, len_ref, own_ref, stats_ref, near_ref, *refs):
+    requests, draft, heads, page_len, long_count = dims
     width = heads * HD
     msgs, out_ref, order_ref, facts_ref = refs[:-3], refs[-3], refs[-2], refs[-1]
     write_order(len_ref, order_ref, requests, page_len)
     tokens = requests * draft
     facts_ref[...] = near_ref[pl.ds(tokens, 6 * requests), :].astype(F32)
     far = [ref[pl.ds(ref.shape[0] - META, META), :].astype(F32) for ref in msgs]
-    factors = []
-    for i, p in enumerate(range(*span)):
+    factors, begins = [], []
+    for p in range(requests):
         r = order_ref[p]
         near = [facts_ref[pl.ds(6 * r + k, 1), :] for k in range(6)]
         tops = [stats_ref[pl.ds(2 * r, 1), :], near[0] + near[1] + near[2]]
         totals = [stats_ref[pl.ds(2 * r + 1, 1), :], near[3] + near[4] + near[5]]
-        for f in far:
-            part = [f[6 * i + k : 6 * i + k + 1] for k in range(6)]
+        for f in far if p < long_count else ():
+            part = [f[6 * p + k : 6 * p + k + 1] for k in range(6)]
             tops.append(part[0] + part[1] + part[2])
             totals.append(part[3] + part[4] + part[5])
         best = functools.reduce(jnp.maximum, tops)
         scales = [jnp.exp(t - best) for t in tops]
         denom = sum(s * t for s, t in zip(scales, totals))
+        begins.append(len(factors))
         factors += [s / denom for s in scales]
-    each = 2 + len(far)
     factors.append(jnp.zeros((128 - len(factors), width), F32))
     columns = jnp.transpose(jnp.concatenate(factors, axis=0))
-    for i, p in enumerate(range(*span)):
+    for p in range(requests):
         rows = pl.ds(pl.multiple_of(order_ref[p] * draft, draft), draft)
         parts = [own_ref[rows, :], near_ref[rows, :].astype(F32)]
-        parts += [ref[pl.ds(i * draft, draft), :].astype(F32) for ref in msgs]
+        parts += [ref[pl.ds(p * draft, draft), :].astype(F32) for ref in (msgs if p < long_count else ())]
         out = None
         for j, part in enumerate(parts):
-            c = each * i + j
+            c = begins[p] + j
             term = part * head_lanes(columns[:, c : c + 1], heads, draft, width)
             out = term if out is None else out + term
-        out_ref[pl.ds(i * draft, draft)] = out.astype(BF16)
+        out_ref[pl.ds(p * draft, draft)] = out.astype(BF16)
 
 
 def norm(values, sums, squares, gain, width_all):
@@ -345,28 +345,19 @@
     att, hid = refs[0:4], refs[4:8]
     wout, (gain_ref, up_ref, down_ref) = refs[8:12], refs[12:15]
     parts, normed_ref = refs[15:19], refs[19]
-    order_ref, z_ref, hid_v, wout_v, up_v, down_v, sems = refs[20:]
-    pairs = [(hid[k], hid_v.at[k]) for k in range(4)] + [(wout[k], wout_v.at[k]) for k in range(4)]
-    pairs += [(up_ref, up_v), (down_ref, down_v)]
-    copies = [pltpu.make_async_copy(src, dst, sems.at[n]) for n, (src, dst) in enumerate(pairs)]
-    for copy in copies:
-        copy.start()
+    order_ref, z_ref = refs[20:]
     me = lax.axis_index("tp")
     share = hid[0].shape[1]
     width_all = z_ref.shape[1]
     write_order(len_ref, order_ref, requests, page_len)
-    for copy in copies[:4]:
-        copy.wait()
     for p in range(count):
         rows = pl.ds(pl.multiple_of(order_ref[first + p] * draft, draft), draft)
         for flip in range(4):
             at = pl.ds(pl.multiple_of((me ^ flip) * share, share), share)
-            z_ref[pl.ds(p * draft, draft), at] = hid_v[flip, rows, :].astype(F32)
-    for copy in copies[4:8]:
-        copy.wait()
+            z_ref[pl.ds(p * draft, draft), at] = hid[flip][rows, :].astype(F32)
     branch = None
     for flip in range(4):
-        term = jnp.dot(att[flip][...], wout_v[flip], preferred_element_type=F32)
+        term = jnp.dot(att[flip][pl.ds(first * draft, count * draft)], wout[flip][...], preferred_element_type=F32)
         branch = term if branch is None else branch + term
     z = z_ref[...] + branch
     sums = jnp.sum(z, axis=-1, keepdims=True)
@@ -375,13 +366,11 @@
     normed = normed_wide.astype(BF16)
     z_ref[...] = normed_wide
     normed_ref[...] = z_ref[:, pl.ds(pl.multiple_of(me * share, share), share)].astype(BF16)
-    copies[8].wait()
-    inner = jnp.dot(normed, up_v[...], preferred_element_type=F32)
+    inner = jnp.dot(normed, up_ref[...], preferred_element_type=F32)
     inner = (0.5 * inner * (1.0 + lax.erf(inner * (0.5 ** 0.5)))).astype(BF16)
-    copies[9].wait()
     for flip in range(4):
         at = pl.ds(pl.multiple_of((me ^ flip) * share, share), share)
-        parts[flip][...] = jnp.dot(inner, down_v[:, at], preferred_element_type=F32).astype(BF16)
+        parts[flip][...] = jnp.dot(inner, down_ref[:, at], preferred_element_type=F32).astype(BF16)
 
 
 def gather_sum_kernel(*refs):
@@ -428,7 +417,7 @@
 def shards(hidden_in, w_qkv, w_out, first_gain, w_up, w_down, second_gain, cache_pool,
            page_table, cache_len, tree_parent, accept_node):
     tokens, share = hidden_in.shape
-    cache_pool, w_up, w_down = [pltpu.with_memory_space_constraint(a, pltpu.HBM) for a in (cache_pool, w_up, w_down)]
+    cache_pool = pltpu.with_memory_space_constraint(cache_pool, pltpu.HBM)
     requests, draft = tree_parent.shape
     width = w_qkv.shape[2]
     heads = width // HD
@@ -465,13 +454,14 @@
     hid_y, _, _ = lax.optimization_barrier((hid_y, bias, page_keys))
     hid_diag = send_tp(hid_y, 1)
     hid = (hidden_in, hid_core, hid_y, hid_diag)
+    wout_core = send_tp(w_out, 1)
     block = shape_of((tokens, width), BF16)
     queries, message, near_message = call(
         functools.partial(query_kernel, (requests, draft, page_len, long_count)),
         [block, shape_of((msg_rows, width), BF16), shape_of((tokens + META, width), BF16)],
         [SMEM] + [VMEM] * 5, [VMEM] * 3, [order],
         (cache_len, *hid, w_planes), "queries",
-        flops=2 * tokens * width_all * width, nbytes=2 * width_all * width, after=(bias, page_keys),
+        flops=2 * tokens * width_all * width, nbytes=2 * width_all * width, after=(bias, page_keys, wout_core),
     )
     near_asked = send_req(near_message, 1)
     queue = sorted(range(2, pages), key=lambda j: (abs(2 * j - pages), j))
@@ -507,41 +497,35 @@
     last = (near_answer,)
 
     w_later, _ = lax.optimization_barrier((w_out, near_answer))
-    wout_core = send_tp(w_later, 1)
     wout_y = send_tp(w_later, 2)
 
-    def merge(span, msgs, name, after):
-        return call(
-            functools.partial(merge_kernel, (requests, draft, heads, page_len), span),
-            shape_of(((span[1] - span[0]) * draft, width), BF16), [SMEM] + [VMEM] * (3 + len(msgs)), VMEM,
-            [order, pltpu.VMEM((6 * requests, width), F32)],
-            (cache_len, own, own_stats, near_got, *msgs), name, after=after,
-        )
-
-    def forward(attended, first, count, name, after):
+    merged = call(
+        functools.partial(merge_kernel, (requests, draft, heads, page_len, long_count)),
+        block, [SMEM] + [VMEM] * (3 + len(answers)), VMEM,
+        [order, pltpu.VMEM((6 * requests, width), F32)],
+        (cache_len, own, own_stats, near_got, *answers), "merge",
+    )
+    att_y = send_tp(merged, 2)
+    att_core = send_tp(merged, 1)
+    wout_y, _ = lax.optimization_barrier((wout_y, near_got))
+    wout = (w_out, wout_core, wout_y, send_tp(wout_y, 1))
+    att = (merged, att_core, att_y, send_tp(att_y, 1))
+
+    def forward(first, count, name, after):
         rows = count * draft
-        att_y = send_tp(attended, 2)
-        att_core = send_tp(attended, 1)
-        att_diag = send_tp(att_y, 1)
         part = shape_of((rows, share), BF16)
         outs = call(
             functools.partial(forward_kernel, (requests, draft, page_len, first, count)),
-            [part] * 5, [SMEM] + [VMEM] * 4 + [ANY] * 8 + [VMEM] + [ANY] * 2, [VMEM] * 5,
-            [order, pltpu.VMEM((rows, width_all), F32), pltpu.VMEM((4, tokens, share), BF16)]
-            + [pltpu.VMEM((4,) + w_out.shape, BF16), pltpu.VMEM(w_up.shape, BF16), pltpu.VMEM(w_down.shape, BF16), dma((10,))],
-            (cache_len, attended, att_core, att_y, att_diag, *stay, gain_1, w_up, w_down), name,
+            [part] * 5, [SMEM] + [VMEM] * 15, [VMEM] * 5,
+            [order, pltpu.VMEM((rows, width_all), F32)],
+            (cache_len, *att, *hid, *wout, gain_1, w_up, w_down), name,
             flops=2 * rows * width_all * (width_all + 2 * w_up.shape[1]), nbytes=3 * 2 * 1024 * 1024, after=after,
         )
         got = [send_tp(outs[flip], flip) for flip in (2, 3, 1)]
         return outs, [outs[0], *got, outs[4]]
 
-    wout_y_later, _ = lax.optimization_barrier((wout_y, near_got))
-    wout = (w_out, wout_core, wout_y, send_tp(wout_y_later, 1))
-    stay = tuple(pltpu.with_memory_space_constraint(a, pltpu.HBM) for a in (*hid, *wout))
-    merged_short = merge((long_count, requests), (), "merge_short", last + tuple(answers) + (wout_y,))
-    outs_short, parts_short = forward(merged_short, long_count, requests - long_count, "forward_short", ())
-    merged_long = merge((0, long_count), answers, "merge_long", (merged_short,))
-    outs_long, parts_long = forward(merged_long, 0, long_count, "forward_long", (outs_short[4],))
+    outs_short, parts_short = forward(long_count, requests - long_count, "forward_short", ())
+    outs_long, parts_long = forward(0, long_count, "forward_long", (outs_short[4],))
 
     x_long, x_short, stats = call(
         gather_sum_kernel,

time: 110 us -> 105 us (0.955)
  waiting for transfers between devices: 35.2 us -> 41.4 us
  starting transfers between devices: 37.7 us -> 31.6 us
  Pallas kernels: 33.6 us -> 28.5 us
    ppermute x14, waiting for transfers between devices: 16 us -> 22 us  [send_req(): lax.ppermute(value, 'req', [(i, (i + by) % size) for i in range(size)])]
    pallas_call x12 -> x11, Pallas kernels: 33.6 us -> 28.5 us  [call(): pl.pallas_call(body, out_shape=outs, in_specs=list(ins) + [ANY] * len(aft...]
    ppermute x14, starting transfers between devices: 24.1 us -> 19.3 us  [send_req(): lax.ppermute(value, 'req', [(i, (i + by) % size) for i in range(size)])]
    ppermute x21 -> x18, starting transfers between devices: 13.7 us -> 12.3 us  [send_tp(): return lax.ppermute(value, 'tp', [(i, i ^ flip) for i in range(size)])]
    ppermute x21 -> x18, waiting for transfers between devices: 19.1 us -> 19.5 us  [send_tp(): return lax.ppermute(value, 'tp', [(i, i ^ flip) for i in range(size)])]
  transfers between devices with their start and end apart: 35 -> 32, of which waited for: 15 -> 13; matrix products, arithmetic and copies ran while one was open for 1% -> 1% of each run, Pallas kernels for 22% -> 14%
where the time goes in v4:
time: 105 us
  waiting for transfers between devices  41.4 us (39%)
  starting transfers between devices  31.6 us (30%)
  Pallas kernels  28.5 us (27%)
  local copies, waits for them, and re-layouts  2.14 us (2%)
    pallas_call x11, Pallas kernels, call(): pl.pallas_call(body, out_shape=outs, in_specs=list(ins) + [ANY] * len(aft...  28.5 us
    ppermute x14, waiting for transfers between devices, send_req(): lax.ppermute(value, 'req', [(i, (i + by) % size) for i in range(size)])  22 us
    ppermute x18, waiting for transfers between devices, send_tp(): return lax.ppermute(value, 'tp', [(i, i ^ flip) for i in range(size)])  19.5 us
    ppermute x14, starting transfers between devices, send_req(): lax.ppermute(value, 'req', [(i, (i + by) % size) for i in range(size)])  19.3 us
    ppermute x18, starting transfers between devices, send_tp(): return lax.ppermute(value, 'tp', [(i, i ^ flip) for i in range(size)])  12.3 us
  transfers between devices with their start and end apart: 32, of which 13 were waited for; matrix products, arithmetic and copies ran while one was open for 1% of the time, Pallas kernels for 14%

profile of v4, /device:TPU:0, one launch (start us, length us, event | category | flops | bytes accessed | tf_op | source)
XLA Modules:
  0.0 104.5 jit_solution(9759475070665437197)
XLA Ops:
  0.6 3.0 %collective-permute-start.1 = (bf16[512,256]{1,0:T(8,128)(2,1)}, bf16[512,256]{1,0:T(8,128)(2,1)S(1)}, u32[]{:S(2)}, u32[]{:S(2)}) collective-permute-start(bf16[512,256]{1,0:T(8,128)(2,1)} %refs_5_.3), channel_id=1, source_target_pairs={{0,2},{1,3},{2,0},{3,1},{4,6},{5,7},{6,4},{7,5},{8,10},{9,11},{10,... | collective-permute-start | bytes 786440 | tf_op jit(solution)/shard_map/ppermute | solution.py:51
  5.6 2.3 %tree.1 = (f32[512,64]{1,0:T(8,128)S(1)}, bf16[2,512,512]{2,1,0:T(8,128)(2,1)S(1)}) custom-call(s32[8]{0:T(128)S(1)} %copy-done.10, s32[2,256]{1,0:T(2,128)S(1)} %reshape.17.refs_1_), custom_call_target="tpu_custom_call" | custom-call | flops 469762048 | tf_op jit(solution)/shard_map/tree/pallas_call | solution.py:32
  8.6 3.3 %pages.1 = (bf16[2,8,128,256]{3,2,1,0:T(8,128)(2,1)S(1)}, bf16[2,8,128,256]{3,2,1,0:T(8,128)(2,1)S(1)}) custom-call(s32[8,8]{1,0:T(8,128)S(1)} %copy-done.5, bf16[64,128,2,256]{3,2,1,0:T(2,128)(2,1)} %refs_10_.1), custom_call_target="tpu_custom_call" | custom-call | flops 536870912 | tf_op jit(solution)/shard_map/pages/pallas_call | solution.py:32
  12.0 1.5 %collective-permute-done.2.refs_4_.refs_3_.refs_8_ = bf16[512,256]{1,0:T(8,128)(2,1)S(1)} collective-permute-done((bf16[512,256]{1,0:T(8,128)(2,1)S(1)}, bf16[512,256]{1,0:T(8,128)(2,1)S(1)}, u32[]{:S(2)}, u32[]{:S(2)}) %collective-permute-start.2) | collective-permute-done | bytes 262176 | tf_op jit(solution)/shard_map/ppermute | solution.py:51
  14.6 1.5 %collective-permute-start.4 = (bf16[528,256]{1,0:T(8,128)(2,1)S(1)}, bf16[528,256]{1,0:T(8,128)(2,1)S(1)}, u32[]{:S(2)}, u32[]{:S(2)}) collective-permute-start(bf16[528,256]{1,0:T(8,128)(2,1)S(1)} %get-tuple-element.48), channel_id=1, source_target_pairs={{0,4},{4,8},{8,12},{12,16},{16,20},{20,24},{24,28},{28,0},{1,5},{5... | collective-permute-start | bytes 811016 | tf_op jit(solution)/shard_map/ppermute | solution.py:46
  16.1 3.2 %collective-permute-start.10 = (bf16[144,256]{1,0:T(8,128)(2,1)S(1)}, bf16[144,256]{1,0:T(8,128)(2,1)S(1)}, u32[]{:S(2)}, u32[]{:S(2)}) collective-permute-start(bf16[144,256]{1,0:T(8,128)(2,1)S(1)} %get-tuple-element.42.refs_6_.refs_7_), channel_id=1, source_target_pairs={{0,28},{4,0},{8,4},{12,8},{16,12},{20,16},{24,20},{28,24},{1,29},{... | collective-permute-start | bytes 221192 | tf_op jit(solution)/shard_map/ppermute | solution.py:46
  19.4 1.8 %collective-permute-start.9 = (bf16[144,256]{1,0:T(8,128)(2,1)S(1)}, bf16[144,256]{1,0:T(8,128)(2,1)S(1)}, u32[]{:S(2)}, u32[]{:S(2)}) collective-permute-start(bf16[144,256]{1,0:T(8,128)(2,1)S(1)} %get-tuple-element.42.refs_6_.refs_7_), channel_id=1, source_target_pairs={{0,24},{4,28},{8,0},{12,4},{16,8},{20,12},{24,16},{28,20},{1,25},{... | collective-permute-start | bytes 221192 | tf_op jit(solution)/shard_map/ppermute | solution.py:46
  22.2 3.6 %collective-permute-done.10.refs_8_ = bf16[144,256]{1,0:T(8,128)(2,1)S(1)} collective-permute-done((bf16[144,256]{1,0:T(8,128)(2,1)S(1)}, bf16[144,256]{1,0:T(8,128)(2,1)S(1)}, u32[]{:S(2)}, u32[]{:S(2)}) %collective-permute-start.10) | collective-permute-done | bytes 73760 | tf_op jit(solution)/shard_map/ppermute | solution.py:46
  26.2 2.2 %collective-permute-start.5 = (bf16[144,256]{1,0:T(8,128)(2,1)S(1)}, bf16[144,256]{1,0:T(8,128)(2,1)S(1)}, u32[]{:S(2)}, u32[]{:S(2)}) collective-permute-start(bf16[144,256]{1,0:T(8,128)(2,1)S(1)} %get-tuple-element.42.refs_6_.refs_7_), channel_id=1, source_target_pairs={{0,16},{4,20},{8,24},{12,28},{16,0},{20,4},{24,8},{28,12},{1,17},{... | collective-permute-start | bytes 221192 | tf_op jit(solution)/shard_map/ppermute | solution.py:46
  28.4 1.9 %keys_values.1 = (bf16[512,256]{1,0:T(8,128)(2,1)S(1)}, bf16[512,256]{1,0:T(8,128)(2,1)S(1)}, bf16[512,2,256]{2,1,0:T(2,128)(2,1)}) custom-call(bf16[512,256]{1,0:T(8,128)(2,1)S(1)} %copy-done.1, bf16[512,256]{1,0:T(8,128)(2,1)S(1)} %collective-permute-done.refs_2_.refs_1_.refs_6_, bf16[512,256]{1,0:T(8,128)(2,1)S(1)} %collective-permute-done.1.refs_3_.refs_2_.refs_7_, ...), custom_call_target="tpu_custom_call" | custom-call | flops 536870912 | bytes 1048576 | tf_op jit(solution)/shard_map/keys_values/pallas_call | solution.py:32
  30.3 3.4 %local_attention.1 = (f32[512,256]{1,0:T(8,128)S(1)}, f32[16,256]{1,0:T(8,128)S(1)}, bf16[144,256]{1,0:T(8,128)(2,1)}) custom-call(s32[8]{0:T(128)S(1)} %copy-done.7, bf16[512,256]{1,0:T(8,128)(2,1)S(1)} %get-tuple-element.40.refs_1_, bf16[512,256]{1,0:T(8,128)(2,1)S(1)} %get-tuple-element.43.refs_2_, bf16[512,256]{1,0:T(8,128)(2,1)S(1)} %get-tuple-element.44.refs_3_, ...), custom_call_target="tpu_custom_call" | custom-call | tf_op jit(solution)/shard_map/local_attention/pallas_call | solution.py:32
  33.7 2.2 %collective-permute-done.6.refs_4_ = bf16[144,256]{1,0:T(8,128)(2,1)S(1)} collective-permute-done((bf16[144,256]{1,0:T(8,128)(2,1)S(1)}, bf16[144,256]{1,0:T(8,128)(2,1)S(1)}, u32[]{:S(2)}, u32[]{:S(2)}) %collective-permute-start.6) | collective-permute-done | bytes 73760 | tf_op jit(solution)/shard_map/ppermute | solution.py:46
  36.0 7.0 %visitors_early.1 = (bf16[560,256]{1,0:T(8,128)(2,1)S(1)}, bf16[144,256]{1,0:T(8,128)(2,1)S(1)}, bf16[144,256]{1,0:T(8,128)(2,1)S(1)}, bf16[144,256]{1,0:T(8,128...) custom-call(bf16[528,256]{1,0:T(8,128)(2,1)S(1)} %collective-permute-done.4.ref, ...), custom_call_target="tpu_custom_call" | custom-call | tf_op jit(solution)/shard_map/visitors_early/pallas_call | solution.py:32
  43.6 3.5 %collective-permute-start.11 = (bf16[560,256]{1,0:T(8,128)(2,1)S(1)}, bf16[560,256]{1,0:T(8,128)(2,1)S(1)}, u32[]{:S(2)}, u32[]{:S(2)}) collective-permute-start(bf16[560,256]{1,0:T(8,128)(2,1)S(1)} %get-tuple-element.49), channel_id=1, source_target_pairs={{0,28},{4,0},{8,4},{12,8},{16,12},{20,16},{24,20},{28,24},{1,29},{... | collective-permute-start | bytes 860168 | tf_op jit(solution)/shard_map/ppermute | solution.py:46
  48.0 2.1 %collective-permute-start.14 = (bf16[144,256]{1,0:T(8,128)(2,1)S(1)}, bf16[144,256]{1,0:T(8,128)(2,1)S(1)}, u32[]{:S(2)}, u32[]{:S(2)}) collective-permute-start(bf16[144,256]{1,0:T(8,128)(2,1)S(1)} %get-tuple-element.52), channel_id=1, source_target_pairs={{0,12},{4,16},{8,20},{12,24},{16,28},{20,0},{24,4},{28,8},{1,13},{... | collective-permute-start | bytes 221192 | tf_op jit(solution)/shard_map/ppermute | solution.py:46
  50.1 9.7 %collective-permute-done.12.refs_4_ = bf16[144,256]{1,0:T(8,128)(2,1)S(1)} collective-permute-done((bf16[144,256]{1,0:T(8,128)(2,1)S(1)}, bf16[144,256]{1,0:T(8,128)(2,1)S(1)}, u32[]{:S(2)}, u32[]{:S(2)}) %collective-permute-start.12) | collective-permute-done | bytes 73760 | tf_op jit(solution)/shard_map/ppermute | solution.py:46
  59.8 1.8 %collective-permute-start.15 = (bf16[144,256]{1,0:T(8,128)(2,1)S(1)}, bf16[144,256]{1,0:T(8,128)(2,1)S(1)}, u32[]{:S(2)}, u32[]{:S(2)}) collective-permute-start(bf16[144,256]{1,0:T(8,128)(2,1)S(1)} %get-tuple-element.53), channel_id=1, source_target_pairs={{0,24},{4,28},{8,0},{12,4},{16,8},{20,12},{24,16},{28,20},{1,25},{... | collective-permute-start | bytes 221192 | tf_op jit(solution)/shard_map/ppermute | solution.py:46
  62.5 1.7 %collective-permute-done.15.refs_7_ = bf16[144,256]{1,0:T(8,128)(2,1)S(1)} collective-permute-done((bf16[144,256]{1,0:T(8,128)(2,1)S(1)}, bf16[144,256]{1,0:T(8,128)(2,1)S(1)}, u32[]{:S(2)}, u32[]{:S(2)}) %collective-permute-start.15) | collective-permute-done | bytes 73760 | tf_op jit(solution)/shard_map/ppermute | solution.py:46
  64.1 3.7 %collective-permute-done.16.refs_8_ = bf16[144,256]{1,0:T(8,128)(2,1)S(1)} collective-permute-done((bf16[144,256]{1,0:T(8,128)(2,1)S(1)}, bf16[144,256]{1,0:T(8,128)(2,1)S(1)}, u32[]{:S(2)}, u32[]{:S(2)}) %collective-permute-start.16) | collective-permute-done | bytes 73760 | tf_op jit(solution)/shard_map/ppermute | solution.py:46
  68.9 1.9 %merge.1.refs_1_ = bf16[512,256]{1,0:T(8,128)(2,1)S(1)} custom-call(s32[8]{0:T(128)S(1)} %copy-done.7, f32[512,256]{1,0:T(8,128)S(1)} %get-tuple-element.46.refs_11_.refs_1_, f32[16,256]{1,0:T(8,128)S(1)} %get-tuple-element.47.refs_2_, bf16[560,256]{1,0:T(8,128)(2,1)S(1)} %collective-permute-done.11.refs_3_, ...), custom_call_target="tpu_custom_call" | custom-call | tf_op jit(solution)/shard_map/merge/pallas_call | solution.py:32
  70.7 1.6 %collective-permute-start.19 = (bf16[512,256]{1,0:T(8,128)(2,1)S(1)}, bf16[512,256]{1,0:T(8,128)(2,1)S(1)}, u32[]{:S(2)}, u32[]{:S(2)}) collective-permute-start(bf16[512,256]{1,0:T(8,128)(2,1)S(1)} %merge.1.refs_1_), channel_id=1, source_target_pairs={{0,2},{1,3},{2,0},{3,1},{4,6},{5,7},{6,4},{7,5},{8,10},{9,11},{10,... | collective-permute-start | bytes 786440 | tf_op jit(solution)/shard_map/ppermute | solution.py:51
  72.9 4.3 %collective-permute-done.19.refs_3_ = bf16[512,256]{1,0:T(8,128)(2,1)S(1)} collective-permute-done((bf16[512,256]{1,0:T(8,128)(2,1)S(1)}, bf16[512,256]{1,0:T(8,128)(2,1)S(1)}, u32[]{:S(2)}, u32[]{:S(2)}) %collective-permute-start.19) | collective-permute-done | bytes 262176 | tf_op jit(solution)/shard_map/ppermute | solution.py:51
  77.2 1.5 %collective-permute-done.20.refs_4_ = bf16[512,256]{1,0:T(8,128)(2,1)S(1)} collective-permute-done((bf16[512,256]{1,0:T(8,128)(2,1)S(1)}, bf16[512,256]{1,0:T(8,128)(2,1)S(1)}, u32[]{:S(2)}, u32[]{:S(2)}) %collective-permute-start.20) | collective-permute-done | bytes 262176 | tf_op jit(solution)/shard_map/ppermute | solution.py:51
  78.7 3.7 %forward_short.1 = (bf16[384,256]{1,0:T(8,128)(2,1)S(1)}, bf16[384,256]{1,0:T(8,128)(2,1)S(1)}, bf16[384,256]{1,0:T(8,128)(2,1)S(1)}, bf16[384,256]{1,0:T(8,128)(2,1)S(1)}, bf16[384,256]{1,0:T(8,128)(2,1)S(1)}) custom-call(s32[8]{0:T(128)S(1)} %copy-done.7, bf16[512,256]{1,0:T(8,128)(2,1)S(1)} %merge.1.refs_1_, ...), custom_call_target="tpu_custom_call" | custom-call | flops 2415919104 | bytes 6291456 | tf_op jit(solution)/shard_map/forward_short/pallas_call | solution.py:32
  82.5 1.6 %collective-permute-start.26 = (bf16[384,256]{1,0:T(8,128)(2,1)S(1)}, bf16[384,256]{1,0:T(8,128)(2,1)S(1)}, u32[]{:S(2)}, u32[]{:S(2)}) collective-permute-start(bf16[384,256]{1,0:T(8,128)(2,1)S(1)} %get-tuple-element.65), channel_id=1, source_target_pairs={{0,2},{1,3},{2,0},{3,1},{4,6},{5,7},{6,4},{7,5},{8,10},{9,11},{10,... | collective-permute-start | bytes 589832 | tf_op jit(solution)/shard_map/ppermute | solution.py:51
  84.7 1.9 %forward_long.1 = (bf16[128,256]{1,0:T(8,128)(2,1)S(1)}, bf16[128,256]{1,0:T(8,128)(2,1)S(1)}, bf16[128,256]{1,0:T(8,128)(2,1)S(1)}, bf16[128,256]{1,0:T(8,128)(2,1)S(1)}, bf16[128,256]{1,0:T(8,128)(2,1)S(1)}) custom-call(s32[8]{0:T(128)S(1)} %copy-done.7, bf16[512,256]{1,0:T(8,128)(2,1)S(1)} %merge.1.refs_1_, ...), custom_call_target="tpu_custom_call" | custom-call | flops 805306368 | bytes 6291456 | tf_op jit(solution)/shard_map/forward_long/pallas_call | solution.py:32
  86.6 1.6 %collective-permute-start.23 = (bf16[128,256]{1,0:T(8,128)(2,1)S(1)}, bf16[128,256]{1,0:T(8,128)(2,1)S(1)}, u32[]{:S(2)}, u32[]{:S(2)}) collective-permute-start(bf16[128,256]{1,0:T(8,128)(2,1)S(1)} %get-tuple-element.60), channel_id=1, source_target_pairs={{0,2},{1,3},{2,0},{3,1},{4,6},{5,7},{6,4},{7,5},{8,10},{9,11},{10,... | collective-permute-start | bytes 196616 | tf_op jit(solution)/shard_map/ppermute | solution.py:51
  88.2 7.6 %collective-permute-done.23.refs_1_ = bf16[128,256]{1,0:T(8,128)(2,1)S(1)} collective-permute-done((bf16[128,256]{1,0:T(8,128)(2,1)S(1)}, bf16[128,256]{1,0:T(8,128)(2,1)S(1)}, u32[]{:S(2)}, u32[]{:S(2)}) %collective-permute-start.23) | collective-permute-done | bytes 65568 | tf_op jit(solution)/shard_map/ppermute | solution.py:51
  95.8 1.2 %collective-permute-done.25.refs_3_ = bf16[128,256]{1,0:T(8,128)(2,1)S(1)} collective-permute-done((bf16[128,256]{1,0:T(8,128)(2,1)S(1)}, bf16[128,256]{1,0:T(8,128)(2,1)S(1)}, u32[]{:S(2)}, u32[]{:S(2)}) %collective-permute-start.25) | collective-permute-done | bytes 65568 | tf_op jit(solution)/shard_map/ppermute | solution.py:51
  97.7 1.5 %collective-permute-start.30 = (f32[8,512]{1,0:T(8,128)S(1)}, f32[8,512]{1,0:T(8,128)S(1)}, u32[]{:S(2)}, u32[]{:S(2)}) collective-permute-start(f32[8,512]{1,0:T(8,128)S(1)} %get-tuple-element.70.refs_4_), channel_id=1, source_target_pairs={{0,3},{1,2},{2,1},{3,0},{4,7},{5,6},{6,5},{7,4},{8,11},{9,10},{10,... | collective-permute-start | bytes 49160 | tf_op jit(solution)/shard_map/ppermute | solution.py:51
  100.8 2.1 %collective-permute-done.29.refs_5_ = f32[8,512]{1,0:T(8,128)S(1)} collective-permute-done((f32[8,512]{1,0:T(8,128)S(1)}, f32[8,512]{1,0:T(8,128)S(1)}, u32[]{:S(2)}, u32[]{:S(2)}) %collective-permute-start.29) | collective-permute-done | bytes 16416 | tf_op jit(solution)/shard_map/ppermute | solution.py:51
  102.9 1.6 %finish.1 = bf16[512,256]{1,0:T(8,128)(2,1)} custom-call(s32[8]{0:T(128)S(1)} %copy-done.7, f32[1,1024]{1,0:T(1,128)S(1)} %bitcast.8, f32[128,256]{1,0:T(8,128)S(1)} %get-tuple-element.68.refs_2_, f32[384,256]{1,0:T(8,128)S(1)} %get-tuple-element.69.refs_3_, f32[8,512]{1,0:T(8,128)S(1)} %get-tuple-element.70.refs_4_, ...), custom_call_target="tpu_custom_call" | custom-call | tf_op jit(solution)/shard_map/finish/pallas_call | solution.py:32
  (66 shorter events, 12.0 us)
Async XLA Ops:
  0.6 11.3 %collective-permute-start.1 = (bf16[512,256]{1,0:T(8,128)(2,1)}, bf16[512,256]{1,0:T(8,128)(2,1)S(1)}, u32[]{:S(2)}, u32[]{:S(2)}) collective-permute-start(bf16[512,256]{1,0:T(8,128)(2,1)} %refs_5_.3), channel_id=1, source_target_pairs={{0,2},{1,3},{2,0},{3,1},{4,6},{5,7},{6,4},{7,5},{8,10},{9,11},{10,... | collective-permute-start | bytes 786440 | tf_op jit(solution)/shard_map/ppermute | solution.py:51
  3.7 8.4 %collective-permute-start.3 = (bf16[256,1024]{1,0:T(8,128)(2,1)}, bf16[256,1024]{1,0:T(8,128)(2,1)S(1)}, u32[]{:S(2)}, u32[]{:S(2)}) collective-permute-start(bf16[256,1024]{1,0:T(8,128)(2,1)} %refs_9_.5), channel_id=1, source_target_pairs={{0,1},{1,0},{2,3},{3,2},{4,5},{5,4},{6,7},{7,6},{8,9},{9,8},{10,11... | collective-permute-start | bytes 1572872 | tf_op jit(solution)/shard_map/ppermute | solution.py:51
  3.7 8.3 %collective-permute-start = (bf16[512,256]{1,0:T(8,128)(2,1)}, bf16[512,256]{1,0:T(8,128)(2,1)S(1)}, u32[]{:S(2)}, u32[]{:S(2)}) collective-permute-start(bf16[512,256]{1,0:T(8,128)(2,1)} %refs_5_.3), channel_id=1, source_target_pairs={{0,1},{1,0},{2,3},{3,2},{4,5},{5,4},{6,7},{7,6},{8,9},{9,8},{10,11... | collective-permute-start | bytes 786440 | tf_op jit(solution)/shard_map/ppermute | solution.py:51
  11.9 1.6 %collective-permute-start.2 = (bf16[512,256]{1,0:T(8,128)(2,1)S(1)}, bf16[512,256]{1,0:T(8,128)(2,1)S(1)}, u32[]{:S(2)}, u32[]{:S(2)}) collective-permute-start(bf16[512,256]{1,0:T(8,128)(2,1)S(1)} %collective-permute-done.1.refs_3_.refs_2_.refs_7_), channel_id=1, source_target_pairs={{0,1},{1,0},{2,3},{3,2},{4,5},{5,4},{6,7},{7,6},{8,9},{9,8},{10,11... | collective-permute-start | bytes 786440 | tf_op jit(solution)/shard_map/ppermute | solution.py:51
  14.6 21.4 %collective-permute-start.4 = (bf16[528,256]{1,0:T(8,128)(2,1)S(1)}, bf16[528,256]{1,0:T(8,128)(2,1)S(1)}, u32[]{:S(2)}, u32[]{:S(2)}) collective-permute-start(bf16[528,256]{1,0:T(8,128)(2,1)S(1)} %get-tuple-element.48), channel_id=1, source_target_pairs={{0,4},{4,8},{8,12},{12,16},{16,20},{20,24},{24,28},{28,0},{1,5},{5... | collective-permute-start | bytes 811016 | tf_op jit(solution)/shard_map/ppermute | solution.py:46
  16.1 9.7 %collective-permute-start.10 = (bf16[144,256]{1,0:T(8,128)(2,1)S(1)}, bf16[144,256]{1,0:T(8,128)(2,1)S(1)}, u32[]{:S(2)}, u32[]{:S(2)}) collective-permute-start(bf16[144,256]{1,0:T(8,128)(2,1)S(1)} %get-tuple-element.42.refs_6_.refs_7_), channel_id=1, source_target_pairs={{0,28},{4,0},{8,4},{12,8},{16,12},{20,16},{24,20},{28,24},{1,29},{... | collective-permute-start | bytes 221192 | tf_op jit(solution)/shard_map/ppermute | solution.py:46
  19.4 6.8 %collective-permute-start.9 = (bf16[144,256]{1,0:T(8,128)(2,1)S(1)}, bf16[144,256]{1,0:T(8,128)(2,1)S(1)}, u32[]{:S(2)}, u32[]{:S(2)}) collective-permute-start(bf16[144,256]{1,0:T(8,128)(2,1)S(1)} %get-tuple-element.42.refs_6_.refs_7_), channel_id=1, source_target_pairs={{0,24},{4,28},{8,0},{12,4},{16,8},{20,12},{24,16},{28,20},{1,25},{... | collective-permute-start | bytes 221192 | tf_op jit(solution)/shard_map/ppermute | solution.py:46
  21.2 12.6 %collective-permute-start.8 = (bf16[144,256]{1,0:T(8,128)(2,1)S(1)}, bf16[144,256]{1,0:T(8,128)(2,1)S(1)}, u32[]{:S(2)}, u32[]{:S(2)}) collective-permute-start(bf16[144,256]{1,0:T(8,128)(2,1)S(1)} %get-tuple-element.42.refs_6_.refs_7_), channel_id=1, source_target_pairs={{0,8},{4,12},{8,16},{12,20},{16,24},{20,28},{24,0},{28,4},{1,9},{5... | collective-permute-start | bytes 221192 | tf_op jit(solution)/shard_map/ppermute | solution.py:46
  21.4 12.3 %collective-permute-start.7 = (bf16[144,256]{1,0:T(8,128)(2,1)S(1)}, bf16[144,256]{1,0:T(8,128)(2,1)S(1)}, u32[]{:S(2)}, u32[]{:S(2)}) collective-permute-start(bf16[144,256]{1,0:T(8,128)(2,1)S(1)} %get-tuple-element.42.refs_6_.refs_7_), channel_id=1, source_target_pairs={{0,20},{4,24},{8,28},{12,0},{16,4},{20,8},{24,12},{28,16},{1,21},{... | collective-permute-start | bytes 221192 | tf_op jit(solution)/shard_map/ppermute | solution.py:46
  25.8 10.1 %collective-permute-start.6 = (bf16[144,256]{1,0:T(8,128)(2,1)S(1)}, bf16[144,256]{1,0:T(8,128)(2,1)S(1)}, u32[]{:S(2)}, u32[]{:S(2)}) collective-permute-start(bf16[144,256]{1,0:T(8,128)(2,1)S(1)} %get-tuple-element.42.refs_6_.refs_7_), channel_id=1, source_target_pairs={{0,12},{4,16},{8,20},{12,24},{16,28},{20,0},{24,4},{28,8},{1,13},{... | collective-permute-start | bytes 221192 | tf_op jit(solution)/shard_map/ppermute | solution.py:46
  26.2 9.8 %collective-permute-start.5 = (bf16[144,256]{1,0:T(8,128)(2,1)S(1)}, bf16[144,256]{1,0:T(8,128)(2,1)S(1)}, u32[]{:S(2)}, u32[]{:S(2)}) collective-permute-start(bf16[144,256]{1,0:T(8,128)(2,1)S(1)} %get-tuple-element.42.refs_6_.refs_7_), channel_id=1, source_target_pairs={{0,16},{4,20},{8,24},{12,28},{16,0},{20,4},{24,8},{28,12},{1,17},{... | collective-permute-start | bytes 221192 | tf_op jit(solution)/shard_map/ppermute | solution.py:46
  43.0 29.3 %collective-permute-start.21 = (bf16[256,1024]{1,0:T(8,128)(2,1)S(1)}, bf16[256,1024]{1,0:T(8,128)(2,1)S(1)}, u32[]{:S(2)}, u32[]{:S(2)}) collective-permute-start(bf16[256,1024]{1,0:T(8,128)(2,1)S(1)} %copy-done.4), channel_id=1, source_target_pairs={{0,2},{1,3},{2,0},{3,1},{4,6},{5,7},{6,4},{7,5},{8,10},{9,11},{10,... | collective-permute-start | bytes 1572872 | tf_op jit(solution)/shard_map/ppermute | solution.py:51
  43.6 25.3 %collective-permute-start.11 = (bf16[560,256]{1,0:T(8,128)(2,1)S(1)}, bf16[560,256]{1,0:T(8,128)(2,1)S(1)}, u32[]{:S(2)}, u32[]{:S(2)}) collective-permute-start(bf16[560,256]{1,0:T(8,128)(2,1)S(1)} %get-tuple-element.49), channel_id=1, source_target_pairs={{0,28},{4,0},{8,4},{12,8},{16,12},{20,16},{24,20},{28,24},{1,29},{... | collective-permute-start | bytes 860168 | tf_op jit(solution)/shard_map/ppermute | solution.py:46
  47.1 12.7 %collective-permute-start.12 = (bf16[144,256]{1,0:T(8,128)(2,1)S(1)}, bf16[144,256]{1,0:T(8,128)(2,1)S(1)}, u32[]{:S(2)}, u32[]{:S(2)}) collective-permute-start(bf16[144,256]{1,0:T(8,128)(2,1)S(1)} %get-tuple-element.50), channel_id=1, source_target_pairs={{0,16},{4,20},{8,24},{12,28},{16,0},{20,4},{24,8},{28,12},{1,17},{... | collective-permute-start | bytes 221192 | tf_op jit(solution)/shard_map/ppermute | solution.py:46
  47.1 14.5 %collective-permute-start.13 = (bf16[144,256]{1,0:T(8,128)(2,1)S(1)}, bf16[144,256]{1,0:T(8,128)(2,1)S(1)}, u32[]{:S(2)}, u32[]{:S(2)}) collective-permute-start(bf16[144,256]{1,0:T(8,128)(2,1)S(1)} %get-tuple-element.51), channel_id=1, source_target_pairs={{0,20},{4,24},{8,28},{12,0},{16,4},{20,8},{24,12},{28,16},{1,21},{... | collective-permute-start | bytes 221192 | tf_op jit(solution)/shard_map/ppermute | solution.py:46
  48.0 13.8 %collective-permute-start.14 = (bf16[144,256]{1,0:T(8,128)(2,1)S(1)}, bf16[144,256]{1,0:T(8,128)(2,1)S(1)}, u32[]{:S(2)}, u32[]{:S(2)}) collective-permute-start(bf16[144,256]{1,0:T(8,128)(2,1)S(1)} %get-tuple-element.52), channel_id=1, source_target_pairs={{0,12},{4,16},{8,20},{12,24},{16,28},{20,0},{24,4},{28,8},{1,13},{... | collective-permute-start | bytes 221192 | tf_op jit(solution)/shard_map/ppermute | solution.py:46
  59.8 4.4 %collective-permute-start.15 = (bf16[144,256]{1,0:T(8,128)(2,1)S(1)}, bf16[144,256]{1,0:T(8,128)(2,1)S(1)}, u32[]{:S(2)}, u32[]{:S(2)}) collective-permute-start(bf16[144,256]{1,0:T(8,128)(2,1)S(1)} %get-tuple-element.53), channel_id=1, source_target_pairs={{0,24},{4,28},{8,0},{12,4},{16,8},{20,12},{24,16},{28,20},{1,25},{... | collective-permute-start | bytes 221192 | tf_op jit(solution)/shard_map/ppermute | solution.py:46
  61.6 6.2 %collective-permute-start.16 = (bf16[144,256]{1,0:T(8,128)(2,1)S(1)}, bf16[144,256]{1,0:T(8,128)(2,1)S(1)}, u32[]{:S(2)}, u32[]{:S(2)}) collective-permute-start(bf16[144,256]{1,0:T(8,128)(2,1)S(1)} %get-tuple-element.54), channel_id=1, source_target_pairs={{0,8},{4,12},{8,16},{12,20},{16,24},{20,28},{24,0},{28,4},{1,9},{5... | collective-permute-start | bytes 221192 | tf_op jit(solution)/shard_map/ppermute | solution.py:46
  61.8 7.1 %collective-permute-start.17 = (bf16[144,256]{1,0:T(8,128)(2,1)S(1)}, bf16[144,256]{1,0:T(8,128)(2,1)S(1)}, u32[]{:S(2)}, u32[]{:S(2)}) collective-permute-start(bf16[144,256]{1,0:T(8,128)(2,1)S(1)} %get-tuple-element.55), channel_id=1, source_target_pairs={{0,4},{4,8},{8,12},{12,16},{16,20},{20,24},{24,28},{28,0},{1,5},{5... | collective-permute-start | bytes 221192 | tf_op jit(solution)/shard_map/ppermute | solution.py:46
  70.7 6.4 %collective-permute-start.19 = (bf16[512,256]{1,0:T(8,128)(2,1)S(1)}, bf16[512,256]{1,0:T(8,128)(2,1)S(1)}, u32[]{:S(2)}, u32[]{:S(2)}) collective-permute-start(bf16[512,256]{1,0:T(8,128)(2,1)S(1)} %merge.1.refs_1_), channel_id=1, source_target_pairs={{0,2},{1,3},{2,0},{3,1},{4,6},{5,7},{6,4},{7,5},{8,10},{9,11},{10,... | collective-permute-start | bytes 786440 | tf_op jit(solution)/shard_map/ppermute | solution.py:51
  72.3 6.4 %collective-permute-start.22 = (bf16[256,1024]{1,0:T(8,128)(2,1)S(1)}, bf16[256,1024]{1,0:T(8,128)(2,1)S(1)}, u32[]{:S(2)}, u32[]{:S(2)}) collective-permute-start(bf16[256,1024]{1,0:T(8,128)(2,1)S(1)} %collective-permute-done.21.refs_11_), channel_id=1, source_target_pairs={{0,1},{1,0},{2,3},{3,2},{4,5},{5,4},{6,7},{7,6},{8,9},{9,8},{10,11... | collective-permute-start | bytes 1572872 | tf_op jit(solution)/shard_map/ppermute | solution.py:51
  72.4 4.8 %collective-permute-start.18 = (bf16[512,256]{1,0:T(8,128)(2,1)S(1)}, bf16[512,256]{1,0:T(8,128)(2,1)S(1)}, u32[]{:S(2)}, u32[]{:S(2)}) collective-permute-start(bf16[512,256]{1,0:T(8,128)(2,1)S(1)} %merge.1.refs_1_), channel_id=1, source_target_pairs={{0,1},{1,0},{2,3},{3,2},{4,5},{5,4},{6,7},{7,6},{8,9},{9,8},{10,11... | collective-permute-start | bytes 786440 | tf_op jit(solution)/shard_map/ppermute | solution.py:51
  77.2 1.5 %collective-permute-start.20 = (bf16[512,256]{1,0:T(8,128)(2,1)S(1)}, bf16[512,256]{1,0:T(8,128)(2,1)S(1)}, u32[]{:S(2)}, u32[]{:S(2)}) collective-permute-start(bf16[512,256]{1,0:T(8,128)(2,1)S(1)} %collective-permute-done.19.refs_3_), channel_id=1, source_target_pairs={{0,1},{1,0},{2,3},{3,2},{4,5},{5,4},{6,7},{7,6},{8,9},{9,8},{10,11... | collective-permute-start | bytes 786440 | tf_op jit(solution)/shard_map/ppermute | solution.py:51
  82.5 14.6 %collective-permute-start.26 = (bf16[384,256]{1,0:T(8,128)(2,1)S(1)}, bf16[384,256]{1,0:T(8,128)(2,1)S(1)}, u32[]{:S(2)}, u32[]{:S(2)}) collective-permute-start(bf16[384,256]{1,0:T(8,128)(2,1)S(1)} %get-tuple-element.65), channel_id=1, source_target_pairs={{0,2},{1,3},{2,0},{3,1},{4,6},{5,7},{6,4},{7,5},{8,10},{9,11},{10,... | collective-permute-start | bytes 589832 | tf_op jit(solution)/shard_map/ppermute | solution.py:51
  84.1 13.0 %collective-permute-start.27 = (bf16[384,256]{1,0:T(8,128)(2,1)S(1)}, bf16[384,256]{1,0:T(8,128)(2,1)S(1)}, u32[]{:S(2)}, u32[]{:S(2)}) collective-permute-start(bf16[384,256]{1,0:T(8,128)(2,1)S(1)} %get-tuple-element.66), channel_id=1, source_target_pairs={{0,3},{1,2},{2,1},{3,0},{4,7},{5,6},{6,5},{7,4},{8,11},{9,10},{10,... | collective-permute-start | bytes 589832 | tf_op jit(solution)/shard_map/ppermute | solution.py:51
  84.1 13.0 %collective-permute-start.28 = (bf16[384,256]{1,0:T(8,128)(2,1)S(1)}, bf16[384,256]{1,0:T(8,128)(2,1)S(1)}, u32[]{:S(2)}, u32[]{:S(2)}) collective-permute-start(bf16[384,256]{1,0:T(8,128)(2,1)S(1)} %get-tuple-element.67), channel_id=1, source_target_pairs={{0,1},{1,0},{2,3},{3,2},{4,5},{5,4},{6,7},{7,6},{8,9},{9,8},{10,11... | collective-permute-start | bytes 589832 | tf_op jit(solution)/shard_map/ppermute | solution.py:51
  86.6 9.2 %collective-permute-start.23 = (bf16[128,256]{1,0:T(8,128)(2,1)S(1)}, bf16[128,256]{1,0:T(8,128)(2,1)S(1)}, u32[]{:S(2)}, u32[]{:S(2)}) collective-permute-start(bf16[128,256]{1,0:T(8,128)(2,1)S(1)} %get-tuple-element.60), channel_id=1, source_target_pairs={{0,2},{1,3},{2,0},{3,1},{4,6},{5,7},{6,4},{7,5},{8,10},{9,11},{10,... | collective-permute-start | bytes 196616 | tf_op jit(solution)/shard_map/ppermute | solution.py:51
  88.2 7.6 %collective-permute-start.24 = (bf16[128,256]{1,0:T(8,128)(2,1)S(1)}, bf16[128,256]{1,0:T(8,128)(2,1)S(1)}, u32[]{:S(2)}, u32[]{:S(2)}) collective-permute-start(bf16[128,256]{1,0:T(8,128)(2,1)S(1)} %get-tuple-element.61), channel_id=1, source_target_pairs={{0,3},{1,2},{2,1},{3,0},{4,7},{5,6},{6,5},{7,4},{8,11},{9,10},{10,... | collective-permute-start | bytes 196616 | tf_op jit(solution)/shard_map/ppermute | solution.py:51
  95.8 1.3 %collective-permute-start.25 = (bf16[128,256]{1,0:T(8,128)(2,1)S(1)}, bf16[128,256]{1,0:T(8,128)(2,1)S(1)}, u32[]{:S(2)}, u32[]{:S(2)}) collective-permute-start(bf16[128,256]{1,0:T(8,128)(2,1)S(1)} %get-tuple-element.62), channel_id=1, source_target_pairs={{0,1},{1,0},{2,3},{3,2},{4,5},{5,4},{6,7},{7,6},{8,9},{9,8},{10,11... | collective-permute-start | bytes 196616 | tf_op jit(solution)/shard_map/ppermute | solution.py:51
  97.5 2.2 %collective-permute-start.31 = (f32[8,512]{1,0:T(8,128)S(1)}, f32[8,512]{1,0:T(8,128)S(1)}, u32[]{:S(2)}, u32[]{:S(2)}) collective-permute-start(f32[8,512]{1,0:T(8,128)S(1)} %get-tuple-element.70.refs_4_), channel_id=1, source_target_pairs={{0,1},{1,0},{2,3},{3,2},{4,5},{5,4},{6,7},{7,6},{8,9},{9,8},{10,11... | collective-permute-start | bytes 49160 | tf_op jit(solution)/shard_map/ppermute | solution.py:51
  97.7 3.2 %collective-permute-start.30 = (f32[8,512]{1,0:T(8,128)S(1)}, f32[8,512]{1,0:T(8,128)S(1)}, u32[]{:S(2)}, u32[]{:S(2)}) collective-permute-start(f32[8,512]{1,0:T(8,128)S(1)} %get-tuple-element.70.refs_4_), channel_id=1, source_target_pairs={{0,3},{1,2},{2,1},{3,0},{4,7},{5,6},{6,5},{7,4},{8,11},{9,10},{10,... | collective-permute-start | bytes 49160 | tf_op jit(solution)/shard_map/ppermute | solution.py:51
  99.2 3.7 %collective-permute-start.29 = (f32[8,512]{1,0:T(8,128)S(1)}, f32[8,512]{1,0:T(8,128)S(1)}, u32[]{:S(2)}, u32[]{:S(2)}) collective-permute-start(f32[8,512]{1,0:T(8,128)S(1)} %get-tuple-element.70.refs_4_), channel_id=1, source_target_pairs={{0,2},{1,3},{2,0},{3,1},{4,6},{5,7},{6,4},{7,5},{8,10},{9,11},{10,... | collective-permute-start | bytes 49160 | tf_op jit(solution)/shard_map/ppermute | solution.py:51
  (11 other events, 175.4 us)

commit v5 on v4

--- a/solution.py
+++ b/solution.py
@@ -101,6 +101,20 @@
     flat = page.reshape(2 * page_len, page.shape[2])
     both = jnp.dot(picker, flat, preferred_element_type=F32).astype(BF16)
     return both[:page_len], both[page_len:]
+
+
+class Rows:
+    def __init__(self, rows):
+        self.lane = lax.broadcasted_iota(jnp.int32, (rows, 128), 1)
+        self.table = jnp.zeros((rows, 128), F32)
+        self.count = 0
+
+    def add(self, column):
+        self.table = jnp.where(self.lane == self.count, column, self.table)
+        self.count += 1
+
+    def rows(self):
+        return jnp.transpose(self.table)
 
 
 def to_row(column):
@@ -216,7 +230,7 @@
         acc_ref[rows] = path.reshape(side, 2, path.shape[1])
 
 
-def remote_kernel(dims, page_indices, *refs, between=None):
+def remote_kernel(dims, page_indices, *refs, between):
     page_len, draft, heads, long_count = dims
     count = len(page_indices)
     msgs, table_ref, pool_ref = refs[:count], refs[count], refs[count + 1]
@@ -238,21 +252,28 @@
             limits.append(length - page_index * page_len)
     picker = unpick(page_len)
     lane = lax.broadcasted_iota(jnp.int32, (heads * draft, page_len), 1).astype(F32)
-    if between is not None:
-        between()
+    table = Rows(heads * draft)
+    near_stats = between()
     for copy in copies:
         copy.wait()
     for n in range(count):
-        stats = []
         for i in range(long_count):
             stacked = head_rows(msgs[n][pl.ds(i * draft, draft), :], heads)
             keys, values = split_page(page_ref[n, i], picker, page_len)
             scores = jnp.where(lane < limits[n * long_count + i], dot_t(stacked, keys), NEG)
             mixed, top, total = attend([scores], [values])
             outs[n][pl.ds(i * draft, draft)] = head_lanes(mixed, heads, draft, width).astype(BF16)
-            stats += list(split3(to_row(top))) + list(split3(to_row(total)))
-        stats.append(jnp.zeros((META - len(stats), width), BF16))
-        outs[n][pl.ds(tokens, META)] = jnp.concatenate([s.astype(F32) for s in stats], axis=0).astype(BF16)
+            table.add(top)
+            table.add(total)
+    for column in near_stats:
+        table.add(column)
+    rows = table.rows()
+    each = 2 * long_count
+    for n in range(count):
+        terms = [t.astype(F32) for k in range(each) for t in split3(rows[each * n + k : each * n + k + 1])]
+        terms.append(jnp.zeros((META - len(terms), width), F32))
+        outs[n][pl.ds(tokens, META)] = jnp.concatenate(terms, axis=0).astype(BF16)
+    return rows[each * count :]
 
 
 def near_pages(dims, msg_ref, key_ref, value_ref, out_ref):
@@ -267,15 +288,18 @@
         scores = jnp.where(lane < limits[r : r + 1], dot_t(stacked, key_ref[1, r]), NEG)
         mixed, top, total = attend([scores], [value_ref[1, r]])
         out_ref[pl.ds(r * draft, draft)] = head_lanes(mixed, heads, draft, width).astype(BF16)
-        stats += list(split3(to_row(top))) + list(split3(to_row(total)))
-    out_ref[pl.ds(tokens, len(stats))] = jnp.concatenate([s.astype(F32) for s in stats], axis=0).astype(BF16)
+        stats += [top, total]
+    return stats
 
 
 def visiting_kernel(dims, page_indices, msg_ref, key_ref, value_ref, *refs):
     page_len, draft, heads, long_count = dims
     count = len(page_indices)
     near = functools.partial(near_pages, (draft, heads), msg_ref, key_ref, value_ref, refs[count + 2])
-    remote_kernel(dims, page_indices, *refs[: count + 2], *refs[count + 3 :], between=near)
+    rows = remote_kernel(dims, page_indices, *refs[: count + 2], *refs[count + 3 :], between=near)
+    requests = key_ref.shape[1]
+    terms = [t.astype(F32) for k in range(2 * requests) for t in split3(rows[k : k + 1])]
+    refs[count + 2][pl.ds(requests * draft, len(terms))] = jnp.concatenate(terms, axis=0).astype(BF16)
 
 
 def local_kernel(dims, len_ref, q_ref, k_ref, v_ref, bias_ref, key_ref, value_ref, keep_ref, out_ref, stats_ref, kept_ref):
@@ -283,7 +307,7 @@
     requests, draft, heads = dims
     page_len, width = key_ref.shape[2:]
     lane = lax.broadcasted_iota(jnp.int32, (heads * draft, page_len), 1)
-    stats = []
+    table = Rows(heads * draft)
     for r in range(requests):
         rows = pl.ds(r * draft, draft)
         stacked = head_rows(q_ref[rows, :], heads)
@@ -293,8 +317,9 @@
             [value_ref[0, r], v_ref[rows, :]],
         )
         out_ref[rows] = head_lanes(mixed, heads, draft, width)
-        stats += [to_row(top), to_row(total)]
-    stats_ref[...] = jnp.concatenate(stats, axis=0)
+        table.add(top)
+        table.add(total)
+    stats_ref[...] = table.rows()[: 2 * requests]
 
 
 def merge_kernel(dims, len_ref, own_ref, stats_ref, near_ref, *refs):
@@ -464,7 +489,7 @@
         flops=2 * tokens * width_all * width, nbytes=2 * width_all * width, after=(bias, page_keys, wout_core),
     )
     near_asked = send_req(near_message, 1)
-    queue = sorted(range(2, pages), key=lambda j: (abs(2 * j - pages), j))
+    queue = [j for j in (7, 6, 3, 2, 5, 4) if j < pages] + list(range(8, pages))
     early, late = queue, []
     asked = {j: send_req(message, j) for j in early}
 
@@ -490,7 +515,7 @@
         [shape_of((tokens + 6 * requests, width), BF16)] + [answer] * len(early),
         [VMEM] * (3 + len(early)) + [SMEM, ANY], [VMEM] * (1 + len(early)), buffers(len(early)),
         (near_asked, page_keys, page_values, *[asked[j] for j in early], page_table, cache_pool), "visitors_early",
-        after=(own,),
+        after=(),
     )
     near_got = send_req(near_answer, -1)
     answers = [send_req(out, -j) for j, out in zip(early, outs)]

time: 105 us -> 101 us (0.962)
  waiting for transfers between devices: 41.4 us -> 30.2 us
  starting transfers between devices: 31.6 us -> 39.9 us
  Pallas kernels: 28.5 us -> 27.3 us
    ppermute x14, waiting for transfers between devices: 22 us -> 10.7 us  [send_req(): lax.ppermute(value, 'req', [(i, (i + by) % size) for i in range(size)])]
    ppermute x14, starting transfers between devices: 19.3 us -> 27.6 us  [send_req(): lax.ppermute(value, 'req', [(i, (i + by) % size) for i in range(size)])]
    pallas_call x11, Pallas kernels: 28.5 us -> 27.3 us  [call(): pl.pallas_call(body, out_shape=outs, in_specs=list(ins) + [ANY] * len(aft...]
where the time goes in v5:
time: 101 us; the launch traced here: 100 us
  starting transfers between devices  39.9 us (40%)
  waiting for transfers between devices  30.2 us (30%)
  Pallas kernels  27.3 us (27%)
  local copies, waits for them, and re-layouts  2.13 us (2%)
    ppermute x14, starting transfers between devices, send_req(): lax.ppermute(value, 'req', [(i, (i + by) % size) for i in range(size)])  27.6 us
    pallas_call x11, Pallas kernels, call(): pl.pallas_call(body, out_shape=outs, in_specs=list(ins) + [ANY] * len(aft...  27.3 us
    ppermute x18, waiting for transfers between devices, send_tp(): return lax.ppermute(value, 'tp', [(i, i ^ flip) for i in range(size)])  19.4 us
    ppermute x18, starting transfers between devices, send_tp(): return lax.ppermute(value, 'tp', [(i, i ^ flip) for i in range(size)])  12.3 us
    ppermute x14, waiting for transfers between devices, send_req(): lax.ppermute(value, 'req', [(i, (i + by) % size) for i in range(size)])  10.7 us
  transfers between devices with their start and end apart: 32, of which 13 were waited for; matrix products, arithmetic and copies ran while one was open for 1% of the time, Pallas kernels for 14%

profile of v5, /device:TPU:0, one launch (start us, length us, event | category | flops | bytes accessed | tf_op | source)
XLA Modules:
  0.0 100.3 jit_solution(872484250831287656)
XLA Ops:
  0.6 3.0 %collective-permute-start.1 = (bf16[512,256]{1,0:T(8,128)(2,1)}, bf16[512,256]{1,0:T(8,128)(2,1)S(1)}, u32[]{:S(2)}, u32[]{:S(2)}) collective-permute-start(bf16[512,256]{1,0:T(8,128)(2,1)} %refs_5_.3), channel_id=1, source_target_pairs={{0,2},{1,3},{2,0},{3,1},{4,6},{5,7},{6,4},{7,5},{8,10},{9,11},{10,... | collective-permute-start | bytes 786440 | tf_op jit(solution)/shard_map/ppermute | solution.py:51
  5.6 2.3 %tree.1 = (f32[512,64]{1,0:T(8,128)S(1)}, bf16[2,512,512]{2,1,0:T(8,128)(2,1)S(1)}) custom-call(s32[8]{0:T(128)S(1)} %copy-done.10, s32[2,256]{1,0:T(2,128)S(1)} %reshape.17.refs_1_), custom_call_target="tpu_custom_call" | custom-call | flops 469762048 | tf_op jit(solution)/shard_map/tree/pallas_call | solution.py:32
  8.6 3.3 %pages.1 = (bf16[2,8,128,256]{3,2,1,0:T(8,128)(2,1)S(1)}, bf16[2,8,128,256]{3,2,1,0:T(8,128)(2,1)S(1)}) custom-call(s32[8,8]{1,0:T(8,128)S(1)} %copy-done.5, bf16[64,128,2,256]{3,2,1,0:T(2,128)(2,1)} %refs_10_.1), custom_call_target="tpu_custom_call" | custom-call | flops 536870912 | tf_op jit(solution)/shard_map/pages/pallas_call | solution.py:32
  12.0 1.5 %collective-permute-done.2.refs_4_.refs_3_.refs_8_ = bf16[512,256]{1,0:T(8,128)(2,1)S(1)} collective-permute-done((bf16[512,256]{1,0:T(8,128)(2,1)S(1)}, bf16[512,256]{1,0:T(8,128)(2,1)S(1)}, u32[]{:S(2)}, u32[]{:S(2)}) %collective-permute-start.2) | collective-permute-done | bytes 262176 | tf_op jit(solution)/shard_map/ppermute | solution.py:51
  14.6 1.5 %collective-permute-start.4 = (bf16[528,256]{1,0:T(8,128)(2,1)S(1)}, bf16[528,256]{1,0:T(8,128)(2,1)S(1)}, u32[]{:S(2)}, u32[]{:S(2)}) collective-permute-start(bf16[528,256]{1,0:T(8,128)(2,1)S(1)} %get-tuple-element.48), channel_id=1, source_target_pairs={{0,4},{4,8},{8,12},{12,16},{16,20},{20,24},{24,28},{28,0},{1,5},{5... | collective-permute-start | bytes 811016 | tf_op jit(solution)/shard_map/ppermute | solution.py:46
  16.1 2.6 %collective-permute-start.10 = (bf16[144,256]{1,0:T(8,128)(2,1)S(1)}, bf16[144,256]{1,0:T(8,128)(2,1)S(1)}, u32[]{:S(2)}, u32[]{:S(2)}) collective-permute-start(bf16[144,256]{1,0:T(8,128)(2,1)S(1)} %get-tuple-element.42.refs_6_.refs_7_), channel_id=1, source_target_pairs={{0,16},{4,20},{8,24},{12,28},{16,0},{20,4},{24,8},{28,12},{1,17},{... | collective-permute-start | bytes 221192 | tf_op jit(solution)/shard_map/ppermute | solution.py:46
  18.7 1.3 %collective-permute-start.9 = (bf16[144,256]{1,0:T(8,128)(2,1)S(1)}, bf16[144,256]{1,0:T(8,128)(2,1)S(1)}, u32[]{:S(2)}, u32[]{:S(2)}) collective-permute-start(bf16[144,256]{1,0:T(8,128)(2,1)S(1)} %get-tuple-element.42.refs_6_.refs_7_), channel_id=1, source_target_pairs={{0,20},{4,24},{8,28},{12,0},{16,4},{20,8},{24,12},{28,16},{1,21},{... | collective-permute-start | bytes 221192 | tf_op jit(solution)/shard_map/ppermute | solution.py:46
  20.0 1.6 %collective-permute-start.8 = (bf16[144,256]{1,0:T(8,128)(2,1)S(1)}, bf16[144,256]{1,0:T(8,128)(2,1)S(1)}, u32[]{:S(2)}, u32[]{:S(2)}) collective-permute-start(bf16[144,256]{1,0:T(8,128)(2,1)S(1)} %get-tuple-element.42.refs_6_.refs_7_), channel_id=1, source_target_pairs={{0,8},{4,12},{8,16},{12,20},{16,24},{20,28},{24,0},{28,4},{1,9},{5... | collective-permute-start | bytes 221192 | tf_op jit(solution)/shard_map/ppermute | solution.py:46
  21.6 1.6 %collective-permute-start.7 = (bf16[144,256]{1,0:T(8,128)(2,1)S(1)}, bf16[144,256]{1,0:T(8,128)(2,1)S(1)}, u32[]{:S(2)}, u32[]{:S(2)}) collective-permute-start(bf16[144,256]{1,0:T(8,128)(2,1)S(1)} %get-tuple-element.42.refs_6_.refs_7_), channel_id=1, source_target_pairs={{0,12},{4,16},{8,20},{12,24},{16,28},{20,0},{24,4},{28,8},{1,13},{... | collective-permute-start | bytes 221192 | tf_op jit(solution)/shard_map/ppermute | solution.py:46
  23.2 4.7 %collective-permute-done.10.refs_8_ = bf16[144,256]{1,0:T(8,128)(2,1)S(1)} collective-permute-done((bf16[144,256]{1,0:T(8,128)(2,1)S(1)}, bf16[144,256]{1,0:T(8,128)(2,1)S(1)}, u32[]{:S(2)}, u32[]{:S(2)}) %collective-permute-start.10) | collective-permute-done | bytes 73760 | tf_op jit(solution)/shard_map/ppermute | solution.py:46
  28.3 6.4 %collective-permute-start.5 = (bf16[144,256]{1,0:T(8,128)(2,1)S(1)}, bf16[144,256]{1,0:T(8,128)(2,1)S(1)}, u32[]{:S(2)}, u32[]{:S(2)}) collective-permute-start(bf16[144,256]{1,0:T(8,128)(2,1)S(1)} %get-tuple-element.42.refs_6_.refs_7_), channel_id=1, source_target_pairs={{0,28},{4,0},{8,4},{12,8},{16,12},{20,16},{24,20},{28,24},{1,29},{... | collective-permute-start | bytes 221192 | tf_op jit(solution)/shard_map/ppermute | solution.py:46
  35.6 2.0 %collective-permute-done.5.refs_3_ = bf16[144,256]{1,0:T(8,128)(2,1)S(1)} collective-permute-done((bf16[144,256]{1,0:T(8,128)(2,1)S(1)}, bf16[144,256]{1,0:T(8,128)(2,1)S(1)}, u32[]{:S(2)}, u32[]{:S(2)}) %collective-permute-start.5) | collective-permute-done | bytes 73760 | tf_op jit(solution)/shard_map/ppermute | solution.py:46
  37.6 6.5 %visitors_early.1 = (bf16[560,256]{1,0:T(8,128)(2,1)S(1)}, bf16[144,256]{1,0:T(8,128)(2,1)S(1)}, bf16[144,256]{1,0:T(8,128)(2,1)S(1)}, bf16[144,256]{1,0:T(8,128...) custom-call(bf16[528,256]{1,0:T(8,128)(2,1)S(1)} %collective-permute-done.4.ref, ...), custom_call_target="tpu_custom_call" | custom-call | tf_op jit(solution)/shard_map/visitors_early/pallas_call | solution.py:32
  44.7 4.2 %collective-permute-start.11 = (bf16[560,256]{1,0:T(8,128)(2,1)S(1)}, bf16[560,256]{1,0:T(8,128)(2,1)S(1)}, u32[]{:S(2)}, u32[]{:S(2)}) collective-permute-start(bf16[560,256]{1,0:T(8,128)(2,1)S(1)} %get-tuple-element.49), channel_id=1, source_target_pairs={{0,28},{4,0},{8,4},{12,8},{16,12},{20,16},{24,20},{28,24},{1,29},{... | collective-permute-start | bytes 860168 | tf_op jit(solution)/shard_map/ppermute | solution.py:46
  49.1 5.1 %collective-permute-start.14 = (bf16[144,256]{1,0:T(8,128)(2,1)S(1)}, bf16[144,256]{1,0:T(8,128)(2,1)S(1)}, u32[]{:S(2)}, u32[]{:S(2)}) collective-permute-start(bf16[144,256]{1,0:T(8,128)(2,1)S(1)} %get-tuple-element.52), channel_id=1, source_target_pairs={{0,20},{4,24},{8,28},{12,0},{16,4},{20,8},{24,12},{28,16},{1,21},{... | collective-permute-start | bytes 221192 | tf_op jit(solution)/shard_map/ppermute | solution.py:46
  54.2 1.8 %collective-permute-done.12.refs_4_ = bf16[144,256]{1,0:T(8,128)(2,1)S(1)} collective-permute-done((bf16[144,256]{1,0:T(8,128)(2,1)S(1)}, bf16[144,256]{1,0:T(8,128)(2,1)S(1)}, u32[]{:S(2)}, u32[]{:S(2)}) %collective-permute-start.12) | collective-permute-done | bytes 73760 | tf_op jit(solution)/shard_map/ppermute | solution.py:46
  56.7 2.2 %collective-permute-start.17 = (bf16[144,256]{1,0:T(8,128)(2,1)S(1)}, bf16[144,256]{1,0:T(8,128)(2,1)S(1)}, u32[]{:S(2)}, u32[]{:S(2)}) collective-permute-start(bf16[144,256]{1,0:T(8,128)(2,1)S(1)} %get-tuple-element.55), channel_id=1, source_target_pairs={{0,16},{4,20},{8,24},{12,28},{16,0},{20,4},{24,8},{28,12},{1,17},{... | collective-permute-start | bytes 221192 | tf_op jit(solution)/shard_map/ppermute | solution.py:46
  58.9 1.9 %keys_values.1 = (bf16[512,256]{1,0:T(8,128)(2,1)S(1)}, bf16[512,256]{1,0:T(8,128)(2,1)S(1)}, bf16[512,2,256]{2,1,0:T(2,128)(2,1)}) custom-call(bf16[512,256]{1,0:T(8,128)(2,1)S(1)} %copy-done.1, bf16[512,256]{1,0:T(8,128)(2,1)S(1)} %collective-permute-done.refs_2_.refs_1_.refs_6_, bf16[512,256]{1,0:T(8,128)(2,1)S(1)} %collective-permute-done.1.refs_3_.refs_2_.refs_7_, ...), custom_call_target="tpu_custom_call" | custom-call | flops 536870912 | bytes 1048576 | tf_op jit(solution)/shard_map/keys_values/pallas_call | solution.py:32
  60.8 2.7 %local_attention.1 = (f32[512,256]{1,0:T(8,128)S(1)}, f32[16,256]{1,0:T(8,128)S(1)}, bf16[144,256]{1,0:T(8,128)(2,1)}) custom-call(s32[8]{0:T(128)S(1)} %copy-done.7, bf16[512,256]{1,0:T(8,128)(2,1)S(1)} %get-tuple-element.40.refs_1_, bf16[512,256]{1,0:T(8,128)(2,1)S(1)} %get-tuple-element.43.refs_2_, bf16[512,256]{1,0:T(8,128)(2,1)S(1)} %get-tuple-element.44.refs_3_, ...), custom_call_target="tpu_custom_call" | custom-call | tf_op jit(solution)/shard_map/local_attention/pallas_call | solution.py:32
  64.6 1.9 %merge.1.refs_1_ = bf16[512,256]{1,0:T(8,128)(2,1)S(1)} custom-call(s32[8]{0:T(128)S(1)} %copy-done.7, f32[512,256]{1,0:T(8,128)S(1)} %get-tuple-element.46.refs_1_, f32[16,256]{1,0:T(8,128)S(1)} %get-tuple-element.47.refs_2_, bf16[560,256]{1,0:T(8,128)(2,1)S(1)} %collective-permute-done.11.refs_3_, bf16[144,256]{1,0:T(8,128)(2,1)S(1)} %collective-permute-done.12.refs_4_, ...), custom_call_target="tpu_custom_call" | custom-call | tf_op jit(solution)/shard_map/merge/pallas_call | solution.py:32
  66.5 1.6 %collective-permute-start.19 = (bf16[512,256]{1,0:T(8,128)(2,1)S(1)}, bf16[512,256]{1,0:T(8,128)(2,1)S(1)}, u32[]{:S(2)}, u32[]{:S(2)}) collective-permute-start(bf16[512,256]{1,0:T(8,128)(2,1)S(1)} %merge.1.refs_1_), channel_id=1, source_target_pairs={{0,2},{1,3},{2,0},{3,1},{4,6},{5,7},{6,4},{7,5},{8,10},{9,11},{10,... | collective-permute-start | bytes 786440 | tf_op jit(solution)/shard_map/ppermute | solution.py:51
  68.6 4.3 %collective-permute-done.19.refs_3_ = bf16[512,256]{1,0:T(8,128)(2,1)S(1)} collective-permute-done((bf16[512,256]{1,0:T(8,128)(2,1)S(1)}, bf16[512,256]{1,0:T(8,128)(2,1)S(1)}, u32[]{:S(2)}, u32[]{:S(2)}) %collective-permute-start.19) | collective-permute-done | bytes 262176 | tf_op jit(solution)/shard_map/ppermute | solution.py:51
  72.9 1.5 %collective-permute-done.20.refs_4_ = bf16[512,256]{1,0:T(8,128)(2,1)S(1)} collective-permute-done((bf16[512,256]{1,0:T(8,128)(2,1)S(1)}, bf16[512,256]{1,0:T(8,128)(2,1)S(1)}, u32[]{:S(2)}, u32[]{:S(2)}) %collective-permute-start.20) | collective-permute-done | bytes 262176 | tf_op jit(solution)/shard_map/ppermute | solution.py:51
  74.5 3.7 %forward_short.1 = (bf16[384,256]{1,0:T(8,128)(2,1)S(1)}, bf16[384,256]{1,0:T(8,128)(2,1)S(1)}, bf16[384,256]{1,0:T(8,128)(2,1)S(1)}, bf16[384,256]{1,0:T(8,128)(2,1)S(1)}, bf16[384,256]{1,0:T(8,128)(2,1)S(1)}) custom-call(s32[8]{0:T(128)S(1)} %copy-done.7, bf16[512,256]{1,0:T(8,128)(2,1)S(1)} %merge.1.refs_1_, ...), custom_call_target="tpu_custom_call" | custom-call | flops 2415919104 | bytes 6291456 | tf_op jit(solution)/shard_map/forward_short/pallas_call | solution.py:32
  78.2 1.6 %collective-permute-start.26 = (bf16[384,256]{1,0:T(8,128)(2,1)S(1)}, bf16[384,256]{1,0:T(8,128)(2,1)S(1)}, u32[]{:S(2)}, u32[]{:S(2)}) collective-permute-start(bf16[384,256]{1,0:T(8,128)(2,1)S(1)} %get-tuple-element.65), channel_id=1, source_target_pairs={{0,2},{1,3},{2,0},{3,1},{4,6},{5,7},{6,4},{7,5},{8,10},{9,11},{10,... | collective-permute-start | bytes 589832 | tf_op jit(solution)/shard_map/ppermute | solution.py:51
  80.4 1.9 %forward_long.1 = (bf16[128,256]{1,0:T(8,128)(2,1)S(1)}, bf16[128,256]{1,0:T(8,128)(2,1)S(1)}, bf16[128,256]{1,0:T(8,128)(2,1)S(1)}, bf16[128,256]{1,0:T(8,128)(2,1)S(1)}, bf16[128,256]{1,0:T(8,128)(2,1)S(1)}) custom-call(s32[8]{0:T(128)S(1)} %copy-done.7, bf16[512,256]{1,0:T(8,128)(2,1)S(1)} %merge.1.refs_1_, ...), custom_call_target="tpu_custom_call" | custom-call | flops 805306368 | bytes 6291456 | tf_op jit(solution)/shard_map/forward_long/pallas_call | solution.py:32
  82.4 1.6 %collective-permute-start.23 = (bf16[128,256]{1,0:T(8,128)(2,1)S(1)}, bf16[128,256]{1,0:T(8,128)(2,1)S(1)}, u32[]{:S(2)}, u32[]{:S(2)}) collective-permute-start(bf16[128,256]{1,0:T(8,128)(2,1)S(1)} %get-tuple-element.60), channel_id=1, source_target_pairs={{0,2},{1,3},{2,0},{3,1},{4,6},{5,7},{6,4},{7,5},{8,10},{9,11},{10,... | collective-permute-start | bytes 196616 | tf_op jit(solution)/shard_map/ppermute | solution.py:51
  84.0 7.5 %collective-permute-done.23.refs_1_ = bf16[128,256]{1,0:T(8,128)(2,1)S(1)} collective-permute-done((bf16[128,256]{1,0:T(8,128)(2,1)S(1)}, bf16[128,256]{1,0:T(8,128)(2,1)S(1)}, u32[]{:S(2)}, u32[]{:S(2)}) %collective-permute-start.23) | collective-permute-done | bytes 65568 | tf_op jit(solution)/shard_map/ppermute | solution.py:51
  91.5 1.2 %collective-permute-done.25.refs_3_ = bf16[128,256]{1,0:T(8,128)(2,1)S(1)} collective-permute-done((bf16[128,256]{1,0:T(8,128)(2,1)S(1)}, bf16[128,256]{1,0:T(8,128)(2,1)S(1)}, u32[]{:S(2)}, u32[]{:S(2)}) %collective-permute-start.25) | collective-permute-done | bytes 65568 | tf_op jit(solution)/shard_map/ppermute | solution.py:51
  93.4 1.5 %collective-permute-start.30 = (f32[8,512]{1,0:T(8,128)S(1)}, f32[8,512]{1,0:T(8,128)S(1)}, u32[]{:S(2)}, u32[]{:S(2)}) collective-permute-start(f32[8,512]{1,0:T(8,128)S(1)} %get-tuple-element.70.refs_4_), channel_id=1, source_target_pairs={{0,3},{1,2},{2,1},{3,0},{4,7},{5,6},{6,5},{7,4},{8,11},{9,10},{10,... | collective-permute-start | bytes 49160 | tf_op jit(solution)/shard_map/ppermute | solution.py:51
  96.6 2.1 %collective-permute-done.29.refs_5_ = f32[8,512]{1,0:T(8,128)S(1)} collective-permute-done((f32[8,512]{1,0:T(8,128)S(1)}, f32[8,512]{1,0:T(8,128)S(1)}, u32[]{:S(2)}, u32[]{:S(2)}) %collective-permute-start.29) | collective-permute-done | bytes 16416 | tf_op jit(solution)/shard_map/ppermute | solution.py:51
  98.7 1.6 %finish.1 = bf16[512,256]{1,0:T(8,128)(2,1)} custom-call(s32[8]{0:T(128)S(1)} %copy-done.7, f32[1,1024]{1,0:T(1,128)S(1)} %bitcast.8, f32[128,256]{1,0:T(8,128)S(1)} %get-tuple-element.68.refs_2_, f32[384,256]{1,0:T(8,128)S(1)} %get-tuple-element.69.refs_3_, f32[8,512]{1,0:T(8,128)S(1)} %get-tuple-element.70.refs_4_, ...), custom_call_target="tpu_custom_call" | custom-call | tf_op jit(solution)/shard_map/finish/pallas_call | solution.py:32
  (66 shorter events, 11.1 us)
Async XLA Ops:
  0.6 11.3 %collective-permute-start.1 = (bf16[512,256]{1,0:T(8,128)(2,1)}, bf16[512,256]{1,0:T(8,128)(2,1)S(1)}, u32[]{:S(2)}, u32[]{:S(2)}) collective-permute-start(bf16[512,256]{1,0:T(8,128)(2,1)} %refs_5_.3), channel_id=1, source_target_pairs={{0,2},{1,3},{2,0},{3,1},{4,6},{5,7},{6,4},{7,5},{8,10},{9,11},{10,... | collective-permute-start | bytes 786440 | tf_op jit(solution)/shard_map/ppermute | solution.py:51
  3.7 8.4 %collective-permute-start.3 = (bf16[256,1024]{1,0:T(8,128)(2,1)}, bf16[256,1024]{1,0:T(8,128)(2,1)S(1)}, u32[]{:S(2)}, u32[]{:S(2)}) collective-permute-start(bf16[256,1024]{1,0:T(8,128)(2,1)} %refs_9_.5), channel_id=1, source_target_pairs={{0,1},{1,0},{2,3},{3,2},{4,5},{5,4},{6,7},{7,6},{8,9},{9,8},{10,11... | collective-permute-start | bytes 1572872 | tf_op jit(solution)/shard_map/ppermute | solution.py:51
  3.7 8.3 %collective-permute-start = (bf16[512,256]{1,0:T(8,128)(2,1)}, bf16[512,256]{1,0:T(8,128)(2,1)S(1)}, u32[]{:S(2)}, u32[]{:S(2)}) collective-permute-start(bf16[512,256]{1,0:T(8,128)(2,1)} %refs_5_.3), channel_id=1, source_target_pairs={{0,1},{1,0},{2,3},{3,2},{4,5},{5,4},{6,7},{7,6},{8,9},{9,8},{10,11... | collective-permute-start | bytes 786440 | tf_op jit(solution)/shard_map/ppermute | solution.py:51
  11.9 1.6 %collective-permute-start.2 = (bf16[512,256]{1,0:T(8,128)(2,1)S(1)}, bf16[512,256]{1,0:T(8,128)(2,1)S(1)}, u32[]{:S(2)}, u32[]{:S(2)}) collective-permute-start(bf16[512,256]{1,0:T(8,128)(2,1)S(1)} %collective-permute-done.1.refs_3_.refs_2_.refs_7_), channel_id=1, source_target_pairs={{0,1},{1,0},{2,3},{3,2},{4,5},{5,4},{6,7},{7,6},{8,9},{9,8},{10,11... | collective-permute-start | bytes 786440 | tf_op jit(solution)/shard_map/ppermute | solution.py:51
  14.6 23.0 %collective-permute-start.4 = (bf16[528,256]{1,0:T(8,128)(2,1)S(1)}, bf16[528,256]{1,0:T(8,128)(2,1)S(1)}, u32[]{:S(2)}, u32[]{:S(2)}) collective-permute-start(bf16[528,256]{1,0:T(8,128)(2,1)S(1)} %get-tuple-element.48), channel_id=1, source_target_pairs={{0,4},{4,8},{8,12},{12,16},{16,20},{20,24},{24,28},{28,0},{1,5},{5... | collective-permute-start | bytes 811016 | tf_op jit(solution)/shard_map/ppermute | solution.py:46
  16.1 11.8 %collective-permute-start.10 = (bf16[144,256]{1,0:T(8,128)(2,1)S(1)}, bf16[144,256]{1,0:T(8,128)(2,1)S(1)}, u32[]{:S(2)}, u32[]{:S(2)}) collective-permute-start(bf16[144,256]{1,0:T(8,128)(2,1)S(1)} %get-tuple-element.42.refs_6_.refs_7_), channel_id=1, source_target_pairs={{0,16},{4,20},{8,24},{12,28},{16,0},{20,4},{24,8},{28,12},{1,17},{... | collective-permute-start | bytes 221192 | tf_op jit(solution)/shard_map/ppermute | solution.py:46
  18.7 9.5 %collective-permute-start.9 = (bf16[144,256]{1,0:T(8,128)(2,1)S(1)}, bf16[144,256]{1,0:T(8,128)(2,1)S(1)}, u32[]{:S(2)}, u32[]{:S(2)}) collective-permute-start(bf16[144,256]{1,0:T(8,128)(2,1)S(1)} %get-tuple-element.42.refs_6_.refs_7_), channel_id=1, source_target_pairs={{0,20},{4,24},{8,28},{12,0},{16,4},{20,8},{24,12},{28,16},{1,21},{... | collective-permute-start | bytes 221192 | tf_op jit(solution)/shard_map/ppermute | solution.py:46
  20.0 14.7 %collective-permute-start.8 = (bf16[144,256]{1,0:T(8,128)(2,1)S(1)}, bf16[144,256]{1,0:T(8,128)(2,1)S(1)}, u32[]{:S(2)}, u32[]{:S(2)}) collective-permute-start(bf16[144,256]{1,0:T(8,128)(2,1)S(1)} %get-tuple-element.42.refs_6_.refs_7_), channel_id=1, source_target_pairs={{0,8},{4,12},{8,16},{12,20},{16,24},{20,28},{24,0},{28,4},{1,9},{5... | collective-permute-start | bytes 221192 | tf_op jit(solution)/shard_map/ppermute | solution.py:46
  21.6 13.9 %collective-permute-start.7 = (bf16[144,256]{1,0:T(8,128)(2,1)S(1)}, bf16[144,256]{1,0:T(8,128)(2,1)S(1)}, u32[]{:S(2)}, u32[]{:S(2)}) collective-permute-start(bf16[144,256]{1,0:T(8,128)(2,1)S(1)} %get-tuple-element.42.refs_6_.refs_7_), channel_id=1, source_target_pairs={{0,12},{4,16},{8,20},{12,24},{16,28},{20,0},{24,4},{28,8},{1,13},{... | collective-permute-start | bytes 221192 | tf_op jit(solution)/shard_map/ppermute | solution.py:46
  27.9 7.7 %collective-permute-start.6 = (bf16[144,256]{1,0:T(8,128)(2,1)S(1)}, bf16[144,256]{1,0:T(8,128)(2,1)S(1)}, u32[]{:S(2)}, u32[]{:S(2)}) collective-permute-start(bf16[144,256]{1,0:T(8,128)(2,1)S(1)} %get-tuple-element.42.refs_6_.refs_7_), channel_id=1, source_target_pairs={{0,24},{4,28},{8,0},{12,4},{16,8},{20,12},{24,16},{28,20},{1,25},{... | collective-permute-start | bytes 221192 | tf_op jit(solution)/shard_map/ppermute | solution.py:46
  28.3 9.3 %collective-permute-start.5 = (bf16[144,256]{1,0:T(8,128)(2,1)S(1)}, bf16[144,256]{1,0:T(8,128)(2,1)S(1)}, u32[]{:S(2)}, u32[]{:S(2)}) collective-permute-start(bf16[144,256]{1,0:T(8,128)(2,1)S(1)} %get-tuple-element.42.refs_6_.refs_7_), channel_id=1, source_target_pairs={{0,28},{4,0},{8,4},{12,8},{16,12},{20,16},{24,20},{28,24},{1,29},{... | collective-permute-start | bytes 221192 | tf_op jit(solution)/shard_map/ppermute | solution.py:46
  44.2 23.9 %collective-permute-start.21 = (bf16[256,1024]{1,0:T(8,128)(2,1)S(1)}, bf16[256,1024]{1,0:T(8,128)(2,1)S(1)}, u32[]{:S(2)}, u32[]{:S(2)}) collective-permute-start(bf16[256,1024]{1,0:T(8,128)(2,1)S(1)} %copy-done.4), channel_id=1, source_target_pairs={{0,2},{1,3},{2,0},{3,1},{4,6},{5,7},{6,4},{7,5},{8,10},{9,11},{10,... | collective-permute-start | bytes 1572872 | tf_op jit(solution)/shard_map/ppermute | solution.py:51
  44.7 19.9 %collective-permute-start.11 = (bf16[560,256]{1,0:T(8,128)(2,1)S(1)}, bf16[560,256]{1,0:T(8,128)(2,1)S(1)}, u32[]{:S(2)}, u32[]{:S(2)}) collective-permute-start(bf16[560,256]{1,0:T(8,128)(2,1)S(1)} %get-tuple-element.49), channel_id=1, source_target_pairs={{0,28},{4,0},{8,4},{12,8},{16,12},{20,16},{24,20},{28,24},{1,29},{... | collective-permute-start | bytes 860168 | tf_op jit(solution)/shard_map/ppermute | solution.py:46
  48.9 7.1 %collective-permute-start.12 = (bf16[144,256]{1,0:T(8,128)(2,1)S(1)}, bf16[144,256]{1,0:T(8,128)(2,1)S(1)}, u32[]{:S(2)}, u32[]{:S(2)}) collective-permute-start(bf16[144,256]{1,0:T(8,128)(2,1)S(1)} %get-tuple-element.50), channel_id=1, source_target_pairs={{0,4},{4,8},{8,12},{12,16},{16,20},{20,24},{24,28},{28,0},{1,5},{5... | collective-permute-start | bytes 221192 | tf_op jit(solution)/shard_map/ppermute | solution.py:46
  48.9 7.1 %collective-permute-start.13 = (bf16[144,256]{1,0:T(8,128)(2,1)S(1)}, bf16[144,256]{1,0:T(8,128)(2,1)S(1)}, u32[]{:S(2)}, u32[]{:S(2)}) collective-permute-start(bf16[144,256]{1,0:T(8,128)(2,1)S(1)} %get-tuple-element.51), channel_id=1, source_target_pairs={{0,8},{4,12},{8,16},{12,20},{16,24},{20,28},{24,0},{28,4},{1,9},{5... | collective-permute-start | bytes 221192 | tf_op jit(solution)/shard_map/ppermute | solution.py:46
  49.1 7.5 %collective-permute-start.14 = (bf16[144,256]{1,0:T(8,128)(2,1)S(1)}, bf16[144,256]{1,0:T(8,128)(2,1)S(1)}, u32[]{:S(2)}, u32[]{:S(2)}) collective-permute-start(bf16[144,256]{1,0:T(8,128)(2,1)S(1)} %get-tuple-element.52), channel_id=1, source_target_pairs={{0,20},{4,24},{8,28},{12,0},{16,4},{20,8},{24,12},{28,16},{1,21},{... | collective-permute-start | bytes 221192 | tf_op jit(solution)/shard_map/ppermute | solution.py:46
  56.0 7.5 %collective-permute-start.15 = (bf16[144,256]{1,0:T(8,128)(2,1)S(1)}, bf16[144,256]{1,0:T(8,128)(2,1)S(1)}, u32[]{:S(2)}, u32[]{:S(2)}) collective-permute-start(bf16[144,256]{1,0:T(8,128)(2,1)S(1)} %get-tuple-element.53), channel_id=1, source_target_pairs={{0,24},{4,28},{8,0},{12,4},{16,8},{20,12},{24,16},{28,20},{1,25},{... | collective-permute-start | bytes 221192 | tf_op jit(solution)/shard_map/ppermute | solution.py:46
  56.0 8.7 %collective-permute-start.16 = (bf16[144,256]{1,0:T(8,128)(2,1)S(1)}, bf16[144,256]{1,0:T(8,128)(2,1)S(1)}, u32[]{:S(2)}, u32[]{:S(2)}) collective-permute-start(bf16[144,256]{1,0:T(8,128)(2,1)S(1)} %get-tuple-element.54), channel_id=1, source_target_pairs={{0,12},{4,16},{8,20},{12,24},{16,28},{20,0},{24,4},{28,8},{1,13},{... | collective-permute-start | bytes 221192 | tf_op jit(solution)/shard_map/ppermute | solution.py:46
  56.7 8.0 %collective-permute-start.17 = (bf16[144,256]{1,0:T(8,128)(2,1)S(1)}, bf16[144,256]{1,0:T(8,128)(2,1)S(1)}, u32[]{:S(2)}, u32[]{:S(2)}) collective-permute-start(bf16[144,256]{1,0:T(8,128)(2,1)S(1)} %get-tuple-element.55), channel_id=1, source_target_pairs={{0,16},{4,20},{8,24},{12,28},{16,0},{20,4},{24,8},{28,12},{1,17},{... | collective-permute-start | bytes 221192 | tf_op jit(solution)/shard_map/ppermute | solution.py:46
  66.5 6.4 %collective-permute-start.19 = (bf16[512,256]{1,0:T(8,128)(2,1)S(1)}, bf16[512,256]{1,0:T(8,128)(2,1)S(1)}, u32[]{:S(2)}, u32[]{:S(2)}) collective-permute-start(bf16[512,256]{1,0:T(8,128)(2,1)S(1)} %merge.1.refs_1_), channel_id=1, source_target_pairs={{0,2},{1,3},{2,0},{3,1},{4,6},{5,7},{6,4},{7,5},{8,10},{9,11},{10,... | collective-permute-start | bytes 786440 | tf_op jit(solution)/shard_map/ppermute | solution.py:51
  68.1 6.4 %collective-permute-start.22 = (bf16[256,1024]{1,0:T(8,128)(2,1)S(1)}, bf16[256,1024]{1,0:T(8,128)(2,1)S(1)}, u32[]{:S(2)}, u32[]{:S(2)}) collective-permute-start(bf16[256,1024]{1,0:T(8,128)(2,1)S(1)} %collective-permute-done.21.refs_11_), channel_id=1, source_target_pairs={{0,1},{1,0},{2,3},{3,2},{4,5},{5,4},{6,7},{7,6},{8,9},{9,8},{10,11... | collective-permute-start | bytes 1572872 | tf_op jit(solution)/shard_map/ppermute | solution.py:51
  68.1 4.8 %collective-permute-start.18 = (bf16[512,256]{1,0:T(8,128)(2,1)S(1)}, bf16[512,256]{1,0:T(8,128)(2,1)S(1)}, u32[]{:S(2)}, u32[]{:S(2)}) collective-permute-start(bf16[512,256]{1,0:T(8,128)(2,1)S(1)} %merge.1.refs_1_), channel_id=1, source_target_pairs={{0,1},{1,0},{2,3},{3,2},{4,5},{5,4},{6,7},{7,6},{8,9},{9,8},{10,11... | collective-permute-start | bytes 786440 | tf_op jit(solution)/shard_map/ppermute | solution.py:51
  72.9 1.5 %collective-permute-start.20 = (bf16[512,256]{1,0:T(8,128)(2,1)S(1)}, bf16[512,256]{1,0:T(8,128)(2,1)S(1)}, u32[]{:S(2)}, u32[]{:S(2)}) collective-permute-start(bf16[512,256]{1,0:T(8,128)(2,1)S(1)} %collective-permute-done.19.refs_3_), channel_id=1, source_target_pairs={{0,1},{1,0},{2,3},{3,2},{4,5},{5,4},{6,7},{7,6},{8,9},{9,8},{10,11... | collective-permute-start | bytes 786440 | tf_op jit(solution)/shard_map/ppermute | solution.py:51
  78.2 14.6 %collective-permute-start.26 = (bf16[384,256]{1,0:T(8,128)(2,1)S(1)}, bf16[384,256]{1,0:T(8,128)(2,1)S(1)}, u32[]{:S(2)}, u32[]{:S(2)}) collective-permute-start(bf16[384,256]{1,0:T(8,128)(2,1)S(1)} %get-tuple-element.65), channel_id=1, source_target_pairs={{0,2},{1,3},{2,0},{3,1},{4,6},{5,7},{6,4},{7,5},{8,10},{9,11},{10,... | collective-permute-start | bytes 589832 | tf_op jit(solution)/shard_map/ppermute | solution.py:51
  79.8 13.0 %collective-permute-start.27 = (bf16[384,256]{1,0:T(8,128)(2,1)S(1)}, bf16[384,256]{1,0:T(8,128)(2,1)S(1)}, u32[]{:S(2)}, u32[]{:S(2)}) collective-permute-start(bf16[384,256]{1,0:T(8,128)(2,1)S(1)} %get-tuple-element.66), channel_id=1, source_target_pairs={{0,3},{1,2},{2,1},{3,0},{4,7},{5,6},{6,5},{7,4},{8,11},{9,10},{10,... | collective-permute-start | bytes 589832 | tf_op jit(solution)/shard_map/ppermute | solution.py:51
  79.8 13.0 %collective-permute-start.28 = (bf16[384,256]{1,0:T(8,128)(2,1)S(1)}, bf16[384,256]{1,0:T(8,128)(2,1)S(1)}, u32[]{:S(2)}, u32[]{:S(2)}) collective-permute-start(bf16[384,256]{1,0:T(8,128)(2,1)S(1)} %get-tuple-element.67), channel_id=1, source_target_pairs={{0,1},{1,0},{2,3},{3,2},{4,5},{5,4},{6,7},{7,6},{8,9},{9,8},{10,11... | collective-permute-start | bytes 589832 | tf_op jit(solution)/shard_map/ppermute | solution.py:51
  82.4 9.2 %collective-permute-start.23 = (bf16[128,256]{1,0:T(8,128)(2,1)S(1)}, bf16[128,256]{1,0:T(8,128)(2,1)S(1)}, u32[]{:S(2)}, u32[]{:S(2)}) collective-permute-start(bf16[128,256]{1,0:T(8,128)(2,1)S(1)} %get-tuple-element.60), channel_id=1, source_target_pairs={{0,2},{1,3},{2,0},{3,1},{4,6},{5,7},{6,4},{7,5},{8,10},{9,11},{10,... | collective-permute-start | bytes 196616 | tf_op jit(solution)/shard_map/ppermute | solution.py:51
  84.0 7.6 %collective-permute-start.24 = (bf16[128,256]{1,0:T(8,128)(2,1)S(1)}, bf16[128,256]{1,0:T(8,128)(2,1)S(1)}, u32[]{:S(2)}, u32[]{:S(2)}) collective-permute-start(bf16[128,256]{1,0:T(8,128)(2,1)S(1)} %get-tuple-element.61), channel_id=1, source_target_pairs={{0,3},{1,2},{2,1},{3,0},{4,7},{5,6},{6,5},{7,4},{8,11},{9,10},{10,... | collective-permute-start | bytes 196616 | tf_op jit(solution)/shard_map/ppermute | solution.py:51
  91.5 1.3 %collective-permute-start.25 = (bf16[128,256]{1,0:T(8,128)(2,1)S(1)}, bf16[128,256]{1,0:T(8,128)(2,1)S(1)}, u32[]{:S(2)}, u32[]{:S(2)}) collective-permute-start(bf16[128,256]{1,0:T(8,128)(2,1)S(1)} %get-tuple-element.62), channel_id=1, source_target_pairs={{0,1},{1,0},{2,3},{3,2},{4,5},{5,4},{6,7},{7,6},{8,9},{9,8},{10,11... | collective-permute-start | bytes 196616 | tf_op jit(solution)/shard_map/ppermute | solution.py:51
  93.2 2.2 %collective-permute-start.31 = (f32[8,512]{1,0:T(8,128)S(1)}, f32[8,512]{1,0:T(8,128)S(1)}, u32[]{:S(2)}, u32[]{:S(2)}) collective-permute-start(f32[8,512]{1,0:T(8,128)S(1)} %get-tuple-element.70.refs_4_), channel_id=1, source_target_pairs={{0,1},{1,0},{2,3},{3,2},{4,5},{5,4},{6,7},{7,6},{8,9},{9,8},{10,11... | collective-permute-start | bytes 49160 | tf_op jit(solution)/shard_map/ppermute | solution.py:51
  93.4 3.2 %collective-permute-start.30 = (f32[8,512]{1,0:T(8,128)S(1)}, f32[8,512]{1,0:T(8,128)S(1)}, u32[]{:S(2)}, u32[]{:S(2)}) collective-permute-start(f32[8,512]{1,0:T(8,128)S(1)} %get-tuple-element.70.refs_4_), channel_id=1, source_target_pairs={{0,3},{1,2},{2,1},{3,0},{4,7},{5,6},{6,5},{7,4},{8,11},{9,10},{10,... | collective-permute-start | bytes 49160 | tf_op jit(solution)/shard_map/ppermute | solution.py:51
  94.9 3.7 %collective-permute-start.29 = (f32[8,512]{1,0:T(8,128)S(1)}, f32[8,512]{1,0:T(8,128)S(1)}, u32[]{:S(2)}, u32[]{:S(2)}) collective-permute-start(f32[8,512]{1,0:T(8,128)S(1)} %get-tuple-element.70.refs_4_), channel_id=1, source_target_pairs={{0,2},{1,3},{2,0},{3,1},{4,6},{5,7},{6,4},{7,5},{8,10},{9,11},{10,... | collective-permute-start | bytes 49160 | tf_op jit(solution)/shard_map/ppermute | solution.py:51
  (11 other events, 106.1 us)

commit v6 on v5

--- a/solution.py
+++ b/solution.py
@@ -489,7 +489,7 @@
         flops=2 * tokens * width_all * width, nbytes=2 * width_all * width, after=(bias, page_keys, wout_core),
     )
     near_asked = send_req(near_message, 1)
-    queue = [j for j in (7, 6, 3, 2, 5, 4) if j < pages] + list(range(8, pages))
+    queue = [j for j in (4, 5, 3, 7, 6, 2) if j < pages] + list(range(8, pages))
     early, late = queue, []
     asked = {j: send_req(message, j) for j in early}
 
@@ -515,10 +515,12 @@
         [shape_of((tokens + 6 * requests, width), BF16)] + [answer] * len(early),
         [VMEM] * (3 + len(early)) + [SMEM, ANY], [VMEM] * (1 + len(early)), buffers(len(early)),
         (near_asked, page_keys, page_values, *[asked[j] for j in early], page_table, cache_pool), "visitors_early",
-        after=(),
+        after=(key_new,),
     )
     near_got = send_req(near_answer, -1)
-    answers = [send_req(out, -j) for j, out in zip(early, outs)]
+    outs = dict(zip(early, outs))
+    back = [j for j in (7, 6, 3, 2, 5, 4) if j < pages] + list(range(8, pages))
+    answers = [send_req(outs[j], -j) for j in back]
     last = (near_answer,)
 
     w_later, _ = lax.optimization_barrier((w_out, near_answer))

time: 101 us -> 99.8 us (0.988)
  waiting for transfers between devices: 30.2 us -> 28.3 us
    ppermute x14, waiting for transfers between devices: 10.7 us -> 8.65 us  [send_req(): lax.ppermute(value, 'req', [(i, (i + by) % size) for i in range(size)])]
    ppermute x18, starting transfers between devices: 12.3 us -> 11.1 us  [send_tp(): return lax.ppermute(value, 'tp', [(i, i ^ flip) for i in range(size)])]
where the time goes in v6:
time: 99.8 us; the launch traced here: 98.2 us
  starting transfers between devices  39.7 us (40%)
  waiting for transfers between devices  28.3 us (28%)
  Pallas kernels  27.3 us (27%)
  local copies, waits for them, and re-layouts  2.13 us (2%)
    ppermute x14, starting transfers between devices, send_req(): lax.ppermute(value, 'req', [(i, (i + by) % size) for i in range(size)])  28.5 us
    pallas_call x11, Pallas kernels, call(): pl.pallas_call(body, out_shape=outs, in_specs=list(ins) + [ANY] * len(aft...  27.3 us
    ppermute x18, waiting for transfers between devices, send_tp(): return lax.ppermute(value, 'tp', [(i, i ^ flip) for i in range(size)])  19.6 us
    ppermute x18, starting transfers between devices, send_tp(): return lax.ppermute(value, 'tp', [(i, i ^ flip) for i in range(size)])  11.1 us
    ppermute x14, waiting for transfers between devices, send_req(): lax.ppermute(value, 'req', [(i, (i + by) % size) for i in range(size)])  8.65 us
  transfers between devices with their start and end apart: 32, of which 13 were waited for; matrix products, arithmetic and copies ran while one was open for 1% of the time, Pallas kernels for 14%

profile of v6, /device:TPU:0, one launch (start us, length us, event | category | flops | bytes accessed | tf_op | source)
XLA Modules:
  0.0 98.2 jit_solution(10149368125471037522)
XLA Ops:
  0.6 3.0 %collective-permute-start.1 = (bf16[512,256]{1,0:T(8,128)(2,1)}, bf16[512,256]{1,0:T(8,128)(2,1)S(1)}, u32[]{:S(2)}, u32[]{:S(2)}) collective-permute-start(bf16[512,256]{1,0:T(8,128)(2,1)} %refs_5_.3), channel_id=1, source_target_pairs={{0,2},{1,3},{2,0},{3,1},{4,6},{5,7},{6,4},{7,5},{8,10},{9,11},{10,... | collective-permute-start | bytes 786440 | tf_op jit(solution)/shard_map/ppermute | solution.py:51
  5.6 2.3 %tree.1 = (f32[512,64]{1,0:T(8,128)S(1)}, bf16[2,512,512]{2,1,0:T(8,128)(2,1)S(1)}) custom-call(s32[8]{0:T(128)S(1)} %copy-done.10, s32[2,256]{1,0:T(2,128)S(1)} %reshape.17.refs_1_), custom_call_target="tpu_custom_call" | custom-call | flops 469762048 | tf_op jit(solution)/shard_map/tree/pallas_call | solution.py:32
  8.6 3.3 %pages.1 = (bf16[2,8,128,256]{3,2,1,0:T(8,128)(2,1)S(1)}, bf16[2,8,128,256]{3,2,1,0:T(8,128)(2,1)S(1)}) custom-call(s32[8,8]{1,0:T(8,128)S(1)} %copy-done.5, bf16[64,128,2,256]{3,2,1,0:T(2,128)(2,1)} %refs_10_.1), custom_call_target="tpu_custom_call" | custom-call | flops 536870912 | tf_op jit(solution)/shard_map/pages/pallas_call | solution.py:32
  12.0 1.5 %collective-permute-done.2.refs_4_.refs_3_.refs_8_ = bf16[512,256]{1,0:T(8,128)(2,1)S(1)} collective-permute-done((bf16[512,256]{1,0:T(8,128)(2,1)S(1)}, bf16[512,256]{1,0:T(8,128)(2,1)S(1)}, u32[]{:S(2)}, u32[]{:S(2)}) %collective-permute-start.2) | collective-permute-done | bytes 262176 | tf_op jit(solution)/shard_map/ppermute | solution.py:51
  13.5 1.1 %queries.1 = (bf16[512,256]{1,0:T(8,128)(2,1)S(1)}, bf16[144,256]{1,0:T(8,128)(2,1)S(1)}, bf16[528,256]{1,0:T(8,128)(2,1)S(1)}) custom-call(s32[8]{0:T(128)S(1)} %copy-done.7, bf16[512,256]{1,0:T(8,128)(2,1)S(1)} %copy-done.1, bf16[512,256]{1,0:T(8,128)(2,1)S(1)} %collective-permute-done.refs_2_.refs_1_.refs_6_, ...), custom_call_target="tpu_custom_call" | custom-call | flops 268435456 | bytes 524288 | tf_op jit(solution)/shard_map/queries/pallas_call | solution.py:32
  14.6 1.5 %collective-permute-start.4 = (bf16[528,256]{1,0:T(8,128)(2,1)S(1)}, bf16[528,256]{1,0:T(8,128)(2,1)S(1)}, u32[]{:S(2)}, u32[]{:S(2)}) collective-permute-start(bf16[528,256]{1,0:T(8,128)(2,1)S(1)} %get-tuple-element.48), channel_id=1, source_target_pairs={{0,4},{4,8},{8,12},{12,16},{16,20},{20,24},{24,28},{28,0},{1,5},{5... | collective-permute-start | bytes 811016 | tf_op jit(solution)/shard_map/ppermute | solution.py:46
  16.1 1.6 %collective-permute-start.10 = (bf16[144,256]{1,0:T(8,128)(2,1)S(1)}, bf16[144,256]{1,0:T(8,128)(2,1)S(1)}, u32[]{:S(2)}, u32[]{:S(2)}) collective-permute-start(bf16[144,256]{1,0:T(8,128)(2,1)S(1)} %get-tuple-element.42.refs_6_.refs_7_), channel_id=1, source_target_pairs={{0,8},{4,12},{8,16},{12,20},{16,24},{20,28},{24,0},{28,4},{1,9},{5... | collective-permute-start | bytes 221192 | tf_op jit(solution)/shard_map/ppermute | solution.py:46
  17.7 2.2 %collective-permute-start.9 = (bf16[144,256]{1,0:T(8,128)(2,1)S(1)}, bf16[144,256]{1,0:T(8,128)(2,1)S(1)}, u32[]{:S(2)}, u32[]{:S(2)}) collective-permute-start(bf16[144,256]{1,0:T(8,128)(2,1)S(1)} %get-tuple-element.42.refs_6_.refs_7_), channel_id=1, source_target_pairs={{0,24},{4,28},{8,0},{12,4},{16,8},{20,12},{24,16},{28,20},{1,25},{... | collective-permute-start | bytes 221192 | tf_op jit(solution)/shard_map/ppermute | solution.py:46
  20.0 1.4 %collective-permute-start.8 = (bf16[144,256]{1,0:T(8,128)(2,1)S(1)}, bf16[144,256]{1,0:T(8,128)(2,1)S(1)}, u32[]{:S(2)}, u32[]{:S(2)}) collective-permute-start(bf16[144,256]{1,0:T(8,128)(2,1)S(1)} %get-tuple-element.42.refs_6_.refs_7_), channel_id=1, source_target_pairs={{0,28},{4,0},{8,4},{12,8},{16,12},{20,16},{24,20},{28,24},{1,29},{... | collective-permute-start | bytes 221192 | tf_op jit(solution)/shard_map/ppermute | solution.py:46
  21.4 1.3 %collective-permute-done.10.refs_8_ = bf16[144,256]{1,0:T(8,128)(2,1)S(1)} collective-permute-done((bf16[144,256]{1,0:T(8,128)(2,1)S(1)}, bf16[144,256]{1,0:T(8,128)(2,1)S(1)}, u32[]{:S(2)}, u32[]{:S(2)}) %collective-permute-start.10) | collective-permute-done | bytes 73760 | tf_op jit(solution)/shard_map/ppermute | solution.py:46
  22.8 11.9 %collective-permute-start.6 = (bf16[144,256]{1,0:T(8,128)(2,1)S(1)}, bf16[144,256]{1,0:T(8,128)(2,1)S(1)}, u32[]{:S(2)}, u32[]{:S(2)}) collective-permute-start(bf16[144,256]{1,0:T(8,128)(2,1)S(1)} %get-tuple-element.42.refs_6_.refs_7_), channel_id=1, source_target_pairs={{0,20},{4,24},{8,28},{12,0},{16,4},{20,8},{24,12},{28,16},{1,21},{... | collective-permute-start | bytes 221192 | tf_op jit(solution)/shard_map/ppermute | solution.py:46
  34.6 1.9 %keys_values.1 = (bf16[512,256]{1,0:T(8,128)(2,1)S(1)}, bf16[512,256]{1,0:T(8,128)(2,1)S(1)}, bf16[512,2,256]{2,1,0:T(2,128)(2,1)}) custom-call(bf16[512,256]{1,0:T(8,128)(2,1)S(1)} %copy-done.1, bf16[512,256]{1,0:T(8,128)(2,1)S(1)} %collective-permute-done.refs_2_.refs_1_.refs_6_, bf16[512,256]{1,0:T(8,128)(2,1)S(1)} %collective-permute-done.1.refs_3_.refs_2_.refs_7_, ...), custom_call_target="tpu_custom_call" | custom-call | flops 536870912 | bytes 1048576 | tf_op jit(solution)/shard_map/keys_values/pallas_call | solution.py:32
  36.6 3.3 %collective-permute-done.5.refs_3_ = bf16[144,256]{1,0:T(8,128)(2,1)S(1)} collective-permute-done((bf16[144,256]{1,0:T(8,128)(2,1)S(1)}, bf16[144,256]{1,0:T(8,128)(2,1)S(1)}, u32[]{:S(2)}, u32[]{:S(2)}) %collective-permute-start.5) | collective-permute-done | bytes 73760 | tf_op jit(solution)/shard_map/ppermute | solution.py:46
  39.9 6.5 %visitors_early.1 = (bf16[560,256]{1,0:T(8,128)(2,1)S(1)}, bf16[144,256]{1,0:T(8,128)(2,1)S(1)}, bf16[144,256]{1,0:T(8,128)(2,1)S(1)}, bf16[144,256]{1,0:T(8,128...) custom-call(bf16[528,256]{1,0:T(8,128)(2,1)S(1)} %collective-permute-done.4.ref, ...), custom_call_target="tpu_custom_call" | custom-call | tf_op jit(solution)/shard_map/visitors_early/pallas_call | solution.py:32
  47.0 2.0 %collective-permute-start.12 = (bf16[144,256]{1,0:T(8,128)(2,1)S(1)}, bf16[144,256]{1,0:T(8,128)(2,1)S(1)}, u32[]{:S(2)}, u32[]{:S(2)}) collective-permute-start(bf16[144,256]{1,0:T(8,128)(2,1)S(1)} %get-tuple-element.50), channel_id=1, source_target_pairs={{0,4},{4,8},{8,12},{12,16},{16,20},{20,24},{24,28},{28,0},{1,5},{5... | collective-permute-start | bytes 221192 | tf_op jit(solution)/shard_map/ppermute | solution.py:46
  49.1 3.3 %collective-permute-start.14 = (bf16[144,256]{1,0:T(8,128)(2,1)S(1)}, bf16[144,256]{1,0:T(8,128)(2,1)S(1)}, u32[]{:S(2)}, u32[]{:S(2)}) collective-permute-start(bf16[144,256]{1,0:T(8,128)(2,1)S(1)} %get-tuple-element.52), channel_id=1, source_target_pairs={{0,20},{4,24},{8,28},{12,0},{16,4},{20,8},{24,12},{28,16},{1,21},{... | collective-permute-start | bytes 221192 | tf_op jit(solution)/shard_map/ppermute | solution.py:46
  52.3 1.9 %collective-permute-done.12.refs_4_ = bf16[144,256]{1,0:T(8,128)(2,1)S(1)} collective-permute-done((bf16[144,256]{1,0:T(8,128)(2,1)S(1)}, bf16[144,256]{1,0:T(8,128)(2,1)S(1)}, u32[]{:S(2)}, u32[]{:S(2)}) %collective-permute-start.12) | collective-permute-done | bytes 73760 | tf_op jit(solution)/shard_map/ppermute | solution.py:46
  54.2 1.6 %collective-permute-start.15 = (bf16[144,256]{1,0:T(8,128)(2,1)S(1)}, bf16[144,256]{1,0:T(8,128)(2,1)S(1)}, u32[]{:S(2)}, u32[]{:S(2)}) collective-permute-start(bf16[144,256]{1,0:T(8,128)(2,1)S(1)} %get-tuple-element.53), channel_id=1, source_target_pairs={{0,24},{4,28},{8,0},{12,4},{16,8},{20,12},{24,16},{28,20},{1,25},{... | collective-permute-start | bytes 221192 | tf_op jit(solution)/shard_map/ppermute | solution.py:46
  56.6 2.9 %collective-permute-start.17 = (bf16[144,256]{1,0:T(8,128)(2,1)S(1)}, bf16[144,256]{1,0:T(8,128)(2,1)S(1)}, u32[]{:S(2)}, u32[]{:S(2)}) collective-permute-start(bf16[144,256]{1,0:T(8,128)(2,1)S(1)} %get-tuple-element.55), channel_id=1, source_target_pairs={{0,16},{4,20},{8,24},{12,28},{16,0},{20,4},{24,8},{28,12},{1,17},{... | collective-permute-start | bytes 221192 | tf_op jit(solution)/shard_map/ppermute | solution.py:46
  59.5 2.7 %local_attention.1 = (f32[512,256]{1,0:T(8,128)S(1)}, f32[16,256]{1,0:T(8,128)S(1)}, bf16[144,256]{1,0:T(8,128)(2,1)}) custom-call(s32[8]{0:T(128)S(1)} %copy-done.7, bf16[512,256]{1,0:T(8,128)(2,1)S(1)} %get-tuple-element.40.refs_1_, bf16[512,256]{1,0:T(8,128)(2,1)S(1)} %get-tuple-element.43.refs_2_.refs_11_, ...), custom_call_target="tpu_custom_call" | custom-call | tf_op jit(solution)/shard_map/local_attention/pallas_call | solution.py:32
  62.2 1.3 %collective-permute-done.16.refs_8_ = bf16[144,256]{1,0:T(8,128)(2,1)S(1)} collective-permute-done((bf16[144,256]{1,0:T(8,128)(2,1)S(1)}, bf16[144,256]{1,0:T(8,128)(2,1)S(1)}, u32[]{:S(2)}, u32[]{:S(2)}) %collective-permute-start.16) | collective-permute-done | bytes 73760 | tf_op jit(solution)/shard_map/ppermute | solution.py:46
  63.5 1.9 %merge.1.refs_1_ = bf16[512,256]{1,0:T(8,128)(2,1)S(1)} custom-call(s32[8]{0:T(128)S(1)} %copy-done.7, f32[512,256]{1,0:T(8,128)S(1)} %get-tuple-element.46.refs_1_, f32[16,256]{1,0:T(8,128)S(1)} %get-tuple-element.47.refs_2_, bf16[560,256]{1,0:T(8,128)(2,1)S(1)} %collective-permute-done.11.refs_3_, bf16[144,256]{1,0:T(8,128)(2,1)S(1)} %collective-permute-done.12.refs_4_, ...), custom_call_target="tpu_custom_call" | custom-call | tf_op jit(solution)/shard_map/merge/pallas_call | solution.py:32
  66.5 5.3 %collective-permute-done.19.refs_3_ = bf16[512,256]{1,0:T(8,128)(2,1)S(1)} collective-permute-done((bf16[512,256]{1,0:T(8,128)(2,1)S(1)}, bf16[512,256]{1,0:T(8,128)(2,1)S(1)}, u32[]{:S(2)}, u32[]{:S(2)}) %collective-permute-start.19) | collective-permute-done | bytes 262176 | tf_op jit(solution)/shard_map/ppermute | solution.py:51
  71.8 1.5 %collective-permute-done.20.refs_4_ = bf16[512,256]{1,0:T(8,128)(2,1)S(1)} collective-permute-done((bf16[512,256]{1,0:T(8,128)(2,1)S(1)}, bf16[512,256]{1,0:T(8,128)(2,1)S(1)}, u32[]{:S(2)}, u32[]{:S(2)}) %collective-permute-start.20) | collective-permute-done | bytes 262176 | tf_op jit(solution)/shard_map/ppermute | solution.py:51
  73.4 3.7 %forward_short.1 = (bf16[384,256]{1,0:T(8,128)(2,1)S(1)}, bf16[384,256]{1,0:T(8,128)(2,1)S(1)}, bf16[384,256]{1,0:T(8,128)(2,1)S(1)}, bf16[384,256]{1,0:T(8,128)(2,1)S(1)}, bf16[384,256]{1,0:T(8,128)(2,1)S(1)}) custom-call(s32[8]{0:T(128)S(1)} %copy-done.7, bf16[512,256]{1,0:T(8,128)(2,1)S(1)} %merge.1.refs_1_, ...), custom_call_target="tpu_custom_call" | custom-call | flops 2415919104 | bytes 6291456 | tf_op jit(solution)/shard_map/forward_short/pallas_call | solution.py:32
  79.3 1.9 %forward_long.1 = (bf16[128,256]{1,0:T(8,128)(2,1)S(1)}, bf16[128,256]{1,0:T(8,128)(2,1)S(1)}, bf16[128,256]{1,0:T(8,128)(2,1)S(1)}, bf16[128,256]{1,0:T(8,128)(2,1)S(1)}, bf16[128,256]{1,0:T(8,128)(2,1)S(1)}) custom-call(s32[8]{0:T(128)S(1)} %copy-done.7, bf16[512,256]{1,0:T(8,128)(2,1)S(1)} %merge.1.refs_1_, ...), custom_call_target="tpu_custom_call" | custom-call | flops 805306368 | bytes 6291456 | tf_op jit(solution)/shard_map/forward_long/pallas_call | solution.py:32
  82.7 7.8 %collective-permute-done.23.refs_1_ = bf16[128,256]{1,0:T(8,128)(2,1)S(1)} collective-permute-done((bf16[128,256]{1,0:T(8,128)(2,1)S(1)}, bf16[128,256]{1,0:T(8,128)(2,1)S(1)}, u32[]{:S(2)}, u32[]{:S(2)}) %collective-permute-start.23) | collective-permute-done | bytes 65568 | tf_op jit(solution)/shard_map/ppermute | solution.py:51
  90.4 1.2 %collective-permute-done.25.refs_3_ = bf16[128,256]{1,0:T(8,128)(2,1)S(1)} collective-permute-done((bf16[128,256]{1,0:T(8,128)(2,1)S(1)}, bf16[128,256]{1,0:T(8,128)(2,1)S(1)}, u32[]{:S(2)}, u32[]{:S(2)}) %collective-permute-start.25) | collective-permute-done | bytes 65568 | tf_op jit(solution)/shard_map/ppermute | solution.py:51
  92.8 1.5 %collective-permute-start.29 = (f32[8,512]{1,0:T(8,128)S(1)}, f32[8,512]{1,0:T(8,128)S(1)}, u32[]{:S(2)}, u32[]{:S(2)}) collective-permute-start(f32[8,512]{1,0:T(8,128)S(1)} %get-tuple-element.70.refs_4_), channel_id=1, source_target_pairs={{0,2},{1,3},{2,0},{3,1},{4,6},{5,7},{6,4},{7,5},{8,10},{9,11},{10,... | collective-permute-start | bytes 49160 | tf_op jit(solution)/shard_map/ppermute | solution.py:51
  94.3 1.2 %collective-permute-done.30.refs_6_ = f32[8,512]{1,0:T(8,128)S(1)} collective-permute-done((f32[8,512]{1,0:T(8,128)S(1)}, f32[8,512]{1,0:T(8,128)S(1)}, u32[]{:S(2)}, u32[]{:S(2)}) %collective-permute-start.30) | collective-permute-done | bytes 16416 | tf_op jit(solution)/shard_map/ppermute | solution.py:51
  95.5 1.1 %collective-permute-done.29.refs_5_ = f32[8,512]{1,0:T(8,128)S(1)} collective-permute-done((f32[8,512]{1,0:T(8,128)S(1)}, f32[8,512]{1,0:T(8,128)S(1)}, u32[]{:S(2)}, u32[]{:S(2)}) %collective-permute-start.29) | collective-permute-done | bytes 16416 | tf_op jit(solution)/shard_map/ppermute | solution.py:51
  96.6 1.6 %finish.1 = bf16[512,256]{1,0:T(8,128)(2,1)} custom-call(s32[8]{0:T(128)S(1)} %copy-done.7, f32[1,1024]{1,0:T(1,128)S(1)} %bitcast.8, f32[128,256]{1,0:T(8,128)S(1)} %get-tuple-element.68.refs_2_, f32[384,256]{1,0:T(8,128)S(1)} %get-tuple-element.69.refs_3_, f32[8,512]{1,0:T(8,128)S(1)} %get-tuple-element.70.refs_4_, ...), custom_call_target="tpu_custom_call" | custom-call | tf_op jit(solution)/shard_map/finish/pallas_call | solution.py:32
  (66 shorter events, 10.0 us)
Async XLA Ops:
  0.6 11.3 %collective-permute-start.1 = (bf16[512,256]{1,0:T(8,128)(2,1)}, bf16[512,256]{1,0:T(8,128)(2,1)S(1)}, u32[]{:S(2)}, u32[]{:S(2)}) collective-permute-start(bf16[512,256]{1,0:T(8,128)(2,1)} %refs_5_.3), channel_id=1, source_target_pairs={{0,2},{1,3},{2,0},{3,1},{4,6},{5,7},{6,4},{7,5},{8,10},{9,11},{10,... | collective-permute-start | bytes 786440 | tf_op jit(solution)/shard_map/ppermute | solution.py:51
  3.7 8.3 %collective-permute-start.3 = (bf16[256,1024]{1,0:T(8,128)(2,1)}, bf16[256,1024]{1,0:T(8,128)(2,1)S(1)}, u32[]{:S(2)}, u32[]{:S(2)}) collective-permute-start(bf16[256,1024]{1,0:T(8,128)(2,1)} %refs_9_.5), channel_id=1, source_target_pairs={{0,1},{1,0},{2,3},{3,2},{4,5},{5,4},{6,7},{7,6},{8,9},{9,8},{10,11... | collective-permute-start | bytes 1572872 | tf_op jit(solution)/shard_map/ppermute | solution.py:51
  3.7 8.3 %collective-permute-start = (bf16[512,256]{1,0:T(8,128)(2,1)}, bf16[512,256]{1,0:T(8,128)(2,1)S(1)}, u32[]{:S(2)}, u32[]{:S(2)}) collective-permute-start(bf16[512,256]{1,0:T(8,128)(2,1)} %refs_5_.3), channel_id=1, source_target_pairs={{0,1},{1,0},{2,3},{3,2},{4,5},{5,4},{6,7},{7,6},{8,9},{9,8},{10,11... | collective-permute-start | bytes 786440 | tf_op jit(solution)/shard_map/ppermute | solution.py:51
  11.9 1.6 %collective-permute-start.2 = (bf16[512,256]{1,0:T(8,128)(2,1)S(1)}, bf16[512,256]{1,0:T(8,128)(2,1)S(1)}, u32[]{:S(2)}, u32[]{:S(2)}) collective-permute-start(bf16[512,256]{1,0:T(8,128)(2,1)S(1)} %collective-permute-done.1.refs_3_.refs_2_.refs_7_), channel_id=1, source_target_pairs={{0,1},{1,0},{2,3},{3,2},{4,5},{5,4},{6,7},{7,6},{8,9},{9,8},{10,11... | collective-permute-start | bytes 786440 | tf_op jit(solution)/shard_map/ppermute | solution.py:51
  14.6 25.3 %collective-permute-start.4 = (bf16[528,256]{1,0:T(8,128)(2,1)S(1)}, bf16[528,256]{1,0:T(8,128)(2,1)S(1)}, u32[]{:S(2)}, u32[]{:S(2)}) collective-permute-start(bf16[528,256]{1,0:T(8,128)(2,1)S(1)} %get-tuple-element.48), channel_id=1, source_target_pairs={{0,4},{4,8},{8,12},{12,16},{16,20},{20,24},{24,28},{28,0},{1,5},{5... | collective-permute-start | bytes 811016 | tf_op jit(solution)/shard_map/ppermute | solution.py:46
  16.1 6.6 %collective-permute-start.10 = (bf16[144,256]{1,0:T(8,128)(2,1)S(1)}, bf16[144,256]{1,0:T(8,128)(2,1)S(1)}, u32[]{:S(2)}, u32[]{:S(2)}) collective-permute-start(bf16[144,256]{1,0:T(8,128)(2,1)S(1)} %get-tuple-element.42.refs_6_.refs_7_), channel_id=1, source_target_pairs={{0,8},{4,12},{8,16},{12,20},{16,24},{20,28},{24,0},{28,4},{1,9},{5... | collective-permute-start | bytes 221192 | tf_op jit(solution)/shard_map/ppermute | solution.py:46
  17.7 16.9 %collective-permute-start.9 = (bf16[144,256]{1,0:T(8,128)(2,1)S(1)}, bf16[144,256]{1,0:T(8,128)(2,1)S(1)}, u32[]{:S(2)}, u32[]{:S(2)}) collective-permute-start(bf16[144,256]{1,0:T(8,128)(2,1)S(1)} %get-tuple-element.42.refs_6_.refs_7_), channel_id=1, source_target_pairs={{0,24},{4,28},{8,0},{12,4},{16,8},{20,12},{24,16},{28,20},{1,25},{... | collective-permute-start | bytes 221192 | tf_op jit(solution)/shard_map/ppermute | solution.py:46
  20.0 16.6 %collective-permute-start.8 = (bf16[144,256]{1,0:T(8,128)(2,1)S(1)}, bf16[144,256]{1,0:T(8,128)(2,1)S(1)}, u32[]{:S(2)}, u32[]{:S(2)}) collective-permute-start(bf16[144,256]{1,0:T(8,128)(2,1)S(1)} %get-tuple-element.42.refs_6_.refs_7_), channel_id=1, source_target_pairs={{0,28},{4,0},{8,4},{12,8},{16,12},{20,16},{24,20},{28,24},{1,29},{... | collective-permute-start | bytes 221192 | tf_op jit(solution)/shard_map/ppermute | solution.py:46
  21.4 15.1 %collective-permute-start.7 = (bf16[144,256]{1,0:T(8,128)(2,1)S(1)}, bf16[144,256]{1,0:T(8,128)(2,1)S(1)}, u32[]{:S(2)}, u32[]{:S(2)}) collective-permute-start(bf16[144,256]{1,0:T(8,128)(2,1)S(1)} %get-tuple-element.42.refs_6_.refs_7_), channel_id=1, source_target_pairs={{0,12},{4,16},{8,20},{12,24},{16,28},{20,0},{24,4},{28,8},{1,13},{... | collective-permute-start | bytes 221192 | tf_op jit(solution)/shard_map/ppermute | solution.py:46
  22.8 13.9 %collective-permute-start.6 = (bf16[144,256]{1,0:T(8,128)(2,1)S(1)}, bf16[144,256]{1,0:T(8,128)(2,1)S(1)}, u32[]{:S(2)}, u32[]{:S(2)}) collective-permute-start(bf16[144,256]{1,0:T(8,128)(2,1)S(1)} %get-tuple-element.42.refs_6_.refs_7_), channel_id=1, source_target_pairs={{0,20},{4,24},{8,28},{12,0},{16,4},{20,8},{24,12},{28,16},{1,21},{... | collective-permute-start | bytes 221192 | tf_op jit(solution)/shard_map/ppermute | solution.py:46
  34.6 5.3 %collective-permute-start.5 = (bf16[144,256]{1,0:T(8,128)(2,1)S(1)}, bf16[144,256]{1,0:T(8,128)(2,1)S(1)}, u32[]{:S(2)}, u32[]{:S(2)}) collective-permute-start(bf16[144,256]{1,0:T(8,128)(2,1)S(1)} %get-tuple-element.42.refs_6_.refs_7_), channel_id=1, source_target_pairs={{0,16},{4,20},{8,24},{12,28},{16,0},{20,4},{24,8},{28,12},{1,17},{... | collective-permute-start | bytes 221192 | tf_op jit(solution)/shard_map/ppermute | solution.py:46
  46.5 19.5 %collective-permute-start.21 = (bf16[256,1024]{1,0:T(8,128)(2,1)S(1)}, bf16[256,1024]{1,0:T(8,128)(2,1)S(1)}, u32[]{:S(2)}, u32[]{:S(2)}) collective-permute-start(bf16[256,1024]{1,0:T(8,128)(2,1)S(1)} %copy-done.4), channel_id=1, source_target_pairs={{0,2},{1,3},{2,0},{3,1},{4,6},{5,7},{6,4},{7,5},{8,10},{9,11},{10,... | collective-permute-start | bytes 1572872 | tf_op jit(solution)/shard_map/ppermute | solution.py:51
  47.0 16.5 %collective-permute-start.11 = (bf16[560,256]{1,0:T(8,128)(2,1)S(1)}, bf16[560,256]{1,0:T(8,128)(2,1)S(1)}, u32[]{:S(2)}, u32[]{:S(2)}) collective-permute-start(bf16[560,256]{1,0:T(8,128)(2,1)S(1)} %get-tuple-element.49), channel_id=1, source_target_pairs={{0,28},{4,0},{8,4},{12,8},{16,12},{20,16},{24,20},{28,24},{1,29},{... | collective-permute-start | bytes 860168 | tf_op jit(solution)/shard_map/ppermute | solution.py:46
  47.0 7.2 %collective-permute-start.12 = (bf16[144,256]{1,0:T(8,128)(2,1)S(1)}, bf16[144,256]{1,0:T(8,128)(2,1)S(1)}, u32[]{:S(2)}, u32[]{:S(2)}) collective-permute-start(bf16[144,256]{1,0:T(8,128)(2,1)S(1)} %get-tuple-element.50), channel_id=1, source_target_pairs={{0,4},{4,8},{8,12},{12,16},{16,20},{20,24},{24,28},{28,0},{1,5},{5... | collective-permute-start | bytes 221192 | tf_op jit(solution)/shard_map/ppermute | solution.py:46
  49.0 7.5 %collective-permute-start.13 = (bf16[144,256]{1,0:T(8,128)(2,1)S(1)}, bf16[144,256]{1,0:T(8,128)(2,1)S(1)}, u32[]{:S(2)}, u32[]{:S(2)}) collective-permute-start(bf16[144,256]{1,0:T(8,128)(2,1)S(1)} %get-tuple-element.51), channel_id=1, source_target_pairs={{0,8},{4,12},{8,16},{12,20},{16,24},{20,28},{24,0},{28,4},{1,9},{5... | collective-permute-start | bytes 221192 | tf_op jit(solution)/shard_map/ppermute | solution.py:46
  49.1 7.5 %collective-permute-start.14 = (bf16[144,256]{1,0:T(8,128)(2,1)S(1)}, bf16[144,256]{1,0:T(8,128)(2,1)S(1)}, u32[]{:S(2)}, u32[]{:S(2)}) collective-permute-start(bf16[144,256]{1,0:T(8,128)(2,1)S(1)} %get-tuple-element.52), channel_id=1, source_target_pairs={{0,20},{4,24},{8,28},{12,0},{16,4},{20,8},{24,12},{28,16},{1,21},{... | collective-permute-start | bytes 221192 | tf_op jit(solution)/shard_map/ppermute | solution.py:46
  54.2 7.9 %collective-permute-start.15 = (bf16[144,256]{1,0:T(8,128)(2,1)S(1)}, bf16[144,256]{1,0:T(8,128)(2,1)S(1)}, u32[]{:S(2)}, u32[]{:S(2)}) collective-permute-start(bf16[144,256]{1,0:T(8,128)(2,1)S(1)} %get-tuple-element.53), channel_id=1, source_target_pairs={{0,24},{4,28},{8,0},{12,4},{16,8},{20,12},{24,16},{28,20},{1,25},{... | collective-permute-start | bytes 221192 | tf_op jit(solution)/shard_map/ppermute | solution.py:46
  56.6 6.9 %collective-permute-start.16 = (bf16[144,256]{1,0:T(8,128)(2,1)S(1)}, bf16[144,256]{1,0:T(8,128)(2,1)S(1)}, u32[]{:S(2)}, u32[]{:S(2)}) collective-permute-start(bf16[144,256]{1,0:T(8,128)(2,1)S(1)} %get-tuple-element.54), channel_id=1, source_target_pairs={{0,12},{4,16},{8,20},{12,24},{16,28},{20,0},{24,4},{28,8},{1,13},{... | collective-permute-start | bytes 221192 | tf_op jit(solution)/shard_map/ppermute | solution.py:46
  56.6 6.9 %collective-permute-start.17 = (bf16[144,256]{1,0:T(8,128)(2,1)S(1)}, bf16[144,256]{1,0:T(8,128)(2,1)S(1)}, u32[]{:S(2)}, u32[]{:S(2)}) collective-permute-start(bf16[144,256]{1,0:T(8,128)(2,1)S(1)} %get-tuple-element.55), channel_id=1, source_target_pairs={{0,16},{4,20},{8,24},{12,28},{16,0},{20,4},{24,8},{28,12},{1,17},{... | collective-permute-start | bytes 221192 | tf_op jit(solution)/shard_map/ppermute | solution.py:46
  65.4 6.4 %collective-permute-start.19 = (bf16[512,256]{1,0:T(8,128)(2,1)S(1)}, bf16[512,256]{1,0:T(8,128)(2,1)S(1)}, u32[]{:S(2)}, u32[]{:S(2)}) collective-permute-start(bf16[512,256]{1,0:T(8,128)(2,1)S(1)} %merge.1.refs_1_), channel_id=1, source_target_pairs={{0,2},{1,3},{2,0},{3,1},{4,6},{5,7},{6,4},{7,5},{8,10},{9,11},{10,... | collective-permute-start | bytes 786440 | tf_op jit(solution)/shard_map/ppermute | solution.py:51
  66.0 7.4 %collective-permute-start.22 = (bf16[256,1024]{1,0:T(8,128)(2,1)S(1)}, bf16[256,1024]{1,0:T(8,128)(2,1)S(1)}, u32[]{:S(2)}, u32[]{:S(2)}) collective-permute-start(bf16[256,1024]{1,0:T(8,128)(2,1)S(1)} %collective-permute-done.21.refs_11_), channel_id=1, source_target_pairs={{0,1},{1,0},{2,3},{3,2},{4,5},{5,4},{6,7},{7,6},{8,9},{9,8},{10,11... | collective-permute-start | bytes 1572872 | tf_op jit(solution)/shard_map/ppermute | solution.py:51
  66.0 5.8 %collective-permute-start.18 = (bf16[512,256]{1,0:T(8,128)(2,1)S(1)}, bf16[512,256]{1,0:T(8,128)(2,1)S(1)}, u32[]{:S(2)}, u32[]{:S(2)}) collective-permute-start(bf16[512,256]{1,0:T(8,128)(2,1)S(1)} %merge.1.refs_1_), channel_id=1, source_target_pairs={{0,1},{1,0},{2,3},{3,2},{4,5},{5,4},{6,7},{7,6},{8,9},{9,8},{10,11... | collective-permute-start | bytes 786440 | tf_op jit(solution)/shard_map/ppermute | solution.py:51
  71.8 1.5 %collective-permute-start.20 = (bf16[512,256]{1,0:T(8,128)(2,1)S(1)}, bf16[512,256]{1,0:T(8,128)(2,1)S(1)}, u32[]{:S(2)}, u32[]{:S(2)}) collective-permute-start(bf16[512,256]{1,0:T(8,128)(2,1)S(1)} %collective-permute-done.19.refs_3_), channel_id=1, source_target_pairs={{0,1},{1,0},{2,3},{3,2},{4,5},{5,4},{6,7},{7,6},{8,9},{9,8},{10,11... | collective-permute-start | bytes 786440 | tf_op jit(solution)/shard_map/ppermute | solution.py:51
  77.1 14.6 %collective-permute-start.26 = (bf16[384,256]{1,0:T(8,128)(2,1)S(1)}, bf16[384,256]{1,0:T(8,128)(2,1)S(1)}, u32[]{:S(2)}, u32[]{:S(2)}) collective-permute-start(bf16[384,256]{1,0:T(8,128)(2,1)S(1)} %get-tuple-element.65), channel_id=1, source_target_pairs={{0,2},{1,3},{2,0},{3,1},{4,6},{5,7},{6,4},{7,5},{8,10},{9,11},{10,... | collective-permute-start | bytes 589832 | tf_op jit(solution)/shard_map/ppermute | solution.py:51
  77.7 14.0 %collective-permute-start.27 = (bf16[384,256]{1,0:T(8,128)(2,1)S(1)}, bf16[384,256]{1,0:T(8,128)(2,1)S(1)}, u32[]{:S(2)}, u32[]{:S(2)}) collective-permute-start(bf16[384,256]{1,0:T(8,128)(2,1)S(1)} %get-tuple-element.66), channel_id=1, source_target_pairs={{0,3},{1,2},{2,1},{3,0},{4,7},{5,6},{6,5},{7,4},{8,11},{9,10},{10,... | collective-permute-start | bytes 589832 | tf_op jit(solution)/shard_map/ppermute | solution.py:51
  78.6 13.0 %collective-permute-start.28 = (bf16[384,256]{1,0:T(8,128)(2,1)S(1)}, bf16[384,256]{1,0:T(8,128)(2,1)S(1)}, u32[]{:S(2)}, u32[]{:S(2)}) collective-permute-start(bf16[384,256]{1,0:T(8,128)(2,1)S(1)} %get-tuple-element.67), channel_id=1, source_target_pairs={{0,1},{1,0},{2,3},{3,2},{4,5},{5,4},{6,7},{7,6},{8,9},{9,8},{10,11... | collective-permute-start | bytes 589832 | tf_op jit(solution)/shard_map/ppermute | solution.py:51
  81.2 9.2 %collective-permute-start.23 = (bf16[128,256]{1,0:T(8,128)(2,1)S(1)}, bf16[128,256]{1,0:T(8,128)(2,1)S(1)}, u32[]{:S(2)}, u32[]{:S(2)}) collective-permute-start(bf16[128,256]{1,0:T(8,128)(2,1)S(1)} %get-tuple-element.60), channel_id=1, source_target_pairs={{0,2},{1,3},{2,0},{3,1},{4,6},{5,7},{6,4},{7,5},{8,10},{9,11},{10,... | collective-permute-start | bytes 196616 | tf_op jit(solution)/shard_map/ppermute | solution.py:51
  81.8 8.6 %collective-permute-start.24 = (bf16[128,256]{1,0:T(8,128)(2,1)S(1)}, bf16[128,256]{1,0:T(8,128)(2,1)S(1)}, u32[]{:S(2)}, u32[]{:S(2)}) collective-permute-start(bf16[128,256]{1,0:T(8,128)(2,1)S(1)} %get-tuple-element.61), channel_id=1, source_target_pairs={{0,3},{1,2},{2,1},{3,0},{4,7},{5,6},{6,5},{7,4},{8,11},{9,10},{10,... | collective-permute-start | bytes 196616 | tf_op jit(solution)/shard_map/ppermute | solution.py:51
  90.4 1.3 %collective-permute-start.25 = (bf16[128,256]{1,0:T(8,128)(2,1)S(1)}, bf16[128,256]{1,0:T(8,128)(2,1)S(1)}, u32[]{:S(2)}, u32[]{:S(2)}) collective-permute-start(bf16[128,256]{1,0:T(8,128)(2,1)S(1)} %get-tuple-element.62), channel_id=1, source_target_pairs={{0,1},{1,0},{2,3},{3,2},{4,5},{5,4},{6,7},{7,6},{8,9},{9,8},{10,11... | collective-permute-start | bytes 196616 | tf_op jit(solution)/shard_map/ppermute | solution.py:51
  92.1 2.2 %collective-permute-start.31 = (f32[8,512]{1,0:T(8,128)S(1)}, f32[8,512]{1,0:T(8,128)S(1)}, u32[]{:S(2)}, u32[]{:S(2)}) collective-permute-start(f32[8,512]{1,0:T(8,128)S(1)} %get-tuple-element.70.refs_4_), channel_id=1, source_target_pairs={{0,1},{1,0},{2,3},{3,2},{4,5},{5,4},{6,7},{7,6},{8,9},{9,8},{10,11... | collective-permute-start | bytes 49160 | tf_op jit(solution)/shard_map/ppermute | solution.py:51
  92.3 3.2 %collective-permute-start.30 = (f32[8,512]{1,0:T(8,128)S(1)}, f32[8,512]{1,0:T(8,128)S(1)}, u32[]{:S(2)}, u32[]{:S(2)}) collective-permute-start(f32[8,512]{1,0:T(8,128)S(1)} %get-tuple-element.70.refs_4_), channel_id=1, source_target_pairs={{0,3},{1,2},{2,1},{3,0},{4,7},{5,6},{6,5},{7,4},{8,11},{9,10},{10,... | collective-permute-start | bytes 49160 | tf_op jit(solution)/shard_map/ppermute | solution.py:51
  92.8 3.7 %collective-permute-start.29 = (f32[8,512]{1,0:T(8,128)S(1)}, f32[8,512]{1,0:T(8,128)S(1)}, u32[]{:S(2)}, u32[]{:S(2)}) collective-permute-start(f32[8,512]{1,0:T(8,128)S(1)} %get-tuple-element.70.refs_4_), channel_id=1, source_target_pairs={{0,2},{1,3},{2,0},{3,1},{4,6},{5,7},{6,4},{7,5},{8,10},{9,11},{10,... | collective-permute-start | bytes 49160 | tf_op jit(solution)/shard_map/ppermute | solution.py:51
  (11 other events, 106.8 us)

commit v7 on v6

--- a/solution.py
+++ b/solution.py
@@ -552,7 +552,7 @@
         return outs, [outs[0], *got, outs[4]]
 
     outs_short, parts_short = forward(long_count, requests - long_count, "forward_short", ())
-    outs_long, parts_long = forward(0, long_count, "forward_long", (outs_short[4],))
+    outs_long, parts_long = forward(0, long_count, "forward_long", (parts_short[3],))
 
     x_long, x_short, stats = call(
         gather_sum_kernel,

time: 99.8 us -> 99.1 us (level)
  waiting for transfers between devices: 28.3 us -> 27 us
    ppermute x18, waiting for transfers between devices: 19.6 us -> 18.4 us  [send_tp(): return lax.ppermute(value, 'tp', [(i, i ^ flip) for i in range(size)])]
  transfers between devices with their start and end apart: 32 -> 32, of which waited for: 13 -> 15; matrix products, arithmetic and copies ran while one was open for 1% -> 1% of each run, Pallas kernels for 14% -> 14%
where the time goes in v7:
time: 99.1 us; the launch traced here: 97.4 us
  starting transfers between devices  40.2 us (41%)
  Pallas kernels  27.3 us (28%)
  waiting for transfers between devices  27 us (27%)
  local copies, waits for them, and re-layouts  2.13 us (2%)
    ppermute x14, starting transfers between devices, send_req(): lax.ppermute(value, 'req', [(i, (i + by) % size) for i in range(size)])  28.5 us
    pallas_call x11, Pallas kernels, call(): pl.pallas_call(body, out_shape=outs, in_specs=list(ins) + [ANY] * len(aft...  27.3 us
    ppermute x18, waiting for transfers between devices, send_tp(): return lax.ppermute(value, 'tp', [(i, i ^ flip) for i in range(size)])  18.4 us
    ppermute x18, starting transfers between devices, send_tp(): return lax.ppermute(value, 'tp', [(i, i ^ flip) for i in range(size)])  11.6 us
    ppermute x14, waiting for transfers between devices, send_req(): lax.ppermute(value, 'req', [(i, (i + by) % size) for i in range(size)])  8.66 us
  transfers between devices with their start and end apart: 32, of which 15 were waited for; matrix products, arithmetic and copies ran while one was open for 1% of the time, Pallas kernels for 14%

profile of v7, /device:TPU:0, one launch (start us, length us, event | category | flops | bytes accessed | tf_op | source)
XLA Modules:
  0.0 97.4 jit_solution(7741865895113975411)
XLA Ops:
  0.6 3.0 %collective-permute-start.1 = (bf16[512,256]{1,0:T(8,128)(2,1)}, bf16[512,256]{1,0:T(8,128)(2,1)S(1)}, u32[]{:S(2)}, u32[]{:S(2)}) collective-permute-start(bf16[512,256]{1,0:T(8,128)(2,1)} %refs_5_.3), channel_id=1, source_target_pairs={{0,2},{1,3},{2,0},{3,1},{4,6},{5,7},{6,4},{7,5},{8,10},{9,11},{10,... | collective-permute-start | bytes 786440 | tf_op jit(solution)/shard_map/ppermute | solution.py:51
  5.6 2.3 %tree.1 = (f32[512,64]{1,0:T(8,128)S(1)}, bf16[2,512,512]{2,1,0:T(8,128)(2,1)S(1)}) custom-call(s32[8]{0:T(128)S(1)} %copy-done.10, s32[2,256]{1,0:T(2,128)S(1)} %reshape.17.refs_1_), custom_call_target="tpu_custom_call" | custom-call | flops 469762048 | tf_op jit(solution)/shard_map/tree/pallas_call | solution.py:32
  8.6 3.3 %pages.1 = (bf16[2,8,128,256]{3,2,1,0:T(8,128)(2,1)S(1)}, bf16[2,8,128,256]{3,2,1,0:T(8,128)(2,1)S(1)}) custom-call(s32[8,8]{1,0:T(8,128)S(1)} %copy-done.5, bf16[64,128,2,256]{3,2,1,0:T(2,128)(2,1)} %refs_10_.1), custom_call_target="tpu_custom_call" | custom-call | flops 536870912 | tf_op jit(solution)/shard_map/pages/pallas_call | solution.py:32
  12.0 1.5 %collective-permute-done.2.refs_4_.refs_3_.refs_8_ = bf16[512,256]{1,0:T(8,128)(2,1)S(1)} collective-permute-done((bf16[512,256]{1,0:T(8,128)(2,1)S(1)}, bf16[512,256]{1,0:T(8,128)(2,1)S(1)}, u32[]{:S(2)}, u32[]{:S(2)}) %collective-permute-start.2) | collective-permute-done | bytes 262176 | tf_op jit(solution)/shard_map/ppermute | solution.py:51
  14.6 1.5 %collective-permute-start.4 = (bf16[528,256]{1,0:T(8,128)(2,1)S(1)}, bf16[528,256]{1,0:T(8,128)(2,1)S(1)}, u32[]{:S(2)}, u32[]{:S(2)}) collective-permute-start(bf16[528,256]{1,0:T(8,128)(2,1)S(1)} %get-tuple-element.48), channel_id=1, source_target_pairs={{0,4},{4,8},{8,12},{12,16},{16,20},{20,24},{24,28},{28,0},{1,5},{5... | collective-permute-start | bytes 811016 | tf_op jit(solution)/shard_map/ppermute | solution.py:46
  16.1 1.6 %collective-permute-start.10 = (bf16[144,256]{1,0:T(8,128)(2,1)S(1)}, bf16[144,256]{1,0:T(8,128)(2,1)S(1)}, u32[]{:S(2)}, u32[]{:S(2)}) collective-permute-start(bf16[144,256]{1,0:T(8,128)(2,1)S(1)} %get-tuple-element.42.refs_6_.refs_7_), channel_id=1, source_target_pairs={{0,8},{4,12},{8,16},{12,20},{16,24},{20,28},{24,0},{28,4},{1,9},{5... | collective-permute-start | bytes 221192 | tf_op jit(solution)/shard_map/ppermute | solution.py:46
  17.7 2.2 %collective-permute-start.9 = (bf16[144,256]{1,0:T(8,128)(2,1)S(1)}, bf16[144,256]{1,0:T(8,128)(2,1)S(1)}, u32[]{:S(2)}, u32[]{:S(2)}) collective-permute-start(bf16[144,256]{1,0:T(8,128)(2,1)S(1)} %get-tuple-element.42.refs_6_.refs_7_), channel_id=1, source_target_pairs={{0,24},{4,28},{8,0},{12,4},{16,8},{20,12},{24,16},{28,20},{1,25},{... | collective-permute-start | bytes 221192 | tf_op jit(solution)/shard_map/ppermute | solution.py:46
  20.0 1.4 %collective-permute-start.8 = (bf16[144,256]{1,0:T(8,128)(2,1)S(1)}, bf16[144,256]{1,0:T(8,128)(2,1)S(1)}, u32[]{:S(2)}, u32[]{:S(2)}) collective-permute-start(bf16[144,256]{1,0:T(8,128)(2,1)S(1)} %get-tuple-element.42.refs_6_.refs_7_), channel_id=1, source_target_pairs={{0,28},{4,0},{8,4},{12,8},{16,12},{20,16},{24,20},{28,24},{1,29},{... | collective-permute-start | bytes 221192 | tf_op jit(solution)/shard_map/ppermute | solution.py:46
  21.4 1.4 %collective-permute-done.10.refs_8_ = bf16[144,256]{1,0:T(8,128)(2,1)S(1)} collective-permute-done((bf16[144,256]{1,0:T(8,128)(2,1)S(1)}, bf16[144,256]{1,0:T(8,128)(2,1)S(1)}, u32[]{:S(2)}, u32[]{:S(2)}) %collective-permute-start.10) | collective-permute-done | bytes 73760 | tf_op jit(solution)/shard_map/ppermute | solution.py:46
  22.8 11.9 %collective-permute-start.6 = (bf16[144,256]{1,0:T(8,128)(2,1)S(1)}, bf16[144,256]{1,0:T(8,128)(2,1)S(1)}, u32[]{:S(2)}, u32[]{:S(2)}) collective-permute-start(bf16[144,256]{1,0:T(8,128)(2,1)S(1)} %get-tuple-element.42.refs_6_.refs_7_), channel_id=1, source_target_pairs={{0,20},{4,24},{8,28},{12,0},{16,4},{20,8},{24,12},{28,16},{1,21},{... | collective-permute-start | bytes 221192 | tf_op jit(solution)/shard_map/ppermute | solution.py:46
  34.6 1.9 %keys_values.1 = (bf16[512,256]{1,0:T(8,128)(2,1)S(1)}, bf16[512,256]{1,0:T(8,128)(2,1)S(1)}, bf16[512,2,256]{2,1,0:T(2,128)(2,1)}) custom-call(bf16[512,256]{1,0:T(8,128)(2,1)S(1)} %copy-done.1, bf16[512,256]{1,0:T(8,128)(2,1)S(1)} %collective-permute-done.refs_2_.refs_1_.refs_6_, bf16[512,256]{1,0:T(8,128)(2,1)S(1)} %collective-permute-done.1.refs_3_.refs_2_.refs_7_, ...), custom_call_target="tpu_custom_call" | custom-call | flops 536870912 | bytes 1048576 | tf_op jit(solution)/shard_map/keys_values/pallas_call | solution.py:32
  36.6 3.3 %collective-permute-done.5.refs_3_ = bf16[144,256]{1,0:T(8,128)(2,1)S(1)} collective-permute-done((bf16[144,256]{1,0:T(8,128)(2,1)S(1)}, bf16[144,256]{1,0:T(8,128)(2,1)S(1)}, u32[]{:S(2)}, u32[]{:S(2)}) %collective-permute-start.5) | collective-permute-done | bytes 73760 | tf_op jit(solution)/shard_map/ppermute | solution.py:46
  39.9 6.5 %visitors_early.1 = (bf16[560,256]{1,0:T(8,128)(2,1)S(1)}, bf16[144,256]{1,0:T(8,128)(2,1)S(1)}, bf16[144,256]{1,0:T(8,128)(2,1)S(1)}, bf16[144,256]{1,0:T(8,128...) custom-call(bf16[528,256]{1,0:T(8,128)(2,1)S(1)} %collective-permute-done.4.ref, ...), custom_call_target="tpu_custom_call" | custom-call | tf_op jit(solution)/shard_map/visitors_early/pallas_call | solution.py:32
  47.0 2.0 %collective-permute-start.12 = (bf16[144,256]{1,0:T(8,128)(2,1)S(1)}, bf16[144,256]{1,0:T(8,128)(2,1)S(1)}, u32[]{:S(2)}, u32[]{:S(2)}) collective-permute-start(bf16[144,256]{1,0:T(8,128)(2,1)S(1)} %get-tuple-element.50), channel_id=1, source_target_pairs={{0,4},{4,8},{8,12},{12,16},{16,20},{20,24},{24,28},{28,0},{1,5},{5... | collective-permute-start | bytes 221192 | tf_op jit(solution)/shard_map/ppermute | solution.py:46
  49.1 3.3 %collective-permute-start.14 = (bf16[144,256]{1,0:T(8,128)(2,1)S(1)}, bf16[144,256]{1,0:T(8,128)(2,1)S(1)}, u32[]{:S(2)}, u32[]{:S(2)}) collective-permute-start(bf16[144,256]{1,0:T(8,128)(2,1)S(1)} %get-tuple-element.52), channel_id=1, source_target_pairs={{0,20},{4,24},{8,28},{12,0},{16,4},{20,8},{24,12},{28,16},{1,21},{... | collective-permute-start | bytes 221192 | tf_op jit(solution)/shard_map/ppermute | solution.py:46
  52.3 1.9 %collective-permute-done.12.refs_4_ = bf16[144,256]{1,0:T(8,128)(2,1)S(1)} collective-permute-done((bf16[144,256]{1,0:T(8,128)(2,1)S(1)}, bf16[144,256]{1,0:T(8,128)(2,1)S(1)}, u32[]{:S(2)}, u32[]{:S(2)}) %collective-permute-start.12) | collective-permute-done | bytes 73760 | tf_op jit(solution)/shard_map/ppermute | solution.py:46
  54.2 1.6 %collective-permute-start.15 = (bf16[144,256]{1,0:T(8,128)(2,1)S(1)}, bf16[144,256]{1,0:T(8,128)(2,1)S(1)}, u32[]{:S(2)}, u32[]{:S(2)}) collective-permute-start(bf16[144,256]{1,0:T(8,128)(2,1)S(1)} %get-tuple-element.53), channel_id=1, source_target_pairs={{0,24},{4,28},{8,0},{12,4},{16,8},{20,12},{24,16},{28,20},{1,25},{... | collective-permute-start | bytes 221192 | tf_op jit(solution)/shard_map/ppermute | solution.py:46
  56.6 2.9 %collective-permute-start.17 = (bf16[144,256]{1,0:T(8,128)(2,1)S(1)}, bf16[144,256]{1,0:T(8,128)(2,1)S(1)}, u32[]{:S(2)}, u32[]{:S(2)}) collective-permute-start(bf16[144,256]{1,0:T(8,128)(2,1)S(1)} %get-tuple-element.55), channel_id=1, source_target_pairs={{0,16},{4,20},{8,24},{12,28},{16,0},{20,4},{24,8},{28,12},{1,17},{... | collective-permute-start | bytes 221192 | tf_op jit(solution)/shard_map/ppermute | solution.py:46
  59.5 2.7 %local_attention.1 = (f32[512,256]{1,0:T(8,128)S(1)}, f32[16,256]{1,0:T(8,128)S(1)}, bf16[144,256]{1,0:T(8,128)(2,1)}) custom-call(s32[8]{0:T(128)S(1)} %copy-done.7, bf16[512,256]{1,0:T(8,128)(2,1)S(1)} %get-tuple-element.40.refs_1_, bf16[512,256]{1,0:T(8,128)(2,1)S(1)} %get-tuple-element.43.refs_2_.refs_11_, ...), custom_call_target="tpu_custom_call" | custom-call | tf_op jit(solution)/shard_map/local_attention/pallas_call | solution.py:32
  62.2 1.3 %collective-permute-done.16.refs_8_ = bf16[144,256]{1,0:T(8,128)(2,1)S(1)} collective-permute-done((bf16[144,256]{1,0:T(8,128)(2,1)S(1)}, bf16[144,256]{1,0:T(8,128)(2,1)S(1)}, u32[]{:S(2)}, u32[]{:S(2)}) %collective-permute-start.16) | collective-permute-done | bytes 73760 | tf_op jit(solution)/shard_map/ppermute | solution.py:46
  63.5 1.9 %merge.1.refs_1_ = bf16[512,256]{1,0:T(8,128)(2,1)S(1)} custom-call(s32[8]{0:T(128)S(1)} %copy-done.7, f32[512,256]{1,0:T(8,128)S(1)} %get-tuple-element.46.refs_1_, f32[16,256]{1,0:T(8,128)S(1)} %get-tuple-element.47.refs_2_, bf16[560,256]{1,0:T(8,128)(2,1)S(1)} %collective-permute-done.11.refs_3_, bf16[144,256]{1,0:T(8,128)(2,1)S(1)} %collective-permute-done.12.refs_4_, ...), custom_call_target="tpu_custom_call" | custom-call | tf_op jit(solution)/shard_map/merge/pallas_call | solution.py:32
  66.5 5.3 %collective-permute-done.19.refs_3_ = bf16[512,256]{1,0:T(8,128)(2,1)S(1)} collective-permute-done((bf16[512,256]{1,0:T(8,128)(2,1)S(1)}, bf16[512,256]{1,0:T(8,128)(2,1)S(1)}, u32[]{:S(2)}, u32[]{:S(2)}) %collective-permute-start.19) | collective-permute-done | bytes 262176 | tf_op jit(solution)/shard_map/ppermute | solution.py:51
  71.8 1.5 %collective-permute-done.20.refs_4_ = bf16[512,256]{1,0:T(8,128)(2,1)S(1)} collective-permute-done((bf16[512,256]{1,0:T(8,128)(2,1)S(1)}, bf16[512,256]{1,0:T(8,128)(2,1)S(1)}, u32[]{:S(2)}, u32[]{:S(2)}) %collective-permute-start.20) | collective-permute-done | bytes 262176 | tf_op jit(solution)/shard_map/ppermute | solution.py:51
  73.4 3.7 %forward_short.1 = (bf16[384,256]{1,0:T(8,128)(2,1)S(1)}, bf16[384,256]{1,0:T(8,128)(2,1)S(1)}, bf16[384,256]{1,0:T(8,128)(2,1)S(1)}, bf16[384,256]{1,0:T(8,128)(2,1)S(1)}, bf16[384,256]{1,0:T(8,128)(2,1)S(1)}) custom-call(s32[8]{0:T(128)S(1)} %copy-done.7, bf16[512,256]{1,0:T(8,128)(2,1)S(1)} %merge.1.refs_1_, ...), custom_call_target="tpu_custom_call" | custom-call | flops 2415919104 | bytes 6291456 | tf_op jit(solution)/shard_map/forward_short/pallas_call | solution.py:32
  79.0 2.0 %forward_long.1 = (bf16[128,256]{1,0:T(8,128)(2,1)S(1)}, bf16[128,256]{1,0:T(8,128)(2,1)S(1)}, bf16[128,256]{1,0:T(8,128)(2,1)S(1)}, bf16[128,256]{1,0:T(8,128)(2,1)S(1)}, bf16[128,256]{1,0:T(8,128)(2,1)S(1)}) custom-call(s32[8]{0:T(128)S(1)} %copy-done.7, bf16[512,256]{1,0:T(8,128)(2,1)S(1)} %merge.1.refs_1_, ...), custom_call_target="tpu_custom_call" | custom-call | flops 805306368 | bytes 6291456 | tf_op jit(solution)/shard_map/forward_long/pallas_call | solution.py:32
  81.6 1.3 %collective-permute-start.25 = (bf16[128,256]{1,0:T(8,128)(2,1)S(1)}, bf16[128,256]{1,0:T(8,128)(2,1)S(1)}, u32[]{:S(2)}, u32[]{:S(2)}) collective-permute-start(bf16[128,256]{1,0:T(8,128)(2,1)S(1)} %get-tuple-element.61), channel_id=1, source_target_pairs={{0,3},{1,2},{2,1},{3,0},{4,7},{5,6},{6,5},{7,4},{8,11},{9,10},{10,... | collective-permute-start | bytes 196616 | tf_op jit(solution)/shard_map/ppermute | solution.py:51
  83.2 1.8 %collective-permute-done.27.refs_6_ = bf16[384,256]{1,0:T(8,128)(2,1)S(1)} collective-permute-done((bf16[384,256]{1,0:T(8,128)(2,1)S(1)}, bf16[384,256]{1,0:T(8,128)(2,1)S(1)}, u32[]{:S(2)}, u32[]{:S(2)}) %collective-permute-start.27) | collective-permute-done | bytes 196640 | tf_op jit(solution)/shard_map/ppermute | solution.py:51
  85.0 3.1 %collective-permute-done.28.refs_7_ = bf16[384,256]{1,0:T(8,128)(2,1)S(1)} collective-permute-done((bf16[384,256]{1,0:T(8,128)(2,1)S(1)}, bf16[384,256]{1,0:T(8,128)(2,1)S(1)}, u32[]{:S(2)}, u32[]{:S(2)}) %collective-permute-start.28) | collective-permute-done | bytes 196640 | tf_op jit(solution)/shard_map/ppermute | solution.py:51
  88.1 2.5 %collective-permute-done.24.refs_1_ = bf16[128,256]{1,0:T(8,128)(2,1)S(1)} collective-permute-done((bf16[128,256]{1,0:T(8,128)(2,1)S(1)}, bf16[128,256]{1,0:T(8,128)(2,1)S(1)}, u32[]{:S(2)}, u32[]{:S(2)}) %collective-permute-start.24) | collective-permute-done | bytes 65568 | tf_op jit(solution)/shard_map/ppermute | solution.py:51
  92.1 1.5 %collective-permute-start.29 = (f32[8,512]{1,0:T(8,128)S(1)}, f32[8,512]{1,0:T(8,128)S(1)}, u32[]{:S(2)}, u32[]{:S(2)}) collective-permute-start(f32[8,512]{1,0:T(8,128)S(1)} %get-tuple-element.70.refs_4_), channel_id=1, source_target_pairs={{0,2},{1,3},{2,0},{3,1},{4,6},{5,7},{6,4},{7,5},{8,10},{9,11},{10,... | collective-permute-start | bytes 49160 | tf_op jit(solution)/shard_map/ppermute | solution.py:51
  93.6 1.4 %collective-permute-done.30.refs_6_ = f32[8,512]{1,0:T(8,128)S(1)} collective-permute-done((f32[8,512]{1,0:T(8,128)S(1)}, f32[8,512]{1,0:T(8,128)S(1)}, u32[]{:S(2)}, u32[]{:S(2)}) %collective-permute-start.30) | collective-permute-done | bytes 16416 | tf_op jit(solution)/shard_map/ppermute | solution.py:51
  95.8 1.6 %finish.1 = bf16[512,256]{1,0:T(8,128)(2,1)} custom-call(s32[8]{0:T(128)S(1)} %copy-done.7, f32[1,1024]{1,0:T(1,128)S(1)} %bitcast.8, f32[128,256]{1,0:T(8,128)S(1)} %get-tuple-element.68.refs_2_, f32[384,256]{1,0:T(8,128)S(1)} %get-tuple-element.69.refs_3_, f32[8,512]{1,0:T(8,128)S(1)} %get-tuple-element.70.refs_4_, ...), custom_call_target="tpu_custom_call" | custom-call | tf_op jit(solution)/shard_map/finish/pallas_call | solution.py:32
  (66 shorter events, 11.4 us)
Async XLA Ops:
  0.6 11.3 %collective-permute-start.1 = (bf16[512,256]{1,0:T(8,128)(2,1)}, bf16[512,256]{1,0:T(8,128)(2,1)S(1)}, u32[]{:S(2)}, u32[]{:S(2)}) collective-permute-start(bf16[512,256]{1,0:T(8,128)(2,1)} %refs_5_.3), channel_id=1, source_target_pairs={{0,2},{1,3},{2,0},{3,1},{4,6},{5,7},{6,4},{7,5},{8,10},{9,11},{10,... | collective-permute-start | bytes 786440 | tf_op jit(solution)/shard_map/ppermute | solution.py:51
  3.7 8.3 %collective-permute-start.3 = (bf16[256,1024]{1,0:T(8,128)(2,1)}, bf16[256,1024]{1,0:T(8,128)(2,1)S(1)}, u32[]{:S(2)}, u32[]{:S(2)}) collective-permute-start(bf16[256,1024]{1,0:T(8,128)(2,1)} %refs_9_.5), channel_id=1, source_target_pairs={{0,1},{1,0},{2,3},{3,2},{4,5},{5,4},{6,7},{7,6},{8,9},{9,8},{10,11... | collective-permute-start | bytes 1572872 | tf_op jit(solution)/shard_map/ppermute | solution.py:51
  3.7 8.3 %collective-permute-start = (bf16[512,256]{1,0:T(8,128)(2,1)}, bf16[512,256]{1,0:T(8,128)(2,1)S(1)}, u32[]{:S(2)}, u32[]{:S(2)}) collective-permute-start(bf16[512,256]{1,0:T(8,128)(2,1)} %refs_5_.3), channel_id=1, source_target_pairs={{0,1},{1,0},{2,3},{3,2},{4,5},{5,4},{6,7},{7,6},{8,9},{9,8},{10,11... | collective-permute-start | bytes 786440 | tf_op jit(solution)/shard_map/ppermute | solution.py:51
  11.9 1.6 %collective-permute-start.2 = (bf16[512,256]{1,0:T(8,128)(2,1)S(1)}, bf16[512,256]{1,0:T(8,128)(2,1)S(1)}, u32[]{:S(2)}, u32[]{:S(2)}) collective-permute-start(bf16[512,256]{1,0:T(8,128)(2,1)S(1)} %collective-permute-done.1.refs_3_.refs_2_.refs_7_), channel_id=1, source_target_pairs={{0,1},{1,0},{2,3},{3,2},{4,5},{5,4},{6,7},{7,6},{8,9},{9,8},{10,11... | collective-permute-start | bytes 786440 | tf_op jit(solution)/shard_map/ppermute | solution.py:51
  14.6 25.3 %collective-permute-start.4 = (bf16[528,256]{1,0:T(8,128)(2,1)S(1)}, bf16[528,256]{1,0:T(8,128)(2,1)S(1)}, u32[]{:S(2)}, u32[]{:S(2)}) collective-permute-start(bf16[528,256]{1,0:T(8,128)(2,1)S(1)} %get-tuple-element.48), channel_id=1, source_target_pairs={{0,4},{4,8},{8,12},{12,16},{16,20},{20,24},{24,28},{28,0},{1,5},{5... | collective-permute-start | bytes 811016 | tf_op jit(solution)/shard_map/ppermute | solution.py:46
  16.1 6.6 %collective-permute-start.10 = (bf16[144,256]{1,0:T(8,128)(2,1)S(1)}, bf16[144,256]{1,0:T(8,128)(2,1)S(1)}, u32[]{:S(2)}, u32[]{:S(2)}) collective-permute-start(bf16[144,256]{1,0:T(8,128)(2,1)S(1)} %get-tuple-element.42.refs_6_.refs_7_), channel_id=1, source_target_pairs={{0,8},{4,12},{8,16},{12,20},{16,24},{20,28},{24,0},{28,4},{1,9},{5... | collective-permute-start | bytes 221192 | tf_op jit(solution)/shard_map/ppermute | solution.py:46
  17.7 16.9 %collective-permute-start.9 = (bf16[144,256]{1,0:T(8,128)(2,1)S(1)}, bf16[144,256]{1,0:T(8,128)(2,1)S(1)}, u32[]{:S(2)}, u32[]{:S(2)}) collective-permute-start(bf16[144,256]{1,0:T(8,128)(2,1)S(1)} %get-tuple-element.42.refs_6_.refs_7_), channel_id=1, source_target_pairs={{0,24},{4,28},{8,0},{12,4},{16,8},{20,12},{24,16},{28,20},{1,25},{... | collective-permute-start | bytes 221192 | tf_op jit(solution)/shard_map/ppermute | solution.py:46
  20.0 16.6 %collective-permute-start.8 = (bf16[144,256]{1,0:T(8,128)(2,1)S(1)}, bf16[144,256]{1,0:T(8,128)(2,1)S(1)}, u32[]{:S(2)}, u32[]{:S(2)}) collective-permute-start(bf16[144,256]{1,0:T(8,128)(2,1)S(1)} %get-tuple-element.42.refs_6_.refs_7_), channel_id=1, source_target_pairs={{0,28},{4,0},{8,4},{12,8},{16,12},{20,16},{24,20},{28,24},{1,29},{... | collective-permute-start | bytes 221192 | tf_op jit(solution)/shard_map/ppermute | solution.py:46
  21.4 15.1 %collective-permute-start.7 = (bf16[144,256]{1,0:T(8,128)(2,1)S(1)}, bf16[144,256]{1,0:T(8,128)(2,1)S(1)}, u32[]{:S(2)}, u32[]{:S(2)}) collective-permute-start(bf16[144,256]{1,0:T(8,128)(2,1)S(1)} %get-tuple-element.42.refs_6_.refs_7_), channel_id=1, source_target_pairs={{0,12},{4,16},{8,20},{12,24},{16,28},{20,0},{24,4},{28,8},{1,13},{... | collective-permute-start | bytes 221192 | tf_op jit(solution)/shard_map/ppermute | solution.py:46
  22.8 13.8 %collective-permute-start.6 = (bf16[144,256]{1,0:T(8,128)(2,1)S(1)}, bf16[144,256]{1,0:T(8,128)(2,1)S(1)}, u32[]{:S(2)}, u32[]{:S(2)}) collective-permute-start(bf16[144,256]{1,0:T(8,128)(2,1)S(1)} %get-tuple-element.42.refs_6_.refs_7_), channel_id=1, source_target_pairs={{0,20},{4,24},{8,28},{12,0},{16,4},{20,8},{24,12},{28,16},{1,21},{... | collective-permute-start | bytes 221192 | tf_op jit(solution)/shard_map/ppermute | solution.py:46
  34.6 5.3 %collective-permute-start.5 = (bf16[144,256]{1,0:T(8,128)(2,1)S(1)}, bf16[144,256]{1,0:T(8,128)(2,1)S(1)}, u32[]{:S(2)}, u32[]{:S(2)}) collective-permute-start(bf16[144,256]{1,0:T(8,128)(2,1)S(1)} %get-tuple-element.42.refs_6_.refs_7_), channel_id=1, source_target_pairs={{0,16},{4,20},{8,24},{12,28},{16,0},{20,4},{24,8},{28,12},{1,17},{... | collective-permute-start | bytes 221192 | tf_op jit(solution)/shard_map/ppermute | solution.py:46
  46.5 19.5 %collective-permute-start.21 = (bf16[256,1024]{1,0:T(8,128)(2,1)S(1)}, bf16[256,1024]{1,0:T(8,128)(2,1)S(1)}, u32[]{:S(2)}, u32[]{:S(2)}) collective-permute-start(bf16[256,1024]{1,0:T(8,128)(2,1)S(1)} %copy-done.4), channel_id=1, source_target_pairs={{0,2},{1,3},{2,0},{3,1},{4,6},{5,7},{6,4},{7,5},{8,10},{9,11},{10,... | collective-permute-start | bytes 1572872 | tf_op jit(solution)/shard_map/ppermute | solution.py:51
  47.0 16.5 %collective-permute-start.11 = (bf16[560,256]{1,0:T(8,128)(2,1)S(1)}, bf16[560,256]{1,0:T(8,128)(2,1)S(1)}, u32[]{:S(2)}, u32[]{:S(2)}) collective-permute-start(bf16[560,256]{1,0:T(8,128)(2,1)S(1)} %get-tuple-element.49), channel_id=1, source_target_pairs={{0,28},{4,0},{8,4},{12,8},{16,12},{20,16},{24,20},{28,24},{1,29},{... | collective-permute-start | bytes 860168 | tf_op jit(solution)/shard_map/ppermute | solution.py:46
  47.0 7.2 %collective-permute-start.12 = (bf16[144,256]{1,0:T(8,128)(2,1)S(1)}, bf16[144,256]{1,0:T(8,128)(2,1)S(1)}, u32[]{:S(2)}, u32[]{:S(2)}) collective-permute-start(bf16[144,256]{1,0:T(8,128)(2,1)S(1)} %get-tuple-element.50), channel_id=1, source_target_pairs={{0,4},{4,8},{8,12},{12,16},{16,20},{20,24},{24,28},{28,0},{1,5},{5... | collective-permute-start | bytes 221192 | tf_op jit(solution)/shard_map/ppermute | solution.py:46
  49.0 7.5 %collective-permute-start.13 = (bf16[144,256]{1,0:T(8,128)(2,1)S(1)}, bf16[144,256]{1,0:T(8,128)(2,1)S(1)}, u32[]{:S(2)}, u32[]{:S(2)}) collective-permute-start(bf16[144,256]{1,0:T(8,128)(2,1)S(1)} %get-tuple-element.51), channel_id=1, source_target_pairs={{0,8},{4,12},{8,16},{12,20},{16,24},{20,28},{24,0},{28,4},{1,9},{5... | collective-permute-start | bytes 221192 | tf_op jit(solution)/shard_map/ppermute | solution.py:46
  49.1 7.5 %collective-permute-start.14 = (bf16[144,256]{1,0:T(8,128)(2,1)S(1)}, bf16[144,256]{1,0:T(8,128)(2,1)S(1)}, u32[]{:S(2)}, u32[]{:S(2)}) collective-permute-start(bf16[144,256]{1,0:T(8,128)(2,1)S(1)} %get-tuple-element.52), channel_id=1, source_target_pairs={{0,20},{4,24},{8,28},{12,0},{16,4},{20,8},{24,12},{28,16},{1,21},{... | collective-permute-start | bytes 221192 | tf_op jit(solution)/shard_map/ppermute | solution.py:46
  54.2 7.9 %collective-permute-start.15 = (bf16[144,256]{1,0:T(8,128)(2,1)S(1)}, bf16[144,256]{1,0:T(8,128)(2,1)S(1)}, u32[]{:S(2)}, u32[]{:S(2)}) collective-permute-start(bf16[144,256]{1,0:T(8,128)(2,1)S(1)} %get-tuple-element.53), channel_id=1, source_target_pairs={{0,24},{4,28},{8,0},{12,4},{16,8},{20,12},{24,16},{28,20},{1,25},{... | collective-permute-start | bytes 221192 | tf_op jit(solution)/shard_map/ppermute | solution.py:46
  56.6 6.9 %collective-permute-start.16 = (bf16[144,256]{1,0:T(8,128)(2,1)S(1)}, bf16[144,256]{1,0:T(8,128)(2,1)S(1)}, u32[]{:S(2)}, u32[]{:S(2)}) collective-permute-start(bf16[144,256]{1,0:T(8,128)(2,1)S(1)} %get-tuple-element.54), channel_id=1, source_target_pairs={{0,12},{4,16},{8,20},{12,24},{16,28},{20,0},{24,4},{28,8},{1,13},{... | collective-permute-start | bytes 221192 | tf_op jit(solution)/shard_map/ppermute | solution.py:46
  56.6 6.9 %collective-permute-start.17 = (bf16[144,256]{1,0:T(8,128)(2,1)S(1)}, bf16[144,256]{1,0:T(8,128)(2,1)S(1)}, u32[]{:S(2)}, u32[]{:S(2)}) collective-permute-start(bf16[144,256]{1,0:T(8,128)(2,1)S(1)} %get-tuple-element.55), channel_id=1, source_target_pairs={{0,16},{4,20},{8,24},{12,28},{16,0},{20,4},{24,8},{28,12},{1,17},{... | collective-permute-start | bytes 221192 | tf_op jit(solution)/shard_map/ppermute | solution.py:46
  65.4 6.4 %collective-permute-start.19 = (bf16[512,256]{1,0:T(8,128)(2,1)S(1)}, bf16[512,256]{1,0:T(8,128)(2,1)S(1)}, u32[]{:S(2)}, u32[]{:S(2)}) collective-permute-start(bf16[512,256]{1,0:T(8,128)(2,1)S(1)} %merge.1.refs_1_), channel_id=1, source_target_pairs={{0,2},{1,3},{2,0},{3,1},{4,6},{5,7},{6,4},{7,5},{8,10},{9,11},{10,... | collective-permute-start | bytes 786440 | tf_op jit(solution)/shard_map/ppermute | solution.py:51
  66.0 7.4 %collective-permute-start.22 = (bf16[256,1024]{1,0:T(8,128)(2,1)S(1)}, bf16[256,1024]{1,0:T(8,128)(2,1)S(1)}, u32[]{:S(2)}, u32[]{:S(2)}) collective-permute-start(bf16[256,1024]{1,0:T(8,128)(2,1)S(1)} %collective-permute-done.21.refs_11_), channel_id=1, source_target_pairs={{0,1},{1,0},{2,3},{3,2},{4,5},{5,4},{6,7},{7,6},{8,9},{9,8},{10,11... | collective-permute-start | bytes 1572872 | tf_op jit(solution)/shard_map/ppermute | solution.py:51
  66.0 5.8 %collective-permute-start.18 = (bf16[512,256]{1,0:T(8,128)(2,1)S(1)}, bf16[512,256]{1,0:T(8,128)(2,1)S(1)}, u32[]{:S(2)}, u32[]{:S(2)}) collective-permute-start(bf16[512,256]{1,0:T(8,128)(2,1)S(1)} %merge.1.refs_1_), channel_id=1, source_target_pairs={{0,1},{1,0},{2,3},{3,2},{4,5},{5,4},{6,7},{7,6},{8,9},{9,8},{10,11... | collective-permute-start | bytes 786440 | tf_op jit(solution)/shard_map/ppermute | solution.py:51
  71.8 1.5 %collective-permute-start.20 = (bf16[512,256]{1,0:T(8,128)(2,1)S(1)}, bf16[512,256]{1,0:T(8,128)(2,1)S(1)}, u32[]{:S(2)}, u32[]{:S(2)}) collective-permute-start(bf16[512,256]{1,0:T(8,128)(2,1)S(1)} %collective-permute-done.19.refs_3_), channel_id=1, source_target_pairs={{0,1},{1,0},{2,3},{3,2},{4,5},{5,4},{6,7},{7,6},{8,9},{9,8},{10,11... | collective-permute-start | bytes 786440 | tf_op jit(solution)/shard_map/ppermute | solution.py:51
  77.1 1.9 %collective-permute-start.23 = (bf16[384,256]{1,0:T(8,128)(2,1)S(1)}, bf16[384,256]{1,0:T(8,128)(2,1)S(1)}, u32[]{:S(2)}, u32[]{:S(2)}) collective-permute-start(bf16[384,256]{1,0:T(8,128)(2,1)S(1)} %get-tuple-element.58), channel_id=1, source_target_pairs={{0,1},{1,0},{2,3},{3,2},{4,5},{5,4},{6,7},{7,6},{8,9},{9,8},{10,11... | collective-permute-start | bytes 589832 | tf_op jit(solution)/shard_map/ppermute | solution.py:51
  77.3 7.7 %collective-permute-start.27 = (bf16[384,256]{1,0:T(8,128)(2,1)S(1)}, bf16[384,256]{1,0:T(8,128)(2,1)S(1)}, u32[]{:S(2)}, u32[]{:S(2)}) collective-permute-start(bf16[384,256]{1,0:T(8,128)(2,1)S(1)} %get-tuple-element.65), channel_id=1, source_target_pairs={{0,2},{1,3},{2,0},{3,1},{4,6},{5,7},{6,4},{7,5},{8,10},{9,11},{10,... | collective-permute-start | bytes 589832 | tf_op jit(solution)/shard_map/ppermute | solution.py:51
  77.9 10.3 %collective-permute-start.28 = (bf16[384,256]{1,0:T(8,128)(2,1)S(1)}, bf16[384,256]{1,0:T(8,128)(2,1)S(1)}, u32[]{:S(2)}, u32[]{:S(2)}) collective-permute-start(bf16[384,256]{1,0:T(8,128)(2,1)S(1)} %get-tuple-element.66), channel_id=1, source_target_pairs={{0,3},{1,2},{2,1},{3,0},{4,7},{5,6},{6,5},{7,4},{8,11},{9,10},{10,... | collective-permute-start | bytes 589832 | tf_op jit(solution)/shard_map/ppermute | solution.py:51
  81.0 9.7 %collective-permute-start.24 = (bf16[128,256]{1,0:T(8,128)(2,1)S(1)}, bf16[128,256]{1,0:T(8,128)(2,1)S(1)}, u32[]{:S(2)}, u32[]{:S(2)}) collective-permute-start(bf16[128,256]{1,0:T(8,128)(2,1)S(1)} %get-tuple-element.60), channel_id=1, source_target_pairs={{0,2},{1,3},{2,0},{3,1},{4,6},{5,7},{6,4},{7,5},{8,10},{9,11},{10,... | collective-permute-start | bytes 196616 | tf_op jit(solution)/shard_map/ppermute | solution.py:51
  81.6 9.4 %collective-permute-start.25 = (bf16[128,256]{1,0:T(8,128)(2,1)S(1)}, bf16[128,256]{1,0:T(8,128)(2,1)S(1)}, u32[]{:S(2)}, u32[]{:S(2)}) collective-permute-start(bf16[128,256]{1,0:T(8,128)(2,1)S(1)} %get-tuple-element.61), channel_id=1, source_target_pairs={{0,3},{1,2},{2,1},{3,0},{4,7},{5,6},{6,5},{7,4},{8,11},{9,10},{10,... | collective-permute-start | bytes 196616 | tf_op jit(solution)/shard_map/ppermute | solution.py:51
  82.8 8.1 %collective-permute-start.26 = (bf16[128,256]{1,0:T(8,128)(2,1)S(1)}, bf16[128,256]{1,0:T(8,128)(2,1)S(1)}, u32[]{:S(2)}, u32[]{:S(2)}) collective-permute-start(bf16[128,256]{1,0:T(8,128)(2,1)S(1)} %get-tuple-element.62), channel_id=1, source_target_pairs={{0,1},{1,0},{2,3},{3,2},{4,5},{5,4},{6,7},{7,6},{8,9},{9,8},{10,11... | collective-permute-start | bytes 196616 | tf_op jit(solution)/shard_map/ppermute | solution.py:51
  91.3 2.2 %collective-permute-start.31 = (f32[8,512]{1,0:T(8,128)S(1)}, f32[8,512]{1,0:T(8,128)S(1)}, u32[]{:S(2)}, u32[]{:S(2)}) collective-permute-start(f32[8,512]{1,0:T(8,128)S(1)} %get-tuple-element.70.refs_4_), channel_id=1, source_target_pairs={{0,1},{1,0},{2,3},{3,2},{4,5},{5,4},{6,7},{7,6},{8,9},{9,8},{10,11... | collective-permute-start | bytes 49160 | tf_op jit(solution)/shard_map/ppermute | solution.py:51
  91.8 3.2 %collective-permute-start.30 = (f32[8,512]{1,0:T(8,128)S(1)}, f32[8,512]{1,0:T(8,128)S(1)}, u32[]{:S(2)}, u32[]{:S(2)}) collective-permute-start(f32[8,512]{1,0:T(8,128)S(1)} %get-tuple-element.70.refs_4_), channel_id=1, source_target_pairs={{0,3},{1,2},{2,1},{3,0},{4,7},{5,6},{6,5},{7,4},{8,11},{9,10},{10,... | collective-permute-start | bytes 49160 | tf_op jit(solution)/shard_map/ppermute | solution.py:51
  92.1 3.8 %collective-permute-start.29 = (f32[8,512]{1,0:T(8,128)S(1)}, f32[8,512]{1,0:T(8,128)S(1)}, u32[]{:S(2)}, u32[]{:S(2)}) collective-permute-start(f32[8,512]{1,0:T(8,128)S(1)} %get-tuple-element.70.refs_4_), channel_id=1, source_target_pairs={{0,2},{1,3},{2,0},{3,1},{4,6},{5,7},{6,4},{7,5},{8,10},{9,11},{10,... | collective-permute-start | bytes 49160 | tf_op jit(solution)/shard_map/ppermute | solution.py:51
  (11 other events, 107.5 us)

commit v8 on v7

--- a/solution.py
+++ b/solution.py
@@ -519,7 +519,7 @@
     )
     near_got = send_req(near_answer, -1)
     outs = dict(zip(early, outs))
-    back = [j for j in (7, 6, 3, 2, 5, 4) if j < pages] + list(range(8, pages))
+    back = [j for j in (6, 7, 3, 2, 5, 4) if j < pages] + list(range(8, pages))
     answers = [send_req(outs[j], -j) for j in back]
     last = (near_answer,)
 

time: 99.1 us -> 98.8 us (level); the launches traced: 97.4 us -> 98.6 us
  waiting for transfers between devices: 27 us -> 30.4 us
  starting transfers between devices: 40.2 us -> 37.9 us
    ppermute x14, waiting for transfers between devices: 8.66 us -> 12.1 us  [send_req(): lax.ppermute(value, 'req', [(i, (i + by) % size) for i in range(size)])]
    ppermute x14, starting transfers between devices: 28.5 us -> 25.4 us  [send_req(): lax.ppermute(value, 'req', [(i, (i + by) % size) for i in range(size)])]
  transfers between devices with their start and end apart: 32 -> 32, of which waited for: 15 -> 16; matrix products, arithmetic and copies ran while one was open for 1% -> 1% of each run, Pallas kernels for 14% -> 14%
where the time goes in v8:
time: 98.8 us; the launch traced here: 98.6 us
  starting transfers between devices  37.9 us (38%)
  waiting for transfers between devices  30.4 us (31%)
  Pallas kernels  27.3 us (28%)
  local copies, waits for them, and re-layouts  2.13 us (2%)
    pallas_call x11, Pallas kernels, call(): pl.pallas_call(body, out_shape=outs, in_specs=list(ins) + [ANY] * len(aft...  27.3 us
    ppermute x14, starting transfers between devices, send_req(): lax.ppermute(value, 'req', [(i, (i + by) % size) for i in range(size)])  25.4 us
    ppermute x18, waiting for transfers between devices, send_tp(): return lax.ppermute(value, 'tp', [(i, i ^ flip) for i in range(size)])  18.3 us
    ppermute x18, starting transfers between devices, send_tp(): return lax.ppermute(value, 'tp', [(i, i ^ flip) for i in range(size)])  12.5 us
    ppermute x14, waiting for transfers between devices, send_req(): lax.ppermute(value, 'req', [(i, (i + by) % size) for i in range(size)])  12.1 us
  transfers between devices with their start and end apart: 32, of which 16 were waited for; matrix products, arithmetic and copies ran while one was open for 1% of the time, Pallas kernels for 14%

profile of v8, /device:TPU:0, one launch (start us, length us, event | category | flops | bytes accessed | tf_op | source)
XLA Modules:
  0.0 98.6 jit_solution(15891216970012901764)
XLA Ops:
  0.6 3.0 %collective-permute-start.1 = (bf16[512,256]{1,0:T(8,128)(2,1)}, bf16[512,256]{1,0:T(8,128)(2,1)S(1)}, u32[]{:S(2)}, u32[]{:S(2)}) collective-permute-start(bf16[512,256]{1,0:T(8,128)(2,1)} %refs_5_.3), channel_id=1, source_target_pairs={{0,2},{1,3},{2,0},{3,1},{4,6},{5,7},{6,4},{7,5},{8,10},{9,11},{10,... | collective-permute-start | bytes 786440 | tf_op jit(solution)/shard_map/ppermute | solution.py:51
  5.6 2.3 %tree.1 = (f32[512,64]{1,0:T(8,128)S(1)}, bf16[2,512,512]{2,1,0:T(8,128)(2,1)S(1)}) custom-call(s32[8]{0:T(128)S(1)} %copy-done.10, s32[2,256]{1,0:T(2,128)S(1)} %reshape.17.refs_1_), custom_call_target="tpu_custom_call" | custom-call | flops 469762048 | tf_op jit(solution)/shard_map/tree/pallas_call | solution.py:32
  8.6 3.3 %pages.1 = (bf16[2,8,128,256]{3,2,1,0:T(8,128)(2,1)S(1)}, bf16[2,8,128,256]{3,2,1,0:T(8,128)(2,1)S(1)}) custom-call(s32[8,8]{1,0:T(8,128)S(1)} %copy-done.5, bf16[64,128,2,256]{3,2,1,0:T(2,128)(2,1)} %refs_10_.1), custom_call_target="tpu_custom_call" | custom-call | flops 536870912 | tf_op jit(solution)/shard_map/pages/pallas_call | solution.py:32
  12.0 1.5 %collective-permute-done.2.refs_4_.refs_3_.refs_8_ = bf16[512,256]{1,0:T(8,128)(2,1)S(1)} collective-permute-done((bf16[512,256]{1,0:T(8,128)(2,1)S(1)}, bf16[512,256]{1,0:T(8,128)(2,1)S(1)}, u32[]{:S(2)}, u32[]{:S(2)}) %collective-permute-start.2) | collective-permute-done | bytes 262176 | tf_op jit(solution)/shard_map/ppermute | solution.py:51
  14.6 1.5 %collective-permute-start.4 = (bf16[528,256]{1,0:T(8,128)(2,1)S(1)}, bf16[528,256]{1,0:T(8,128)(2,1)S(1)}, u32[]{:S(2)}, u32[]{:S(2)}) collective-permute-start(bf16[528,256]{1,0:T(8,128)(2,1)S(1)} %get-tuple-element.48), channel_id=1, source_target_pairs={{0,4},{4,8},{8,12},{12,16},{16,20},{20,24},{24,28},{28,0},{1,5},{5... | collective-permute-start | bytes 811016 | tf_op jit(solution)/shard_map/ppermute | solution.py:46
  16.1 1.6 %collective-permute-start.10 = (bf16[144,256]{1,0:T(8,128)(2,1)S(1)}, bf16[144,256]{1,0:T(8,128)(2,1)S(1)}, u32[]{:S(2)}, u32[]{:S(2)}) collective-permute-start(bf16[144,256]{1,0:T(8,128)(2,1)S(1)} %get-tuple-element.42.refs_6_.refs_7_), channel_id=1, source_target_pairs={{0,8},{4,12},{8,16},{12,20},{16,24},{20,28},{24,0},{28,4},{1,9},{5... | collective-permute-start | bytes 221192 | tf_op jit(solution)/shard_map/ppermute | solution.py:46
  17.7 2.2 %collective-permute-start.9 = (bf16[144,256]{1,0:T(8,128)(2,1)S(1)}, bf16[144,256]{1,0:T(8,128)(2,1)S(1)}, u32[]{:S(2)}, u32[]{:S(2)}) collective-permute-start(bf16[144,256]{1,0:T(8,128)(2,1)S(1)} %get-tuple-element.42.refs_6_.refs_7_), channel_id=1, source_target_pairs={{0,24},{4,28},{8,0},{12,4},{16,8},{20,12},{24,16},{28,20},{1,25},{... | collective-permute-start | bytes 221192 | tf_op jit(solution)/shard_map/ppermute | solution.py:46
  20.0 1.4 %collective-permute-start.8 = (bf16[144,256]{1,0:T(8,128)(2,1)S(1)}, bf16[144,256]{1,0:T(8,128)(2,1)S(1)}, u32[]{:S(2)}, u32[]{:S(2)}) collective-permute-start(bf16[144,256]{1,0:T(8,128)(2,1)S(1)} %get-tuple-element.42.refs_6_.refs_7_), channel_id=1, source_target_pairs={{0,28},{4,0},{8,4},{12,8},{16,12},{20,16},{24,20},{28,24},{1,29},{... | collective-permute-start | bytes 221192 | tf_op jit(solution)/shard_map/ppermute | solution.py:46
  21.4 1.4 %collective-permute-done.10.refs_8_ = bf16[144,256]{1,0:T(8,128)(2,1)S(1)} collective-permute-done((bf16[144,256]{1,0:T(8,128)(2,1)S(1)}, bf16[144,256]{1,0:T(8,128)(2,1)S(1)}, u32[]{:S(2)}, u32[]{:S(2)}) %collective-permute-start.10) | collective-permute-done | bytes 73760 | tf_op jit(solution)/shard_map/ppermute | solution.py:46
  22.8 11.9 %collective-permute-start.6 = (bf16[144,256]{1,0:T(8,128)(2,1)S(1)}, bf16[144,256]{1,0:T(8,128)(2,1)S(1)}, u32[]{:S(2)}, u32[]{:S(2)}) collective-permute-start(bf16[144,256]{1,0:T(8,128)(2,1)S(1)} %get-tuple-element.42.refs_6_.refs_7_), channel_id=1, source_target_pairs={{0,20},{4,24},{8,28},{12,0},{16,4},{20,8},{24,12},{28,16},{1,21},{... | collective-permute-start | bytes 221192 | tf_op jit(solution)/shard_map/ppermute | solution.py:46
  34.6 1.9 %keys_values.1 = (bf16[512,256]{1,0:T(8,128)(2,1)S(1)}, bf16[512,256]{1,0:T(8,128)(2,1)S(1)}, bf16[512,2,256]{2,1,0:T(2,128)(2,1)}) custom-call(bf16[512,256]{1,0:T(8,128)(2,1)S(1)} %copy-done.1, bf16[512,256]{1,0:T(8,128)(2,1)S(1)} %collective-permute-done.refs_2_.refs_1_.refs_6_, bf16[512,256]{1,0:T(8,128)(2,1)S(1)} %collective-permute-done.1.refs_3_.refs_2_.refs_7_, ...), custom_call_target="tpu_custom_call" | custom-call | flops 536870912 | bytes 1048576 | tf_op jit(solution)/shard_map/keys_values/pallas_call | solution.py:32
  36.6 3.3 %collective-permute-done.5.refs_3_ = bf16[144,256]{1,0:T(8,128)(2,1)S(1)} collective-permute-done((bf16[144,256]{1,0:T(8,128)(2,1)S(1)}, bf16[144,256]{1,0:T(8,128)(2,1)S(1)}, u32[]{:S(2)}, u32[]{:S(2)}) %collective-permute-start.5) | collective-permute-done | bytes 73760 | tf_op jit(solution)/shard_map/ppermute | solution.py:46
  39.9 6.5 %visitors_early.1 = (bf16[560,256]{1,0:T(8,128)(2,1)S(1)}, bf16[144,256]{1,0:T(8,128)(2,1)S(1)}, bf16[144,256]{1,0:T(8,128)(2,1)S(1)}, bf16[144,256]{1,0:T(8,128...) custom-call(bf16[528,256]{1,0:T(8,128)(2,1)S(1)} %collective-permute-done.4.ref, ...), custom_call_target="tpu_custom_call" | custom-call | tf_op jit(solution)/shard_map/visitors_early/pallas_call | solution.py:32
  49.0 3.3 %collective-permute-start.14 = (bf16[144,256]{1,0:T(8,128)(2,1)S(1)}, bf16[144,256]{1,0:T(8,128)(2,1)S(1)}, u32[]{:S(2)}, u32[]{:S(2)}) collective-permute-start(bf16[144,256]{1,0:T(8,128)(2,1)S(1)} %get-tuple-element.52), channel_id=1, source_target_pairs={{0,20},{4,24},{8,28},{12,0},{16,4},{20,8},{24,12},{28,16},{1,21},{... | collective-permute-start | bytes 221192 | tf_op jit(solution)/shard_map/ppermute | solution.py:46
  52.3 4.6 %collective-permute-done.12.refs_4_ = bf16[144,256]{1,0:T(8,128)(2,1)S(1)} collective-permute-done((bf16[144,256]{1,0:T(8,128)(2,1)S(1)}, bf16[144,256]{1,0:T(8,128)(2,1)S(1)}, u32[]{:S(2)}, u32[]{:S(2)}) %collective-permute-start.12) | collective-permute-done | bytes 73760 | tf_op jit(solution)/shard_map/ppermute | solution.py:46
  56.9 1.5 %collective-permute-start.17 = (bf16[144,256]{1,0:T(8,128)(2,1)S(1)}, bf16[144,256]{1,0:T(8,128)(2,1)S(1)}, u32[]{:S(2)}, u32[]{:S(2)}) collective-permute-start(bf16[144,256]{1,0:T(8,128)(2,1)S(1)} %get-tuple-element.55), channel_id=1, source_target_pairs={{0,16},{4,20},{8,24},{12,28},{16,0},{20,4},{24,8},{28,12},{1,17},{... | collective-permute-start | bytes 221192 | tf_op jit(solution)/shard_map/ppermute | solution.py:46
  58.4 2.7 %local_attention.1 = (f32[512,256]{1,0:T(8,128)S(1)}, f32[16,256]{1,0:T(8,128)S(1)}, bf16[144,256]{1,0:T(8,128)(2,1)}) custom-call(s32[8]{0:T(128)S(1)} %copy-done.7, bf16[512,256]{1,0:T(8,128)(2,1)S(1)} %get-tuple-element.40.refs_1_, bf16[512,256]{1,0:T(8,128)(2,1)S(1)} %get-tuple-element.43.refs_2_.refs_11_, ...), custom_call_target="tpu_custom_call" | custom-call | tf_op jit(solution)/shard_map/local_attention/pallas_call | solution.py:32
  61.3 1.8 %collective-permute-done.16.refs_8_ = bf16[144,256]{1,0:T(8,128)(2,1)S(1)} collective-permute-done((bf16[144,256]{1,0:T(8,128)(2,1)S(1)}, bf16[144,256]{1,0:T(8,128)(2,1)S(1)}, u32[]{:S(2)}, u32[]{:S(2)}) %collective-permute-start.16) | collective-permute-done | bytes 73760 | tf_op jit(solution)/shard_map/ppermute | solution.py:46
  63.8 1.9 %merge.1.refs_1_ = bf16[512,256]{1,0:T(8,128)(2,1)S(1)} custom-call(s32[8]{0:T(128)S(1)} %copy-done.7, f32[512,256]{1,0:T(8,128)S(1)} %get-tuple-element.46.refs_1_, f32[16,256]{1,0:T(8,128)S(1)} %get-tuple-element.47.refs_2_, bf16[560,256]{1,0:T(8,128)(2,1)S(1)} %collective-permute-done.11.refs_3_, bf16[144,256]{1,0:T(8,128)(2,1)S(1)} %collective-permute-done.12.refs_4_, ...), custom_call_target="tpu_custom_call" | custom-call | tf_op jit(solution)/shard_map/merge/pallas_call | solution.py:32
  65.7 1.5 %collective-permute-start.19 = (bf16[512,256]{1,0:T(8,128)(2,1)S(1)}, bf16[512,256]{1,0:T(8,128)(2,1)S(1)}, u32[]{:S(2)}, u32[]{:S(2)}) collective-permute-start(bf16[512,256]{1,0:T(8,128)(2,1)S(1)} %merge.1.refs_1_), channel_id=1, source_target_pairs={{0,2},{1,3},{2,0},{3,1},{4,6},{5,7},{6,4},{7,5},{8,10},{9,11},{10,... | collective-permute-start | bytes 786440 | tf_op jit(solution)/shard_map/ppermute | solution.py:51
  67.7 4.5 %collective-permute-done.19.refs_3_ = bf16[512,256]{1,0:T(8,128)(2,1)S(1)} collective-permute-done((bf16[512,256]{1,0:T(8,128)(2,1)S(1)}, bf16[512,256]{1,0:T(8,128)(2,1)S(1)}, u32[]{:S(2)}, u32[]{:S(2)}) %collective-permute-start.19) | collective-permute-done | bytes 262176 | tf_op jit(solution)/shard_map/ppermute | solution.py:51
  72.2 1.5 %collective-permute-done.20.refs_4_ = bf16[512,256]{1,0:T(8,128)(2,1)S(1)} collective-permute-done((bf16[512,256]{1,0:T(8,128)(2,1)S(1)}, bf16[512,256]{1,0:T(8,128)(2,1)S(1)}, u32[]{:S(2)}, u32[]{:S(2)}) %collective-permute-start.20) | collective-permute-done | bytes 262176 | tf_op jit(solution)/shard_map/ppermute | solution.py:51
  73.7 3.7 %forward_short.1 = (bf16[384,256]{1,0:T(8,128)(2,1)S(1)}, bf16[384,256]{1,0:T(8,128)(2,1)S(1)}, bf16[384,256]{1,0:T(8,128)(2,1)S(1)}, bf16[384,256]{1,0:T(8,128)(2,1)S(1)}, bf16[384,256]{1,0:T(8,128)(2,1)S(1)}) custom-call(s32[8]{0:T(128)S(1)} %copy-done.7, bf16[512,256]{1,0:T(8,128)(2,1)S(1)} %merge.1.refs_1_, ...), custom_call_target="tpu_custom_call" | custom-call | flops 2415919104 | bytes 6291456 | tf_op jit(solution)/shard_map/forward_short/pallas_call | solution.py:32
  77.6 1.4 %collective-permute-start.27 = (bf16[384,256]{1,0:T(8,128)(2,1)S(1)}, bf16[384,256]{1,0:T(8,128)(2,1)S(1)}, u32[]{:S(2)}, u32[]{:S(2)}) collective-permute-start(bf16[384,256]{1,0:T(8,128)(2,1)S(1)} %get-tuple-element.65), channel_id=1, source_target_pairs={{0,2},{1,3},{2,0},{3,1},{4,6},{5,7},{6,4},{7,5},{8,10},{9,11},{10,... | collective-permute-start | bytes 589832 | tf_op jit(solution)/shard_map/ppermute | solution.py:51
  79.4 2.0 %forward_long.1 = (bf16[128,256]{1,0:T(8,128)(2,1)S(1)}, bf16[128,256]{1,0:T(8,128)(2,1)S(1)}, bf16[128,256]{1,0:T(8,128)(2,1)S(1)}, bf16[128,256]{1,0:T(8,128)(2,1)S(1)}, bf16[128,256]{1,0:T(8,128)(2,1)S(1)}) custom-call(s32[8]{0:T(128)S(1)} %copy-done.7, bf16[512,256]{1,0:T(8,128)(2,1)S(1)} %merge.1.refs_1_, ...), custom_call_target="tpu_custom_call" | custom-call | flops 805306368 | bytes 6291456 | tf_op jit(solution)/shard_map/forward_long/pallas_call | solution.py:32
  81.3 1.4 %collective-permute-start.24 = (bf16[128,256]{1,0:T(8,128)(2,1)S(1)}, bf16[128,256]{1,0:T(8,128)(2,1)S(1)}, u32[]{:S(2)}, u32[]{:S(2)}) collective-permute-start(bf16[128,256]{1,0:T(8,128)(2,1)S(1)} %get-tuple-element.60), channel_id=1, source_target_pairs={{0,2},{1,3},{2,0},{3,1},{4,6},{5,7},{6,4},{7,5},{8,10},{9,11},{10,... | collective-permute-start | bytes 196616 | tf_op jit(solution)/shard_map/ppermute | solution.py:51
  83.6 1.8 %collective-permute-done.27.refs_6_ = bf16[384,256]{1,0:T(8,128)(2,1)S(1)} collective-permute-done((bf16[384,256]{1,0:T(8,128)(2,1)S(1)}, bf16[384,256]{1,0:T(8,128)(2,1)S(1)}, u32[]{:S(2)}, u32[]{:S(2)}) %collective-permute-start.27) | collective-permute-done | bytes 196640 | tf_op jit(solution)/shard_map/ppermute | solution.py:51
  85.4 3.1 %collective-permute-done.28.refs_7_ = bf16[384,256]{1,0:T(8,128)(2,1)S(1)} collective-permute-done((bf16[384,256]{1,0:T(8,128)(2,1)S(1)}, bf16[384,256]{1,0:T(8,128)(2,1)S(1)}, u32[]{:S(2)}, u32[]{:S(2)}) %collective-permute-start.28) | collective-permute-done | bytes 196640 | tf_op jit(solution)/shard_map/ppermute | solution.py:51
  88.5 2.5 %collective-permute-done.24.refs_1_ = bf16[128,256]{1,0:T(8,128)(2,1)S(1)} collective-permute-done((bf16[128,256]{1,0:T(8,128)(2,1)S(1)}, bf16[128,256]{1,0:T(8,128)(2,1)S(1)}, u32[]{:S(2)}, u32[]{:S(2)}) %collective-permute-start.24) | collective-permute-done | bytes 65568 | tf_op jit(solution)/shard_map/ppermute | solution.py:51
  93.9 1.4 %collective-permute-done.30.refs_6_ = f32[8,512]{1,0:T(8,128)S(1)} collective-permute-done((f32[8,512]{1,0:T(8,128)S(1)}, f32[8,512]{1,0:T(8,128)S(1)}, u32[]{:S(2)}, u32[]{:S(2)}) %collective-permute-start.30) | collective-permute-done | bytes 16416 | tf_op jit(solution)/shard_map/ppermute | solution.py:51
  95.3 1.7 %collective-permute-done.29.refs_5_ = f32[8,512]{1,0:T(8,128)S(1)} collective-permute-done((f32[8,512]{1,0:T(8,128)S(1)}, f32[8,512]{1,0:T(8,128)S(1)}, u32[]{:S(2)}, u32[]{:S(2)}) %collective-permute-start.29) | collective-permute-done | bytes 16416 | tf_op jit(solution)/shard_map/ppermute | solution.py:51
  97.0 1.6 %finish.1 = bf16[512,256]{1,0:T(8,128)(2,1)} custom-call(s32[8]{0:T(128)S(1)} %copy-done.7, f32[1,1024]{1,0:T(1,128)S(1)} %bitcast.8, f32[128,256]{1,0:T(8,128)S(1)} %get-tuple-element.68.refs_2_, f32[384,256]{1,0:T(8,128)S(1)} %get-tuple-element.69.refs_3_, f32[8,512]{1,0:T(8,128)S(1)} %get-tuple-element.70.refs_4_, ...), custom_call_target="tpu_custom_call" | custom-call | tf_op jit(solution)/shard_map/finish/pallas_call | solution.py:32
  (66 shorter events, 12.2 us)
Async XLA Ops:
  0.6 11.3 %collective-permute-start.1 = (bf16[512,256]{1,0:T(8,128)(2,1)}, bf16[512,256]{1,0:T(8,128)(2,1)S(1)}, u32[]{:S(2)}, u32[]{:S(2)}) collective-permute-start(bf16[512,256]{1,0:T(8,128)(2,1)} %refs_5_.3), channel_id=1, source_target_pairs={{0,2},{1,3},{2,0},{3,1},{4,6},{5,7},{6,4},{7,5},{8,10},{9,11},{10,... | collective-permute-start | bytes 786440 | tf_op jit(solution)/shard_map/ppermute | solution.py:51
  3.7 8.3 %collective-permute-start.3 = (bf16[256,1024]{1,0:T(8,128)(2,1)}, bf16[256,1024]{1,0:T(8,128)(2,1)S(1)}, u32[]{:S(2)}, u32[]{:S(2)}) collective-permute-start(bf16[256,1024]{1,0:T(8,128)(2,1)} %refs_9_.5), channel_id=1, source_target_pairs={{0,1},{1,0},{2,3},{3,2},{4,5},{5,4},{6,7},{7,6},{8,9},{9,8},{10,11... | collective-permute-start | bytes 1572872 | tf_op jit(solution)/shard_map/ppermute | solution.py:51
  3.7 8.3 %collective-permute-start = (bf16[512,256]{1,0:T(8,128)(2,1)}, bf16[512,256]{1,0:T(8,128)(2,1)S(1)}, u32[]{:S(2)}, u32[]{:S(2)}) collective-permute-start(bf16[512,256]{1,0:T(8,128)(2,1)} %refs_5_.3), channel_id=1, source_target_pairs={{0,1},{1,0},{2,3},{3,2},{4,5},{5,4},{6,7},{7,6},{8,9},{9,8},{10,11... | collective-permute-start | bytes 786440 | tf_op jit(solution)/shard_map/ppermute | solution.py:51
  11.9 1.6 %collective-permute-start.2 = (bf16[512,256]{1,0:T(8,128)(2,1)S(1)}, bf16[512,256]{1,0:T(8,128)(2,1)S(1)}, u32[]{:S(2)}, u32[]{:S(2)}) collective-permute-start(bf16[512,256]{1,0:T(8,128)(2,1)S(1)} %collective-permute-done.1.refs_3_.refs_2_.refs_7_), channel_id=1, source_target_pairs={{0,1},{1,0},{2,3},{3,2},{4,5},{5,4},{6,7},{7,6},{8,9},{9,8},{10,11... | collective-permute-start | bytes 786440 | tf_op jit(solution)/shard_map/ppermute | solution.py:51
  14.6 25.3 %collective-permute-start.4 = (bf16[528,256]{1,0:T(8,128)(2,1)S(1)}, bf16[528,256]{1,0:T(8,128)(2,1)S(1)}, u32[]{:S(2)}, u32[]{:S(2)}) collective-permute-start(bf16[528,256]{1,0:T(8,128)(2,1)S(1)} %get-tuple-element.48), channel_id=1, source_target_pairs={{0,4},{4,8},{8,12},{12,16},{16,20},{20,24},{24,28},{28,0},{1,5},{5... | collective-permute-start | bytes 811016 | tf_op jit(solution)/shard_map/ppermute | solution.py:46
  16.1 6.6 %collective-permute-start.10 = (bf16[144,256]{1,0:T(8,128)(2,1)S(1)}, bf16[144,256]{1,0:T(8,128)(2,1)S(1)}, u32[]{:S(2)}, u32[]{:S(2)}) collective-permute-start(bf16[144,256]{1,0:T(8,128)(2,1)S(1)} %get-tuple-element.42.refs_6_.refs_7_), channel_id=1, source_target_pairs={{0,8},{4,12},{8,16},{12,20},{16,24},{20,28},{24,0},{28,4},{1,9},{5... | collective-permute-start | bytes 221192 | tf_op jit(solution)/shard_map/ppermute | solution.py:46
  17.7 16.9 %collective-permute-start.9 = (bf16[144,256]{1,0:T(8,128)(2,1)S(1)}, bf16[144,256]{1,0:T(8,128)(2,1)S(1)}, u32[]{:S(2)}, u32[]{:S(2)}) collective-permute-start(bf16[144,256]{1,0:T(8,128)(2,1)S(1)} %get-tuple-element.42.refs_6_.refs_7_), channel_id=1, source_target_pairs={{0,24},{4,28},{8,0},{12,4},{16,8},{20,12},{24,16},{28,20},{1,25},{... | collective-permute-start | bytes 221192 | tf_op jit(solution)/shard_map/ppermute | solution.py:46
  20.0 16.6 %collective-permute-start.8 = (bf16[144,256]{1,0:T(8,128)(2,1)S(1)}, bf16[144,256]{1,0:T(8,128)(2,1)S(1)}, u32[]{:S(2)}, u32[]{:S(2)}) collective-permute-start(bf16[144,256]{1,0:T(8,128)(2,1)S(1)} %get-tuple-element.42.refs_6_.refs_7_), channel_id=1, source_target_pairs={{0,28},{4,0},{8,4},{12,8},{16,12},{20,16},{24,20},{28,24},{1,29},{... | collective-permute-start | bytes 221192 | tf_op jit(solution)/shard_map/ppermute | solution.py:46
  21.4 15.1 %collective-permute-start.7 = (bf16[144,256]{1,0:T(8,128)(2,1)S(1)}, bf16[144,256]{1,0:T(8,128)(2,1)S(1)}, u32[]{:S(2)}, u32[]{:S(2)}) collective-permute-start(bf16[144,256]{1,0:T(8,128)(2,1)S(1)} %get-tuple-element.42.refs_6_.refs_7_), channel_id=1, source_target_pairs={{0,12},{4,16},{8,20},{12,24},{16,28},{20,0},{24,4},{28,8},{1,13},{... | collective-permute-start | bytes 221192 | tf_op jit(solution)/shard_map/ppermute | solution.py:46
  22.8 13.9 %collective-permute-start.6 = (bf16[144,256]{1,0:T(8,128)(2,1)S(1)}, bf16[144,256]{1,0:T(8,128)(2,1)S(1)}, u32[]{:S(2)}, u32[]{:S(2)}) collective-permute-start(bf16[144,256]{1,0:T(8,128)(2,1)S(1)} %get-tuple-element.42.refs_6_.refs_7_), channel_id=1, source_target_pairs={{0,20},{4,24},{8,28},{12,0},{16,4},{20,8},{24,12},{28,16},{1,21},{... | collective-permute-start | bytes 221192 | tf_op jit(solution)/shard_map/ppermute | solution.py:46
  34.6 5.3 %collective-permute-start.5 = (bf16[144,256]{1,0:T(8,128)(2,1)S(1)}, bf16[144,256]{1,0:T(8,128)(2,1)S(1)}, u32[]{:S(2)}, u32[]{:S(2)}) collective-permute-start(bf16[144,256]{1,0:T(8,128)(2,1)S(1)} %get-tuple-element.42.refs_6_.refs_7_), channel_id=1, source_target_pairs={{0,16},{4,20},{8,24},{12,28},{16,0},{20,4},{24,8},{28,12},{1,17},{... | collective-permute-start | bytes 221192 | tf_op jit(solution)/shard_map/ppermute | solution.py:46
  46.5 20.7 %collective-permute-start.21 = (bf16[256,1024]{1,0:T(8,128)(2,1)S(1)}, bf16[256,1024]{1,0:T(8,128)(2,1)S(1)}, u32[]{:S(2)}, u32[]{:S(2)}) collective-permute-start(bf16[256,1024]{1,0:T(8,128)(2,1)S(1)} %copy-done.4), channel_id=1, source_target_pairs={{0,2},{1,3},{2,0},{3,1},{4,6},{5,7},{6,4},{7,5},{8,10},{9,11},{10,... | collective-permute-start | bytes 1572872 | tf_op jit(solution)/shard_map/ppermute | solution.py:51
  47.0 16.8 %collective-permute-start.11 = (bf16[560,256]{1,0:T(8,128)(2,1)S(1)}, bf16[560,256]{1,0:T(8,128)(2,1)S(1)}, u32[]{:S(2)}, u32[]{:S(2)}) collective-permute-start(bf16[560,256]{1,0:T(8,128)(2,1)S(1)} %get-tuple-element.49), channel_id=1, source_target_pairs={{0,28},{4,0},{8,4},{12,8},{16,12},{20,16},{24,20},{28,24},{1,29},{... | collective-permute-start | bytes 860168 | tf_op jit(solution)/shard_map/ppermute | solution.py:46
  47.0 9.9 %collective-permute-start.12 = (bf16[144,256]{1,0:T(8,128)(2,1)S(1)}, bf16[144,256]{1,0:T(8,128)(2,1)S(1)}, u32[]{:S(2)}, u32[]{:S(2)}) collective-permute-start(bf16[144,256]{1,0:T(8,128)(2,1)S(1)} %get-tuple-element.50), channel_id=1, source_target_pairs={{0,8},{4,12},{8,16},{12,20},{16,24},{20,28},{24,0},{28,4},{1,9},{5... | collective-permute-start | bytes 221192 | tf_op jit(solution)/shard_map/ppermute | solution.py:46
  47.7 9.2 %collective-permute-start.13 = (bf16[144,256]{1,0:T(8,128)(2,1)S(1)}, bf16[144,256]{1,0:T(8,128)(2,1)S(1)}, u32[]{:S(2)}, u32[]{:S(2)}) collective-permute-start(bf16[144,256]{1,0:T(8,128)(2,1)S(1)} %get-tuple-element.51), channel_id=1, source_target_pairs={{0,4},{4,8},{8,12},{12,16},{16,20},{20,24},{24,28},{28,0},{1,5},{5... | collective-permute-start | bytes 221192 | tf_op jit(solution)/shard_map/ppermute | solution.py:46
  49.0 7.9 %collective-permute-start.14 = (bf16[144,256]{1,0:T(8,128)(2,1)S(1)}, bf16[144,256]{1,0:T(8,128)(2,1)S(1)}, u32[]{:S(2)}, u32[]{:S(2)}) collective-permute-start(bf16[144,256]{1,0:T(8,128)(2,1)S(1)} %get-tuple-element.52), channel_id=1, source_target_pairs={{0,20},{4,24},{8,28},{12,0},{16,4},{20,8},{24,12},{28,16},{1,21},{... | collective-permute-start | bytes 221192 | tf_op jit(solution)/shard_map/ppermute | solution.py:46
  56.9 4.4 %collective-permute-start.15 = (bf16[144,256]{1,0:T(8,128)(2,1)S(1)}, bf16[144,256]{1,0:T(8,128)(2,1)S(1)}, u32[]{:S(2)}, u32[]{:S(2)}) collective-permute-start(bf16[144,256]{1,0:T(8,128)(2,1)S(1)} %get-tuple-element.53), channel_id=1, source_target_pairs={{0,24},{4,28},{8,0},{12,4},{16,8},{20,12},{24,16},{28,20},{1,25},{... | collective-permute-start | bytes 221192 | tf_op jit(solution)/shard_map/ppermute | solution.py:46
  56.9 6.2 %collective-permute-start.16 = (bf16[144,256]{1,0:T(8,128)(2,1)S(1)}, bf16[144,256]{1,0:T(8,128)(2,1)S(1)}, u32[]{:S(2)}, u32[]{:S(2)}) collective-permute-start(bf16[144,256]{1,0:T(8,128)(2,1)S(1)} %get-tuple-element.54), channel_id=1, source_target_pairs={{0,12},{4,16},{8,20},{12,24},{16,28},{20,0},{24,4},{28,8},{1,13},{... | collective-permute-start | bytes 221192 | tf_op jit(solution)/shard_map/ppermute | solution.py:46
  56.9 6.9 %collective-permute-start.17 = (bf16[144,256]{1,0:T(8,128)(2,1)S(1)}, bf16[144,256]{1,0:T(8,128)(2,1)S(1)}, u32[]{:S(2)}, u32[]{:S(2)}) collective-permute-start(bf16[144,256]{1,0:T(8,128)(2,1)S(1)} %get-tuple-element.55), channel_id=1, source_target_pairs={{0,16},{4,20},{8,24},{12,28},{16,0},{20,4},{24,8},{28,12},{1,17},{... | collective-permute-start | bytes 221192 | tf_op jit(solution)/shard_map/ppermute | solution.py:46
  65.7 6.4 %collective-permute-start.19 = (bf16[512,256]{1,0:T(8,128)(2,1)S(1)}, bf16[512,256]{1,0:T(8,128)(2,1)S(1)}, u32[]{:S(2)}, u32[]{:S(2)}) collective-permute-start(bf16[512,256]{1,0:T(8,128)(2,1)S(1)} %merge.1.refs_1_), channel_id=1, source_target_pairs={{0,2},{1,3},{2,0},{3,1},{4,6},{5,7},{6,4},{7,5},{8,10},{9,11},{10,... | collective-permute-start | bytes 786440 | tf_op jit(solution)/shard_map/ppermute | solution.py:51
  67.2 6.5 %collective-permute-start.22 = (bf16[256,1024]{1,0:T(8,128)(2,1)S(1)}, bf16[256,1024]{1,0:T(8,128)(2,1)S(1)}, u32[]{:S(2)}, u32[]{:S(2)}) collective-permute-start(bf16[256,1024]{1,0:T(8,128)(2,1)S(1)} %collective-permute-done.21.refs_11_), channel_id=1, source_target_pairs={{0,1},{1,0},{2,3},{3,2},{4,5},{5,4},{6,7},{7,6},{8,9},{9,8},{10,11... | collective-permute-start | bytes 1572872 | tf_op jit(solution)/shard_map/ppermute | solution.py:51
  67.2 5.0 %collective-permute-start.18 = (bf16[512,256]{1,0:T(8,128)(2,1)S(1)}, bf16[512,256]{1,0:T(8,128)(2,1)S(1)}, u32[]{:S(2)}, u32[]{:S(2)}) collective-permute-start(bf16[512,256]{1,0:T(8,128)(2,1)S(1)} %merge.1.refs_1_), channel_id=1, source_target_pairs={{0,1},{1,0},{2,3},{3,2},{4,5},{5,4},{6,7},{7,6},{8,9},{9,8},{10,11... | collective-permute-start | bytes 786440 | tf_op jit(solution)/shard_map/ppermute | solution.py:51
  72.1 1.5 %collective-permute-start.20 = (bf16[512,256]{1,0:T(8,128)(2,1)S(1)}, bf16[512,256]{1,0:T(8,128)(2,1)S(1)}, u32[]{:S(2)}, u32[]{:S(2)}) collective-permute-start(bf16[512,256]{1,0:T(8,128)(2,1)S(1)} %collective-permute-done.19.refs_3_), channel_id=1, source_target_pairs={{0,1},{1,0},{2,3},{3,2},{4,5},{5,4},{6,7},{7,6},{8,9},{9,8},{10,11... | collective-permute-start | bytes 786440 | tf_op jit(solution)/shard_map/ppermute | solution.py:51
  77.4 1.9 %collective-permute-start.23 = (bf16[384,256]{1,0:T(8,128)(2,1)S(1)}, bf16[384,256]{1,0:T(8,128)(2,1)S(1)}, u32[]{:S(2)}, u32[]{:S(2)}) collective-permute-start(bf16[384,256]{1,0:T(8,128)(2,1)S(1)} %get-tuple-element.58), channel_id=1, source_target_pairs={{0,1},{1,0},{2,3},{3,2},{4,5},{5,4},{6,7},{7,6},{8,9},{9,8},{10,11... | collective-permute-start | bytes 589832 | tf_op jit(solution)/shard_map/ppermute | solution.py:51
  77.6 7.7 %collective-permute-start.27 = (bf16[384,256]{1,0:T(8,128)(2,1)S(1)}, bf16[384,256]{1,0:T(8,128)(2,1)S(1)}, u32[]{:S(2)}, u32[]{:S(2)}) collective-permute-start(bf16[384,256]{1,0:T(8,128)(2,1)S(1)} %get-tuple-element.65), channel_id=1, source_target_pairs={{0,2},{1,3},{2,0},{3,1},{4,6},{5,7},{6,4},{7,5},{8,10},{9,11},{10,... | collective-permute-start | bytes 589832 | tf_op jit(solution)/shard_map/ppermute | solution.py:51
  79.0 9.4 %collective-permute-start.28 = (bf16[384,256]{1,0:T(8,128)(2,1)S(1)}, bf16[384,256]{1,0:T(8,128)(2,1)S(1)}, u32[]{:S(2)}, u32[]{:S(2)}) collective-permute-start(bf16[384,256]{1,0:T(8,128)(2,1)S(1)} %get-tuple-element.66), channel_id=1, source_target_pairs={{0,3},{1,2},{2,1},{3,0},{4,7},{5,6},{6,5},{7,4},{8,11},{9,10},{10,... | collective-permute-start | bytes 589832 | tf_op jit(solution)/shard_map/ppermute | solution.py:51
  81.3 9.6 %collective-permute-start.24 = (bf16[128,256]{1,0:T(8,128)(2,1)S(1)}, bf16[128,256]{1,0:T(8,128)(2,1)S(1)}, u32[]{:S(2)}, u32[]{:S(2)}) collective-permute-start(bf16[128,256]{1,0:T(8,128)(2,1)S(1)} %get-tuple-element.60), channel_id=1, source_target_pairs={{0,2},{1,3},{2,0},{3,1},{4,6},{5,7},{6,4},{7,5},{8,10},{9,11},{10,... | collective-permute-start | bytes 196616 | tf_op jit(solution)/shard_map/ppermute | solution.py:51
  82.7 8.5 %collective-permute-start.25 = (bf16[128,256]{1,0:T(8,128)(2,1)S(1)}, bf16[128,256]{1,0:T(8,128)(2,1)S(1)}, u32[]{:S(2)}, u32[]{:S(2)}) collective-permute-start(bf16[128,256]{1,0:T(8,128)(2,1)S(1)} %get-tuple-element.61), channel_id=1, source_target_pairs={{0,3},{1,2},{2,1},{3,0},{4,7},{5,6},{6,5},{7,4},{8,11},{9,10},{10,... | collective-permute-start | bytes 196616 | tf_op jit(solution)/shard_map/ppermute | solution.py:51
  83.1 8.1 %collective-permute-start.26 = (bf16[128,256]{1,0:T(8,128)(2,1)S(1)}, bf16[128,256]{1,0:T(8,128)(2,1)S(1)}, u32[]{:S(2)}, u32[]{:S(2)}) collective-permute-start(bf16[128,256]{1,0:T(8,128)(2,1)S(1)} %get-tuple-element.62), channel_id=1, source_target_pairs={{0,1},{1,0},{2,3},{3,2},{4,5},{5,4},{6,7},{7,6},{8,9},{9,8},{10,11... | collective-permute-start | bytes 196616 | tf_op jit(solution)/shard_map/ppermute | solution.py:51
  91.7 2.2 %collective-permute-start.31 = (f32[8,512]{1,0:T(8,128)S(1)}, f32[8,512]{1,0:T(8,128)S(1)}, u32[]{:S(2)}, u32[]{:S(2)}) collective-permute-start(f32[8,512]{1,0:T(8,128)S(1)} %get-tuple-element.70.refs_4_), channel_id=1, source_target_pairs={{0,1},{1,0},{2,3},{3,2},{4,5},{5,4},{6,7},{7,6},{8,9},{9,8},{10,11... | collective-permute-start | bytes 49160 | tf_op jit(solution)/shard_map/ppermute | solution.py:51
  92.1 3.2 %collective-permute-start.30 = (f32[8,512]{1,0:T(8,128)S(1)}, f32[8,512]{1,0:T(8,128)S(1)}, u32[]{:S(2)}, u32[]{:S(2)}) collective-permute-start(f32[8,512]{1,0:T(8,128)S(1)} %get-tuple-element.70.refs_4_), channel_id=1, source_target_pairs={{0,3},{1,2},{2,1},{3,0},{4,7},{5,6},{6,5},{7,4},{8,11},{9,10},{10,... | collective-permute-start | bytes 49160 | tf_op jit(solution)/shard_map/ppermute | solution.py:51
  93.2 3.8 %collective-permute-start.29 = (f32[8,512]{1,0:T(8,128)S(1)}, f32[8,512]{1,0:T(8,128)S(1)}, u32[]{:S(2)}, u32[]{:S(2)}) collective-permute-start(f32[8,512]{1,0:T(8,128)S(1)} %get-tuple-element.70.refs_4_), channel_id=1, source_target_pairs={{0,2},{1,3},{2,0},{3,1},{4,6},{5,7},{6,4},{7,5},{8,10},{9,11},{10,... | collective-permute-start | bytes 49160 | tf_op jit(solution)/shard_map/ppermute | solution.py:51
  (11 other events, 111.8 us)
